TPU v7x, 32 devices: a whole 2x2x4 slice. The times are simulated.
32 devices in a mesh: row: 16 (over z, x, core), col: 2 (over y).
Axes of the slice: x: 2, y: 2, z: 4, core: 2. Of those that a mesh axis runs over, the one named last changes fastest.
Arguments:
- activations: bfloat16 [256, 8192], P('col', 'row'), may hold values from -6 to 6
- cotangent: bfloat16 [256, 14336], P('row', 'col'), may hold values from -0.15625 to 0.15625
- accumulated: bfloat16 [8192, 14336], P('row', 'col'), may hold values from -3 to 3
- band_old: float32 [8192, 8, 512], P('row', 'col'), may hold values from -6 to 6
- diagonal_old: float32 [8192, 512], P(('row', 'col')), may hold values from -6 to 6
Outputs:
- band_new: float32 [8192, 8, 512], P('row', 'col')
- diagonal_new: float32 [8192, 512], P(('row', 'col'))
All inputs are finite; a program needn't handle non-finite values.
Results may differ from a plain program's by a relative error of at most 0.0018.
Values may be sent and summed in bfloat16 or wider, within the bound.
No kernel may reach another device: no remote copies, remote signals or barrier semaphores. Data moves between devices by JAX's collectives and lax.ppermute only.
A program may use at most 128 MiB of HBM per device.

v0:
```python
import jax
import jax.numpy as jnp
from jax import lax
from jax.sharding import PartitionSpec as P

decay_rate = 0.95


def from_behind(shard, axis, by):
    count = lax.axis_size(axis)
    return lax.ppermute(shard, axis, [(i, (i + by) % count) for i in range(count)])


def gradient_tile(columns, cotangent_all, accumulated):
    product = lax.dot_general(
        columns, cotangent_all, (((0,), (0,)), ((), ())), preferred_element_type=jnp.float32
    )
    return (product + accumulated.astype(jnp.float32)).astype(jnp.bfloat16)


def block_product(left, right):
    return lax.dot_general(
        left, right, (((1,), (1,)), ((), ())), preferred_element_type=jnp.float32
    )


def store_block(partials, gram_block, offset):
    start = jnp.asarray(offset, jnp.int32) - 1
    anchor_index = jnp.zeros((), jnp.int32)
    return lax.dynamic_update_slice(
        partials, gram_block[:, None, :], (anchor_index, start, anchor_index)
    )


def body(activations, cotangent, accumulated, band_old, diagonal_old):
    columns = lax.all_gather(activations, "col", axis=0, tiled=True)
    cotangent_all = lax.all_gather(cotangent, "row", axis=0, tiled=True)
    own_panel = gradient_tile(columns, cotangent_all, accumulated)
    block_rows = own_panel.shape[0]
    band_count = lax.axis_size("row") // 2
    diagonal_part = block_product(own_panel, own_panel)
    partials = jnp.zeros((block_rows, band_count, block_rows), jnp.float32)

    def cycle_step(offset, loop_state):
        moving, partials = loop_state
        moving = from_behind(moving, "row", 1)
        partials = store_block(partials, block_product(own_panel, moving), offset)
        return (moving, partials)

    moving, partials = lax.fori_loop(1, band_count + 1, cycle_step, (own_panel, partials))
    summed_band, summed_diagonal = lax.psum((partials, diagonal_part), "col")
    position = lax.axis_index("col")
    share_width = band_count // lax.axis_size("col")
    share_rows = block_rows // lax.axis_size("col")
    band_sum = lax.dynamic_slice_in_dim(summed_band, position * share_width, share_width, 1)
    diagonal_sum = lax.dynamic_slice_in_dim(summed_diagonal, position * share_rows, share_rows, 0)
    band_new = decay_rate * band_old + (1.0 - decay_rate) * band_sum
    diagonal_new = decay_rate * diagonal_old + (1.0 - decay_rate) * diagonal_sum
    return (band_new, diagonal_new)


def solution(mesh):
    in_specs = (
        P("col", "row"),
        P("row", "col"),
        P("row", "col"),
        P("row", "col", None),
        P(("row", "col"), None),
    )
    out_specs = (P("row", "col", None), P(("row", "col"), None))
    return jax.shard_map(body, mesh=mesh, in_specs=in_specs, out_specs=out_specs, check_vma=False)
```

profile of v0, /device:TPU:0, one launch (start us, length us, event | category | flops | bytes accessed | tf_op | source)
XLA Modules:
  0.0 1290.5 jit_solution(4808116336807576809)
XLA Ops:
  7.2 0.0 all-gather.2.cloned.1.call-start
  7.2 0.7 all-gather.2.cloned.1.call-update
  7.9 0.0 all-reduce.3.cloned.1.call-start
  8.0 7.4 all_gather.6
  15.3 45.2 %all-gather.2.cloned.1.call-done = bf16[256,7168]{1,0:T(8,128)(2,1)} async-done(((bf16[16,7168]{1,0:T(8,128)(2,1)}), bf16[256,7168]{1,0:T(8,128)(2,1)}) %all-gather.2.cloned.1.call-update) | async-done | bytes 3670032 | tf_op jit(solution)/shard_map/all_gather | solution.py:37
  60.5 6.3 add_convert_fusion
  66.8 0.0 copy-start
  66.8 3.1 copy.14
  69.9 4.9 fusion
  74.8 0.0 copy-done
  74.8 980.8 %while.19 = (s32[]{:T(128)}, bf16[512,7168]{1,0:T(8,128)(2,1)}, f32[512,8,512]{2,1,0:T(8,128)}, bf16[512,7168]{1,0:T(8,128)(2,1)}, s32[]{:T(128)}, /*index=5*/s32[]{:T(128)}) while((s32[]{:T(128)}, bf16[512,7168]{1,0:T(8,128)(2,1)}, f32[512,8,512]{2,1,0:T(8,128)}, bf16[512,7168]{1,0:T(8,128)(2,1)}, s32[]{:T(128)}, /*index=5*/s32[]{:T(128)}) %tuple.56), condition=%wide.region_1.0_spmd, body=%wide.region_0.0_spmd.sunk | while | flops 3758096384 | bytes 63963256 | solution.py:50
  74.8 0.2 collective-permute-start
  75.1 84.4 %collective-permute-done = bf16[512,7168]{1,0:T(8,128)(2,1)} collective-permute-done((bf16[512,7168]{1,0:T(8,128)(2,1)}, bf16[512,7168]{1,0:T(8,128)(2,1)}, u32[]{:S(2)}, u32[]{:S(2)}) %collective-permute-start) | collective-permute-done | bytes 7340064 | tf_op jit(solution)/shard_map/while/body/eval_jaxpr/ppermute | solution.py:11
  159.5 8.5 convolution_bitcast_fusion.2
  168.0 1.1 copy.11
  169.1 21.8 %dynamic_update_slice.14 = f32[512,8,512]{2,1,0:T(8,128)} dynamic-update-slice(f32[512,8,512]{2,1,0:T(8,128)} %get-tuple-element.187, f32[512,1,512]{2,1,0:T(1,128)S(1)} %copy.11, s32[]{:T(128)} %constant.65.clone.1..sunk, s32[]{:T(128)S(6)} %copy.16, s32[]{:T(128)} %constant.65.clone.1..sunk) | dynamic-update-slice | bytes 2097156 | tf_op jit(solution)/shard_map/while/body/eval_jaxpr/dynamic_update_slice | solution.py:30
  190.9 6.6 copy.20
  197.4 0.0 collective-permute-start
  197.4 84.6 %collective-permute-done = bf16[512,7168]{1,0:T(8,128)(2,1)} collective-permute-done((bf16[512,7168]{1,0:T(8,128)(2,1)}, bf16[512,7168]{1,0:T(8,128)(2,1)}, u32[]{:S(2)}, u32[]{:S(2)}) %collective-permute-start) | collective-permute-done | bytes 7340064 | tf_op jit(solution)/shard_map/while/body/eval_jaxpr/ppermute | solution.py:11
  282.1 8.5 convolution_bitcast_fusion.2
  290.6 1.1 copy.11
  291.7 21.8 %dynamic_update_slice.14 = f32[512,8,512]{2,1,0:T(8,128)} dynamic-update-slice(f32[512,8,512]{2,1,0:T(8,128)} %get-tuple-element.187, f32[512,1,512]{2,1,0:T(1,128)S(1)} %copy.11, s32[]{:T(128)} %constant.65.clone.1..sunk, s32[]{:T(128)S(6)} %copy.16, s32[]{:T(128)} %constant.65.clone.1..sunk) | dynamic-update-slice | bytes 2097156 | tf_op jit(solution)/shard_map/while/body/eval_jaxpr/dynamic_update_slice | solution.py:30
  313.4 6.6 copy.20
  320.0 0.0 collective-permute-start
  320.0 84.6 %collective-permute-done = bf16[512,7168]{1,0:T(8,128)(2,1)} collective-permute-done((bf16[512,7168]{1,0:T(8,128)(2,1)}, bf16[512,7168]{1,0:T(8,128)(2,1)}, u32[]{:S(2)}, u32[]{:S(2)}) %collective-permute-start) | collective-permute-done | bytes 7340064 | tf_op jit(solution)/shard_map/while/body/eval_jaxpr/ppermute | solution.py:11
  404.7 8.5 convolution_bitcast_fusion.2
  413.2 1.1 copy.11
  414.3 21.8 %dynamic_update_slice.14 = f32[512,8,512]{2,1,0:T(8,128)} dynamic-update-slice(f32[512,8,512]{2,1,0:T(8,128)} %get-tuple-element.187, f32[512,1,512]{2,1,0:T(1,128)S(1)} %copy.11, s32[]{:T(128)} %constant.65.clone.1..sunk, s32[]{:T(128)S(6)} %copy.16, s32[]{:T(128)} %constant.65.clone.1..sunk) | dynamic-update-slice | bytes 2097156 | tf_op jit(solution)/shard_map/while/body/eval_jaxpr/dynamic_update_slice | solution.py:30
  436.0 6.6 copy.20
  442.6 0.0 collective-permute-start
  442.6 84.6 %collective-permute-done = bf16[512,7168]{1,0:T(8,128)(2,1)} collective-permute-done((bf16[512,7168]{1,0:T(8,128)(2,1)}, bf16[512,7168]{1,0:T(8,128)(2,1)}, u32[]{:S(2)}, u32[]{:S(2)}) %collective-permute-start) | collective-permute-done | bytes 7340064 | tf_op jit(solution)/shard_map/while/body/eval_jaxpr/ppermute | solution.py:11
  527.3 8.5 convolution_bitcast_fusion.2
  535.8 1.1 copy.11
  536.9 21.8 %dynamic_update_slice.14 = f32[512,8,512]{2,1,0:T(8,128)} dynamic-update-slice(f32[512,8,512]{2,1,0:T(8,128)} %get-tuple-element.187, f32[512,1,512]{2,1,0:T(1,128)S(1)} %copy.11, s32[]{:T(128)} %constant.65.clone.1..sunk, s32[]{:T(128)S(6)} %copy.16, s32[]{:T(128)} %constant.65.clone.1..sunk) | dynamic-update-slice | bytes 2097156 | tf_op jit(solution)/shard_map/while/body/eval_jaxpr/dynamic_update_slice | solution.py:30
  558.6 6.6 copy.20
  565.2 0.0 collective-permute-start
  565.2 84.6 %collective-permute-done = bf16[512,7168]{1,0:T(8,128)(2,1)} collective-permute-done((bf16[512,7168]{1,0:T(8,128)(2,1)}, bf16[512,7168]{1,0:T(8,128)(2,1)}, u32[]{:S(2)}, u32[]{:S(2)}) %collective-permute-start) | collective-permute-done | bytes 7340064 | tf_op jit(solution)/shard_map/while/body/eval_jaxpr/ppermute | solution.py:11
  649.9 8.5 convolution_bitcast_fusion.2
  658.4 1.1 copy.11
  659.5 21.8 %dynamic_update_slice.14 = f32[512,8,512]{2,1,0:T(8,128)} dynamic-update-slice(f32[512,8,512]{2,1,0:T(8,128)} %get-tuple-element.187, f32[512,1,512]{2,1,0:T(1,128)S(1)} %copy.11, s32[]{:T(128)} %constant.65.clone.1..sunk, s32[]{:T(128)S(6)} %copy.16, s32[]{:T(128)} %constant.65.clone.1..sunk) | dynamic-update-slice | bytes 2097156 | tf_op jit(solution)/shard_map/while/body/eval_jaxpr/dynamic_update_slice | solution.py:30
  681.2 6.6 copy.20
  687.8 0.0 collective-permute-start
  687.8 84.6 %collective-permute-done = bf16[512,7168]{1,0:T(8,128)(2,1)} collective-permute-done((bf16[512,7168]{1,0:T(8,128)(2,1)}, bf16[512,7168]{1,0:T(8,128)(2,1)}, u32[]{:S(2)}, u32[]{:S(2)}) %collective-permute-start) | collective-permute-done | bytes 7340064 | tf_op jit(solution)/shard_map/while/body/eval_jaxpr/ppermute | solution.py:11
  772.5 8.5 convolution_bitcast_fusion.2
  781.0 1.1 copy.11
  782.1 21.8 %dynamic_update_slice.14 = f32[512,8,512]{2,1,0:T(8,128)} dynamic-update-slice(f32[512,8,512]{2,1,0:T(8,128)} %get-tuple-element.187, f32[512,1,512]{2,1,0:T(1,128)S(1)} %copy.11, s32[]{:T(128)} %constant.65.clone.1..sunk, s32[]{:T(128)S(6)} %copy.16, s32[]{:T(128)} %constant.65.clone.1..sunk) | dynamic-update-slice | bytes 2097156 | tf_op jit(solution)/shard_map/while/body/eval_jaxpr/dynamic_update_slice | solution.py:30
  803.8 6.6 copy.20
  810.4 0.0 collective-permute-start
  810.4 84.6 %collective-permute-done = bf16[512,7168]{1,0:T(8,128)(2,1)} collective-permute-done((bf16[512,7168]{1,0:T(8,128)(2,1)}, bf16[512,7168]{1,0:T(8,128)(2,1)}, u32[]{:S(2)}, u32[]{:S(2)}) %collective-permute-start) | collective-permute-done | bytes 7340064 | tf_op jit(solution)/shard_map/while/body/eval_jaxpr/ppermute | solution.py:11
  895.1 8.5 convolution_bitcast_fusion.2
  903.6 1.1 copy.11
  904.7 21.8 %dynamic_update_slice.14 = f32[512,8,512]{2,1,0:T(8,128)} dynamic-update-slice(f32[512,8,512]{2,1,0:T(8,128)} %get-tuple-element.187, f32[512,1,512]{2,1,0:T(1,128)S(1)} %copy.11, s32[]{:T(128)} %constant.65.clone.1..sunk, s32[]{:T(128)S(6)} %copy.16, s32[]{:T(128)} %constant.65.clone.1..sunk) | dynamic-update-slice | bytes 2097156 | tf_op jit(solution)/shard_map/while/body/eval_jaxpr/dynamic_update_slice | solution.py:30
  926.4 6.6 copy.20
  933.0 0.0 collective-permute-start
  933.0 84.6 %collective-permute-done = bf16[512,7168]{1,0:T(8,128)(2,1)} collective-permute-done((bf16[512,7168]{1,0:T(8,128)(2,1)}, bf16[512,7168]{1,0:T(8,128)(2,1)}, u32[]{:S(2)}, u32[]{:S(2)}) %collective-permute-start) | collective-permute-done | bytes 7340064 | tf_op jit(solution)/shard_map/while/body/eval_jaxpr/ppermute | solution.py:11
  1017.7 8.5 convolution_bitcast_fusion.2
  1026.2 1.1 copy.11
  1027.3 21.8 %dynamic_update_slice.14 = f32[512,8,512]{2,1,0:T(8,128)} dynamic-update-slice(f32[512,8,512]{2,1,0:T(8,128)} %get-tuple-element.187, f32[512,1,512]{2,1,0:T(1,128)S(1)} %copy.11, s32[]{:T(128)} %constant.65.clone.1..sunk, s32[]{:T(128)S(6)} %copy.16, s32[]{:T(128)} %constant.65.clone.1..sunk) | dynamic-update-slice | bytes 2097156 | tf_op jit(solution)/shard_map/while/body/eval_jaxpr/dynamic_update_slice | solution.py:30
  1049.0 6.6 copy.20
  1055.6 0.0 all-reduce.3.cloned.1.call-update
  1055.6 0.0 copy-start.1
  1055.6 218.5 %all-reduce.3.cloned.1.call-done = (f32[512,8,512]{2,1,0:T(8,128)}, f32[512,512]{1,0:T(8,128)}) async-done(((f32[512,8,512]{2,1,0:T(8,128)}, f32[512,512]{1,0:T(8,128)}), (f32[512,8,512]{2,1,0:T(8,128)}, f32[512,512]{1,0:T(8,128)})) %all-reduce.3.cloned.1.call-update) | async-done | bytes 9437200 | tf_op jit(solution)/shard_map/psum | solution.py:51
  1274.2 8.5 multiply_add_fusion
  1282.7 0.9 multiply_add_fusion.1
  (4 shorter events, 0.0 us)
Async XLA Ops:
  7.2 53.3 %all-gather.2.cloned.1.call-start = ((), (), s32[]{:S(2)}) async-start(), calls=%async_computation | async-start | bytes 3899392 | tf_op jit(solution)/shard_map/all_gather | solution.py:37
  7.9 1266.3 %all-reduce.3.cloned.1.call-start = ((), (), s32[]{:S(2)}) async-start(), calls=%async_computation.1 | async-start | bytes 18874368 | tf_op jit(solution)/shard_map/psum | solution.py:51
  66.8 8.0 copy-start
  74.8 84.6 %collective-permute-start = (bf16[512,7168]{1,0:T(8,128)(2,1)}, bf16[512,7168]{1,0:T(8,128)(2,1)}, u32[]{:S(2)}, u32[]{:S(2)}) collective-permute-start(bf16[512,7168]{1,0:T(8,128)(2,1)} %get-tuple-element.186), channel_id=1, source_target_pairs={{0,2},{2,4},{4,6},{6,8},{8,10},{10,12},{12,14},{14,16},{16,18},{18... | collective-permute-start | bytes 22020104 | tf_op jit(solution)/shard_map/while/body/eval_jaxpr/ppermute | solution.py:11
  197.4 84.6 %collective-permute-start = (bf16[512,7168]{1,0:T(8,128)(2,1)}, bf16[512,7168]{1,0:T(8,128)(2,1)}, u32[]{:S(2)}, u32[]{:S(2)}) collective-permute-start(bf16[512,7168]{1,0:T(8,128)(2,1)} %get-tuple-element.186), channel_id=1, source_target_pairs={{0,2},{2,4},{4,6},{6,8},{8,10},{10,12},{12,14},{14,16},{16,18},{18... | collective-permute-start | bytes 22020104 | tf_op jit(solution)/shard_map/while/body/eval_jaxpr/ppermute | solution.py:11
  320.0 84.6 %collective-permute-start = (bf16[512,7168]{1,0:T(8,128)(2,1)}, bf16[512,7168]{1,0:T(8,128)(2,1)}, u32[]{:S(2)}, u32[]{:S(2)}) collective-permute-start(bf16[512,7168]{1,0:T(8,128)(2,1)} %get-tuple-element.186), channel_id=1, source_target_pairs={{0,2},{2,4},{4,6},{6,8},{8,10},{10,12},{12,14},{14,16},{16,18},{18... | collective-permute-start | bytes 22020104 | tf_op jit(solution)/shard_map/while/body/eval_jaxpr/ppermute | solution.py:11
  442.6 84.6 %collective-permute-start = (bf16[512,7168]{1,0:T(8,128)(2,1)}, bf16[512,7168]{1,0:T(8,128)(2,1)}, u32[]{:S(2)}, u32[]{:S(2)}) collective-permute-start(bf16[512,7168]{1,0:T(8,128)(2,1)} %get-tuple-element.186), channel_id=1, source_target_pairs={{0,2},{2,4},{4,6},{6,8},{8,10},{10,12},{12,14},{14,16},{16,18},{18... | collective-permute-start | bytes 22020104 | tf_op jit(solution)/shard_map/while/body/eval_jaxpr/ppermute | solution.py:11
  565.2 84.6 %collective-permute-start = (bf16[512,7168]{1,0:T(8,128)(2,1)}, bf16[512,7168]{1,0:T(8,128)(2,1)}, u32[]{:S(2)}, u32[]{:S(2)}) collective-permute-start(bf16[512,7168]{1,0:T(8,128)(2,1)} %get-tuple-element.186), channel_id=1, source_target_pairs={{0,2},{2,4},{4,6},{6,8},{8,10},{10,12},{12,14},{14,16},{16,18},{18... | collective-permute-start | bytes 22020104 | tf_op jit(solution)/shard_map/while/body/eval_jaxpr/ppermute | solution.py:11
  687.8 84.6 %collective-permute-start = (bf16[512,7168]{1,0:T(8,128)(2,1)}, bf16[512,7168]{1,0:T(8,128)(2,1)}, u32[]{:S(2)}, u32[]{:S(2)}) collective-permute-start(bf16[512,7168]{1,0:T(8,128)(2,1)} %get-tuple-element.186), channel_id=1, source_target_pairs={{0,2},{2,4},{4,6},{6,8},{8,10},{10,12},{12,14},{14,16},{16,18},{18... | collective-permute-start | bytes 22020104 | tf_op jit(solution)/shard_map/while/body/eval_jaxpr/ppermute | solution.py:11
  810.4 84.6 %collective-permute-start = (bf16[512,7168]{1,0:T(8,128)(2,1)}, bf16[512,7168]{1,0:T(8,128)(2,1)}, u32[]{:S(2)}, u32[]{:S(2)}) collective-permute-start(bf16[512,7168]{1,0:T(8,128)(2,1)} %get-tuple-element.186), channel_id=1, source_target_pairs={{0,2},{2,4},{4,6},{6,8},{8,10},{10,12},{12,14},{14,16},{16,18},{18... | collective-permute-start | bytes 22020104 | tf_op jit(solution)/shard_map/while/body/eval_jaxpr/ppermute | solution.py:11
  933.0 84.6 %collective-permute-start = (bf16[512,7168]{1,0:T(8,128)(2,1)}, bf16[512,7168]{1,0:T(8,128)(2,1)}, u32[]{:S(2)}, u32[]{:S(2)}) collective-permute-start(bf16[512,7168]{1,0:T(8,128)(2,1)} %get-tuple-element.186), channel_id=1, source_target_pairs={{0,2},{2,4},{4,6},{6,8},{8,10},{10,12},{12,14},{14,16},{16,18},{18... | collective-permute-start | bytes 22020104 | tf_op jit(solution)/shard_map/while/body/eval_jaxpr/ppermute | solution.py:11
  1055.6 227.1 %copy-start.1 = (f32[256,512]{1,0:T(8,128)S(1)}, f32[256,512]{1,0:T(8,128)}, u32[]{:S(2)}) copy-start(f32[256,512]{1,0:T(8,128)} %param.11) | copy-start | bytes 1572868
  1274.2 8.5 copy-start.2
Sparse Core Ops, SparseCore 0:
  10.3 50.1 all-gather.1
  1055.7 218.3 all-reduce.2
where the time goes:
time: 1300 us; the launch traced here: 1290 us
  waiting for transfers between devices  941 us (72%)
  local copies, waits for them, and re-layouts  238 us (18%)
  matrix products  79.4 us (6%)
  between operations  14.1 us (1%)
    ppermute x8, waiting for transfers between devices, from_behind(): lax.ppermute(shard, axis, [(i, (i + by) % count) for i in range(count)])  677 us
    psum x1, waiting for transfers between devices, body(): summed_band, summed_diagonal = lax.psum((partials, diagonal_part), 'col')  219 us
    dynamic_update_slice x16, local copies, waits for them, and re-layouts, store_block(): lax.dynamic_update_slice(partials, gram_block[:, None, :], (anchor_index,...  183 us
    dot_general x9, matrix products, block_product(): lax.dot_general(left, right, (((1,), (1,)), ((), ())), preferred_element_...  73.1 us
    while x8, local copies, waits for them, and re-layouts  52.6 us
    all_gather x1, waiting for transfers between devices, body(): cotangent_all = lax.all_gather(cotangent, 'row', axis=0, tiled=True)  45.2 us
  transfers between devices with their start and end apart: 10, of which 10 were waited for; matrix products, arithmetic and copies ran while one was open for 0% of the time, Pallas kernels for 0%

commit v1 on v0

v1 whole, which is shorter than its diff:
```python
import jax
import jax.numpy as jnp
from jax import lax
from jax.sharding import PartitionSpec as P

decay_rate = 0.95
GROUP = 4


def swap(array, mask):
    count = lax.axis_size("row")
    return lax.ppermute(array, "row", [(i, i ^ mask) for i in range(count)])


def from_behind(array, by):
    count = lax.axis_size("row")
    return lax.ppermute(array, "row", [(i, (i + by) % count) for i in range(count)])


def gradient_tile(columns, cotangent_all, accumulated):
    product = lax.dot_general(
        columns, cotangent_all, (((0,), (0,)), ((), ())), preferred_element_type=jnp.float32
    )
    return (product + accumulated.astype(jnp.float32)).astype(jnp.bfloat16)


def block_product(left, right):
    return lax.dot_general(
        left, right, (((1,), (1,)), ((), ())), preferred_element_type=jnp.float32
    )


def body(activations, cotangent, accumulated, band_old, diagonal_old):
    columns = lax.all_gather(activations, "col", axis=0, tiled=True)
    cotangent_all = lax.all_gather(cotangent, "row", axis=0, tiled=True)
    own = gradient_tile(columns, cotangent_all, accumulated)
    n_row, n_col = lax.axis_size("row"), lax.axis_size("col")
    block = own.shape[0]
    band = n_row // 2
    steps = band // GROUP
    place = lax.axis_index("row") % GROUP
    position = lax.axis_index("col")

    across = swap(own, 2)
    group = [own, swap(own, 1), across, swap(across, 1)]

    blocks = [None] * (steps + 1)
    blocks[steps] = [block_product(own, panel) for panel in group]
    moving = own
    for step in range(1, steps + 1):
        moving = from_behind(moving, GROUP)
        made = [block_product(panel, moving) for panel in group]
        blocks[steps - step] = [made[0]] + [swap(made[u], u) for u in range(1, GROUP)]
    stacked = jnp.stack([piece for row in blocks for piece in row])

    def at(offset):
        t = band + place - offset
        return lax.dynamic_index_in_dim(
            stacked, t - t % GROUP + ((t % GROUP) ^ place), 0, keepdims=False
        )

    share = band // n_col
    summed = lax.psum_scatter(
        jnp.stack([at(s) for s in range(1, band + 1)]), "col", scatter_dimension=0, tiled=True
    )
    diagonal = lax.psum_scatter(
        blocks[steps][0], "col", scatter_dimension=0, tiled=True
    )
    band_new = decay_rate * band_old + (1.0 - decay_rate) * jnp.swapaxes(summed, 0, 1)
    diagonal_new = decay_rate * diagonal_old + (1.0 - decay_rate) * diagonal
    return (band_new, diagonal_new)


def solution(mesh):
    in_specs = (
        P("col", "row"),
        P("row", "col"),
        P("row", "col"),
        P("row", "col", None),
        P(("row", "col"), None),
    )
    out_specs = (P("row", "col", None), P(("row", "col"), None))
    return jax.shard_map(body, mesh=mesh, in_specs=in_specs, out_specs=out_specs, check_vma=False)
```

time: 1300 us -> 668 us (0.51)
  waiting for transfers between devices: 941 us -> 468 us
  local copies, waits for them, and re-layouts: 238 us -> 29.5 us
  matrix products: 79.4 us -> 122 us
  starting transfers between devices: 0.34 us -> 15.6 us
    ppermute x8 -> x11, waiting for transfers between devices: 677 us -> 327 us  [the longest x2 302 us: from_behind(): lax.ppermute(array, 'row', [(i, (i + by) % count) for i in range(count)])]
    psum x1 -> x0, waiting for transfers between devices: 219 us -> none  [body(): summed_band, summed_diagonal = lax.psum((partials, diagonal_part), 'col')]
    dynamic_update_slice x16 -> x0, local copies, waits for them, and re-layouts: 183 us -> none  [store_block(): lax.dynamic_update_slice(partials, gram_block[:, None, :], (anchor_index,...]
    reduce_scatter x0 -> x2, waiting for transfers between devices: none -> 94.7 us  [the longest x1 94.7 us: body(): lax.psum_scatter(jnp.stack([at(s) for s in range(1, band + 1)]), 'col', s...]
    while x8 -> x0, local copies, waits for them, and re-layouts: 52.6 us -> none
    dot_general x9 -> x12, matrix products: 73.1 us -> 113 us  [block_product(): lax.dot_general(left, right, (((1,), (1,)), ((), ())), preferred_element_...]
    unnamed x7 -> x16, local copies, waits for them, and re-layouts: 3.06 us -> 27.2 us
  transfers between devices with their start and end apart: 10 -> 14, of which waited for: 10 -> 6; matrix products, arithmetic and copies ran while one was open for 0% -> 19% of each run, Pallas kernels for 0% -> 0%
where the time goes in v1:
time: 668 us; the launch traced here: 664 us
  waiting for transfers between devices  468 us (70%)
  matrix products  122 us (18%)
  local copies, waits for them, and re-layouts  29.5 us (4%)
  starting transfers between devices  15.6 us (2%)
  between operations  14.1 us (2%)
  other arithmetic  7.51 us (1%)
  blocking collectives  7.39 us (1%)
    ppermute x2, waiting for transfers between devices, from_behind(): lax.ppermute(array, 'row', [(i, (i + by) % count) for i in range(count)])  302 us
    dot_general x12, matrix products, block_product(): lax.dot_general(left, right, (((1,), (1,)), ((), ())), preferred_element_...  113 us
    reduce_scatter x1, waiting for transfers between devices, body(): lax.psum_scatter(jnp.stack([at(s) for s in range(1, band + 1)]), 'col', s...  94.7 us
    all_gather x1, waiting for transfers between devices, body(): cotangent_all = lax.all_gather(cotangent, 'row', axis=0, tiled=True)  45.2 us
    unnamed x16, local copies, waits for them, and re-layouts  27.2 us
    ppermute x9, waiting for transfers between devices, swap(): return lax.ppermute(array, 'row', [(i, i ^ mask) for i in range(count)])  24.7 us
  transfers between devices with their start and end apart: 14, of which 6 were waited for; matrix products, arithmetic and copies ran while one was open for 19% of the time, Pallas kernels for 0%

profile of v1, /device:TPU:0, one launch (start us, length us, event | category | flops | bytes accessed | tf_op | source)
XLA Modules:
  0.0 663.8 jit_solution(4123298732223985481)
XLA Ops:
  7.2 0.0 all-gather.2.cloned.1.call-start
  7.2 0.7 all-gather.2.cloned.1.call-update
  7.9 0.0 reduce-scatter.5.cloned.1.call-start
  7.9 7.4 %all_gather.6 = bf16[256,512]{1,0:T(8,128)(2,1)S(1)} all-gather(bf16[128,512]{1,0:T(8,128)(2,1)} %param.5), channel_id=1, replica_groups=mesh['row'=16,'col'=2] {'col'}, dimensions={0}, use_global_device_ids=true | all-gather | bytes 393216 | tf_op jit(solution)/shard_map/all_gather | solution.py:34
  15.3 45.2 %all-gather.2.cloned.1.call-done = bf16[256,7168]{1,0:T(8,128)(2,1)} async-done(((bf16[16,7168]{1,0:T(8,128)(2,1)}), bf16[256,7168]{1,0:T(8,128)(2,1)}) %all-gather.2.cloned.1.call-update) | async-done | bytes 3670032 | tf_op jit(solution)/shard_map/all_gather | solution.py:35
  60.5 9.2 %add_convert_fusion = bf16[512,7168]{1,0:T(8,128)(2,1)} fusion(bf16[512,7168]{1,0:T(8,128)(2,1)} %param.7, bf16[256,512]{1,0:T(8,128)(2,1)S(1)} %all_gather.6, bf16[256,7168]{1,0:T(8,128)(2,1)} %all-gather.2.cloned.1.call-done), kind=kOutput, calls=%fused_computation | convolution fusion | flops 1890058240 | bytes 18612224 | tf_op jit(solution)/shard_map/dot_general | solution.py:21
  69.7 2.1 collective-permute-start
  71.8 0.6 collective-permute-start.4
  72.4 0.0 collective-permute-start.2
  72.4 159.6 %collective-permute-done = bf16[512,7168]{1,0:T(8,128)(2,1)} collective-permute-done((bf16[512,7168]{1,0:T(8,128)(2,1)}, bf16[512,7168]{1,0:T(8,128)(2,1)}, u32[]{:S(2)}, u32[]{:S(2)}) %collective-permute-start) | collective-permute-done | bytes 7340064 | tf_op jit(solution)/shard_map/ppermute | solution.py:17
  232.0 0.3 collective-permute-start.1
  232.3 0.0 collective-permute-done.4
  232.3 0.0 collective-permute-start.6
  232.3 0.0 collective-permute-done.2
  232.3 8.5 %fusion.8 = f32[512,512]{1,0:T(8,128)S(1)} fusion(bf16[512,7168]{1,0:T(8,128)(2,1)} %collective-permute-done.2, bf16[512,7168]{1,0:T(8,128)(2,1)} %collective-permute-done), kind=kOutput, calls=%fused_computation.32 | convolution fusion | flops 3758096384 | bytes 15728640 | tf_op jit(solution)/shard_map/dot_general | solution.py:28
  240.8 0.6 collective-permute-start.8
  241.4 8.5 %fusion.9 = f32[512,512]{1,0:T(8,128)S(1)} fusion(bf16[512,7168]{1,0:T(8,128)(2,1)} %collective-permute-done.4, bf16[512,7168]{1,0:T(8,128)(2,1)} %collective-permute-done), kind=kOutput, calls=%fused_computation.33 | convolution fusion | flops 3758096384 | bytes 15728640 | tf_op jit(solution)/shard_map/dot_general | solution.py:28
  249.9 0.6 collective-permute-start.9
  250.5 142.9 %collective-permute-done.1 = bf16[512,7168]{1,0:T(8,128)(2,1)} collective-permute-done((bf16[512,7168]{1,0:T(8,128)(2,1)}, bf16[512,7168]{1,0:T(8,128)(2,1)}, u32[]{:S(2)}, u32[]{:S(2)}) %collective-permute-start.1) | collective-permute-done | bytes 7340064 | tf_op jit(solution)/shard_map/ppermute | solution.py:17
  393.4 8.5 %fusion.5 = f32[512,512]{1,0:T(8,128)S(1)} fusion(bf16[512,7168]{1,0:T(8,128)(2,1)} %collective-permute-done.2, bf16[512,7168]{1,0:T(8,128)(2,1)} %collective-permute-done.1), kind=kOutput, calls=%fused_computation.29 | convolution fusion | flops 3758096384 | bytes 15728640 | tf_op jit(solution)/shard_map/dot_general | solution.py:28
  402.0 0.1 collective-permute-start.3
  402.0 8.5 %fusion.6 = f32[512,512]{1,0:T(8,128)S(1)} fusion(bf16[512,7168]{1,0:T(8,128)(2,1)} %collective-permute-done.4, bf16[512,7168]{1,0:T(8,128)(2,1)} %collective-permute-done.1), kind=kOutput, calls=%fused_computation.30 | convolution fusion | flops 3758096384 | bytes 15728640 | tf_op jit(solution)/shard_map/dot_general | solution.py:28
  410.6 0.6 collective-permute-start.5
  411.2 0.0 collective-permute-done.6
  411.2 8.8 %fusion.7 = f32[512,512]{1,0:T(8,128)S(1)} fusion(bf16[512,7168]{1,0:T(8,128)(2,1)} %collective-permute-done.6, bf16[512,7168]{1,0:T(8,128)(2,1)} %collective-permute-done.1), kind=kOutput, calls=%fused_computation.31 | convolution fusion | flops 3758096384 | bytes 15728640 | tf_op jit(solution)/shard_map/dot_general | solution.py:28
  420.0 1.3 collective-permute-start.7
  421.3 10.1 %fusion.4 = f32[12,512,512]{2,1,0:T(8,128)} fusion(bf16[512,7168]{1,0:T(8,128)(2,1)} %add_convert_fusion, bf16[512,7168]{1,0:T(8,128)(2,1)} %collective-permute-done.1), kind=kOutput, calls=%fused_computation.12 | convolution fusion | flops 3758096384 | bytes 15728640 | tf_op jit(solution)/shard_map/dot_general | solution.py:28
  431.5 8.5 %fusion.10 = f32[512,512]{1,0:T(8,128)S(1)} fusion(bf16[512,7168]{1,0:T(8,128)(2,1)} %collective-permute-done.6, bf16[512,7168]{1,0:T(8,128)(2,1)} %collective-permute-done), kind=kOutput, calls=%fused_computation.34 | convolution fusion | flops 3758096384 | bytes 15728640 | tf_op jit(solution)/shard_map/dot_general | solution.py:28
  440.0 0.0 collective-permute-done.3
  440.0 0.5 collective-permute-start.10
  440.5 1.1 bitcast_dynamic-update-slice_fusion.6
  441.6 0.0 collective-permute-done.5
  441.6 1.0 bitcast_dynamic-update-slice_fusion.5
  442.6 15.6 %collective-permute-done.7 = f32[512,512]{1,0:T(8,128)S(1)} collective-permute-done((f32[512,512]{1,0:T(8,128)S(1)}, f32[512,512]{1,0:T(8,128)S(1)}, u32[]{:S(2)}, u32[]{:S(2)}) %collective-permute-start.7) | collective-permute-done | bytes 1048608 | tf_op jit(solution)/shard_map/ppermute | solution.py:12
  458.2 1.1 bitcast_dynamic-update-slice_fusion.4
  459.3 10.1 %fusion.3 = f32[12,512,512]{2,1,0:T(8,128)} fusion(f32[12,512,512]{2,1,0:T(8,128)} %bitcast_dynamic-update-slice_fusion.4, bf16[512,7168]{1,0:T(8,128)(2,1)} %add_convert_fusion, bf16[512,7168]{1,0:T(8,128)(2,1)} %collective-permute-done), kind=kOutput, calls=%fused_computation.10 | convolution fusion | flops 3758096384 | bytes 15728640 | tf_op jit(solution)/shard_map/dot_general | solution.py:28
  469.4 0.0 collective-permute-done.8
  469.4 1.1 bitcast_dynamic-update-slice_fusion.3
  470.5 0.0 collective-permute-done.9
  470.5 1.1 bitcast_dynamic-update-slice_fusion.2
  471.6 9.1 %collective-permute-done.10 = f32[512,512]{1,0:T(8,128)S(1)} collective-permute-done((f32[512,512]{1,0:T(8,128)S(1)}, f32[512,512]{1,0:T(8,128)S(1)}, u32[]{:S(2)}, u32[]{:S(2)}) %collective-permute-start.10) | collective-permute-done | bytes 1048608 | tf_op jit(solution)/shard_map/ppermute | solution.py:12
  480.7 1.1 bitcast_dynamic-update-slice_fusion.1
  481.8 10.6 %bitcast_dynamic-update-slice_fusion = (f32[12,512,512]{2,1,0:T(8,128)}, f32[512,512]{1,0:T(8,128)}) fusion(f32[12,512,512]{2,1,0:T(8,128)} %bitcast_dynamic-update-slice_fusion.1, bf16[512,7168]{1,0:T(8,128)(2,1)} %add_convert_fusion), kind=kOutput, calls=%fused_computation.13 | convolution fusion | flops 3758096384 | bytes 16777216 | tf_op jit(solution)/shard_map/dot_general | solution.py:28
  492.4 0.0 reduce-scatter.5.cloned.1.call-update
  492.4 8.8 %reduce-scatter.3.cloned.1.call-start = ((), (), s32[]{:S(2)}) async-start(), calls=%async_computation.3 | async-start | bytes 12582912 | tf_op jit(solution)/shard_map/reduce_scatter | solution.py:63
  501.2 10.2 %fusion.2 = f32[12,512,512]{2,1,0:T(8,128)} fusion(f32[12,512,512]{2,1,0:T(8,128)} %get-tuple-element.4, bf16[512,7168]{1,0:T(8,128)(2,1)} %add_convert_fusion, bf16[512,7168]{1,0:T(8,128)(2,1)} %collective-permute-done.2), kind=kOutput, calls=%fused_computation.8 | convolution fusion | flops 3758096384 | bytes 15728640 | tf_op jit(solution)/shard_map/dot_general | solution.py:28
  511.4 10.2 %fusion.1 = f32[12,512,512]{2,1,0:T(8,128)} fusion(f32[12,512,512]{2,1,0:T(8,128)} %fusion.2, bf16[512,7168]{1,0:T(8,128)(2,1)} %add_convert_fusion, bf16[512,7168]{1,0:T(8,128)(2,1)} %collective-permute-done.4), kind=kOutput, calls=%fused_computation.6 | convolution fusion | flops 3758096384 | bytes 15728640 | tf_op jit(solution)/shard_map/dot_general | solution.py:28
  521.6 10.2 %fusion = f32[12,512,512]{2,1,0:T(8,128)} fusion(f32[12,512,512]{2,1,0:T(8,128)} %fusion.1, bf16[512,7168]{1,0:T(8,128)(2,1)} %add_convert_fusion, bf16[512,7168]{1,0:T(8,128)(2,1)} %collective-permute-done.6), kind=kOutput, calls=%fused_computation.4 | convolution fusion | flops 3758096384 | bytes 15728640 | tf_op jit(solution)/shard_map/dot_general | solution.py:28
  531.7 2.3 dynamic-slice_dynamic-update-slice_fusion.7
  534.1 2.3 dynamic-slice_dynamic-update-slice_fusion.6
  536.3 2.3 dynamic-slice_dynamic-update-slice_fusion.5
  538.6 2.3 dynamic-slice_dynamic-update-slice_fusion.4
  540.9 2.3 dynamic-slice_dynamic-update-slice_fusion.3
  543.2 0.0 copy-start
  543.2 2.3 dynamic-slice_dynamic-update-slice_fusion.2
  545.5 2.3 dynamic-slice_dynamic-update-slice_fusion.1
  547.8 2.3 dynamic-slice_dynamic-update-slice_fusion
  550.1 0.0 reduce-scatter.3.cloned.1.call-update
  550.1 0.0 reduce-scatter.5.cloned.1.call-done
  550.1 0.0 copy-done
  550.1 1.9 multiply_add_fusion
  552.1 94.7 %reduce-scatter.3.cloned.1.call-done = f32[4,512,512]{2,1,0:T(8,128)} async-done(((f32[8,512,512]{2,1,0:T(8,128)}), f32[4,512,512]{2,1,0:T(8,128)}) %reduce-scatter.3.cloned.1.call-update) | async-done | bytes 4194320 | tf_op jit(solution)/shard_map/reduce_scatter | solution.py:63
  646.7 5.6 bitcast_add_fusion
  652.3 4.7 copy.8
Async XLA Ops:
  7.2 53.3 %all-gather.2.cloned.1.call-start = ((), (), s32[]{:S(2)}) async-start(), calls=%async_computation.2 | async-start | bytes 3899392 | tf_op jit(solution)/shard_map/all_gather | solution.py:35
  7.9 542.2 %reduce-scatter.5.cloned.1.call-start = ((), (), s32[]{:S(2)}) async-start(), calls=%async_computation.4 | async-start | bytes 1572864 | tf_op jit(solution)/shard_map/reduce_scatter | solution.py:66
  69.7 162.3 %collective-permute-start = (bf16[512,7168]{1,0:T(8,128)(2,1)}, bf16[512,7168]{1,0:T(8,128)(2,1)}, u32[]{:S(2)}, u32[]{:S(2)}) collective-permute-start(bf16[512,7168]{1,0:T(8,128)(2,1)} %add_convert_fusion), channel_id=1, source_target_pairs={{0,8},{2,10},{4,12},{6,14},{8,16},{10,18},{12,20},{14,22},{16,24},... | collective-permute-start | bytes 22020104 | tf_op jit(solution)/shard_map/ppermute | solution.py:17
  71.8 160.5 %collective-permute-start.4 = (bf16[512,7168]{1,0:T(8,128)(2,1)}, bf16[512,7168]{1,0:T(8,128)(2,1)}, u32[]{:S(2)}, u32[]{:S(2)}) collective-permute-start(bf16[512,7168]{1,0:T(8,128)(2,1)} %add_convert_fusion), channel_id=1, source_target_pairs={{0,4},{2,6},{4,0},{6,2},{8,12},{10,14},{12,8},{14,10},{16,20},{18,... | collective-permute-start | bytes 22020104 | tf_op jit(solution)/shard_map/ppermute | solution.py:12
  72.4 159.9 %collective-permute-start.2 = (bf16[512,7168]{1,0:T(8,128)(2,1)}, bf16[512,7168]{1,0:T(8,128)(2,1)}, u32[]{:S(2)}, u32[]{:S(2)}) collective-permute-start(bf16[512,7168]{1,0:T(8,128)(2,1)} %add_convert_fusion), channel_id=1, source_target_pairs={{0,2},{2,0},{4,6},{6,4},{8,10},{10,8},{12,14},{14,12},{16,18},{18,... | collective-permute-start | bytes 22020104 | tf_op jit(solution)/shard_map/ppermute | solution.py:12
  232.0 161.4 %collective-permute-start.1 = (bf16[512,7168]{1,0:T(8,128)(2,1)}, bf16[512,7168]{1,0:T(8,128)(2,1)}, u32[]{:S(2)}, u32[]{:S(2)}) collective-permute-start(bf16[512,7168]{1,0:T(8,128)(2,1)} %collective-permute-done), channel_id=1, source_target_pairs={{0,8},{2,10},{4,12},{6,14},{8,16},{10,18},{12,20},{14,22},{16,24},... | collective-permute-start | bytes 22020104 | tf_op jit(solution)/shard_map/ppermute | solution.py:17
  232.3 178.9 %collective-permute-start.6 = (bf16[512,7168]{1,0:T(8,128)(2,1)}, bf16[512,7168]{1,0:T(8,128)(2,1)}, u32[]{:S(2)}, u32[]{:S(2)}) collective-permute-start(bf16[512,7168]{1,0:T(8,128)(2,1)} %collective-permute-done.4), channel_id=1, source_target_pairs={{0,2},{2,0},{4,6},{6,4},{8,10},{10,8},{12,14},{14,12},{16,18},{18,... | collective-permute-start | bytes 22020104 | tf_op jit(solution)/shard_map/ppermute | solution.py:12
  240.8 228.6 %collective-permute-start.8 = (f32[512,512]{1,0:T(8,128)S(1)}, f32[512,512]{1,0:T(8,128)S(1)}, u32[]{:S(2)}, u32[]{:S(2)}) collective-permute-start(f32[512,512]{1,0:T(8,128)S(1)} %fusion.8), channel_id=1, source_target_pairs={{0,2},{2,0},{4,6},{6,4},{8,10},{10,8},{12,14},{14,12},{16,18},{18,... | collective-permute-start | bytes 3145736 | tf_op jit(solution)/shard_map/ppermute | solution.py:12
  249.9 220.6 %collective-permute-start.9 = (f32[512,512]{1,0:T(8,128)S(1)}, f32[512,512]{1,0:T(8,128)S(1)}, u32[]{:S(2)}, u32[]{:S(2)}) collective-permute-start(f32[512,512]{1,0:T(8,128)S(1)} %fusion.9), channel_id=1, source_target_pairs={{0,4},{2,6},{4,0},{6,2},{8,12},{10,14},{12,8},{14,10},{16,20},{18,... | collective-permute-start | bytes 3145736 | tf_op jit(solution)/shard_map/ppermute | solution.py:12
  402.0 38.0 %collective-permute-start.3 = (f32[512,512]{1,0:T(8,128)S(1)}, f32[512,512]{1,0:T(8,128)S(1)}, u32[]{:S(2)}, u32[]{:S(2)}) collective-permute-start(f32[512,512]{1,0:T(8,128)S(1)} %fusion.5), channel_id=1, source_target_pairs={{0,2},{2,0},{4,6},{6,4},{8,10},{10,8},{12,14},{14,12},{16,18},{18,... | collective-permute-start | bytes 3145736 | tf_op jit(solution)/shard_map/ppermute | solution.py:12
  410.6 31.0 %collective-permute-start.5 = (f32[512,512]{1,0:T(8,128)S(1)}, f32[512,512]{1,0:T(8,128)S(1)}, u32[]{:S(2)}, u32[]{:S(2)}) collective-permute-start(f32[512,512]{1,0:T(8,128)S(1)} %fusion.6), channel_id=1, source_target_pairs={{0,4},{2,6},{4,0},{6,2},{8,12},{10,14},{12,8},{14,10},{16,20},{18,... | collective-permute-start | bytes 3145736 | tf_op jit(solution)/shard_map/ppermute | solution.py:12
  420.0 38.2 %collective-permute-start.7 = (f32[512,512]{1,0:T(8,128)S(1)}, f32[512,512]{1,0:T(8,128)S(1)}, u32[]{:S(2)}, u32[]{:S(2)}) collective-permute-start(f32[512,512]{1,0:T(8,128)S(1)} %fusion.7), channel_id=1, source_target_pairs={{0,6},{2,4},{4,2},{6,0},{8,14},{10,12},{12,10},{14,8},{16,22},{18,... | collective-permute-start | bytes 3145736 | tf_op jit(solution)/shard_map/ppermute | solution.py:12
  440.0 40.7 %collective-permute-start.10 = (f32[512,512]{1,0:T(8,128)S(1)}, f32[512,512]{1,0:T(8,128)S(1)}, u32[]{:S(2)}, u32[]{:S(2)}) collective-permute-start(f32[512,512]{1,0:T(8,128)S(1)} %fusion.10), channel_id=1, source_target_pairs={{0,6},{2,4},{4,2},{6,0},{8,14},{10,12},{12,10},{14,8},{16,22},{18,... | collective-permute-start | bytes 3145736 | tf_op jit(solution)/shard_map/ppermute | solution.py:12
  492.4 154.3 %reduce-scatter.3.cloned.1.call-start = ((), (), s32[]{:S(2)}) async-start(), calls=%async_computation.3 | async-start | bytes 12582912 | tf_op jit(solution)/shard_map/reduce_scatter | solution.py:63
  543.2 7.0 %copy-start = (f32[256,512]{1,0:T(8,128)S(1)}, f32[256,512]{1,0:T(8,128)}, u32[]{:S(2)}) copy-start(f32[256,512]{1,0:T(8,128)} %param.9) | copy-start | bytes 1572868
Sparse Core Ops, SparseCore 0:
  10.3 50.1 all-gather.1
  492.5 17.5 reduce-scatter.4
  550.2 96.4 reduce-scatter.2

commit v2 on v1

--- a/solution.py
+++ b/solution.py
@@ -30,7 +30,7 @@
     )
 
 
-def body(activations, cotangent, accumulated, band_old, diagonal_old):
+def ring_body(activations, cotangent, accumulated, band_old, diagonal_old):
     columns = lax.all_gather(activations, "col", axis=0, tiled=True)
     cotangent_all = lax.all_gather(cotangent, "row", axis=0, tiled=True)
     own = gradient_tile(columns, cotangent_all, accumulated)
@@ -71,7 +71,170 @@
     return (band_new, diagonal_new)
 
 
+def move(array, pairs):
+    return lax.ppermute(
+        array,
+        "row",
+        [(a * GROUP + place, b * GROUP + place) for a, b in pairs for place in range(GROUP)],
+    )
+
+
+def trade(array):
+    return lax.ppermute(array, "col", [(0, 1), (1, 0)])
+
+
+def split_body(activations, cotangent, accumulated, band_old, diagonal_old):
+    row, y = lax.axis_index("row"), lax.axis_index("col")
+    z, place = row // GROUP, row % GROUP
+    outer = (z == 0) | (z == 3)
+    upper = z // 2
+    block, width = accumulated.shape
+    half, cut = width // 2, block // 2
+    parts = range(2)
+
+    def side(array, which):
+        return lax.dynamic_slice_in_dim(array, which * half, half, 1)
+
+    def part(array, c):
+        return array[c * cut : (c + 1) * cut]
+
+    kept, crossing = side(accumulated, upper), side(accumulated, 1 - upper)
+    direct = [move(part(crossing, c), [(1, 2), (2, 1)]) for c in parts]
+    relay = [move(part(crossing, c), [(0, 1), (3, 2)]) for c in parts]
+    across_kept = swap(kept, 2)
+    onward = [move(direct[c], [(1, 0), (2, 3)]) for c in parts]
+    second = [move(relay[c], [(1, 2), (2, 1)]) for c in parts]
+    inner_kept = [move(part(kept, c), [(0, 1), (3, 2)]) for c in parts]
+    across_crossing = swap(crossing, 2)
+    second_onward = [move(second[c], [(1, 0), (2, 3)]) for c in parts]
+
+    columns = lax.all_gather(activations, "col", axis=0, tiled=True)
+    cotangent_all = lax.all_gather(cotangent, "row", axis=0, tiled=True)
+    cot_kept, cot_crossing = side(cotangent_all, upper), side(cotangent_all, 1 - upper)
+    columns_across = swap(columns, 2)
+    columns_inner = swap(columns, GROUP)
+    columns_two, columns_three = swap(columns, 2 * GROUP), swap(columns, 3 * GROUP)
+    columns_near = jnp.where(outer, columns_two, columns_three)
+    columns_far = jnp.where(outer, columns_three, columns_two)
+
+    def group_of(cot, own_raw, across_raw):
+        own = gradient_tile(columns, cot, own_raw)
+        across = gradient_tile(columns_across, cot, across_raw)
+        return [own, swap(own, 1), across, swap(across, 1)]
+
+    group_kept = group_of(cot_kept, kept, across_kept)
+    group_crossing = group_of(cot_crossing, crossing, across_crossing)
+
+    def reduced(pieces, c):
+        pieces = jnp.stack(pieces)
+        keep = c ^ y
+        mine = lax.dynamic_slice_in_dim(pieces, keep * cut, cut, 1)
+        theirs = lax.dynamic_slice_in_dim(pieces, (1 - keep) * cut, cut, 1)
+        return mine + trade(theirs.astype(jnp.bfloat16)).astype(jnp.float32)
+
+    def to_owners(pieces):
+        return jnp.stack([pieces[0]] + [swap(pieces[u], u) for u in range(1, GROUP)])
+
+    def tile_part(cols, c):
+        return cols[:, c * cut : (c + 1) * cut]
+
+    near, far, inner = [], [], []
+    for c in parts:
+        panel = gradient_tile(
+            tile_part(columns_near, c), cot_kept, jnp.where(outer, onward[c], direct[c])
+        )
+        near.append(reduced([block_product(left, panel) for left in group_kept], c))
+    for c in parts:
+        panel = gradient_tile(tile_part(columns_inner, c), cot_kept, inner_kept[c])
+        panel_crossing = gradient_tile(tile_part(columns_inner, c), cot_crossing, relay[c])
+        inner.append(
+            reduced(
+                [
+                    block_product(left, panel) + block_product(left_crossing, panel_crossing)
+                    for left, left_crossing in zip(group_kept, group_crossing)
+                ],
+                c,
+            )
+        )
+    own_products = [
+        block_product(group_kept[0], right) + block_product(group_crossing[0], right_crossing)
+        for right, right_crossing in zip(group_kept, group_crossing)
+    ]
+    for c in parts:
+        panel = gradient_tile(
+            tile_part(columns_far, c), cot_kept, jnp.where(outer, second_onward[c], second[c])
+        )
+        far.append(reduced([block_product(left, panel) for left in group_kept], c))
+
+    one_behind, two_behind = [], []
+    here = [[to_owners(kind[c]) for c in parts] for kind in (near, inner, far)]
+    narrow = [[kind[c].astype(jnp.bfloat16) for c in parts] for kind in (near, inner, far)]
+    for c in parts:
+        mine = jnp.where(z == 0, here[2][c], jnp.where(z == 2, here[0][c], here[1][c]))
+        one_behind.append(jnp.where(z == 3, 0.0, mine))
+        two_behind.append(jnp.where(outer, here[0][c], here[2][c]))
+    quarters = []
+    for h in parts:
+        one = [
+            move(narrow[0][h], [(1, 2)]),
+            move(narrow[1][h], [(2, 3)]),
+            move(narrow[2][h], [(3, 0)]),
+        ]
+        two = [move(narrow[0][h], [(0, 2), (3, 1)]), move(narrow[2][h], [(2, 0), (1, 3)])]
+        pieces = []
+        for mine, arrived in ((two_behind, two), (one_behind, one)):
+            total = sum(a.astype(jnp.float32) for a in arrived)
+            pieces.append(
+                jnp.where(y == 0, mine[h], mine[1 - h]) + jnp.swapaxes(total, 1, 2)
+            )
+        quarters.append(jnp.concatenate(pieces))
+    quarters = jnp.stack(quarters, axis=1)
+
+    band = 2 * GROUP
+
+    def where_is(offset):
+        t = band + place - offset
+        u = (t % GROUP) ^ place
+        return t, u
+
+    def quarters_of(offset):
+        t, u = where_is(offset)
+        return lax.dynamic_index_in_dim(
+            quarters, jnp.minimum(t // GROUP, 1) * GROUP + u, 0, keepdims=False
+        )
+
+    share = band // 2
+    theirs = jnp.stack([quarters_of(s + (1 - y) * share) for s in range(1, share + 1)])
+    arrived = trade(theirs)
+    own_rest = jnp.stack(own_products[1:])
+    own_sum = own_rest + trade(own_rest.astype(jnp.bfloat16)).astype(jnp.float32)
+    blocks = []
+    for s in range(1, share + 1):
+        offset = s + y * share
+        mine, other = quarters_of(offset), arrived[s - 1]
+        even, odd = jnp.where(y == 0, mine, other), jnp.where(y == 0, other, mine)
+        whole = jnp.concatenate(
+            [
+                jnp.concatenate([even[0], odd[0]], axis=1),
+                jnp.concatenate([odd[1], even[1]], axis=1),
+            ]
+        )
+        t, u = where_is(offset)
+        local = lax.dynamic_index_in_dim(own_sum, jnp.maximum(u - 1, 0), 0, keepdims=False)
+        blocks.append(jnp.where(t >= band, local, whole))
+    band_new = decay_rate * band_old + (1.0 - decay_rate) * jnp.stack(blocks, axis=1)
+
+    own_own = own_products[0]
+    diagonal = lax.dynamic_slice_in_dim(own_own, y * cut, cut, 0) + trade(
+        lax.dynamic_slice_in_dim(own_own, (1 - y) * cut, cut, 0)
+    )
+    diagonal_new = decay_rate * diagonal_old + (1.0 - decay_rate) * diagonal
+    return (band_new, diagonal_new)
+
+
 def solution(mesh):
+    line = mesh.shape["row"] == 4 * GROUP and mesh.shape["col"] == 2
+    body = split_body if line else ring_body
     in_specs = (
         P("col", "row"),
         P("row", "col"),

time: 668 us -> 752 us (1.13)
  starting transfers between devices: 15.6 us -> 87.5 us
  waiting for transfers between devices: 468 us -> 423 us
  other arithmetic: 7.51 us -> 43.2 us
  local copies, waits for them, and re-layouts: 29.5 us -> 54.7 us
  matrix products: 122 us -> 112 us
    ppermute x9 -> x28, waiting for transfers between devices: 24.7 us -> 195 us  [swap(): return lax.ppermute(array, 'row', [(i, i ^ mask) for i in range(count)])]
    reduce_scatter x2 -> x0, waiting for transfers between devices: 94.7 us -> none  [the longest x1 94.7 us: body(): lax.psum_scatter(jnp.stack([at(s) for s in range(1, band + 1)]), 'col', s...]
    ppermute x2 -> x31, waiting for transfers between devices: 302 us -> 227 us  [the longest x9 116 us: trade(): return lax.ppermute(array, 'col', [(0, 1), (1, 0)])]
    ppermute x2 -> x31, starting transfers between devices: 2.38 us -> 70.3 us  [the longest x22 62.6 us: move(): lax.ppermute(array, 'row', [(a * GROUP + place, b * GROUP + place) for a,...]
    all_gather x1, waiting for transfers between devices: 45.2 us -> 0.01 us  [split_body(): cotangent_all = lax.all_gather(cotangent, 'row', axis=0, tiled=True)]
    dot_general x12 -> x40, matrix products: 113 us -> 76.3 us  [block_product(): lax.dot_general(left, right, (((1,), (1,)), ((), ())), preferred_element_...]
    dot_general x1 -> x12, matrix products: 9.21 us -> 35.7 us  [gradient_tile(): lax.dot_general(columns, cotangent_all, (((0,), (0,)), ((), ())), preferr...]
    convert_element_type x0 -> x8, other arithmetic: none -> 14.6 us  [the longest x1 7.06 us: gradient_tile(): return (product + accumulated.astype(jnp.float32)).astype(jnp.bfloat16)]
  transfers between devices with their start and end apart: 14 -> 60, of which waited for: 6 -> 25; matrix products, arithmetic and copies ran while one was open for 19% -> 23% of each run, Pallas kernels for 0% -> 0%
where the time goes in v2:
time: 752 us; the launch traced here: 741 us
  waiting for transfers between devices  423 us (56%)
  matrix products  112 us (15%)
  starting transfers between devices  87.5 us (12%)
  local copies, waits for them, and re-layouts  54.7 us (7%)
  other arithmetic  43.2 us (6%)
  between operations  15.6 us (2%)
    ppermute x28, waiting for transfers between devices, swap(): return lax.ppermute(array, 'row', [(i, i ^ mask) for i in range(count)])  195 us
    ppermute x9, waiting for transfers between devices, trade(): return lax.ppermute(array, 'col', [(0, 1), (1, 0)])  116 us
    ppermute x22, waiting for transfers between devices, move(): lax.ppermute(array, 'row', [(a * GROUP + place, b * GROUP + place) for a,...  110 us
    dot_general x40, matrix products, block_product(): lax.dot_general(left, right, (((1,), (1,)), ((), ())), preferred_element_...  76.3 us
    ppermute x22, starting transfers between devices, move(): lax.ppermute(array, 'row', [(a * GROUP + place, b * GROUP + place) for a,...  62.6 us
    dot_general x12, matrix products, gradient_tile(): lax.dot_general(columns, cotangent_all, (((0,), (0,)), ((), ())), preferr...  35.7 us
    unnamed x101, local copies, waits for them, and re-layouts  28.8 us
    ppermute x28, starting transfers between devices, swap(): return lax.ppermute(array, 'row', [(i, i ^ mask) for i in range(count)])  17.2 us
  transfers between devices with their start and end apart: 60, of which 25 were waited for; matrix products, arithmetic and copies ran while one was open for 23% of the time, Pallas kernels for 0%

profile of v2, /device:TPU:0, one launch (start us, length us, event | category | flops | bytes accessed | tf_op | source)
XLA Modules:
  0.0 741.2 jit_solution(8790796922284300489)
XLA Ops:
  7.9 6.7 constant_dynamic-slice_fusion.2
  14.7 5.9 copy.40
  20.6 3.6 fusion.94
  26.1 7.8 %collective-permute-start.16 = (bf16[256,3584]{0,1:T(8,128)(2,1)S(1)}, bf16[256,3584]{0,1:T(8,128)(2,1)}, u32[]{:S(2)}, u32[]{:S(2)}) collective-permute-start(bf16[256,3584]{0,1:T(8,128)(2,1)S(1)} %get-tuple-element.34), channel_id=1, source_target_pairs={{0,8},{2,10},{4,12},{6,14},{24,16},{26,18},{28,20},{30,22},{1,9},{... | collective-permute-start | bytes 5505032 | tf_op jit(solution)/shard_map/ppermute | solution.py:75
  33.9 2.5 collective-permute-start.29
  37.9 5.6 all_gather.7
  44.9 6.0 copy.39
  50.8 82.9 %collective-permute-done.9 = bf16[256,512]{1,0:T(8,128)(2,1)S(1)} collective-permute-done((bf16[256,512]{1,0:T(8,128)(2,1)S(1)}, bf16[256,512]{1,0:T(8,128)(2,1)S(1)}, u32[]{:S(2)}, u32[]{:S(2)}) %collective-permute-start.9) | collective-permute-done | bytes 262176 | tf_op jit(solution)/shard_map/ppermute | solution.py:12
  135.0 4.1 fusion.93
  139.1 7.6 %collective-permute-done.8 = bf16[256,512]{1,0:T(8,128)(2,1)S(1)} collective-permute-done((bf16[256,512]{1,0:T(8,128)(2,1)S(1)}, bf16[256,512]{1,0:T(8,128)(2,1)S(1)}, u32[]{:S(2)}, u32[]{:S(2)}) %collective-permute-start.8) | collective-permute-done | bytes 262176 | tf_op jit(solution)/shard_map/ppermute | solution.py:12
  152.2 3.9 fusion.3
  156.1 4.6 fusion.2
  160.7 23.7 %collective-permute-done.24 = bf16[256,3584]{0,1:T(8,128)(2,1)} collective-permute-done((bf16[256,3584]{0,1:T(8,128)(2,1)}, bf16[256,3584]{0,1:T(8,128)(2,1)}, u32[]{:S(2)}, u32[]{:S(2)}) %collective-permute-start.24) | collective-permute-done | bytes 1835040 | tf_op jit(solution)/shard_map/ppermute | solution.py:75
  186.1 3.8 add_convert_fusion.1
  189.9 2.7 fusion.51
  192.9 2.4 fusion.9
  195.3 72.7 %collective-permute-done.2 = bf16[256,512]{1,0:T(8,128)(2,1)S(1)} collective-permute-done((bf16[256,512]{1,0:T(8,128)(2,1)S(1)}, bf16[256,512]{1,0:T(8,128)(2,1)S(1)}, u32[]{:S(2)}, u32[]{:S(2)}) %collective-permute-start.2) | collective-permute-done | bytes 262176 | tf_op jit(solution)/shard_map/ppermute | solution.py:12
  270.0 3.4 collective-permute-start.39
  276.4 3.2 fusion
  281.7 2.7 fusion.55
  284.4 2.2 fusion.11
  291.7 18.9 %collective-permute-start.44 = (bf16[256,3584]{0,1:T(8,128)(2,1)}, bf16[256,3584]{0,1:T(8,128)(2,1)}, u32[]{:S(2)}, u32[]{:S(2)}) collective-permute-start(bf16[256,3584]{0,1:T(8,128)(2,1)} %get-tuple-element.33), channel_id=1, source_target_pairs={{0,8},{2,10},{4,12},{6,14},{24,16},{26,18},{28,20},{30,22},{1,9},{... | collective-permute-start | bytes 5505032 | tf_op jit(solution)/shard_map/ppermute | solution.py:75
  312.1 3.0 fusion.1
  315.1 3.3 collective-permute-done.18
  319.7 38.1 %collective-permute-done.31 = bf16[256,3584]{0,1:T(8,128)(2,1)S(1)} collective-permute-done((bf16[256,3584]{0,1:T(8,128)(2,1)}, bf16[256,3584]{0,1:T(8,128)(2,1)S(1)}, u32[]{:S(2)}, u32[]{:S(2)}) %collective-permute-start.31) | collective-permute-done | bytes 1835040 | tf_op jit(solution)/shard_map/ppermute | solution.py:75
  359.0 7.1 add_convert_fusion
  366.6 2.2 fusion.8
  376.9 2.3 fusion.10
  384.2 7.1 collective-permute-done.11
  391.2 2.6 add_convert_fusion.3
  397.8 3.1 fusion.112
  415.0 3.2 fusion.105
  418.2 3.2 fusion.107
  434.3 3.4 fusion.109
  437.7 4.1 fusion.101
  441.9 3.2 fusion.111
  445.1 3.1 fusion.16
  453.0 2.5 collective-permute-done.19
  456.5 10.2 %collective-permute-done.25 = bf16[4,256,256]{1,2,0:T(8,128)(2,1)S(1)} collective-permute-done((bf16[4,256,256]{1,2,0:T(8,128)(2,1)S(1)}, bf16[4,256,256]{1,2,0:T(8,128)(2,1)S(1)}, u32[]{:S(2)}, u32[]{:S(2)}) %collective-permute-start.25) | collective-permute-done | bytes 524320 | tf_op jit(solution)/shard_map/ppermute | solution.py:83
  469.0 9.0 %collective-permute-done.32 = bf16[4,256,256]{1,2,0:T(8,128)(2,1)S(1)} collective-permute-done((bf16[4,256,256]{1,2,0:T(8,128)(2,1)S(1)}, bf16[4,256,256]{1,2,0:T(8,128)(2,1)S(1)}, u32[]{:S(2)}, u32[]{:S(2)}) %collective-permute-start.32) | collective-permute-done | bytes 524320 | tf_op jit(solution)/shard_map/ppermute | solution.py:83
  479.2 14.4 %collective-permute-done.45 = bf16[4,256,256]{1,2,0:T(8,128)(2,1)S(1)} collective-permute-done((bf16[4,256,256]{1,2,0:T(8,128)(2,1)S(1)}, bf16[4,256,256]{1,2,0:T(8,128)(2,1)S(1)}, u32[]{:S(2)}, u32[]{:S(2)}) %collective-permute-start.45) | collective-permute-done | bytes 524320 | tf_op jit(solution)/shard_map/ppermute | solution.py:83
  498.3 3.8 collective-permute-done.22
  502.1 4.8 collective-permute-done.21
  509.2 4.2 collective-permute-done.28
  513.4 4.8 collective-permute-done.27
  521.6 3.0 collective-permute-done.35
  524.6 4.8 collective-permute-done.34
  531.7 4.2 collective-permute-done.48
  535.8 5.1 fusion.103
  542.4 3.5 collective-permute-start.52
  547.1 3.7 collective-permute-start.36
  557.1 2.5 copy.18
  559.6 2.3 pad_maximum_fusion.9
  562.0 2.6 copy.14
  564.5 2.4 broadcast_select_fusion.1
  569.8 25.7 %collective-permute-done.37 = bf16[4,256,256]{1,2,0:T(8,128)(2,1)} collective-permute-done((bf16[4,256,256]{1,2,0:T(8,128)(2,1)}, bf16[4,256,256]{1,2,0:T(8,128)(2,1)}, u32[]{:S(2)}, u32[]{:S(2)}) %collective-permute-start.37) | collective-permute-done | bytes 524320 | tf_op jit(solution)/shard_map/ppermute | solution.py:75
  598.8 2.6 copy.19
  603.4 3.3 collective-permute-done.53
  607.6 2.5 bitcast_add_fusion.5
  612.1 7.7 %collective-permute-done.51 = bf16[4,256,256]{1,2,0:T(8,128)(2,1)S(1)} collective-permute-done((bf16[4,256,256]{1,2,0:T(8,128)(2,1)}, bf16[4,256,256]{1,2,0:T(8,128)(2,1)S(1)}, u32[]{:S(2)}, u32[]{:S(2)}) %collective-permute-start.51) | collective-permute-done | bytes 524320 | tf_op jit(solution)/shard_map/ppermute | solution.py:75
  635.0 80.1 %collective-permute-done.58 = f32[256,512]{1,0:T(8,128)} collective-permute-done((f32[256,512]{1,0:T(8,128)}, f32[256,512]{1,0:T(8,128)}, u32[]{:S(2)}, u32[]{:S(2)}) %collective-permute-start.58) | collective-permute-done | bytes 524320 | tf_op jit(solution)/shard_map/ppermute | solution.py:83
  715.1 2.3 multiply_add_fusion
  717.4 2.8 convert_add_fusion
  729.4 4.7 copy.34
  (283 shorter events, 140.4 us)
Async XLA Ops:
  7.2 145.0 %all-gather.2.cloned.1.call-start = ((), (), s32[]{:S(2)}) async-start(), calls=%async_computation | async-start | bytes 3899392 | tf_op jit(solution)/shard_map/all_gather | solution.py:112
  24.2 109.5 %collective-permute-start.23 = (bf16[256,3584]{0,1:T(8,128)(2,1)}, bf16[256,3584]{0,1:T(8,128)(2,1)}, u32[]{:S(2)}, u32[]{:S(2)}) collective-permute-start(bf16[256,3584]{0,1:T(8,128)(2,1)} %get-tuple-element.35), channel_id=1, source_target_pairs={{8,16},{10,18},{12,20},{14,22},{16,8},{18,10},{20,12},{22,14},{9,1... | collective-permute-start | bytes 5505032 | tf_op jit(solution)/shard_map/ppermute | solution.py:75
  26.1 122.3 %collective-permute-start.16 = (bf16[256,3584]{0,1:T(8,128)(2,1)S(1)}, bf16[256,3584]{0,1:T(8,128)(2,1)}, u32[]{:S(2)}, u32[]{:S(2)}) collective-permute-start(bf16[256,3584]{0,1:T(8,128)(2,1)S(1)} %get-tuple-element.34), channel_id=1, source_target_pairs={{0,8},{2,10},{4,12},{6,14},{24,16},{26,18},{28,20},{30,22},{1,9},{... | collective-permute-start | bytes 5505032 | tf_op jit(solution)/shard_map/ppermute | solution.py:75
  33.9 116.4 %collective-permute-start.29 = (bf16[256,3584]{0,1:T(8,128)(2,1)}, bf16[256,3584]{0,1:T(8,128)(2,1)}, u32[]{:S(2)}, u32[]{:S(2)}) collective-permute-start(bf16[256,3584]{0,1:T(8,128)(2,1)} %get-tuple-element.35), channel_id=1, source_target_pairs={{0,8},{2,10},{4,12},{6,14},{24,16},{26,18},{28,20},{30,22},{1,9},{... | collective-permute-start | bytes 5505032 | tf_op jit(solution)/shard_map/ppermute | solution.py:75
  36.4 238.2 %collective-permute-start.4 = (bf16[512,3584]{0,1:T(8,128)(2,1)}, bf16[512,3584]{0,1:T(8,128)(2,1)}, u32[]{:S(2)}, u32[]{:S(2)}) collective-permute-start(bf16[512,3584]{0,1:T(8,128)(2,1)} %copy.40), channel_id=1, source_target_pairs={{0,4},{2,6},{4,0},{6,2},{8,12},{10,14},{12,8},{14,10},{16,20},{18,... | collective-permute-start | bytes 11010056 | tf_op jit(solution)/shard_map/ppermute | solution.py:12
  43.5 90.2 %collective-permute-start.9 = (bf16[256,512]{1,0:T(8,128)(2,1)S(1)}, bf16[256,512]{1,0:T(8,128)(2,1)S(1)}, u32[]{:S(2)}, u32[]{:S(2)}) collective-permute-start(bf16[256,512]{1,0:T(8,128)(2,1)S(1)} %all_gather.7), channel_id=1, source_target_pairs={{0,24},{2,26},{4,28},{6,30},{8,16},{10,18},{12,20},{14,22},{16,8},... | collective-permute-start | bytes 786440 | tf_op jit(solution)/shard_map/ppermute | solution.py:12
  133.7 13.0 %collective-permute-start.8 = (bf16[256,512]{1,0:T(8,128)(2,1)S(1)}, bf16[256,512]{1,0:T(8,128)(2,1)S(1)}, u32[]{:S(2)}, u32[]{:S(2)}) collective-permute-start(bf16[256,512]{1,0:T(8,128)(2,1)S(1)} %all_gather.7), channel_id=1, source_target_pairs={{0,16},{2,18},{4,20},{6,22},{8,24},{10,26},{12,28},{14,30},{16,0},... | collective-permute-start | bytes 786440 | tf_op jit(solution)/shard_map/ppermute | solution.py:12
  133.7 50.7 %collective-permute-start.24 = (bf16[256,3584]{0,1:T(8,128)(2,1)}, bf16[256,3584]{0,1:T(8,128)(2,1)}, u32[]{:S(2)}, u32[]{:S(2)}) collective-permute-start(bf16[256,3584]{0,1:T(8,128)(2,1)} %collective-permute-done.23), channel_id=1, source_target_pairs={{8,0},{10,2},{12,4},{14,6},{16,24},{18,26},{20,28},{22,30},{9,1},{... | collective-permute-start | bytes 5505032 | tf_op jit(solution)/shard_map/ppermute | solution.py:75
  147.4 45.2 %collective-permute-start.38 = (bf16[256,512]{1,0:T(8,128)(2,1)S(1)}, bf16[256,512]{1,0:T(8,128)(2,1)S(1)}, u32[]{:S(2)}, u32[]{:S(2)}) collective-permute-start(bf16[256,512]{1,0:T(8,128)(2,1)S(1)} %all_gather.7), channel_id=1, source_target_pairs={{0,8},{2,10},{4,12},{6,14},{8,0},{10,2},{12,4},{14,6},{16,24},{18,... | collective-permute-start | bytes 786440 | tf_op jit(solution)/shard_map/ppermute | solution.py:12
  148.4 121.6 %collective-permute-start.17 = (bf16[256,3584]{0,1:T(8,128)(2,1)}, bf16[256,3584]{0,1:T(8,128)(2,1)}, u32[]{:S(2)}, u32[]{:S(2)}) collective-permute-start(bf16[256,3584]{0,1:T(8,128)(2,1)} %collective-permute-done.16), channel_id=1, source_target_pairs={{8,16},{10,18},{12,20},{14,22},{16,8},{18,10},{20,12},{22,14},{9,1... | collective-permute-start | bytes 5505032 | tf_op jit(solution)/shard_map/ppermute | solution.py:75
  150.3 123.1 %collective-permute-start.30 = (bf16[256,3584]{0,1:T(8,128)(2,1)}, bf16[256,3584]{0,1:T(8,128)(2,1)}, u32[]{:S(2)}, u32[]{:S(2)}) collective-permute-start(bf16[256,3584]{0,1:T(8,128)(2,1)} %collective-permute-done.29), channel_id=1, source_target_pairs={{8,16},{10,18},{12,20},{14,22},{16,8},{18,10},{20,12},{22,14},{9,1... | collective-permute-start | bytes 5505032 | tf_op jit(solution)/shard_map/ppermute | solution.py:75
  156.1 289.0 %copy-start.2 = (bf16[512,3584]{0,1:T(8,128)(2,1)}, bf16[512,3584]{0,1:T(8,128)(2,1)S(1)}, u32[]{:S(2)}) copy-start(bf16[512,3584]{0,1:T(8,128)(2,1)S(1)} %fusion.3) | copy-start | bytes 11010052
  160.7 375.1 %copy-start = (bf16[512,3584]{0,1:T(8,128)(2,1)}, bf16[512,3584]{0,1:T(8,128)(2,1)S(1)}, u32[]{:S(2)}) copy-start(bf16[512,3584]{0,1:T(8,128)(2,1)S(1)} %fusion.2) | copy-start | bytes 11010052
  184.4 126.2 %collective-permute-start.3 = (bf16[512,3584]{0,1:T(8,128)(2,1)S(1)}, bf16[512,3584]{0,1:T(8,128)(2,1)S(1)}, u32[]{:S(2)}, u32[]{:S(2)}) collective-permute-start(bf16[512,3584]{0,1:T(8,128)(2,1)S(1)} %copy-done.5), channel_id=1, source_target_pairs={{0,4},{2,6},{4,0},{6,2},{8,12},{10,14},{12,8},{14,10},{16,20},{18,... | collective-permute-start | bytes 11010056 | tf_op jit(solution)/shard_map/ppermute | solution.py:12
  192.5 75.5 %copy-start.20 = (bf16[256,3584]{0,1:T(8,128)(2,1)S(1)}, bf16[256,3584]{0,1:T(8,128)(2,1)}, u32[]{:S(2)}) copy-start(bf16[256,3584]{0,1:T(8,128)(2,1)} %copy-done.19) | copy-start | bytes 5505028
  192.6 75.5 %collective-permute-start.2 = (bf16[256,512]{1,0:T(8,128)(2,1)S(1)}, bf16[256,512]{1,0:T(8,128)(2,1)S(1)}, u32[]{:S(2)}, u32[]{:S(2)}) collective-permute-start(bf16[256,512]{1,0:T(8,128)(2,1)S(1)} %all_gather.7), channel_id=1, source_target_pairs={{0,4},{2,6},{4,0},{6,2},{8,12},{10,14},{12,8},{14,10},{16,20},{18,... | collective-permute-start | bytes 786440 | tf_op jit(solution)/shard_map/ppermute | solution.py:12
  195.3 95.2 %copy-start.23 = (bf16[256,3584]{0,1:T(8,128)(2,1)}, bf16[256,3584]{0,1:T(8,128)(2,1)S(1)}, u32[]{:S(2)}) copy-start(bf16[256,3584]{0,1:T(8,128)(2,1)S(1)} %fusion.9) | copy-start | bytes 5505028
  268.1 23.7 %collective-permute-start.10 = (bf16[256,3584]{0,1:T(8,128)(2,1)S(1)}, bf16[256,3584]{0,1:T(8,128)(2,1)}, u32[]{:S(2)}, u32[]{:S(2)}) collective-permute-start(bf16[256,3584]{0,1:T(8,128)(2,1)S(1)} %copy-done.20), channel_id=1, source_target_pairs={{8,16},{10,18},{12,20},{14,22},{16,8},{18,10},{20,12},{22,14},{9,1... | collective-permute-start | bytes 5505032 | tf_op jit(solution)/shard_map/ppermute | solution.py:75
  270.0 96.0 %collective-permute-start.39 = (bf16[256,3584]{0,1:T(8,128)(2,1)}, bf16[256,3584]{0,1:T(8,128)(2,1)}, u32[]{:S(2)}, u32[]{:S(2)}) collective-permute-start(bf16[256,3584]{0,1:T(8,128)(2,1)} %get-tuple-element.32), channel_id=1, source_target_pairs={{0,8},{2,10},{4,12},{6,14},{24,16},{26,18},{28,20},{30,22},{1,9},{... | collective-permute-start | bytes 5505032 | tf_op jit(solution)/shard_map/ppermute | solution.py:75
  273.4 45.0 %collective-permute-start.18 = (bf16[256,3584]{0,1:T(8,128)(2,1)}, bf16[256,3584]{0,1:T(8,128)(2,1)S(1)}, u32[]{:S(2)}, u32[]{:S(2)}) collective-permute-start(bf16[256,3584]{0,1:T(8,128)(2,1)} %collective-permute-done.17), channel_id=1, source_target_pairs={{8,0},{10,2},{12,4},{14,6},{16,24},{18,26},{20,28},{22,30},{9,1},{... | collective-permute-start | bytes 5505032 | tf_op jit(solution)/shard_map/ppermute | solution.py:75
  274.7 83.1 %collective-permute-start.31 = (bf16[256,3584]{0,1:T(8,128)(2,1)}, bf16[256,3584]{0,1:T(8,128)(2,1)S(1)}, u32[]{:S(2)}, u32[]{:S(2)}) collective-permute-start(bf16[256,3584]{0,1:T(8,128)(2,1)} %collective-permute-done.30), channel_id=1, source_target_pairs={{8,0},{10,2},{12,4},{14,6},{16,24},{18,26},{20,28},{22,30},{9,1},{... | collective-permute-start | bytes 5505032 | tf_op jit(solution)/shard_map/ppermute | solution.py:75
  291.7 85.0 %collective-permute-start.44 = (bf16[256,3584]{0,1:T(8,128)(2,1)}, bf16[256,3584]{0,1:T(8,128)(2,1)}, u32[]{:S(2)}, u32[]{:S(2)}) collective-permute-start(bf16[256,3584]{0,1:T(8,128)(2,1)} %get-tuple-element.33), channel_id=1, source_target_pairs={{0,8},{2,10},{4,12},{6,14},{24,16},{26,18},{28,20},{30,22},{1,9},{... | collective-permute-start | bytes 5505032 | tf_op jit(solution)/shard_map/ppermute | solution.py:75
  310.6 80.6 %collective-permute-start.11 = (bf16[256,3584]{0,1:T(8,128)(2,1)}, bf16[256,3584]{0,1:T(8,128)(2,1)}, u32[]{:S(2)}, u32[]{:S(2)}) collective-permute-start(bf16[256,3584]{0,1:T(8,128)(2,1)} %collective-permute-done.10), channel_id=1, source_target_pairs={{8,0},{10,2},{12,4},{14,6},{16,24},{18,26},{20,28},{22,30},{9,1},{... | collective-permute-start | bytes 5505032 | tf_op jit(solution)/shard_map/ppermute | solution.py:75
  318.4 95.4 %collective-permute-start.1 = (bf16[512,3584]{0,1:T(8,128)(2,1)S(1)}, bf16[512,3584]{0,1:T(8,128)(2,1)}, u32[]{:S(2)}, u32[]{:S(2)}) collective-permute-start(bf16[512,3584]{0,1:T(8,128)(2,1)S(1)} %fusion.2), channel_id=1, source_target_pairs={{0,2},{2,0},{4,6},{6,4},{8,10},{10,8},{12,14},{14,12},{16,18},{18,... | collective-permute-start | bytes 11010056 | tf_op jit(solution)/shard_map/ppermute | solution.py:12
  359.0 59.3 %collective-permute-start.6 = (bf16[512,3584]{0,1:T(8,128)(2,1)S(1)}, bf16[512,3584]{0,1:T(8,128)(2,1)}, u32[]{:S(2)}, u32[]{:S(2)}) collective-permute-start(bf16[512,3584]{0,1:T(8,128)(2,1)S(1)} %fusion), channel_id=1, source_target_pairs={{0,2},{2,0},{4,6},{6,4},{8,10},{10,8},{12,14},{14,12},{16,18},{18,... | collective-permute-start | bytes 11010056 | tf_op jit(solution)/shard_map/ppermute | solution.py:12
  366.0 41.3 %collective-permute-start = (bf16[512,3584]{0,1:T(8,128)(2,1)S(1)}, bf16[512,3584]{0,1:T(8,128)(2,1)S(1)}, u32[]{:S(2)}, u32[]{:S(2)}) collective-permute-start(bf16[512,3584]{0,1:T(8,128)(2,1)S(1)} %fusion.3), channel_id=1, source_target_pairs={{0,2},{2,0},{4,6},{6,4},{8,10},{10,8},{12,14},{14,12},{16,18},{18,... | collective-permute-start | bytes 11010056 | tf_op jit(solution)/shard_map/ppermute | solution.py:12
  376.8 31.8 %collective-permute-start.5 = (bf16[512,3584]{0,1:T(8,128)(2,1)S(1)}, bf16[512,3584]{0,1:T(8,128)(2,1)S(1)}, u32[]{:S(2)}, u32[]{:S(2)}) collective-permute-start(bf16[512,3584]{0,1:T(8,128)(2,1)S(1)} %copy-done.6), channel_id=1, source_target_pairs={{0,2},{2,0},{4,6},{6,4},{8,10},{10,8},{12,14},{14,12},{16,18},{18,... | collective-permute-start | bytes 11010056 | tf_op jit(solution)/shard_map/ppermute | solution.py:12
  429.3 21.4 %collective-permute-start.12 = (bf16[4,256,256]{1,2,0:T(8,128)(2,1)S(1)}, bf16[4,256,256]{1,2,0:T(8,128)(2,1)S(1)}, u32[]{:S(2)}, u32[]{:S(2)}) collective-permute-start(bf16[4,256,256]{1,2,0:T(8,128)(2,1)S(1)} %dynamic-slice_convert_fusion.5), channel_id=1, source_target_pairs={{0,1},{1,0},{2,3},{3,2},{4,5},{5,4},{6,7},{7,6},{8,9},{9,8},{10,11... | collective-permute-start | bytes 1572872 | tf_op jit(solution)/shard_map/ppermute | solution.py:83
  430.3 25.2 %collective-permute-start.19 = (bf16[4,256,256]{1,2,0:T(8,128)(2,1)S(1)}, bf16[4,256,256]{1,2,0:T(8,128)(2,1)S(1)}, u32[]{:S(2)}, u32[]{:S(2)}) collective-permute-start(bf16[4,256,256]{1,2,0:T(8,128)(2,1)S(1)} %dynamic-slice_convert_fusion.4), channel_id=1, source_target_pairs={{0,1},{1,0},{2,3},{3,2},{4,5},{5,4},{6,7},{7,6},{8,9},{9,8},{10,11... | collective-permute-start | bytes 1572872 | tf_op jit(solution)/shard_map/ppermute | solution.py:83
  431.4 35.3 %collective-permute-start.25 = (bf16[4,256,256]{1,2,0:T(8,128)(2,1)S(1)}, bf16[4,256,256]{1,2,0:T(8,128)(2,1)S(1)}, u32[]{:S(2)}, u32[]{:S(2)}) collective-permute-start(bf16[4,256,256]{1,2,0:T(8,128)(2,1)S(1)} %dynamic-slice_convert_fusion.3), channel_id=1, source_target_pairs={{0,1},{1,0},{2,3},{3,2},{4,5},{5,4},{6,7},{7,6},{8,9},{9,8},{10,11... | collective-permute-start | bytes 1572872 | tf_op jit(solution)/shard_map/ppermute | solution.py:83
  432.3 45.7 %collective-permute-start.32 = (bf16[4,256,256]{1,2,0:T(8,128)(2,1)S(1)}, bf16[4,256,256]{1,2,0:T(8,128)(2,1)S(1)}, u32[]{:S(2)}, u32[]{:S(2)}) collective-permute-start(bf16[4,256,256]{1,2,0:T(8,128)(2,1)S(1)} %dynamic-slice_convert_fusion.2), channel_id=1, source_target_pairs={{0,1},{1,0},{2,3},{3,2},{4,5},{5,4},{6,7},{7,6},{8,9},{9,8},{10,11... | collective-permute-start | bytes 1572872 | tf_op jit(solution)/shard_map/ppermute | solution.py:83
  433.4 61.2 %collective-permute-start.40 = (bf16[4,256,256]{1,2,0:T(8,128)(2,1)S(1)}, bf16[4,256,256]{1,2,0:T(8,128)(2,1)S(1)}, u32[]{:S(2)}, u32[]{:S(2)}) collective-permute-start(bf16[4,256,256]{1,2,0:T(8,128)(2,1)S(1)} %dynamic-slice_convert_fusion.1), channel_id=1, source_target_pairs={{0,1},{1,0},{2,3},{3,2},{4,5},{5,4},{6,7},{7,6},{8,9},{9,8},{10,11... | collective-permute-start | bytes 1572872 | tf_op jit(solution)/shard_map/ppermute | solution.py:83
  450.8 42.8 %collective-permute-start.45 = (bf16[4,256,256]{1,2,0:T(8,128)(2,1)S(1)}, bf16[4,256,256]{1,2,0:T(8,128)(2,1)S(1)}, u32[]{:S(2)}, u32[]{:S(2)}) collective-permute-start(bf16[4,256,256]{1,2,0:T(8,128)(2,1)S(1)} %dynamic-slice_convert_fusion), channel_id=1, source_target_pairs={{0,1},{1,0},{2,3},{3,2},{4,5},{5,4},{6,7},{7,6},{8,9},{9,8},{10,11... | collective-permute-start | bytes 1572872 | tf_op jit(solution)/shard_map/ppermute | solution.py:83
  455.5 40.1 %collective-permute-start.15 = (f32[256,256]{0,1:T(8,128)S(1)}, f32[256,256]{0,1:T(8,128)S(1)}, u32[]{:S(2)}, u32[]{:S(2)}) collective-permute-start(f32[256,256]{0,1:T(8,128)S(1)} %get-tuple-element.47), channel_id=1, source_target_pairs={{0,6},{2,4},{4,2},{6,0},{8,14},{10,12},{12,10},{14,8},{16,22},{18,... | collective-permute-start | bytes 786440 | tf_op jit(solution)/shard_map/ppermute | solution.py:12
  466.7 29.7 %collective-permute-start.14 = (f32[256,256]{0,1:T(8,128)S(1)}, f32[256,256]{0,1:T(8,128)S(1)}, u32[]{:S(2)}, u32[]{:S(2)}) collective-permute-start(f32[256,256]{0,1:T(8,128)S(1)} %get-tuple-element.48), channel_id=1, source_target_pairs={{0,4},{2,6},{4,0},{6,2},{8,12},{10,14},{12,8},{14,10},{16,20},{18,... | collective-permute-start | bytes 786440 | tf_op jit(solution)/shard_map/ppermute | solution.py:12
  478.0 19.2 %collective-permute-start.13 = (f32[256,256]{0,1:T(8,128)S(1)}, f32[256,256]{0,1:T(8,128)S(1)}, u32[]{:S(2)}, u32[]{:S(2)}) collective-permute-start(f32[256,256]{0,1:T(8,128)S(1)} %get-tuple-element.49), channel_id=1, source_target_pairs={{0,2},{2,0},{4,6},{6,4},{8,10},{10,8},{12,14},{14,12},{16,18},{18,... | collective-permute-start | bytes 786440 | tf_op jit(solution)/shard_map/ppermute | solution.py:12
  493.6 8.5 %collective-permute-start.22 = (f32[256,256]{0,1:T(8,128)S(1)}, f32[256,256]{0,1:T(8,128)S(1)}, u32[]{:S(2)}, u32[]{:S(2)}) collective-permute-start(f32[256,256]{0,1:T(8,128)S(1)} %get-tuple-element.43), channel_id=1, source_target_pairs={{0,6},{2,4},{4,2},{6,0},{8,14},{10,12},{12,10},{14,8},{16,22},{18,... | collective-permute-start | bytes 786440 | tf_op jit(solution)/shard_map/ppermute | solution.py:12
  494.6 12.4 %collective-permute-start.21 = (f32[256,256]{0,1:T(8,128)S(1)}, f32[256,256]{0,1:T(8,128)S(1)}, u32[]{:S(2)}, u32[]{:S(2)}) collective-permute-start(f32[256,256]{0,1:T(8,128)S(1)} %get-tuple-element.44), channel_id=1, source_target_pairs={{0,4},{2,6},{4,0},{6,2},{8,12},{10,14},{12,8},{14,10},{16,20},{18,... | collective-permute-start | bytes 786440 | tf_op jit(solution)/shard_map/ppermute | solution.py:12
  495.6 12.6 %collective-permute-start.20 = (f32[256,256]{0,1:T(8,128)S(1)}, f32[256,256]{0,1:T(8,128)S(1)}, u32[]{:S(2)}, u32[]{:S(2)}) collective-permute-start(f32[256,256]{0,1:T(8,128)S(1)} %get-tuple-element.45), channel_id=1, source_target_pairs={{0,2},{2,0},{4,6},{6,4},{8,10},{10,8},{12,14},{14,12},{16,18},{18,... | collective-permute-start | bytes 786440 | tf_op jit(solution)/shard_map/ppermute | solution.py:12
  496.5 16.9 %collective-permute-start.28 = (f32[256,256]{0,1:T(8,128)S(1)}, f32[256,256]{0,1:T(8,128)S(1)}, u32[]{:S(2)}, u32[]{:S(2)}) collective-permute-start(f32[256,256]{0,1:T(8,128)S(1)} %get-tuple-element.59), channel_id=1, source_target_pairs={{0,6},{2,4},{4,2},{6,0},{8,14},{10,12},{12,10},{14,8},{16,22},{18,... | collective-permute-start | bytes 786440 | tf_op jit(solution)/shard_map/ppermute | solution.py:12
  497.1 21.1 %collective-permute-start.27 = (f32[256,256]{0,1:T(8,128)S(1)}, f32[256,256]{0,1:T(8,128)S(1)}, u32[]{:S(2)}, u32[]{:S(2)}) collective-permute-start(f32[256,256]{0,1:T(8,128)S(1)} %get-tuple-element.60), channel_id=1, source_target_pairs={{0,4},{2,6},{4,0},{6,2},{8,12},{10,14},{12,8},{14,10},{16,20},{18,... | collective-permute-start | bytes 786440 | tf_op jit(solution)/shard_map/ppermute | solution.py:12
  502.1 18.3 %collective-permute-start.26 = (f32[256,256]{0,1:T(8,128)S(1)}, f32[256,256]{0,1:T(8,128)S(1)}, u32[]{:S(2)}, u32[]{:S(2)}) collective-permute-start(f32[256,256]{0,1:T(8,128)S(1)} %get-tuple-element.61), channel_id=1, source_target_pairs={{0,2},{2,0},{4,6},{6,4},{8,10},{10,8},{12,14},{14,12},{16,18},{18,... | collective-permute-start | bytes 786440 | tf_op jit(solution)/shard_map/ppermute | solution.py:12
  507.0 17.6 %collective-permute-start.35 = (f32[256,256]{0,1:T(8,128)S(1)}, f32[256,256]{0,1:T(8,128)S(1)}, u32[]{:S(2)}, u32[]{:S(2)}) collective-permute-start(f32[256,256]{0,1:T(8,128)S(1)} %get-tuple-element.55), channel_id=1, source_target_pairs={{0,6},{2,4},{4,2},{6,0},{8,14},{10,12},{12,10},{14,8},{16,22},{18,... | collective-permute-start | bytes 786440 | tf_op jit(solution)/shard_map/ppermute | solution.py:12
  508.1 21.3 %collective-permute-start.34 = (f32[256,256]{0,1:T(8,128)S(1)}, f32[256,256]{0,1:T(8,128)S(1)}, u32[]{:S(2)}, u32[]{:S(2)}) collective-permute-start(f32[256,256]{0,1:T(8,128)S(1)} %get-tuple-element.56), channel_id=1, source_target_pairs={{0,4},{2,6},{4,0},{6,2},{8,12},{10,14},{12,8},{14,10},{16,20},{18,... | collective-permute-start | bytes 786440 | tf_op jit(solution)/shard_map/ppermute | solution.py:12
  513.4 17.3 %collective-permute-start.33 = (f32[256,256]{0,1:T(8,128)S(1)}, f32[256,256]{0,1:T(8,128)S(1)}, u32[]{:S(2)}, u32[]{:S(2)}) collective-permute-start(f32[256,256]{0,1:T(8,128)S(1)} %get-tuple-element.57), channel_id=1, source_target_pairs={{0,2},{2,0},{4,6},{6,4},{8,10},{10,8},{12,14},{14,12},{16,18},{18,... | collective-permute-start | bytes 786440 | tf_op jit(solution)/shard_map/ppermute | solution.py:12
  518.2 17.6 %collective-permute-start.48 = (f32[256,256]{0,1:T(8,128)S(1)}, f32[256,256]{0,1:T(8,128)S(1)}, u32[]{:S(2)}, u32[]{:S(2)}) collective-permute-start(f32[256,256]{0,1:T(8,128)S(1)} %get-tuple-element.63), channel_id=1, source_target_pairs={{0,6},{2,4},{4,2},{6,0},{8,14},{10,12},{12,10},{14,8},{16,22},{18,... | collective-permute-start | bytes 786440 | tf_op jit(solution)/shard_map/ppermute | solution.py:12
  520.5 20.5 %collective-permute-start.47 = (f32[256,256]{0,1:T(8,128)S(1)}, f32[256,256]{0,1:T(8,128)S(1)}, u32[]{:S(2)}, u32[]{:S(2)}) collective-permute-start(f32[256,256]{0,1:T(8,128)S(1)} %get-tuple-element.64), channel_id=1, source_target_pairs={{0,4},{2,6},{4,0},{6,2},{8,12},{10,14},{12,8},{14,10},{16,20},{18,... | collective-permute-start | bytes 786440 | tf_op jit(solution)/shard_map/ppermute | solution.py:12
  524.6 17.8 %collective-permute-start.46 = (f32[256,256]{0,1:T(8,128)S(1)}, f32[256,256]{0,1:T(8,128)S(1)}, u32[]{:S(2)}, u32[]{:S(2)}) collective-permute-start(f32[256,256]{0,1:T(8,128)S(1)} %get-tuple-element.65), channel_id=1, source_target_pairs={{0,2},{2,0},{4,6},{6,4},{8,10},{10,8},{12,14},{14,12},{16,18},{18,... | collective-permute-start | bytes 786440 | tf_op jit(solution)/shard_map/ppermute | solution.py:12
  529.4 17.6 %collective-permute-start.43 = (f32[256,256]{0,1:T(8,128)S(1)}, f32[256,256]{0,1:T(8,128)S(1)}, u32[]{:S(2)}, u32[]{:S(2)}) collective-permute-start(f32[256,256]{0,1:T(8,128)S(1)} %get-tuple-element.51), channel_id=1, source_target_pairs={{0,6},{2,4},{4,2},{6,0},{8,14},{10,12},{12,10},{14,8},{16,22},{18,... | collective-permute-start | bytes 786440 | tf_op jit(solution)/shard_map/ppermute | solution.py:12
  530.6 21.3 %collective-permute-start.42 = (f32[256,256]{0,1:T(8,128)S(1)}, f32[256,256]{0,1:T(8,128)S(1)}, u32[]{:S(2)}, u32[]{:S(2)}) collective-permute-start(f32[256,256]{0,1:T(8,128)S(1)} %get-tuple-element.52), channel_id=1, source_target_pairs={{0,4},{2,6},{4,0},{6,2},{8,12},{10,14},{12,8},{14,10},{16,20},{18,... | collective-permute-start | bytes 786440 | tf_op jit(solution)/shard_map/ppermute | solution.py:12
  535.8 17.4 %collective-permute-start.41 = (f32[256,256]{0,1:T(8,128)S(1)}, f32[256,256]{0,1:T(8,128)S(1)}, u32[]{:S(2)}, u32[]{:S(2)}) collective-permute-start(f32[256,256]{0,1:T(8,128)S(1)} %get-tuple-element.53), channel_id=1, source_target_pairs={{0,2},{2,0},{4,6},{6,4},{8,10},{10,8},{12,14},{14,12},{16,18},{18,... | collective-permute-start | bytes 786440 | tf_op jit(solution)/shard_map/ppermute | solution.py:12
  541.0 60.4 %collective-permute-start.54 = (bf16[4,256,256]{1,2,0:T(8,128)(2,1)}, bf16[4,256,256]{1,2,0:T(8,128)(2,1)}, u32[]{:S(2)}, u32[]{:S(2)}) collective-permute-start(bf16[4,256,256]{1,2,0:T(8,128)(2,1)} %get-tuple-element.4), channel_id=1, source_target_pairs={{8,16},{10,18},{12,20},{14,22},{9,17},{11,19},{13,21},{15,23}} | collective-permute-start | bytes 1572872 | tf_op jit(solution)/shard_map/ppermute | solution.py:75
  542.4 59.7 %collective-permute-start.52 = (bf16[4,256,256]{1,2,0:T(8,128)(2,1)}, bf16[4,256,256]{1,2,0:T(8,128)(2,1)}, u32[]{:S(2)}, u32[]{:S(2)}) collective-permute-start(bf16[4,256,256]{1,2,0:T(8,128)(2,1)} %get-tuple-element.4), channel_id=1, source_target_pairs={{0,16},{2,18},{4,20},{6,22},{24,8},{26,10},{28,12},{30,14},{1,17},... | collective-permute-start | bytes 1572872 | tf_op jit(solution)/shard_map/ppermute | solution.py:75
  547.1 21.5 %collective-permute-start.36 = (bf16[4,256,256]{1,2,0:T(8,128)(2,1)}, bf16[4,256,256]{1,2,0:T(8,128)(2,1)}, u32[]{:S(2)}, u32[]{:S(2)}) collective-permute-start(bf16[4,256,256]{1,2,0:T(8,128)(2,1)} %get-tuple-element.13), channel_id=1, source_target_pairs={{0,16},{2,18},{4,20},{6,22},{24,8},{26,10},{28,12},{30,14},{1,17},... | collective-permute-start | bytes 1572872 | tf_op jit(solution)/shard_map/ppermute | solution.py:75
  551.9 43.6 %collective-permute-start.37 = (bf16[4,256,256]{1,2,0:T(8,128)(2,1)}, bf16[4,256,256]{1,2,0:T(8,128)(2,1)}, u32[]{:S(2)}, u32[]{:S(2)}) collective-permute-start(bf16[4,256,256]{1,2,0:T(8,128)(2,1)} %get-tuple-element.17), channel_id=1, source_target_pairs={{16,0},{18,2},{20,4},{22,6},{8,24},{10,26},{12,28},{14,30},{17,1},... | collective-permute-start | bytes 1572872 | tf_op jit(solution)/shard_map/ppermute | solution.py:75
  553.2 53.5 %collective-permute-start.53 = (bf16[4,256,256]{1,2,0:T(8,128)(2,1)}, bf16[4,256,256]{1,2,0:T(8,128)(2,1)}, u32[]{:S(2)}, u32[]{:S(2)}) collective-permute-start(bf16[4,256,256]{1,2,0:T(8,128)(2,1)} %get-tuple-element.8), channel_id=1, source_target_pairs={{16,0},{18,2},{20,4},{22,6},{8,24},{10,26},{12,28},{14,30},{17,1},... | collective-permute-start | bytes 1572872 | tf_op jit(solution)/shard_map/ppermute | solution.py:75
  568.6 41.6 %collective-permute-start.56 = (bf16[4,256,256]{1,2,0:T(8,128)(2,1)}, bf16[4,256,256]{1,2,0:T(8,128)(2,1)}, u32[]{:S(2)}, u32[]{:S(2)}) collective-permute-start(bf16[4,256,256]{1,2,0:T(8,128)(2,1)} %get-tuple-element.8), channel_id=1, source_target_pairs={{24,0},{26,2},{28,4},{30,6},{25,1},{27,3},{29,5},{31,7}} | collective-permute-start | bytes 1572872 | tf_op jit(solution)/shard_map/ppermute | solution.py:75
  595.6 14.6 %collective-permute-start.55 = (bf16[4,256,256]{1,2,0:T(8,128)(2,1)}, bf16[4,256,256]{1,2,0:T(8,128)(2,1)}, u32[]{:S(2)}, u32[]{:S(2)}) collective-permute-start(bf16[4,256,256]{1,2,0:T(8,128)(2,1)} %get-tuple-element.6), channel_id=1, source_target_pairs={{16,24},{18,26},{20,28},{22,30},{17,25},{19,27},{21,29},{23,31}} | collective-permute-start | bytes 1572872 | tf_op jit(solution)/shard_map/ppermute | solution.py:75
  601.4 10.7 %collective-permute-start.49 = (bf16[4,256,256]{1,2,0:T(8,128)(2,1)}, bf16[4,256,256]{1,2,0:T(8,128)(2,1)S(1)}, u32[]{:S(2)}, u32[]{:S(2)}) collective-permute-start(bf16[4,256,256]{1,2,0:T(8,128)(2,1)} %get-tuple-element.13), channel_id=1, source_target_pairs={{8,16},{10,18},{12,20},{14,22},{9,17},{11,19},{13,21},{15,23}} | collective-permute-start | bytes 1572872 | tf_op jit(solution)/shard_map/ppermute | solution.py:75
  602.1 17.7 %collective-permute-start.51 = (bf16[4,256,256]{1,2,0:T(8,128)(2,1)}, bf16[4,256,256]{1,2,0:T(8,128)(2,1)S(1)}, u32[]{:S(2)}, u32[]{:S(2)}) collective-permute-start(bf16[4,256,256]{1,2,0:T(8,128)(2,1)} %get-tuple-element.17), channel_id=1, source_target_pairs={{24,0},{26,2},{28,4},{30,6},{25,1},{27,3},{29,5},{31,7}} | collective-permute-start | bytes 1572872 | tf_op jit(solution)/shard_map/ppermute | solution.py:75
  606.7 13.1 %collective-permute-start.50 = (bf16[4,256,256]{1,2,0:T(8,128)(2,1)}, bf16[4,256,256]{1,2,0:T(8,128)(2,1)S(1)}, u32[]{:S(2)}, u32[]{:S(2)}) collective-permute-start(bf16[4,256,256]{1,2,0:T(8,128)(2,1)} %get-tuple-element.15), channel_id=1, source_target_pairs={{16,24},{18,26},{20,28},{22,30},{17,25},{19,27},{21,29},{23,31}} | collective-permute-start | bytes 1572872 | tf_op jit(solution)/shard_map/ppermute | solution.py:75
  623.1 97.0 %collective-permute-start.57 = (f32[4,2,256,256]{3,2,1,0:T(8,128)}, f32[4,2,256,256]{3,2,1,0:T(8,128)}, u32[]{:S(2)}, u32[]{:S(2)}) collective-permute-start(f32[4,2,256,256]{3,2,1,0:T(8,128)} %pad_maximum_fusion.7), channel_id=1, source_target_pairs={{0,1},{1,0},{2,3},{3,2},{4,5},{5,4},{6,7},{7,6},{8,9},{9,8},{10,11... | collective-permute-start | bytes 6291464 | tf_op jit(solution)/shard_map/ppermute | solution.py:83
  629.4 87.9 %collective-permute-start.7 = (bf16[3,512,512]{2,1,0:T(8,128)(2,1)}, bf16[3,512,512]{2,1,0:T(8,128)(2,1)}, u32[]{:S(2)}, u32[]{:S(2)}) collective-permute-start(bf16[3,512,512]{2,1,0:T(8,128)(2,1)} %fusion.13), channel_id=1, source_target_pairs={{0,1},{1,0},{2,3},{3,2},{4,5},{5,4},{6,7},{7,6},{8,9},{9,8},{10,11... | collective-permute-start | bytes 4718600 | tf_op jit(solution)/shard_map/ppermute | solution.py:83
  634.5 80.6 %collective-permute-start.58 = (f32[256,512]{1,0:T(8,128)}, f32[256,512]{1,0:T(8,128)}, u32[]{:S(2)}, u32[]{:S(2)}) collective-permute-start(f32[256,512]{1,0:T(8,128)} %constant_dynamic-slice_fusion), channel_id=1, source_target_pairs={{0,1},{1,0},{2,3},{3,2},{4,5},{5,4},{6,7},{7,6},{8,9},{9,8},{10,11... | collective-permute-start | bytes 1572872 | tf_op jit(solution)/shard_map/ppermute | solution.py:83
  (45 other events, 694.1 us)
Sparse Core Ops, SparseCore 0:
  10.3 63.5 all-gather.1

commit v3 on v1

v3 whole, which is shorter than its diff:
```python
import jax
import jax.numpy as jnp
from jax import lax
from jax.experimental import pallas as pl
from jax.experimental.pallas import tpu as pltpu
from jax.sharding import PartitionSpec as P

decay_rate = 0.95
GROUP = 4
CHUNKS = 2


def swap(array, mask):
    count = lax.axis_size("row")
    return lax.ppermute(array, "row", [(i, i ^ mask) for i in range(count)])


def from_behind(array, by):
    count = lax.axis_size("row")
    return lax.ppermute(array, "row", [(i, (i + by) % count) for i in range(count)])


def trade(array):
    return lax.ppermute(array, "col", [(0, 1), (1, 0)])


def gradient_tile(columns, cotangent_all, accumulated):
    product = lax.dot_general(
        columns, cotangent_all, (((1,), (0,)), ((), ())), preferred_element_type=jnp.float32
    )
    return (product + accumulated.astype(jnp.float32)).astype(jnp.bfloat16)


def block_product(left, right):
    return lax.dot_general(
        left, right, (((1,), (1,)), ((), ())), preferred_element_type=jnp.float32
    )


def products_kernel(*refs):
    *lefts, raw, columns, cotangent, out = refs
    panel = gradient_tile(columns[...], cotangent[...], raw[...])
    parts = [block_product(left[...], panel) for left in lefts]

    @pl.when(pl.program_id(0) == 0)
    def _():
        for u, part in enumerate(parts):
            out[u] = part

    @pl.when(pl.program_id(0) > 0)
    def _():
        for u, part in enumerate(parts):
            out[u] += part


def panel_products(group, raw, columns, cotangent_all):
    block, width = group[0].shape
    rows, tokens = columns.shape
    depth = max(d for d in range(128, 1025, 128) if width % d == 0)
    return pl.pallas_call(
        products_kernel,
        grid=(width // depth,),
        in_specs=[pl.BlockSpec((block, depth), lambda k: (0, k))] * len(group)
        + [
            pl.BlockSpec((rows, depth), lambda k: (0, k)),
            pl.BlockSpec((rows, tokens), lambda k: (0, 0)),
            pl.BlockSpec((tokens, depth), lambda k: (0, k)),
        ],
        out_specs=pl.BlockSpec((len(group), block, rows), lambda k: (0, 0, 0)),
        out_shape=jax.ShapeDtypeStruct((len(group), block, rows), jnp.float32),
        compiler_params=pltpu.CompilerParams(
            dimension_semantics=("arbitrary",), vmem_limit_bytes=48 * 2**20
        ),
        cost_estimate=pl.CostEstimate(
            flops=2 * rows * width * (len(group) * block + tokens),
            bytes_accessed=2 * width * (len(group) * block + rows + tokens)
            + 4 * len(group) * block * rows,
            transcendentals=0,
        ),
    )(*group, raw, columns, cotangent_all)


def body(activations, cotangent, accumulated, band_old, diagonal_old):
    n_row, n_col = lax.axis_size("row"), lax.axis_size("col")
    block, width = accumulated.shape
    band = n_row // 2
    steps = band // GROUP
    place = lax.axis_index("row") % GROUP
    y = lax.axis_index("col")

    columns = lax.all_gather(activations, "col", axis=0, tiled=True)
    parcel = jnp.concatenate([accumulated, columns.T], axis=1)
    moving = from_behind(parcel, GROUP)
    across_parcel = swap(parcel, 2)
    cotangent_all = lax.all_gather(cotangent, "row", axis=0, tiled=True)

    def gradient_of(parcel):
        return gradient_tile(parcel[:, width:], cotangent_all, parcel[:, :width])

    def products(parcel):
        return panel_products(group, parcel[:, :width], parcel[:, width:], cotangent_all)

    def to_owners(made):
        return jnp.stack([made[0]] + [swap(made[u], u) for u in range(1, GROUP)])

    own = gradient_of(parcel)
    across = gradient_of(across_parcel)
    group = [own, swap(own, 1), across, swap(across, 1)]

    sums = [None] * (steps + 1)
    own_products = [block_product(own, panel) for panel in group]
    for step in range(1, steps):
        arrived = moving
        moving = from_behind(arrived, GROUP) if step < steps - 1 else [
            from_behind(piece, GROUP) for piece in jnp.split(arrived, CHUNKS)
        ]
        made = products(arrived)
        if step == steps - 1:
            moving[0], made, own_products = lax.optimization_barrier(
                (moving[0], made, own_products)
            )
        sums[steps - step] = to_owners(made)
    sums[steps] = jnp.stack(own_products)

    if n_col == 2:
        sums[steps] += trade(sums[steps].astype(jnp.bfloat16)).astype(jnp.float32)
        for step in range(1, steps):
            narrow = sums[steps - step].astype(jnp.bfloat16)
            sums[steps - step] += trade(narrow).astype(jnp.float32)
    last = []
    for piece in moving:
        part = to_owners(products(piece))
        if n_col == 2:
            part += trade(part.astype(jnp.bfloat16)).astype(jnp.float32)
        last.append(part)
    sums[0] = jnp.concatenate(last, axis=2)
    stacked = jnp.concatenate(sums)

    def at(offset):
        t = band + place - offset
        return lax.dynamic_index_in_dim(
            stacked, t - t % GROUP + ((t % GROUP) ^ place), 0, keepdims=False
        )

    share = band // n_col
    if n_col == 2:
        band_sum = jnp.stack([at(s + y * share) for s in range(1, share + 1)], axis=1)
        diagonal = lax.dynamic_slice_in_dim(sums[steps][0], y * (block // 2), block // 2, 0)
    else:
        band_sum = jnp.swapaxes(
            lax.psum_scatter(
                jnp.stack([at(s) for s in range(1, band + 1)]),
                "col",
                scatter_dimension=0,
                tiled=True,
            ),
            0,
            1,
        )
        diagonal = lax.psum_scatter(own_products[0], "col", scatter_dimension=0, tiled=True)
    band_new = decay_rate * band_old + (1.0 - decay_rate) * band_sum
    diagonal_new = decay_rate * diagonal_old + (1.0 - decay_rate) * diagonal
    return (band_new, diagonal_new)


def solution(mesh):
    in_specs = (
        P("col", "row"),
        P("row", "col"),
        P("row", "col"),
        P("row", "col", None),
        P(("row", "col"), None),
    )
    out_specs = (P("row", "col", None), P(("row", "col"), None))
    return jax.shard_map(body, mesh=mesh, in_specs=in_specs, out_specs=out_specs, check_vma=False)
```

time: 668 us -> 579 us (0.87)
  waiting for transfers between devices: 468 us -> 370 us
  matrix products: 122 us -> 51.1 us
  Pallas kernels: 0 us -> 58.7 us
  other arithmetic: 7.51 us -> 26.8 us
    ppermute x2 -> x3, waiting for transfers between devices: 302 us -> 84.8 us  [from_behind(): lax.ppermute(array, 'row', [(i, (i + by) % count) for i in range(count)])]
    ppermute x9 -> x12, waiting for transfers between devices: 24.7 us -> 154 us  [swap(): return lax.ppermute(array, 'row', [(i, i ^ mask) for i in range(count)])]
    reduce_scatter x2 -> x0, waiting for transfers between devices: 94.7 us -> none  [the longest x1 94.7 us: body(): lax.psum_scatter(jnp.stack([at(s) for s in range(1, band + 1)]), 'col', s...]
    dot_general x12 -> x4, matrix products: 113 us -> 35.3 us  [block_product(): lax.dot_general(left, right, (((1,), (1,)), ((), ())), preferred_element_...]
    ppermute x0 -> x4, waiting for transfers between devices: none -> 75.4 us  [trade(): return lax.ppermute(array, 'col', [(0, 1), (1, 0)])]
    pallas_call x0 -> x3, Pallas kernels: none -> 58.7 us  [panel_products(): pl.pallas_call(products_kernel, grid=(width // depth,), in_specs=[pl.Bloc...]
    unnamed x16 -> x52, local copies, waits for them, and re-layouts: 27.2 us -> 9.36 us
    slice x0 -> x10, local copies, waits for them, and re-layouts: none -> 17 us  [the longest x3 11.1 us: products(): parcel[:, :width]]
  transfers between devices with their start and end apart: 14 -> 20, of which waited for: 6 -> 10; matrix products, arithmetic and copies ran while one was open for 19% -> 16% of each run, Pallas kernels for 0% -> 10%
where the time goes in v3:
time: 579 us
  waiting for transfers between devices  370 us (64%)
  Pallas kernels  58.7 us (10%)
  matrix products  51.1 us (9%)
  local copies, waits for them, and re-layouts  32.3 us (6%)
  other arithmetic  26.8 us (5%)
  starting transfers between devices  18.5 us (3%)
  between operations  14.4 us (2%)
  blocking collectives  7.16 us (1%)
    ppermute x12, waiting for transfers between devices, swap(): return lax.ppermute(array, 'row', [(i, i ^ mask) for i in range(count)])  154 us
    ppermute x3, waiting for transfers between devices, from_behind(): lax.ppermute(array, 'row', [(i, (i + by) % count) for i in range(count)])  84.8 us
    ppermute x4, waiting for transfers between devices, trade(): return lax.ppermute(array, 'col', [(0, 1), (1, 0)])  75.4 us
    pallas_call x3, Pallas kernels, panel_products(): pl.pallas_call(products_kernel, grid=(width // depth,), in_specs=[pl.Bloc...  58.7 us
    all_gather x1, waiting for transfers between devices, body(): cotangent_all = lax.all_gather(cotangent, 'row', axis=0, tiled=True)  54.8 us
    dot_general x4, matrix products, block_product(): lax.dot_general(left, right, (((1,), (1,)), ((), ())), preferred_element_...  35.3 us
    dot_general x2, matrix products, gradient_tile(): lax.dot_general(columns, cotangent_all, (((1,), (0,)), ((), ())), preferr...  15.7 us
  transfers between devices with their start and end apart: 20, of which 10 were waited for; matrix products, arithmetic and copies ran while one was open for 16% of the time, Pallas kernels for 10%

profile of v3, /device:TPU:0, one launch (start us, length us, event | category | flops | bytes accessed | tf_op | source)
XLA Modules:
  0.0 578.6 jit_solution(13717989861819410075)
XLA Ops:
  7.2 0.7 all-gather.2.cloned.1.call-update
  7.9 1.0 copy.9
  8.9 7.2 %all_gather.6 = bf16[256,512]{0,1:T(8,128)(2,1)S(1)} all-gather(bf16[128,512]{0,1:T(8,128)(2,1)S(1)} %copy.9), channel_id=1, replica_groups=mesh['row'=16,'col'=2] {'col'}, dimensions={0}, use_global_device_ids=true | all-gather | bytes 393216 | tf_op jit(solution)/shard_map/all_gather | solution.py:91
  16.1 6.6 %pad_maximum_fusion.1 = bf16[512,7424]{1,0:T(8,128)(2,1)} fusion(bf16[512,256]{1,0:T(8,128)(2,1)S(1)} %bitcast.67, bf16[512,7168]{1,0:T(8,128)(2,1)} %param.7), kind=kLoop, calls=%fused_computation.3 | loop fusion | flops 15204352 | bytes 15204352 | tf_op jit(solution)/shard_map/concatenate | solution.py:92
  22.7 1.7 collective-permute-start.1
  24.5 1.6 collective-permute-start.3
  26.0 54.8 %all-gather.2.cloned.1.call-done.refs_6_ = bf16[256,7168]{1,0:T(8,128)(2,1)} async-done(((bf16[16,7168]{1,0:T(8,128)(2,1)}), bf16[256,7168]{1,0:T(8,128)(2,1)}) %all-gather.2.cloned.1.call-update) | async-done | bytes 3670032 | tf_op jit(solution)/shard_map/all_gather | solution.py:95
  80.8 9.5 %add_convert_fusion.1.refs_0_ = bf16[512,7168]{1,0:T(8,128)(2,1)} fusion(bf16[512,7168]{1,0:T(8,128)(2,1)} %param.7, bf16[256,512]{0,1:T(8,128)(2,1)S(1)} %all_gather.6, bf16[256,7168]{1,0:T(8,128)(2,1)} %all-gather.2.cloned.1.call-done.refs_6_), kind=kOutput, calls=%fused_computation.1 | convolution fusion | flops 1890058240 | bytes 18612224 | tf_op jit(solution)/shard_map/dot_general | solution.py:28
  90.3 0.3 collective-permute-start
  90.5 108.4 %collective-permute-done.1 = bf16[512,7424]{1,0:T(8,128)(2,1)} collective-permute-done((bf16[512,7424]{1,0:T(8,128)(2,1)}, bf16[512,7424]{1,0:T(8,128)(2,1)}, u32[]{:S(2)}, u32[]{:S(2)}) %collective-permute-start.1) | collective-permute-done | bytes 7602208 | tf_op jit(solution)/shard_map/ppermute | solution.py:15
  199.0 6.3 %add_convert_fusion.refs_2_ = bf16[512,7168]{1,0:T(8,128)(2,1)} fusion(bf16[256,7168]{1,0:T(8,128)(2,1)S(1)} %copy-done, bf16[512,7424]{1,0:T(8,128)(2,1)} %collective-permute-done.1), kind=kOutput, calls=%fused_computation | convolution fusion | flops 1890058240 | bytes 18612224 | tf_op jit(solution)/shard_map/dot_general | solution.py:28
  205.2 9.4 %fusion.10 = f32[512,512]{1,0:T(8,128)S(1)} fusion(bf16[512,7168]{1,0:T(8,128)(2,1)} %add_convert_fusion.1.refs_0_), kind=kOutput, calls=%fused_computation.38 | convolution fusion | flops 3758096384 | bytes 8388608 | tf_op jit(solution)/shard_map/dot_general | solution.py:35
  214.7 5.4 fusion.6
  220.1 1.5 collective-permute-start.4
  221.6 8.5 %fusion.12 = f32[512,512]{1,0:T(8,128)S(1)} fusion(bf16[512,7168]{1,0:T(8,128)(2,1)} %add_convert_fusion.1.refs_0_, bf16[512,7168]{1,0:T(8,128)(2,1)} %add_convert_fusion.refs_2_), kind=kOutput, calls=%fused_computation.40 | convolution fusion | flops 3758096384 | bytes 15728640 | tf_op jit(solution)/shard_map/dot_general | solution.py:35
  230.1 1.7 collective-permute-start.9
  231.8 1.0 slice.87.refs_5_
  232.8 6.6 %slice.86.refs_4_ = bf16[512,7168]{1,0:T(8,128)(2,1)} slice(bf16[512,7424]{1,0:T(8,128)(2,1)} %collective-permute-done.3), slice={[0:512], [0:7168]} | slice | bytes 14680064 | tf_op jit(solution)/shard_map/slice | solution.py:101
  239.3 8.5 %fusion.11 = f32[512,512]{1,0:T(8,128)S(1)} fusion(bf16[512,7168]{1,0:T(8,128)(2,1)} %add_convert_fusion.1.refs_0_, bf16[512,7168]{1,0:T(8,128)(2,1)} %collective-permute-done.refs_1_), kind=kOutput, calls=%fused_computation.39 | convolution fusion | flops 3758096384 | bytes 15728640 | tf_op jit(solution)/shard_map/dot_general | solution.py:35
  247.9 8.9 %fusion.13 = f32[512,512]{1,0:T(8,128)S(1)} fusion(bf16[512,7168]{1,0:T(8,128)(2,1)} %add_convert_fusion.1.refs_0_, bf16[512,7168]{1,0:T(8,128)(2,1)} %collective-permute-done.2.refs_3_), kind=kOutput, calls=%fused_computation.41 | convolution fusion | flops 3758096384 | bytes 15728640 | tf_op jit(solution)/shard_map/dot_general | solution.py:35
  256.8 26.2 %shard_map.68 = f32[4,512,512]{2,1,0:T(8,128)} custom-call(bf16[512,7168]{1,0:T(8,128)(2,1)} %add_convert_fusion.1.refs_0_, bf16[512,7168]{1,0:T(8,128)(2,1)} %collective-permute-done.refs_1_, bf16[512,7168]{1,0:T(8,128)(2,1)} %add_convert_fusion.refs_2_, bf16[512,7168]{1,0:T(8,128)(2,1)} %collective-permute-done.2.refs_3_, ...), custom_call_target="tpu_custom_call" | custom-call | flops 16911433728 | bytes 44564480 | tf_op jit(solution)/shard_map/pallas_call | solution.py:60
  283.0 24.2 %collective-permute-done.4 = bf16[256,7424]{1,0:T(8,128)(2,1)} collective-permute-done((bf16[256,7424]{1,0:T(8,128)(2,1)}, bf16[256,7424]{1,0:T(8,128)(2,1)}, u32[]{:S(2)}, u32[]{:S(2)}) %collective-permute-start.4) | collective-permute-done | bytes 3801120 | tf_op jit(solution)/shard_map/ppermute | solution.py:20
  307.1 0.9 slice.68.refs_5_
  308.1 2.3 slice.67.refs_4_
  310.3 16.0 %shard_map.69 = f32[4,512,256]{2,1,0:T(8,128)S(1)} custom-call(bf16[512,7168]{1,0:T(8,128)(2,1)} %add_convert_fusion.1.refs_0_, bf16[512,7168]{1,0:T(8,128)(2,1)} %collective-permute-done.refs_1_, bf16[512,7168]{1,0:T(8,128)(2,1)} %add_convert_fusion.refs_2_, bf16[512,7168]{1,0:T(8,128)(2,1)} %collective-permute-done.2.refs_3_, ...), custom_call_target="tpu_custom_call" | custom-call | flops 8455716864 | bytes 38797312 | tf_op jit(solution)/shard_map/pallas_call | solution.py:60
  326.4 1.2 fusion.8
  327.6 60.7 %collective-permute-done.9 = bf16[256,7424]{1,0:T(8,128)(2,1)} collective-permute-done((bf16[256,7424]{1,0:T(8,128)(2,1)}, bf16[256,7424]{1,0:T(8,128)(2,1)}, u32[]{:S(2)}, u32[]{:S(2)}) %collective-permute-start.9) | collective-permute-done | bytes 3801120 | tf_op jit(solution)/shard_map/ppermute | solution.py:20
  388.2 0.9 slice.93.refs_5_
  389.1 2.3 slice.92.refs_4_
  391.4 0.4 collective-permute-start.6
  391.8 1.8 fusion.7
  393.6 1.8 collective-permute-start.16
  395.4 0.3 collective-permute-start.15
  395.7 16.4 %shard_map.70 = f32[4,512,256]{2,1,0:T(8,128)S(1)} custom-call(bf16[512,7168]{1,0:T(8,128)(2,1)} %add_convert_fusion.1.refs_0_, bf16[512,7168]{1,0:T(8,128)(2,1)} %collective-permute-done.refs_1_, bf16[512,7168]{1,0:T(8,128)(2,1)} %add_convert_fusion.refs_2_, bf16[512,7168]{1,0:T(8,128)(2,1)} %collective-permute-done.2.refs_3_, ...), custom_call_target="tpu_custom_call" | custom-call | flops 8455716864 | bytes 38797312 | tf_op jit(solution)/shard_map/pallas_call | solution.py:60
  412.2 1.7 fusion.1
  414.0 0.8 copy-done.16
  414.8 1.7 collective-permute-start.18
  416.6 1.2 collective-permute-start.12
  417.8 9.2 %collective-permute-done.16 = f32[512,512]{1,0:T(8,128)S(1)} collective-permute-done((f32[512,512]{1,0:T(8,128)}, f32[512,512]{1,0:T(8,128)S(1)}, u32[]{:S(2)}, u32[]{:S(2)}) %collective-permute-start.16) | collective-permute-done | bytes 1048608 | tf_op jit(solution)/shard_map/ppermute | solution.py:15
  426.9 1.7 collective-permute-start.11
  428.6 22.8 %collective-permute-done.15 = f32[512,512]{1,0:T(8,128)S(1)} collective-permute-done((f32[512,512]{1,0:T(8,128)}, f32[512,512]{1,0:T(8,128)S(1)}, u32[]{:S(2)}, u32[]{:S(2)}) %collective-permute-start.15) | collective-permute-done | bytes 1048608 | tf_op jit(solution)/shard_map/ppermute | solution.py:15
  451.5 2.7 fusion.4
  454.2 1.5 collective-permute-start.8
  455.7 1.8 fusion.2
  457.5 3.1 collective-permute-done.12
  460.5 1.7 collective-permute-start.17
  462.2 10.4 %collective-permute-done.11 = f32[512,256]{1,0:T(8,128)S(1)} collective-permute-done((f32[512,256]{1,0:T(8,128)S(1)}, f32[512,256]{1,0:T(8,128)S(1)}, u32[]{:S(2)}, u32[]{:S(2)}) %collective-permute-start.11) | collective-permute-done | bytes 524320 | tf_op jit(solution)/shard_map/ppermute | solution.py:15
  472.7 1.3 fusion.3
  474.0 1.5 collective-permute-start.13
  475.5 10.5 %collective-permute-done.8 = bf16[4,512,256]{2,1,0:T(8,128)(2,1)} collective-permute-done((bf16[4,512,256]{2,1,0:T(8,128)(2,1)}, bf16[4,512,256]{2,1,0:T(8,128)(2,1)}, u32[]{:S(2)}, u32[]{:S(2)}) %collective-permute-start.8) | collective-permute-done | bytes 1048608 | tf_op jit(solution)/shard_map/ppermute | solution.py:24
  486.0 1.9 convert_add_fusion.3
  487.9 64.9 %collective-permute-done.13 = bf16[4,512,256]{2,1,0:T(8,128)(2,1)} collective-permute-done((bf16[4,512,256]{2,1,0:T(8,128)(2,1)}, bf16[4,512,256]{2,1,0:T(8,128)(2,1)}, u32[]{:S(2)}, u32[]{:S(2)}) %collective-permute-start.13) | collective-permute-done | bytes 1048608 | tf_op jit(solution)/shard_map/ppermute | solution.py:24
  552.8 1.4 convert_add_fusion.2
  554.3 2.4 convert_add_fusion
  556.9 0.9 bitcast_add_fusion
  557.8 0.4 copy-done.10
  558.2 0.3 copy-done.12
  558.5 0.3 copy-done.14
  558.8 2.3 convert_add_fusion.1
  561.2 2.0 pad_maximum_fusion
  563.2 0.5 dynamic-slice_bitcast_fusion.3
  563.7 1.7 copy-done.1
  565.4 1.6 fusion
  567.0 4.7 copy.10
  (63 shorter events, 0.4 us)
Async XLA Ops:
  7.2 73.6 %all-gather.2.cloned.1.call-start = ((), (), s32[]{:S(2)}) async-start(), calls=%async_computation | async-start | bytes 3899392 | tf_op jit(solution)/shard_map/all_gather | solution.py:95
  22.7 176.2 %collective-permute-start.1 = (bf16[512,7424]{1,0:T(8,128)(2,1)}, bf16[512,7424]{1,0:T(8,128)(2,1)}, u32[]{:S(2)}, u32[]{:S(2)}) collective-permute-start(bf16[512,7424]{1,0:T(8,128)(2,1)} %pad_maximum_fusion.1), channel_id=1, source_target_pairs={{0,4},{2,6},{4,0},{6,2},{8,12},{10,14},{12,8},{14,10},{16,20},{18,... | collective-permute-start | bytes 22806536 | tf_op jit(solution)/shard_map/ppermute | solution.py:15
  24.5 190.2 %collective-permute-start.3 = (bf16[512,7424]{1,0:T(8,128)(2,1)}, bf16[512,7424]{1,0:T(8,128)(2,1)}, u32[]{:S(2)}, u32[]{:S(2)}) collective-permute-start(bf16[512,7424]{1,0:T(8,128)(2,1)} %pad_maximum_fusion.1), channel_id=1, source_target_pairs={{0,8},{2,10},{4,12},{6,14},{8,16},{10,18},{12,20},{14,22},{16,24},... | collective-permute-start | bytes 22806536 | tf_op jit(solution)/shard_map/ppermute | solution.py:20
  80.8 118.2 %copy-start = (bf16[256,7168]{1,0:T(8,128)(2,1)S(1)}, bf16[256,7168]{1,0:T(8,128)(2,1)}, u32[]{:S(2)}) copy-start(bf16[256,7168]{1,0:T(8,128)(2,1)} %all-gather.2.cloned.1.call-done.refs_6_) | copy-start | bytes 11010052
  90.3 149.1 %collective-permute-start = (bf16[512,7168]{1,0:T(8,128)(2,1)}, bf16[512,7168]{1,0:T(8,128)(2,1)}, u32[]{:S(2)}, u32[]{:S(2)}) collective-permute-start(bf16[512,7168]{1,0:T(8,128)(2,1)} %add_convert_fusion.1.refs_0_), channel_id=1, source_target_pairs={{0,2},{2,0},{4,6},{6,4},{8,10},{10,8},{12,14},{14,12},{16,18},{18,... | collective-permute-start | bytes 22020104 | tf_op jit(solution)/shard_map/ppermute | solution.py:15
  205.2 42.6 %collective-permute-start.2 = (bf16[512,7168]{1,0:T(8,128)(2,1)}, bf16[512,7168]{1,0:T(8,128)(2,1)}, u32[]{:S(2)}, u32[]{:S(2)}) collective-permute-start(bf16[512,7168]{1,0:T(8,128)(2,1)} %add_convert_fusion.refs_2_), channel_id=1, source_target_pairs={{0,2},{2,0},{4,6},{6,4},{8,10},{10,8},{12,14},{14,12},{16,18},{18,... | collective-permute-start | bytes 22020104 | tf_op jit(solution)/shard_map/ppermute | solution.py:15
  220.1 87.1 %collective-permute-start.4 = (bf16[256,7424]{1,0:T(8,128)(2,1)}, bf16[256,7424]{1,0:T(8,128)(2,1)}, u32[]{:S(2)}, u32[]{:S(2)}) collective-permute-start(bf16[256,7424]{1,0:T(8,128)(2,1)} %get-tuple-element.21), channel_id=1, source_target_pairs={{0,8},{2,10},{4,12},{6,14},{8,16},{10,18},{12,20},{14,22},{16,24},... | collective-permute-start | bytes 11403272 | tf_op jit(solution)/shard_map/ppermute | solution.py:20
  230.1 182.1 %copy-start.3 = (f32[512,512]{1,0:T(8,128)}, f32[512,512]{1,0:T(8,128)S(1)}, u32[]{:S(2)}) copy-start(f32[512,512]{1,0:T(8,128)S(1)} %fusion.12) | copy-start | bytes 3145732
  230.1 158.1 %collective-permute-start.9 = (bf16[256,7424]{1,0:T(8,128)(2,1)}, bf16[256,7424]{1,0:T(8,128)(2,1)}, u32[]{:S(2)}, u32[]{:S(2)}) collective-permute-start(bf16[256,7424]{1,0:T(8,128)(2,1)} %get-tuple-element.20), channel_id=1, source_target_pairs={{0,8},{2,10},{4,12},{6,14},{8,16},{10,18},{12,20},{14,22},{16,24},... | collective-permute-start | bytes 11403272 | tf_op jit(solution)/shard_map/ppermute | solution.py:20
  247.9 164.3 %copy-start.5 = (f32[512,512]{1,0:T(8,128)}, f32[512,512]{1,0:T(8,128)S(1)}, u32[]{:S(2)}) copy-start(f32[512,512]{1,0:T(8,128)S(1)} %fusion.11) | copy-start | bytes 3145732
  256.8 155.5 %copy-start.7 = (f32[512,512]{1,0:T(8,128)}, f32[512,512]{1,0:T(8,128)S(1)}, u32[]{:S(2)}) copy-start(f32[512,512]{1,0:T(8,128)S(1)} %fusion.13) | copy-start | bytes 3145732
  327.6 64.3 %copy-start.2 = (f32[4,512,512]{2,1,0:T(8,128)S(1)}, f32[4,512,512]{2,1,0:T(8,128)}, u32[]{:S(2)}) copy-start(f32[4,512,512]{2,1,0:T(8,128)} %shard_map.68) | copy-start | bytes 12582916
  327.6 68.2 %collective-permute-start.7 = (f32[512,256]{1,0:T(8,128)S(1)}, f32[512,256]{1,0:T(8,128)S(1)}, u32[]{:S(2)}, u32[]{:S(2)}) collective-permute-start(f32[512,256]{1,0:T(8,128)S(1)} %get-tuple-element.27), channel_id=1, source_target_pairs={{0,6},{2,4},{4,2},{6,0},{8,14},{10,12},{12,10},{14,8},{16,22},{18,... | collective-permute-start | bytes 1572872 | tf_op jit(solution)/shard_map/ppermute | solution.py:15
  391.4 22.6 %collective-permute-start.6 = (f32[512,256]{1,0:T(8,128)}, f32[512,256]{1,0:T(8,128)S(1)}, u32[]{:S(2)}, u32[]{:S(2)}) collective-permute-start(f32[512,256]{1,0:T(8,128)} %get-tuple-element.28), channel_id=1, source_target_pairs={{0,4},{2,6},{4,0},{6,2},{8,12},{10,14},{12,8},{14,10},{16,20},{18,... | collective-permute-start | bytes 1572872 | tf_op jit(solution)/shard_map/ppermute | solution.py:15
  391.8 24.8 %collective-permute-start.5 = (f32[512,256]{1,0:T(8,128)}, f32[512,256]{1,0:T(8,128)}, u32[]{:S(2)}, u32[]{:S(2)}) collective-permute-start(f32[512,256]{1,0:T(8,128)} %get-tuple-element.29), channel_id=1, source_target_pairs={{0,2},{2,0},{4,6},{6,4},{8,10},{10,8},{12,14},{14,12},{16,18},{18,... | collective-permute-start | bytes 1572872 | tf_op jit(solution)/shard_map/ppermute | solution.py:15
  393.6 33.3 %collective-permute-start.16 = (f32[512,512]{1,0:T(8,128)}, f32[512,512]{1,0:T(8,128)S(1)}, u32[]{:S(2)}, u32[]{:S(2)}) collective-permute-start(f32[512,512]{1,0:T(8,128)} %get-tuple-element.23), channel_id=1, source_target_pairs={{0,6},{2,4},{4,2},{6,0},{8,14},{10,12},{12,10},{14,8},{16,22},{18,... | collective-permute-start | bytes 3145736 | tf_op jit(solution)/shard_map/ppermute | solution.py:15
  395.4 56.1 %collective-permute-start.15 = (f32[512,512]{1,0:T(8,128)}, f32[512,512]{1,0:T(8,128)S(1)}, u32[]{:S(2)}, u32[]{:S(2)}) collective-permute-start(f32[512,512]{1,0:T(8,128)} %get-tuple-element.24), channel_id=1, source_target_pairs={{0,4},{2,6},{4,0},{6,2},{8,12},{10,14},{12,8},{14,10},{16,20},{18,... | collective-permute-start | bytes 3145736 | tf_op jit(solution)/shard_map/ppermute | solution.py:15
  395.7 55.7 %copy-start.15 = (f32[512,256]{1,0:T(8,128)}, f32[512,256]{1,0:T(8,128)S(1)}, u32[]{:S(2)}) copy-start(f32[512,256]{1,0:T(8,128)S(1)} %collective-permute-done.7) | copy-start | bytes 1572868
  395.7 58.4 %collective-permute-start.14 = (f32[512,512]{1,0:T(8,128)}, f32[512,512]{1,0:T(8,128)S(1)}, u32[]{:S(2)}, u32[]{:S(2)}) collective-permute-start(f32[512,512]{1,0:T(8,128)} %get-tuple-element.25), channel_id=1, source_target_pairs={{0,2},{2,0},{4,6},{6,4},{8,10},{10,8},{12,14},{14,12},{16,18},{18,... | collective-permute-start | bytes 3145736 | tf_op jit(solution)/shard_map/ppermute | solution.py:15
  414.0 0.8 copy-start.16
  414.8 139.5 %collective-permute-start.18 = (bf16[4,512,512]{2,1,0:T(8,128)(2,1)}, bf16[4,512,512]{2,1,0:T(8,128)(2,1)}, u32[]{:S(2)}, u32[]{:S(2)}) collective-permute-start(bf16[4,512,512]{2,1,0:T(8,128)(2,1)} %fusion.1), channel_id=1, source_target_pairs={{0,1},{1,0},{2,3},{3,2},{4,5},{5,4},{6,7},{7,6},{8,9},{9,8},{10,11... | collective-permute-start | bytes 6291464 | tf_op jit(solution)/shard_map/ppermute | solution.py:24
  416.5 35.0 %copy-start.17 = (f32[512,256]{1,0:T(8,128)S(1)}, f32[512,256]{1,0:T(8,128)}, u32[]{:S(2)}) copy-start(f32[512,256]{1,0:T(8,128)} %copy-done.16) | copy-start | bytes 1572868
  416.6 43.9 %collective-permute-start.12 = (f32[512,256]{1,0:T(8,128)S(1)}, f32[512,256]{1,0:T(8,128)S(1)}, u32[]{:S(2)}, u32[]{:S(2)}) collective-permute-start(f32[512,256]{1,0:T(8,128)S(1)} %get-tuple-element.31), channel_id=1, source_target_pairs={{0,6},{2,4},{4,2},{6,0},{8,14},{10,12},{12,10},{14,8},{16,22},{18,... | collective-permute-start | bytes 1572872 | tf_op jit(solution)/shard_map/ppermute | solution.py:15
  426.9 30.5 %copy-start.9 = (f32[512,512]{1,0:T(8,128)}, f32[512,512]{1,0:T(8,128)S(1)}, u32[]{:S(2)}) copy-start(f32[512,512]{1,0:T(8,128)S(1)} %collective-permute-done.16) | copy-start | bytes 3145732
  426.9 45.7 %collective-permute-start.11 = (f32[512,256]{1,0:T(8,128)S(1)}, f32[512,256]{1,0:T(8,128)S(1)}, u32[]{:S(2)}, u32[]{:S(2)}) collective-permute-start(f32[512,256]{1,0:T(8,128)S(1)} %get-tuple-element.32), channel_id=1, source_target_pairs={{0,4},{2,6},{4,0},{6,2},{8,12},{10,14},{12,8},{14,10},{16,20},{18,... | collective-permute-start | bytes 1572872 | tf_op jit(solution)/shard_map/ppermute | solution.py:15
  451.5 6.0 %copy-start.11 = (f32[512,512]{1,0:T(8,128)}, f32[512,512]{1,0:T(8,128)S(1)}, u32[]{:S(2)}) copy-start(f32[512,512]{1,0:T(8,128)S(1)} %collective-permute-done.15) | copy-start | bytes 3145732
  451.5 21.2 %collective-permute-start.10 = (f32[512,256]{1,0:T(8,128)S(1)}, f32[512,256]{1,0:T(8,128)S(1)}, u32[]{:S(2)}, u32[]{:S(2)}) collective-permute-start(f32[512,256]{1,0:T(8,128)S(1)} %get-tuple-element.33), channel_id=1, source_target_pairs={{0,2},{2,0},{4,6},{6,4},{8,10},{10,8},{12,14},{14,12},{16,18},{18,... | collective-permute-start | bytes 1572872 | tf_op jit(solution)/shard_map/ppermute | solution.py:15
  454.2 19.8 %copy-start.13 = (f32[512,512]{1,0:T(8,128)}, f32[512,512]{1,0:T(8,128)S(1)}, u32[]{:S(2)}) copy-start(f32[512,512]{1,0:T(8,128)S(1)} %collective-permute-done.14) | copy-start | bytes 3145732
  454.2 31.8 %collective-permute-start.8 = (bf16[4,512,256]{2,1,0:T(8,128)(2,1)}, bf16[4,512,256]{2,1,0:T(8,128)(2,1)}, u32[]{:S(2)}, u32[]{:S(2)}) collective-permute-start(bf16[4,512,256]{2,1,0:T(8,128)(2,1)} %fusion.4), channel_id=1, source_target_pairs={{0,1},{1,0},{2,3},{3,2},{4,5},{5,4},{6,7},{7,6},{8,9},{9,8},{10,11... | collective-permute-start | bytes 3145736 | tf_op jit(solution)/shard_map/ppermute | solution.py:24
  460.5 14.9 %copy-start.18 = (f32[512,256]{1,0:T(8,128)}, f32[512,256]{1,0:T(8,128)S(1)}, u32[]{:S(2)}) copy-start(f32[512,256]{1,0:T(8,128)S(1)} %collective-permute-done.12) | copy-start | bytes 1572868
  460.5 97.2 %collective-permute-start.17 = (bf16[4,512,512]{2,1,0:T(8,128)(2,1)}, bf16[4,512,512]{2,1,0:T(8,128)(2,1)}, u32[]{:S(2)}, u32[]{:S(2)}) collective-permute-start(bf16[4,512,512]{2,1,0:T(8,128)(2,1)} %fusion.2), channel_id=1, source_target_pairs={{0,1},{1,0},{2,3},{3,2},{4,5},{5,4},{6,7},{7,6},{8,9},{9,8},{10,11... | collective-permute-start | bytes 6291464 | tf_op jit(solution)/shard_map/ppermute | solution.py:24
  472.6 2.8 copy-start.20
  472.7 2.8 copy-start.22
  474.0 78.8 %collective-permute-start.13 = (bf16[4,512,256]{2,1,0:T(8,128)(2,1)}, bf16[4,512,256]{2,1,0:T(8,128)(2,1)}, u32[]{:S(2)}, u32[]{:S(2)}) collective-permute-start(bf16[4,512,256]{2,1,0:T(8,128)(2,1)} %fusion.3), channel_id=1, source_target_pairs={{0,1},{1,0},{2,3},{3,2},{4,5},{5,4},{6,7},{7,6},{8,9},{9,8},{10,11... | collective-permute-start | bytes 3145736 | tf_op jit(solution)/shard_map/ppermute | solution.py:24
  475.5 77.4 %copy-start.19 = (f32[512,256]{1,0:T(8,128)S(1)}, f32[512,256]{1,0:T(8,128)}, u32[]{:S(2)}) copy-start(f32[512,256]{1,0:T(8,128)} %copy-done.18) | copy-start | bytes 1572868
  475.5 77.4 %copy-start.21 = (f32[512,256]{1,0:T(8,128)S(1)}, f32[512,256]{1,0:T(8,128)}, u32[]{:S(2)}) copy-start(f32[512,256]{1,0:T(8,128)} %copy-done.20) | copy-start | bytes 1572868
  475.5 77.3 %copy-start.23 = (f32[512,256]{1,0:T(8,128)S(1)}, f32[512,256]{1,0:T(8,128)}, u32[]{:S(2)}) copy-start(f32[512,256]{1,0:T(8,128)} %copy-done.22) | copy-start | bytes 1572868
  475.5 78.8 %copy-start.4 = (f32[512,512]{1,0:T(8,128)S(1)}, f32[512,512]{1,0:T(8,128)}, u32[]{:S(2)}) copy-start(f32[512,512]{1,0:T(8,128)} %copy-done.3) | copy-start | bytes 3145732
  475.5 78.8 %copy-start.6 = (f32[512,512]{1,0:T(8,128)S(1)}, f32[512,512]{1,0:T(8,128)}, u32[]{:S(2)}) copy-start(f32[512,512]{1,0:T(8,128)} %copy-done.5) | copy-start | bytes 3145732
  475.5 78.8 %copy-start.8 = (f32[512,512]{1,0:T(8,128)S(1)}, f32[512,512]{1,0:T(8,128)}, u32[]{:S(2)}) copy-start(f32[512,512]{1,0:T(8,128)} %copy-done.7) | copy-start | bytes 3145732
  554.3 2.6 copy-start.24
  556.8 1.4 copy-start.10
  556.8 1.7 copy-start.12
  556.8 2.0 copy-start.14
  563.2 2.2 copy-start.1
Sparse Core Ops, SparseCore 0:
  10.3 70.4 all-gather.1

commit v4 on v3

--- a/solution.py
+++ b/solution.py
@@ -7,7 +7,6 @@
 
 decay_rate = 0.95
 GROUP = 4
-CHUNKS = 2
 
 
 def swap(array, mask):
@@ -112,7 +111,8 @@
     for step in range(1, steps):
         arrived = moving
         moving = from_behind(arrived, GROUP) if step < steps - 1 else [
-            from_behind(piece, GROUP) for piece in jnp.split(arrived, CHUNKS)
+            from_behind(piece, GROUP)
+            for piece in jnp.split(arrived, [block // 2, 3 * block // 4])
         ]
         made = products(arrived)
         if step == steps - 1:
@@ -129,6 +129,8 @@
             sums[steps - step] += trade(narrow).astype(jnp.float32)
     last = []
     for piece in moving:
+        if last:
+            piece, sums[1:], last = lax.optimization_barrier((piece, sums[1:], last))
         part = to_owners(products(piece))
         if n_col == 2:
             part += trade(part.astype(jnp.bfloat16)).astype(jnp.float32)

time: 579 us -> 621 us (1.073)
  waiting for transfers between devices: 370 us -> 404 us
  Pallas kernels: 58.7 us -> 73.1 us
    ppermute x3 -> x4, waiting for transfers between devices: 84.8 us -> 26.1 us  [from_behind(): lax.ppermute(array, 'row', [(i, (i + by) % count) for i in range(count)])]
    ppermute x4 -> x5, waiting for transfers between devices: 75.4 us -> 126 us  [trade(): return lax.ppermute(array, 'col', [(0, 1), (1, 0)])]
    ppermute x12 -> x15, waiting for transfers between devices: 154 us -> 197 us  [swap(): return lax.ppermute(array, 'row', [(i, i ^ mask) for i in range(count)])]
    pallas_call x3 -> x4, Pallas kernels: 58.7 us -> 73.1 us  [panel_products(): pl.pallas_call(products_kernel, grid=(width // depth,), in_specs=[pl.Bloc...]
  transfers between devices with their start and end apart: 20 -> 25, of which waited for: 10 -> 13; matrix products, arithmetic and copies ran while one was open for 16% -> 14% of each run, Pallas kernels for 10% -> 7%
where the time goes in v4:
time: 621 us
  waiting for transfers between devices  404 us (65%)
  Pallas kernels  73.1 us (12%)
  matrix products  50.9 us (8%)
  local copies, waits for them, and re-layouts  26.8 us (4%)
  other arithmetic  24.9 us (4%)
  starting transfers between devices  19.5 us (3%)
  between operations  14.4 us (2%)
  blocking collectives  7.16 us (1%)
    ppermute x15, waiting for transfers between devices, swap(): return lax.ppermute(array, 'row', [(i, i ^ mask) for i in range(count)])  197 us
    ppermute x5, waiting for transfers between devices, trade(): return lax.ppermute(array, 'col', [(0, 1), (1, 0)])  126 us
    pallas_call x4, Pallas kernels, panel_products(): pl.pallas_call(products_kernel, grid=(width // depth,), in_specs=[pl.Bloc...  73.1 us
    all_gather x1, waiting for transfers between devices, body(): cotangent_all = lax.all_gather(cotangent, 'row', axis=0, tiled=True)  54.7 us
    dot_general x4, matrix products, block_product(): lax.dot_general(left, right, (((1,), (1,)), ((), ())), preferred_element_...  35.1 us
    ppermute x4, waiting for transfers between devices, from_behind(): lax.ppermute(array, 'row', [(i, (i + by) % count) for i in range(count)])  26.1 us
    dot_general x2, matrix products, gradient_tile(): lax.dot_general(columns, cotangent_all, (((1,), (0,)), ((), ())), preferr...  15.8 us
  transfers between devices with their start and end apart: 25, of which 13 were waited for; matrix products, arithmetic and copies ran while one was open for 14% of the time, Pallas kernels for 7%

profile of v4, /device:TPU:0, one launch (start us, length us, event | category | flops | bytes accessed | tf_op | source)
XLA Modules:
  0.0 620.6 jit_solution(13566880375874513249)
XLA Ops:
  7.2 0.7 all-gather.2.cloned.1.call-update
  7.9 1.0 copy.9
  8.9 7.2 %all_gather.6 = bf16[256,512]{0,1:T(8,128)(2,1)S(1)} all-gather(bf16[128,512]{0,1:T(8,128)(2,1)S(1)} %copy.9), channel_id=1, replica_groups=mesh['row'=16,'col'=2] {'col'}, dimensions={0}, use_global_device_ids=true | all-gather | bytes 393216 | tf_op jit(solution)/shard_map/all_gather | solution.py:90
  16.1 6.7 %pad_maximum_fusion.1 = bf16[512,7424]{1,0:T(8,128)(2,1)} fusion(bf16[512,256]{1,0:T(8,128)(2,1)S(1)} %bitcast.76, bf16[512,7168]{1,0:T(8,128)(2,1)} %param.7), kind=kLoop, calls=%fused_computation.3 | loop fusion | flops 15204352 | bytes 15204352 | tf_op jit(solution)/shard_map/concatenate | solution.py:91
  22.7 1.7 collective-permute-start.5
  24.5 1.6 collective-permute-start
  26.1 54.7 %all-gather.2.cloned.1.call-done.refs_6_ = bf16[256,7168]{1,0:T(8,128)(2,1)} async-done(((bf16[16,7168]{1,0:T(8,128)(2,1)}), bf16[256,7168]{1,0:T(8,128)(2,1)}) %all-gather.2.cloned.1.call-update) | async-done | bytes 3670032 | tf_op jit(solution)/shard_map/all_gather | solution.py:94
  80.8 9.5 %add_convert_fusion.1.refs_0_ = bf16[512,7168]{1,0:T(8,128)(2,1)} fusion(bf16[512,7168]{1,0:T(8,128)(2,1)} %param.7, bf16[256,512]{0,1:T(8,128)(2,1)S(1)} %all_gather.6, bf16[256,7168]{1,0:T(8,128)(2,1)} %all-gather.2.cloned.1.call-done.refs_6_), kind=kOutput, calls=%fused_computation.1 | convolution fusion | flops 1890058240 | bytes 18612224 | tf_op jit(solution)/shard_map/dot_general | solution.py:27
  90.5 108.4 %collective-permute-done.5 = bf16[512,7424]{1,0:T(8,128)(2,1)} collective-permute-done((bf16[512,7424]{1,0:T(8,128)(2,1)}, bf16[512,7424]{1,0:T(8,128)(2,1)}, u32[]{:S(2)}, u32[]{:S(2)}) %collective-permute-start.5) | collective-permute-done | bytes 7602208 | tf_op jit(solution)/shard_map/ppermute | solution.py:14
  199.0 6.4 %add_convert_fusion.refs_2_ = bf16[512,7168]{1,0:T(8,128)(2,1)} fusion(bf16[256,7168]{1,0:T(8,128)(2,1)S(1)} %copy-done, bf16[512,7424]{1,0:T(8,128)(2,1)} %collective-permute-done.5), kind=kOutput, calls=%fused_computation | convolution fusion | flops 1890058240 | bytes 18612224 | tf_op jit(solution)/shard_map/dot_general | solution.py:27
  205.3 9.5 %fusion.12 = f32[512,512]{1,0:T(8,128)S(1)} fusion(bf16[512,7168]{1,0:T(8,128)(2,1)} %add_convert_fusion.1.refs_0_), kind=kOutput, calls=%fused_computation.45 | convolution fusion | flops 3758096384 | bytes 8388608 | tf_op jit(solution)/shard_map/dot_general | solution.py:34
  214.9 4.2 split.14
  219.1 1.5 collective-permute-start.3
  220.5 8.5 %fusion.14 = f32[512,512]{1,0:T(8,128)S(1)} fusion(bf16[512,7168]{1,0:T(8,128)(2,1)} %add_convert_fusion.1.refs_0_, bf16[512,7168]{1,0:T(8,128)(2,1)} %add_convert_fusion.refs_2_), kind=kOutput, calls=%fused_computation.47 | convolution fusion | flops 3758096384 | bytes 15728640 | tf_op jit(solution)/shard_map/dot_general | solution.py:34
  229.1 6.6 %slice.110.refs_4_ = bf16[512,7168]{1,0:T(8,128)(2,1)} slice(bf16[512,7424]{1,0:T(8,128)(2,1)} %collective-permute-done), slice={[0:512], [0:7168]} | slice | bytes 14680064 | tf_op jit(solution)/shard_map/slice | solution.py:100
  235.6 1.0 slice.111.refs_5_
  236.6 8.5 %fusion.13 = f32[512,512]{1,0:T(8,128)S(1)} fusion(bf16[512,7168]{1,0:T(8,128)(2,1)} %add_convert_fusion.1.refs_0_, bf16[512,7168]{1,0:T(8,128)(2,1)} %collective-permute-done.4.refs_1_), kind=kOutput, calls=%fused_computation.46 | convolution fusion | flops 3758096384 | bytes 15728640 | tf_op jit(solution)/shard_map/dot_general | solution.py:34
  245.1 8.5 %fusion.15 = f32[512,512]{1,0:T(8,128)S(1)} fusion(bf16[512,7168]{1,0:T(8,128)(2,1)} %add_convert_fusion.1.refs_0_, bf16[512,7168]{1,0:T(8,128)(2,1)} %collective-permute-done.6.refs_3_), kind=kOutput, calls=%fused_computation.48 | convolution fusion | flops 3758096384 | bytes 15728640 | tf_op jit(solution)/shard_map/dot_general | solution.py:34
  253.7 25.8 %shard_map.68 = f32[4,512,512]{2,1,0:T(8,128)} custom-call(bf16[512,7168]{1,0:T(8,128)(2,1)} %add_convert_fusion.1.refs_0_, bf16[512,7168]{1,0:T(8,128)(2,1)} %collective-permute-done.4.refs_1_, bf16[512,7168]{1,0:T(8,128)(2,1)} %add_convert_fusion.refs_2_, bf16[512,7168]{1,0:T(8,128)(2,1)} %collective-permute-done.6.refs_3_, ...), custom_call_target="tpu_custom_call" | custom-call | flops 16911433728 | bytes 44564480 | tf_op jit(solution)/shard_map/pallas_call | solution.py:59
  279.5 26.1 %collective-permute-done.3 = bf16[256,7424]{1,0:T(8,128)(2,1)S(1)} collective-permute-done((bf16[256,7424]{1,0:T(8,128)(2,1)}, bf16[256,7424]{1,0:T(8,128)(2,1)S(1)}, u32[]{:S(2)}, u32[]{:S(2)}) %collective-permute-start.3) | collective-permute-done | bytes 3801120 | tf_op jit(solution)/shard_map/ppermute | solution.py:19
  305.6 0.4 slice.89.refs_4_
  306.1 16.3 %shard_map.69 = f32[4,512,256]{2,1,0:T(8,128)S(1)} custom-call(bf16[512,7168]{1,0:T(8,128)(2,1)} %add_convert_fusion.1.refs_0_, bf16[512,7168]{1,0:T(8,128)(2,1)} %collective-permute-done.4.refs_1_, bf16[512,7168]{1,0:T(8,128)(2,1)} %add_convert_fusion.refs_2_, bf16[512,7168]{1,0:T(8,128)(2,1)} %collective-permute-done.6.refs_3_, ...), custom_call_target="tpu_custom_call" | custom-call | flops 8455716864 | bytes 38797312 | tf_op jit(solution)/shard_map/pallas_call | solution.py:59
  322.6 1.9 copy-done.4
  324.5 0.5 fusion.8
  325.1 1.3 collective-permute-start.8
  326.5 0.5 collective-permute-start.7
  327.0 0.4 collective-permute-start.13
  327.3 9.5 %collective-permute-done.14 = f32[512,256]{1,0:T(8,128)S(1)} collective-permute-done((f32[512,256]{1,0:T(8,128)S(1)}, f32[512,256]{1,0:T(8,128)S(1)}, u32[]{:S(2)}, u32[]{:S(2)}) %collective-permute-start.14) | collective-permute-done | bytes 524320 | tf_op jit(solution)/shard_map/ppermute | solution.py:14
  336.8 0.4 fusion.1
  337.2 55.6 %collective-permute-done.13 = f32[512,256]{1,0:T(8,128)S(1)} collective-permute-done((f32[512,256]{1,0:T(8,128)S(1)}, f32[512,256]{1,0:T(8,128)S(1)}, u32[]{:S(2)}, u32[]{:S(2)}) %collective-permute-start.13) | collective-permute-done | bytes 524320 | tf_op jit(solution)/shard_map/ppermute | solution.py:14
  392.8 1.5 collective-permute-start.11
  394.6 0.6 collective-permute-start.15
  395.2 0.4 fusion.2
  395.6 1.6 collective-permute-start.10
  397.2 3.7 fusion.7
  400.8 1.2 collective-permute-start.1
  402.0 61.7 %collective-permute-done.15 = bf16[4,512,256]{2,1,0:T(8,128)(2,1)S(1)} collective-permute-done((bf16[4,512,256]{2,1,0:T(8,128)(2,1)S(1)}, bf16[4,512,256]{2,1,0:T(8,128)(2,1)S(1)}, u32[]{:S(2)}, u32[]{:S(2)}) %collective-permute-start.15) | collective-permute-done | bytes 1048608 | tf_op jit(solution)/shard_map/ppermute | solution.py:23
  463.8 0.3 convert_add_fusion.2
  464.0 2.9 convert_add_fusion
  466.9 41.0 %collective-permute-done.10 = bf16[4,512,512]{2,1,0:T(8,128)(2,1)S(1)} collective-permute-done((bf16[4,512,512]{2,1,0:T(8,128)(2,1)S(1)}, bf16[4,512,512]{2,1,0:T(8,128)(2,1)S(1)}, u32[]{:S(2)}, u32[]{:S(2)}) %collective-permute-start.10) | collective-permute-done | bytes 2097184 | tf_op jit(solution)/shard_map/ppermute | solution.py:23
  507.9 2.8 convert_add_fusion.1
  510.9 15.5 %shard_map.70 = f32[4,512,128]{2,1,0:T(8,128)S(1)} custom-call(bf16[512,7168]{1,0:T(8,128)(2,1)} %add_convert_fusion.1.refs_0_, bf16[512,7168]{1,0:T(8,128)(2,1)} %collective-permute-done.4.refs_1_, bf16[512,7168]{1,0:T(8,128)(2,1)} %add_convert_fusion.refs_2_, bf16[512,7168]{1,0:T(8,128)(2,1)} %collective-permute-done.6.refs_3_, ...), custom_call_target="tpu_custom_call" | custom-call | flops 4227858432 | bytes 35913728 | tf_op jit(solution)/shard_map/pallas_call | solution.py:59
  526.5 0.9 collective-permute-start.17
  527.4 1.0 collective-permute-start.16
  528.4 6.7 %collective-permute-done.18 = f32[512,128]{1,0:T(8,128)S(1)} collective-permute-done((f32[512,128]{1,0:T(8,128)S(1)}, f32[512,128]{1,0:T(8,128)S(1)}, u32[]{:S(2)}, u32[]{:S(2)}) %collective-permute-start.18) | collective-permute-done | bytes 262176 | tf_op jit(solution)/shard_map/ppermute | solution.py:14
  535.0 4.7 collective-permute-done.17
  539.8 1.6 collective-permute-start.19
  541.4 12.6 %collective-permute-done.19 = bf16[4,512,128]{2,1,0:T(8,128)(2,1)S(1)} collective-permute-done((bf16[4,512,128]{2,1,0:T(8,128)(2,1)S(1)}, bf16[4,512,128]{2,1,0:T(8,128)(2,1)S(1)}, u32[]{:S(2)}, u32[]{:S(2)}) %collective-permute-start.19) | collective-permute-done | bytes 524320 | tf_op jit(solution)/shard_map/ppermute | solution.py:23
  554.0 1.1 convert_add_fusion.4
  555.3 15.5 %shard_map.71 = f32[4,512,128]{2,1,0:T(8,128)S(1)} custom-call(bf16[512,7168]{1,0:T(8,128)(2,1)} %add_convert_fusion.1.refs_0_, bf16[512,7168]{1,0:T(8,128)(2,1)} %collective-permute-done.4.refs_1_, bf16[512,7168]{1,0:T(8,128)(2,1)} %add_convert_fusion.refs_2_, bf16[512,7168]{1,0:T(8,128)(2,1)} %collective-permute-done.6.refs_3_, ...), custom_call_target="tpu_custom_call" | custom-call | flops 4227858432 | bytes 35913728 | tf_op jit(solution)/shard_map/pallas_call | solution.py:59
  571.0 1.2 collective-permute-start.21
  572.2 0.6 collective-permute-start.20
  572.8 6.7 %collective-permute-done.22 = f32[512,128]{1,0:T(8,128)S(1)} collective-permute-done((f32[512,128]{1,0:T(8,128)S(1)}, f32[512,128]{1,0:T(8,128)S(1)}, u32[]{:S(2)}, u32[]{:S(2)}) %collective-permute-start.22) | collective-permute-done | bytes 262176 | tf_op jit(solution)/shard_map/ppermute | solution.py:14
  579.5 5.0 collective-permute-done.21
  584.6 1.0 fusion.4
  585.6 1.8 collective-permute-start.23
  587.4 2.1 bitcast_add_fusion
  589.5 10.4 %collective-permute-done.23 = bf16[4,512,128]{2,1,0:T(8,128)(2,1)} collective-permute-done((bf16[4,512,128]{2,1,0:T(8,128)(2,1)}, bf16[4,512,128]{2,1,0:T(8,128)(2,1)}, u32[]{:S(2)}, u32[]{:S(2)}) %collective-permute-start.23) | collective-permute-done | bytes 524320 | tf_op jit(solution)/shard_map/ppermute | solution.py:23
  599.9 1.4 convert_add_fusion.3
  601.3 4.0 pad_maximum_fusion
  605.3 0.5 dynamic-slice_bitcast_fusion.3
  605.7 1.7 copy-done.2
  607.5 1.6 fusion
  609.1 4.7 copy.10
  (47 shorter events, 1.7 us)
Async XLA Ops:
  7.2 73.6 %all-gather.2.cloned.1.call-start = ((), (), s32[]{:S(2)}) async-start(), calls=%async_computation | async-start | bytes 3899392 | tf_op jit(solution)/shard_map/all_gather | solution.py:94
  22.7 176.2 %collective-permute-start.5 = (bf16[512,7424]{1,0:T(8,128)(2,1)}, bf16[512,7424]{1,0:T(8,128)(2,1)}, u32[]{:S(2)}, u32[]{:S(2)}) collective-permute-start(bf16[512,7424]{1,0:T(8,128)(2,1)} %pad_maximum_fusion.1), channel_id=1, source_target_pairs={{0,4},{2,6},{4,0},{6,2},{8,12},{10,14},{12,8},{14,10},{16,20},{18,... | collective-permute-start | bytes 22806536 | tf_op jit(solution)/shard_map/ppermute | solution.py:14
  24.5 190.4 %collective-permute-start = (bf16[512,7424]{1,0:T(8,128)(2,1)}, bf16[512,7424]{1,0:T(8,128)(2,1)}, u32[]{:S(2)}, u32[]{:S(2)}) collective-permute-start(bf16[512,7424]{1,0:T(8,128)(2,1)} %pad_maximum_fusion.1), channel_id=1, source_target_pairs={{0,8},{2,10},{4,12},{6,14},{8,16},{10,18},{12,20},{14,22},{16,24},... | collective-permute-start | bytes 22806536 | tf_op jit(solution)/shard_map/ppermute | solution.py:19
  80.8 118.2 %copy-start = (bf16[256,7168]{1,0:T(8,128)(2,1)S(1)}, bf16[256,7168]{1,0:T(8,128)(2,1)}, u32[]{:S(2)}) copy-start(bf16[256,7168]{1,0:T(8,128)(2,1)} %all-gather.2.cloned.1.call-done.refs_6_) | copy-start | bytes 11010052
  90.3 146.3 %collective-permute-start.4 = (bf16[512,7168]{1,0:T(8,128)(2,1)}, bf16[512,7168]{1,0:T(8,128)(2,1)}, u32[]{:S(2)}, u32[]{:S(2)}) collective-permute-start(bf16[512,7168]{1,0:T(8,128)(2,1)} %add_convert_fusion.1.refs_0_), channel_id=1, source_target_pairs={{0,2},{2,0},{4,6},{6,4},{8,10},{10,8},{12,14},{14,12},{16,18},{18,... | collective-permute-start | bytes 22020104 | tf_op jit(solution)/shard_map/ppermute | solution.py:14
  205.3 39.8 %collective-permute-start.6 = (bf16[512,7168]{1,0:T(8,128)(2,1)}, bf16[512,7168]{1,0:T(8,128)(2,1)}, u32[]{:S(2)}, u32[]{:S(2)}) collective-permute-start(bf16[512,7168]{1,0:T(8,128)(2,1)} %add_convert_fusion.refs_2_), channel_id=1, source_target_pairs={{0,2},{2,0},{4,6},{6,4},{8,10},{10,8},{12,14},{14,12},{16,18},{18,... | collective-permute-start | bytes 22020104 | tf_op jit(solution)/shard_map/ppermute | solution.py:14
  219.1 86.6 %collective-permute-start.3 = (bf16[256,7424]{1,0:T(8,128)(2,1)}, bf16[256,7424]{1,0:T(8,128)(2,1)S(1)}, u32[]{:S(2)}, u32[]{:S(2)}) collective-permute-start(bf16[256,7424]{1,0:T(8,128)(2,1)} %split.14), channel_id=1, source_target_pairs={{0,8},{2,10},{4,12},{6,14},{8,16},{10,18},{12,20},{14,22},{16,24},... | collective-permute-start | bytes 11403272 | tf_op jit(solution)/shard_map/ppermute | solution.py:19
  322.4 2.2 copy-start.4
  322.5 14.3 %collective-permute-start.14 = (f32[512,256]{1,0:T(8,128)S(1)}, f32[512,256]{1,0:T(8,128)S(1)}, u32[]{:S(2)}, u32[]{:S(2)}) collective-permute-start(f32[512,256]{1,0:T(8,128)S(1)} %get-tuple-element.45), channel_id=1, source_target_pairs={{0,6},{2,4},{4,2},{6,0},{8,14},{10,12},{12,10},{14,8},{16,22},{18,... | collective-permute-start | bytes 1572872 | tf_op jit(solution)/shard_map/ppermute | solution.py:14
  325.0 70.1 %collective-permute-start.9 = (f32[512,512]{1,0:T(8,128)S(1)}, f32[512,512]{1,0:T(8,128)S(1)}, u32[]{:S(2)}, u32[]{:S(2)}) collective-permute-start(f32[512,512]{1,0:T(8,128)S(1)} %get-tuple-element.41), channel_id=1, source_target_pairs={{0,6},{2,4},{4,2},{6,0},{8,14},{10,12},{12,10},{14,8},{16,22},{18,... | collective-permute-start | bytes 3145736 | tf_op jit(solution)/shard_map/ppermute | solution.py:14
  325.1 70.0 %collective-permute-start.8 = (f32[512,512]{1,0:T(8,128)S(1)}, f32[512,512]{1,0:T(8,128)S(1)}, u32[]{:S(2)}, u32[]{:S(2)}) collective-permute-start(f32[512,512]{1,0:T(8,128)S(1)} %get-tuple-element.42), channel_id=1, source_target_pairs={{0,4},{2,6},{4,0},{6,2},{8,12},{10,14},{12,8},{14,10},{16,20},{18,... | collective-permute-start | bytes 3145736 | tf_op jit(solution)/shard_map/ppermute | solution.py:14
  326.5 68.7 %collective-permute-start.7 = (f32[512,512]{1,0:T(8,128)S(1)}, f32[512,512]{1,0:T(8,128)S(1)}, u32[]{:S(2)}, u32[]{:S(2)}) collective-permute-start(f32[512,512]{1,0:T(8,128)S(1)} %get-tuple-element.43), channel_id=1, source_target_pairs={{0,2},{2,0},{4,6},{6,4},{8,10},{10,8},{12,14},{14,12},{16,18},{18,... | collective-permute-start | bytes 3145736 | tf_op jit(solution)/shard_map/ppermute | solution.py:14
  327.0 65.8 %collective-permute-start.13 = (f32[512,256]{1,0:T(8,128)S(1)}, f32[512,256]{1,0:T(8,128)S(1)}, u32[]{:S(2)}, u32[]{:S(2)}) collective-permute-start(f32[512,256]{1,0:T(8,128)S(1)} %get-tuple-element.46), channel_id=1, source_target_pairs={{0,4},{2,6},{4,0},{6,2},{8,12},{10,14},{12,8},{14,10},{16,20},{18,... | collective-permute-start | bytes 1572872 | tf_op jit(solution)/shard_map/ppermute | solution.py:14
  336.8 57.5 %collective-permute-start.12 = (f32[512,256]{1,0:T(8,128)S(1)}, f32[512,256]{1,0:T(8,128)S(1)}, u32[]{:S(2)}, u32[]{:S(2)}) collective-permute-start(f32[512,256]{1,0:T(8,128)S(1)} %get-tuple-element.47), channel_id=1, source_target_pairs={{0,2},{2,0},{4,6},{6,4},{8,10},{10,8},{12,14},{14,12},{16,18},{18,... | collective-permute-start | bytes 1572872 | tf_op jit(solution)/shard_map/ppermute | solution.py:14
  392.8 71.2 %collective-permute-start.11 = (bf16[4,512,512]{2,1,0:T(8,128)(2,1)S(1)}, bf16[4,512,512]{2,1,0:T(8,128)(2,1)S(1)}, u32[]{:S(2)}, u32[]{:S(2)}) collective-permute-start(bf16[4,512,512]{2,1,0:T(8,128)(2,1)S(1)} %fusion.1), channel_id=1, source_target_pairs={{0,1},{1,0},{2,3},{3,2},{4,5},{5,4},{6,7},{7,6},{8,9},{9,8},{10,11... | collective-permute-start | bytes 6291464 | tf_op jit(solution)/shard_map/ppermute | solution.py:23
  394.6 69.2 %collective-permute-start.15 = (bf16[4,512,256]{2,1,0:T(8,128)(2,1)S(1)}, bf16[4,512,256]{2,1,0:T(8,128)(2,1)S(1)}, u32[]{:S(2)}, u32[]{:S(2)}) collective-permute-start(bf16[4,512,256]{2,1,0:T(8,128)(2,1)S(1)} %fusion.3), channel_id=1, source_target_pairs={{0,1},{1,0},{2,3},{3,2},{4,5},{5,4},{6,7},{7,6},{8,9},{9,8},{10,11... | collective-permute-start | bytes 3145736 | tf_op jit(solution)/shard_map/ppermute | solution.py:23
  395.6 112.3 %collective-permute-start.10 = (bf16[4,512,512]{2,1,0:T(8,128)(2,1)S(1)}, bf16[4,512,512]{2,1,0:T(8,128)(2,1)S(1)}, u32[]{:S(2)}, u32[]{:S(2)}) collective-permute-start(bf16[4,512,512]{2,1,0:T(8,128)(2,1)S(1)} %fusion.2), channel_id=1, source_target_pairs={{0,1},{1,0},{2,3},{3,2},{4,5},{5,4},{6,7},{7,6},{8,9},{9,8},{10,11... | collective-permute-start | bytes 6291464 | tf_op jit(solution)/shard_map/ppermute | solution.py:23
  400.8 109.8 %collective-permute-start.2 = (bf16[128,7424]{1,0:T(8,128)(2,1)S(1)}, bf16[128,7424]{1,0:T(8,128)(2,1)S(1)}, u32[]{:S(2)}, u32[]{:S(2)}) collective-permute-start(bf16[128,7424]{1,0:T(8,128)(2,1)S(1)} %get-tuple-element.38), channel_id=1, source_target_pairs={{0,8},{2,10},{4,12},{6,14},{8,16},{10,18},{12,20},{14,22},{16,24},... | collective-permute-start | bytes 5701640 | tf_op jit(solution)/shard_map/ppermute | solution.py:19
  400.8 154.2 %collective-permute-start.1 = (bf16[128,7424]{1,0:T(8,128)(2,1)}, bf16[128,7424]{1,0:T(8,128)(2,1)S(1)}, u32[]{:S(2)}, u32[]{:S(2)}) collective-permute-start(bf16[128,7424]{1,0:T(8,128)(2,1)} %get-tuple-element.39), channel_id=1, source_target_pairs={{0,8},{2,10},{4,12},{6,14},{8,16},{10,18},{12,20},{14,22},{16,24},... | collective-permute-start | bytes 5701640 | tf_op jit(solution)/shard_map/ppermute | solution.py:19
  526.4 8.6 %collective-permute-start.18 = (f32[512,128]{1,0:T(8,128)S(1)}, f32[512,128]{1,0:T(8,128)S(1)}, u32[]{:S(2)}, u32[]{:S(2)}) collective-permute-start(f32[512,128]{1,0:T(8,128)S(1)} %get-tuple-element.53), channel_id=1, source_target_pairs={{0,6},{2,4},{4,2},{6,0},{8,14},{10,12},{12,10},{14,8},{16,22},{18,... | collective-permute-start | bytes 786440 | tf_op jit(solution)/shard_map/ppermute | solution.py:14
  526.5 13.2 %collective-permute-start.17 = (f32[512,128]{1,0:T(8,128)S(1)}, f32[512,128]{1,0:T(8,128)S(1)}, u32[]{:S(2)}, u32[]{:S(2)}) collective-permute-start(f32[512,128]{1,0:T(8,128)S(1)} %get-tuple-element.54), channel_id=1, source_target_pairs={{0,4},{2,6},{4,0},{6,2},{8,12},{10,14},{12,8},{14,10},{16,20},{18,... | collective-permute-start | bytes 786440 | tf_op jit(solution)/shard_map/ppermute | solution.py:14
  527.4 12.3 %collective-permute-start.16 = (f32[512,128]{1,0:T(8,128)S(1)}, f32[512,128]{1,0:T(8,128)S(1)}, u32[]{:S(2)}, u32[]{:S(2)}) collective-permute-start(f32[512,128]{1,0:T(8,128)S(1)} %get-tuple-element.55), channel_id=1, source_target_pairs={{0,2},{2,0},{4,6},{6,4},{8,10},{10,8},{12,14},{14,12},{16,18},{18,... | collective-permute-start | bytes 786440 | tf_op jit(solution)/shard_map/ppermute | solution.py:14
  539.8 14.2 %collective-permute-start.19 = (bf16[4,512,128]{2,1,0:T(8,128)(2,1)S(1)}, bf16[4,512,128]{2,1,0:T(8,128)(2,1)S(1)}, u32[]{:S(2)}, u32[]{:S(2)}) collective-permute-start(bf16[4,512,128]{2,1,0:T(8,128)(2,1)S(1)} %fusion.5), channel_id=1, source_target_pairs={{0,1},{1,0},{2,3},{3,2},{4,5},{5,4},{6,7},{7,6},{8,9},{9,8},{10,11... | collective-permute-start | bytes 1572872 | tf_op jit(solution)/shard_map/ppermute | solution.py:23
  570.8 16.6 %slice-start = ((f32[4,512,512]{2,1,0:T(8,128)}), f32[1,512,512]{2,1,0:T(8,128)S(1)}, s32[]{:S(2)}) async-start(f32[4,512,512]{2,1,0:T(8,128)} %convert_add_fusion), calls=%async_computation.1 | async-start | bytes 2097152 | tf_op jit(solution)/shard_map/slice | solution.py:150
  570.9 8.7 %collective-permute-start.22 = (f32[512,128]{1,0:T(8,128)S(1)}, f32[512,128]{1,0:T(8,128)S(1)}, u32[]{:S(2)}, u32[]{:S(2)}) collective-permute-start(f32[512,128]{1,0:T(8,128)S(1)} %get-tuple-element.49), channel_id=1, source_target_pairs={{0,6},{2,4},{4,2},{6,0},{8,14},{10,12},{12,10},{14,8},{16,22},{18,... | collective-permute-start | bytes 786440 | tf_op jit(solution)/shard_map/ppermute | solution.py:14
  571.0 13.6 %collective-permute-start.21 = (f32[512,128]{1,0:T(8,128)S(1)}, f32[512,128]{1,0:T(8,128)S(1)}, u32[]{:S(2)}, u32[]{:S(2)}) collective-permute-start(f32[512,128]{1,0:T(8,128)S(1)} %get-tuple-element.50), channel_id=1, source_target_pairs={{0,4},{2,6},{4,0},{6,2},{8,12},{10,14},{12,8},{14,10},{16,20},{18,... | collective-permute-start | bytes 786440 | tf_op jit(solution)/shard_map/ppermute | solution.py:14
  572.2 12.4 %collective-permute-start.20 = (f32[512,128]{1,0:T(8,128)S(1)}, f32[512,128]{1,0:T(8,128)S(1)}, u32[]{:S(2)}, u32[]{:S(2)}) collective-permute-start(f32[512,128]{1,0:T(8,128)S(1)} %get-tuple-element.51), channel_id=1, source_target_pairs={{0,2},{2,0},{4,6},{6,4},{8,10},{10,8},{12,14},{14,12},{16,18},{18,... | collective-permute-start | bytes 786440 | tf_op jit(solution)/shard_map/ppermute | solution.py:14
  579.5 5.0 copy-start.5
  584.6 1.0 copy-start.6
  584.6 2.8 copy-start.7
  585.6 14.3 %collective-permute-start.23 = (bf16[4,512,128]{2,1,0:T(8,128)(2,1)}, bf16[4,512,128]{2,1,0:T(8,128)(2,1)}, u32[]{:S(2)}, u32[]{:S(2)}) collective-permute-start(bf16[4,512,128]{2,1,0:T(8,128)(2,1)} %fusion.4), channel_id=1, source_target_pairs={{0,1},{1,0},{2,3},{3,2},{4,5},{5,4},{6,7},{7,6},{8,9},{9,8},{10,11... | collective-permute-start | bytes 1572872 | tf_op jit(solution)/shard_map/ppermute | solution.py:23
  587.4 13.9 %copy-start.1 = (f32[4,512,512]{2,1,0:T(8,128)S(1)}, f32[4,512,512]{2,1,0:T(8,128)}, u32[]{:S(2)}) copy-start(f32[4,512,512]{2,1,0:T(8,128)} %convert_add_fusion) | copy-start | bytes 12582916
  587.4 13.9 %copy-start.3 = (f32[4,512,128]{2,1,0:T(8,128)S(1)}, f32[4,512,128]{2,1,0:T(8,128)}, u32[]{:S(2)}) copy-start(f32[4,512,128]{2,1,0:T(8,128)} %convert_add_fusion.4) | copy-start | bytes 3145732
  605.3 2.2 copy-start.2
Sparse Core Ops, SparseCore 0:
  10.3 70.4 all-gather.1

commit v5 on v3

--- a/solution.py
+++ b/solution.py
@@ -7,7 +7,6 @@
 
 decay_rate = 0.95
 GROUP = 4
-CHUNKS = 2
 
 
 def swap(array, mask):
@@ -88,6 +87,8 @@
     place = lax.axis_index("row") % GROUP
     y = lax.axis_index("col")
 
+    phase = lax.optimization_barrier
+
     columns = lax.all_gather(activations, "col", axis=0, tiled=True)
     parcel = jnp.concatenate([accumulated, columns.T], axis=1)
     moving = from_behind(parcel, GROUP)
@@ -101,38 +102,65 @@
         return panel_products(group, parcel[:, :width], parcel[:, width:], cotangent_all)
 
     def to_owners(made):
-        return jnp.stack([made[0]] + [swap(made[u], u) for u in range(1, GROUP)])
+        return [made[0]] + [swap(made[u], u) for u in range(1, GROUP)]
+
+    def over_columns(sums):
+        if n_col != 2:
+            return jnp.stack(sums)
+        sums = jnp.stack(sums)
+        return sums + trade(sums.astype(jnp.bfloat16)).astype(jnp.float32)
 
     own = gradient_of(parcel)
-    across = gradient_of(across_parcel)
-    group = [own, swap(own, 1), across, swap(across, 1)]
+    beside = swap(own, 1)
+    own_products = [block_product(own, panel) for panel in (own, beside)]
+    moving, across_parcel, beside, own_products = phase(
+        (moving, across_parcel, beside, own_products)
+    )
 
     sums = [None] * (steps + 1)
-    own_products = [block_product(own, panel) for panel in group]
+    made, handed = None, None
     for step in range(1, steps):
         arrived = moving
-        moving = from_behind(arrived, GROUP) if step < steps - 1 else [
-            from_behind(piece, GROUP) for piece in jnp.split(arrived, CHUNKS)
-        ]
+        quarters = jnp.split(arrived, 4)
+        first = from_behind(quarters[0], GROUP)
+        if step == 1:
+            across = gradient_of(across_parcel)
+            group = [own, beside, across, swap(across, 1)]
+        else:
+            handed = to_owners(made)
+        first, group, handed = phase((first, group, handed))
+        if step > 1:
+            sums[steps - step + 1] = over_columns(handed)
+        second = from_behind(quarters[1], GROUP)
         made = products(arrived)
-        if step == steps - 1:
-            moving[0], made, own_products = lax.optimization_barrier(
-                (moving[0], made, own_products)
-            )
-        sums[steps - step] = to_owners(made)
-    sums[steps] = jnp.stack(own_products)
-
-    if n_col == 2:
-        sums[steps] += trade(sums[steps].astype(jnp.bfloat16)).astype(jnp.float32)
-        for step in range(1, steps):
-            narrow = sums[steps - step].astype(jnp.bfloat16)
-            sums[steps - step] += trade(narrow).astype(jnp.float32)
-    last = []
-    for piece in moving:
-        part = to_owners(products(piece))
-        if n_col == 2:
-            part += trade(part.astype(jnp.bfloat16)).astype(jnp.float32)
-        last.append(part)
+        first, second, made, sums = phase((first, second, made, sums))
+        if step < steps - 1:
+            rest = [from_behind(piece, GROUP) for piece in quarters[2:]]
+            moving = jnp.concatenate([first, second, *rest])
+
+    half = jnp.concatenate([first, second])
+    third = from_behind(quarters[2], GROUP)
+    handed = to_owners(made)
+    made = products(half)
+    own_products += [block_product(own, panel) for panel in group[2:]]
+    third, handed, made, own_products = phase((third, handed, made, own_products))
+
+    fourth = from_behind(quarters[3], GROUP)
+    sums[1] = over_columns(handed)
+    handed = to_owners(made)
+    made = products(third)
+    fourth, sums[1], handed, made = phase((fourth, sums[1], handed, made))
+
+    sums[steps] = over_columns(own_products)
+    last = [over_columns(handed)]
+    handed = to_owners(made)
+    made = products(fourth)
+    last, handed, made = phase((last, handed, made))
+
+    last.append(over_columns(handed))
+    handed = to_owners(made)
+    last, handed = phase((last, handed))
+    last.append(over_columns(handed))
     sums[0] = jnp.concatenate(last, axis=2)
     stacked = jnp.concatenate(sums)
 

time: 579 us -> 556 us (0.960)
  waiting for transfers between devices: 370 us -> 343 us
  Pallas kernels: 58.7 us -> 73.4 us
  local copies, waits for them, and re-layouts: 32.3 us -> 26 us
    ppermute x3 -> x5, waiting for transfers between devices: 84.8 us -> 58.3 us  [from_behind(): lax.ppermute(array, 'row', [(i, (i + by) % count) for i in range(count)])]
    pallas_call x3 -> x4, Pallas kernels: 58.7 us -> 73.4 us  [panel_products(): pl.pallas_call(products_kernel, grid=(width // depth,), in_specs=[pl.Bloc...]
    all_gather x1, waiting for transfers between devices: 54.8 us -> 44.4 us  [body(): cotangent_all = lax.all_gather(cotangent, 'row', axis=0, tiled=True)]
    ppermute x4 -> x5, waiting for transfers between devices: 75.4 us -> 84 us  [trade(): return lax.ppermute(array, 'col', [(0, 1), (1, 0)])]
    ppermute x12 -> x15, waiting for transfers between devices: 154 us -> 155 us  [swap(): return lax.ppermute(array, 'row', [(i, i ^ mask) for i in range(count)])]
  transfers between devices with their start and end apart: 20 -> 26, of which waited for: 10 -> 11; matrix products, arithmetic and copies ran while one was open for 16% -> 13% of each run, Pallas kernels for 10% -> 13%
where the time goes in v5:
time: 556 us; the launch traced here: 555 us
  waiting for transfers between devices  343 us (62%)
  Pallas kernels  73.4 us (13%)
  matrix products  50.4 us (9%)
  local copies, waits for them, and re-layouts  26 us (5%)
  other arithmetic  22.1 us (4%)
  starting transfers between devices  18.9 us (3%)
  between operations  14.5 us (3%)
  blocking collectives  7.16 us (1%)
    ppermute x15, waiting for transfers between devices, swap(): return lax.ppermute(array, 'row', [(i, i ^ mask) for i in range(count)])  155 us
    ppermute x5, waiting for transfers between devices, trade(): return lax.ppermute(array, 'col', [(0, 1), (1, 0)])  84 us
    pallas_call x4, Pallas kernels, panel_products(): pl.pallas_call(products_kernel, grid=(width // depth,), in_specs=[pl.Bloc...  73.4 us
    ppermute x5, waiting for transfers between devices, from_behind(): lax.ppermute(array, 'row', [(i, (i + by) % count) for i in range(count)])  58.3 us
    all_gather x1, waiting for transfers between devices, body(): cotangent_all = lax.all_gather(cotangent, 'row', axis=0, tiled=True)  44.4 us
    dot_general x4, matrix products, block_product(): lax.dot_general(left, right, (((1,), (1,)), ((), ())), preferred_element_...  36.8 us
    dot_general x2, matrix products, gradient_tile(): lax.dot_general(columns, cotangent_all, (((1,), (0,)), ((), ())), preferr...  13.5 us
  transfers between devices with their start and end apart: 26, of which 11 were waited for; matrix products, arithmetic and copies ran while one was open for 13% of the time, Pallas kernels for 13%

profile of v5, /device:TPU:0, one launch (start us, length us, event | category | flops | bytes accessed | tf_op | source)
XLA Modules:
  0.0 555.2 jit_solution(3690080624465508192)
XLA Ops:
  7.2 0.7 all-gather.2.cloned.1.call-update
  7.9 1.0 copy.9
  8.9 7.2 %all_gather.6 = bf16[256,512]{0,1:T(8,128)(2,1)S(1)} all-gather(bf16[128,512]{0,1:T(8,128)(2,1)S(1)} %copy.9), channel_id=1, replica_groups=mesh['row'=16,'col'=2] {'col'}, dimensions={0}, use_global_device_ids=true | all-gather | bytes 393216 | tf_op jit(solution)/shard_map/all_gather | solution.py:92
  16.1 44.4 %all-gather.2.cloned.1.call-done.refs_6_ = bf16[256,7168]{1,0:T(8,128)(2,1)} async-done(((bf16[16,7168]{1,0:T(8,128)(2,1)}), bf16[256,7168]{1,0:T(8,128)(2,1)}) %all-gather.2.cloned.1.call-update) | async-done | bytes 3670032 | tf_op jit(solution)/shard_map/all_gather | solution.py:96
  60.5 9.3 %add_convert_fusion.1.refs_0_ = bf16[512,7168]{1,0:T(8,128)(2,1)} fusion(bf16[512,7168]{1,0:T(8,128)(2,1)} %param.7, bf16[256,512]{0,1:T(8,128)(2,1)S(1)} %all_gather.6, bf16[256,7168]{1,0:T(8,128)(2,1)} %all-gather.2.cloned.1.call-done.refs_6_), kind=kOutput, calls=%fused_computation.1 | convolution fusion | flops 1890058240 | bytes 18612224 | tf_op jit(solution)/shard_map/dot_general | solution.py:27
  70.0 6.6 %pad_maximum_fusion.1 = bf16[512,7424]{1,0:T(8,128)(2,1)} fusion(bf16[512,256]{1,0:T(8,128)(2,1)S(1)} %bitcast.92, bf16[512,7168]{1,0:T(8,128)(2,1)} %param.7), kind=kLoop, calls=%fused_computation.3 | loop fusion | flops 15204352 | bytes 15204352 | tf_op jit(solution)/shard_map/concatenate | solution.py:93
  76.6 0.6 collective-permute-start.1
  77.2 2.1 collective-permute-start
  79.2 9.2 %fusion.8 = f32[512,512]{1,0:T(8,128)S(1)} fusion(bf16[512,7168]{1,0:T(8,128)(2,1)} %add_convert_fusion.1.refs_0_), kind=kOutput, calls=%fused_computation.47 | convolution fusion | flops 3758096384 | bytes 8388608 | tf_op jit(solution)/shard_map/dot_general | solution.py:34
  88.5 10.6 %fusion.9 = f32[512,512]{1,0:T(8,128)} fusion(bf16[512,7168]{1,0:T(8,128)(2,1)} %add_convert_fusion.1.refs_0_, bf16[512,7168]{1,0:T(8,128)(2,1)} %collective-permute-done.2.refs_1_), kind=kOutput, calls=%fused_computation.48 | convolution fusion | flops 3758096384 | bytes 15728640 | tf_op jit(solution)/shard_map/dot_general | solution.py:34
  99.1 143.5 %collective-permute-done.1 = bf16[512,7424]{1,0:T(8,128)(2,1)S(1)} collective-permute-done((bf16[512,7424]{1,0:T(8,128)(2,1)}, bf16[512,7424]{1,0:T(8,128)(2,1)S(1)}, u32[]{:S(2)}, u32[]{:S(2)}) %collective-permute-start.1) | collective-permute-done | bytes 7602208 | tf_op jit(solution)/shard_map/ppermute | solution.py:14
  242.6 2.1 collective-permute-done
  244.7 4.2 add_convert_fusion.refs_2_
  248.9 3.1 fusion.7
  252.3 4.0 slice.83.refs_4_
  256.3 0.8 collective-permute-start.7
  257.2 0.6 collective-permute-start.4
  257.7 40.6 %collective-permute-done.5 = bf16[128,7424]{1,0:T(8,128)(2,1)} collective-permute-done((bf16[128,7424]{1,0:T(8,128)(2,1)}, bf16[128,7424]{1,0:T(8,128)(2,1)}, u32[]{:S(2)}, u32[]{:S(2)}) %collective-permute-start.5) | collective-permute-done | bytes 1900576 | tf_op jit(solution)/shard_map/ppermute | solution.py:19
  298.4 8.5 %fusion.10 = f32[512,512]{1,0:T(8,128)S(1)} fusion(bf16[512,7168]{1,0:T(8,128)(2,1)} %add_convert_fusion.1.refs_0_, bf16[512,7168]{1,0:T(8,128)(2,1)} %add_convert_fusion.refs_2_), kind=kOutput, calls=%fused_computation.49 | convolution fusion | flops 3758096384 | bytes 15728640 | tf_op jit(solution)/shard_map/dot_general | solution.py:34
  306.9 26.2 %shard_map.68 = f32[4,512,512]{2,1,0:T(8,128)} custom-call(bf16[512,7168]{1,0:T(8,128)(2,1)} %add_convert_fusion.1.refs_0_, bf16[512,7168]{1,0:T(8,128)(2,1)} %collective-permute-done.2.refs_1_, bf16[512,7168]{1,0:T(8,128)(2,1)} %add_convert_fusion.refs_2_, bf16[512,7168]{1,0:T(8,128)(2,1)} %collective-permute-done.6.refs_3_, ...), custom_call_target="tpu_custom_call" | custom-call | flops 16911433728 | bytes 44564480 | tf_op jit(solution)/shard_map/pallas_call | solution.py:59
  333.1 5.9 %collective-permute-done.7 = bf16[128,7424]{1,0:T(8,128)(2,1)S(1)} collective-permute-done((bf16[128,7424]{1,0:T(8,128)(2,1)}, bf16[128,7424]{1,0:T(8,128)(2,1)S(1)}, u32[]{:S(2)}, u32[]{:S(2)}) %collective-permute-start.7) | collective-permute-done | bytes 1900576 | tf_op jit(solution)/shard_map/ppermute | solution.py:19
  339.0 1.6 constant_dynamic-update-slice_fusion.1
  340.8 1.7 slice_bitcast_fusion
  342.5 0.5 slice.108.refs_4_
  343.0 0.5 collective-permute-start.10
  343.5 1.1 collective-permute-start.9
  344.9 16.1 %shard_map.69 = f32[4,512,256]{2,1,0:T(8,128)S(1)} custom-call(bf16[512,7168]{1,0:T(8,128)(2,1)} %add_convert_fusion.1.refs_0_, bf16[512,7168]{1,0:T(8,128)(2,1)} %collective-permute-done.2.refs_1_, bf16[512,7168]{1,0:T(8,128)(2,1)} %add_convert_fusion.refs_2_, bf16[512,7168]{1,0:T(8,128)(2,1)} %collective-permute-done.6.refs_3_, ...), custom_call_target="tpu_custom_call" | custom-call | flops 8455716864 | bytes 38797312 | tf_op jit(solution)/shard_map/pallas_call | solution.py:59
  361.1 8.5 %fusion.11 = f32[512,512]{1,0:T(8,128)S(1)} fusion(bf16[512,7168]{1,0:T(8,128)(2,1)} %add_convert_fusion.1.refs_0_, bf16[512,7168]{1,0:T(8,128)(2,1)} %collective-permute-done.6.refs_3_), kind=kOutput, calls=%fused_computation.50 | convolution fusion | flops 3758096384 | bytes 15728640 | tf_op jit(solution)/shard_map/dot_general | solution.py:34
  369.6 9.7 %collective-permute-done.4 = bf16[128,7424]{1,0:T(8,128)(2,1)S(1)} collective-permute-done((bf16[128,7424]{1,0:T(8,128)(2,1)}, bf16[128,7424]{1,0:T(8,128)(2,1)S(1)}, u32[]{:S(2)}, u32[]{:S(2)}) %collective-permute-start.4) | collective-permute-done | bytes 1900576 | tf_op jit(solution)/shard_map/ppermute | solution.py:19
  379.3 11.9 %collective-permute-done.9 = f32[512,512]{1,0:T(8,128)S(1)} collective-permute-done((f32[512,512]{1,0:T(8,128)}, f32[512,512]{1,0:T(8,128)S(1)}, u32[]{:S(2)}, u32[]{:S(2)}) %collective-permute-start.9) | collective-permute-done | bytes 1048608 | tf_op jit(solution)/shard_map/ppermute | solution.py:14
  391.2 1.7 fusion.2
  392.9 1.5 collective-permute-start.11
  394.4 0.8 slice.96.refs_5_
  395.3 1.6 slice.95.refs_4_
  396.9 1.1 slice_bitcast_fusion.4
  398.2 1.3 collective-permute-start.13
  399.9 15.6 %shard_map.70 = f32[4,512,128]{2,1,0:T(8,128)S(1)} custom-call(bf16[512,7168]{1,0:T(8,128)(2,1)} %add_convert_fusion.1.refs_0_, bf16[512,7168]{1,0:T(8,128)(2,1)} %collective-permute-done.2.refs_1_, bf16[512,7168]{1,0:T(8,128)(2,1)} %add_convert_fusion.refs_2_, bf16[512,7168]{1,0:T(8,128)(2,1)} %collective-permute-done.6.refs_3_, ...), custom_call_target="tpu_custom_call" | custom-call | flops 4227858432 | bytes 35913728 | tf_op jit(solution)/shard_map/pallas_call | solution.py:59
  415.5 25.3 %collective-permute-done.11 = bf16[4,512,512]{2,1,0:T(8,128)(2,1)S(1)} collective-permute-done((bf16[4,512,512]{2,1,0:T(8,128)(2,1)}, bf16[4,512,512]{2,1,0:T(8,128)(2,1)S(1)}, u32[]{:S(2)}, u32[]{:S(2)}) %collective-permute-start.11) | collective-permute-done | bytes 2097184 | tf_op jit(solution)/shard_map/ppermute | solution.py:23
  440.8 2.8 convert_add_fusion.1
  443.9 1.5 collective-permute-start.15
  445.4 1.7 fusion.1
  447.1 0.6 collective-permute-start.24
  447.7 0.8 slice.102.refs_5_
  448.5 1.6 slice.101.refs_4_
  450.3 0.8 collective-permute-start.17
  451.1 1.1 collective-permute-start.16
  452.2 15.6 %shard_map.71 = f32[4,512,128]{2,1,0:T(8,128)S(1)} custom-call(bf16[512,7168]{1,0:T(8,128)(2,1)} %add_convert_fusion.1.refs_0_, bf16[512,7168]{1,0:T(8,128)(2,1)} %collective-permute-done.2.refs_1_, bf16[512,7168]{1,0:T(8,128)(2,1)} %add_convert_fusion.refs_2_, bf16[512,7168]{1,0:T(8,128)(2,1)} %collective-permute-done.6.refs_3_, ...), custom_call_target="tpu_custom_call" | custom-call | flops 4227858432 | bytes 35913728 | tf_op jit(solution)/shard_map/pallas_call | solution.py:59
  467.7 2.3 collective-permute-done.15
  470.4 0.6 copy-done.17
  471.0 0.9 fusion.5
  471.9 1.5 collective-permute-start.19
  473.5 0.8 collective-permute-start.21
  474.3 1.1 collective-permute-start.20
  475.4 49.2 %collective-permute-done.19 = bf16[4,512,128]{2,1,0:T(8,128)(2,1)} collective-permute-done((bf16[4,512,128]{2,1,0:T(8,128)(2,1)}, bf16[4,512,128]{2,1,0:T(8,128)(2,1)}, u32[]{:S(2)}, u32[]{:S(2)}) %collective-permute-start.19) | collective-permute-done | bytes 524320 | tf_op jit(solution)/shard_map/ppermute | solution.py:23
  524.5 1.4 convert_add_fusion.4
  526.1 1.5 collective-permute-start.23
  527.6 2.4 convert_add_fusion
  530.2 0.9 bitcast_add_fusion
  531.1 7.2 %collective-permute-done.23 = bf16[4,512,128]{2,1,0:T(8,128)(2,1)S(1)} collective-permute-done((bf16[4,512,128]{2,1,0:T(8,128)(2,1)S(1)}, bf16[4,512,128]{2,1,0:T(8,128)(2,1)S(1)}, u32[]{:S(2)}, u32[]{:S(2)}) %collective-permute-start.23) | collective-permute-done | bytes 524320 | tf_op jit(solution)/shard_map/ppermute | solution.py:23
  538.4 1.3 pad_maximum_fusion
  539.8 0.5 dynamic-slice_bitcast_fusion.3
  540.3 1.7 copy-done.2
  542.0 1.7 fusion
  543.6 4.7 copy.10
  (75 shorter events, 2.8 us)
Async XLA Ops:
  7.2 53.3 %all-gather.2.cloned.1.call-start = ((), (), s32[]{:S(2)}) async-start(), calls=%async_computation | async-start | bytes 3899392 | tf_op jit(solution)/shard_map/all_gather | solution.py:96
  69.8 18.7 %collective-permute-start.2 = (bf16[512,7168]{1,0:T(8,128)(2,1)}, bf16[512,7168]{1,0:T(8,128)(2,1)}, u32[]{:S(2)}, u32[]{:S(2)}) collective-permute-start(bf16[512,7168]{1,0:T(8,128)(2,1)} %add_convert_fusion.1.refs_0_), channel_id=1, source_target_pairs={{0,2},{2,0},{4,6},{6,4},{8,10},{10,8},{12,14},{14,12},{16,18},{18,... | collective-permute-start | bytes 22020104 | tf_op jit(solution)/shard_map/ppermute | solution.py:14
  76.6 166.0 %collective-permute-start.1 = (bf16[512,7424]{1,0:T(8,128)(2,1)}, bf16[512,7424]{1,0:T(8,128)(2,1)S(1)}, u32[]{:S(2)}, u32[]{:S(2)}) collective-permute-start(bf16[512,7424]{1,0:T(8,128)(2,1)} %pad_maximum_fusion.1), channel_id=1, source_target_pairs={{0,4},{2,6},{4,0},{6,2},{8,12},{10,14},{12,8},{14,10},{16,20},{18,... | collective-permute-start | bytes 22806536 | tf_op jit(solution)/shard_map/ppermute | solution.py:14
  77.2 167.5 %collective-permute-start = (bf16[512,7424]{1,0:T(8,128)(2,1)}, bf16[512,7424]{1,0:T(8,128)(2,1)S(1)}, u32[]{:S(2)}, u32[]{:S(2)}) collective-permute-start(bf16[512,7424]{1,0:T(8,128)(2,1)} %pad_maximum_fusion.1), channel_id=1, source_target_pairs={{0,8},{2,10},{4,12},{6,14},{8,16},{10,18},{12,20},{14,22},{16,24},... | collective-permute-start | bytes 22806536 | tf_op jit(solution)/shard_map/ppermute | solution.py:19
  88.5 356.9 %copy-start.4 = (f32[512,512]{1,0:T(8,128)}, f32[512,512]{1,0:T(8,128)S(1)}, u32[]{:S(2)}) copy-start(f32[512,512]{1,0:T(8,128)S(1)} %fusion.8) | copy-start | bytes 3145732
  88.5 156.2 %copy-start = (bf16[256,7168]{1,0:T(8,128)(2,1)S(1)}, bf16[256,7168]{1,0:T(8,128)(2,1)}, u32[]{:S(2)}) copy-start(bf16[256,7168]{1,0:T(8,128)(2,1)} %all-gather.2.cloned.1.call-done.refs_6_) | copy-start | bytes 11010052
  248.9 49.5 %collective-permute-start.6 = (bf16[512,7168]{1,0:T(8,128)(2,1)}, bf16[512,7168]{1,0:T(8,128)(2,1)}, u32[]{:S(2)}, u32[]{:S(2)}) collective-permute-start(bf16[512,7168]{1,0:T(8,128)(2,1)} %add_convert_fusion.refs_2_), channel_id=1, source_target_pairs={{0,2},{2,0},{4,6},{6,4},{8,10},{10,8},{12,14},{14,12},{16,18},{18,... | collective-permute-start | bytes 22020104 | tf_op jit(solution)/shard_map/ppermute | solution.py:14
  252.0 46.3 %collective-permute-start.5 = (bf16[128,7424]{1,0:T(8,128)(2,1)}, bf16[128,7424]{1,0:T(8,128)(2,1)}, u32[]{:S(2)}, u32[]{:S(2)}) collective-permute-start(bf16[128,7424]{1,0:T(8,128)(2,1)} %get-tuple-element.94), channel_id=1, source_target_pairs={{0,8},{2,10},{4,12},{6,14},{8,16},{10,18},{12,20},{14,22},{16,24},... | collective-permute-start | bytes 5701640 | tf_op jit(solution)/shard_map/ppermute | solution.py:19
  256.3 82.6 %collective-permute-start.7 = (bf16[128,7424]{1,0:T(8,128)(2,1)}, bf16[128,7424]{1,0:T(8,128)(2,1)S(1)}, u32[]{:S(2)}, u32[]{:S(2)}) collective-permute-start(bf16[128,7424]{1,0:T(8,128)(2,1)} %get-tuple-element.93), channel_id=1, source_target_pairs={{0,8},{2,10},{4,12},{6,14},{8,16},{10,18},{12,20},{14,22},{16,24},... | collective-permute-start | bytes 5701640 | tf_op jit(solution)/shard_map/ppermute | solution.py:19
  257.2 122.2 %collective-permute-start.4 = (bf16[128,7424]{1,0:T(8,128)(2,1)}, bf16[128,7424]{1,0:T(8,128)(2,1)S(1)}, u32[]{:S(2)}, u32[]{:S(2)}) collective-permute-start(bf16[128,7424]{1,0:T(8,128)(2,1)} %get-tuple-element.95), channel_id=1, source_target_pairs={{0,8},{2,10},{4,12},{6,14},{8,16},{10,18},{12,20},{14,22},{16,24},... | collective-permute-start | bytes 5701640 | tf_op jit(solution)/shard_map/ppermute | solution.py:19
  306.9 138.5 %copy-start.8 = (f32[512,512]{1,0:T(8,128)}, f32[512,512]{1,0:T(8,128)S(1)}, u32[]{:S(2)}) copy-start(f32[512,512]{1,0:T(8,128)S(1)} %fusion.10) | copy-start | bytes 3145732
  333.1 7.7 %copy-start.3 = (f32[4,512,512]{2,1,0:T(8,128)S(1)}, f32[4,512,512]{2,1,0:T(8,128)}, u32[]{:S(2)}) copy-start(f32[4,512,512]{2,1,0:T(8,128)} %shard_map.68) | copy-start | bytes 12582916
  343.0 36.3 %collective-permute-start.10 = (f32[512,512]{1,0:T(8,128)}, f32[512,512]{1,0:T(8,128)S(1)}, u32[]{:S(2)}, u32[]{:S(2)}) collective-permute-start(f32[512,512]{1,0:T(8,128)} %get-tuple-element.96), channel_id=1, source_target_pairs={{0,6},{2,4},{4,2},{6,0},{8,14},{10,12},{12,10},{14,8},{16,22},{18,... | collective-permute-start | bytes 3145736 | tf_op jit(solution)/shard_map/ppermute | solution.py:14
  343.5 47.7 %collective-permute-start.9 = (f32[512,512]{1,0:T(8,128)}, f32[512,512]{1,0:T(8,128)S(1)}, u32[]{:S(2)}, u32[]{:S(2)}) collective-permute-start(f32[512,512]{1,0:T(8,128)} %get-tuple-element.97), channel_id=1, source_target_pairs={{0,4},{2,6},{4,0},{6,2},{8,12},{10,14},{12,8},{14,10},{16,20},{18,... | collective-permute-start | bytes 3145736 | tf_op jit(solution)/shard_map/ppermute | solution.py:14
  344.6 46.6 %collective-permute-start.8 = (f32[512,512]{1,0:T(8,128)S(1)}, f32[512,512]{1,0:T(8,128)S(1)}, u32[]{:S(2)}, u32[]{:S(2)}) collective-permute-start(f32[512,512]{1,0:T(8,128)S(1)} %get-tuple-element.98), channel_id=1, source_target_pairs={{0,2},{2,0},{4,6},{6,4},{8,10},{10,8},{12,14},{14,12},{16,18},{18,... | collective-permute-start | bytes 3145736 | tf_op jit(solution)/shard_map/ppermute | solution.py:14
  369.6 75.8 %copy-start.10 = (f32[512,512]{1,0:T(8,128)}, f32[512,512]{1,0:T(8,128)S(1)}, u32[]{:S(2)}) copy-start(f32[512,512]{1,0:T(8,128)S(1)} %fusion.11) | copy-start | bytes 3145732
  379.3 11.9 %copy-start.16 = (bf16[128,7424]{1,0:T(8,128)(2,1)}, bf16[128,7424]{1,0:T(8,128)(2,1)S(1)}, u32[]{:S(2)}) copy-start(bf16[128,7424]{1,0:T(8,128)(2,1)S(1)} %collective-permute-done.4) | copy-start | bytes 5701636
  392.9 47.8 %collective-permute-start.11 = (bf16[4,512,512]{2,1,0:T(8,128)(2,1)}, bf16[4,512,512]{2,1,0:T(8,128)(2,1)S(1)}, u32[]{:S(2)}, u32[]{:S(2)}) collective-permute-start(bf16[4,512,512]{2,1,0:T(8,128)(2,1)} %fusion.2), channel_id=1, source_target_pairs={{0,1},{1,0},{2,3},{3,2},{4,5},{5,4},{6,7},{7,6},{8,9},{9,8},{10,11... | collective-permute-start | bytes 6291464 | tf_op jit(solution)/shard_map/ppermute | solution.py:23
  394.4 49.2 %collective-permute-start.3 = (bf16[128,7424]{1,0:T(8,128)(2,1)}, bf16[128,7424]{1,0:T(8,128)(2,1)}, u32[]{:S(2)}, u32[]{:S(2)}) collective-permute-start(bf16[128,7424]{1,0:T(8,128)(2,1)} %get-tuple-element.92), channel_id=1, source_target_pairs={{0,8},{2,10},{4,12},{6,14},{8,16},{10,18},{12,20},{14,22},{16,24},... | collective-permute-start | bytes 5701640 | tf_op jit(solution)/shard_map/ppermute | solution.py:19
  398.0 45.5 %collective-permute-start.14 = (f32[512,256]{1,0:T(8,128)}, f32[512,256]{1,0:T(8,128)S(1)}, u32[]{:S(2)}, u32[]{:S(2)}) collective-permute-start(f32[512,256]{1,0:T(8,128)} %get-tuple-element.100), channel_id=1, source_target_pairs={{0,6},{2,4},{4,2},{6,0},{8,14},{10,12},{12,10},{14,8},{16,22},{18,... | collective-permute-start | bytes 1572872 | tf_op jit(solution)/shard_map/ppermute | solution.py:14
  398.2 45.4 %collective-permute-start.13 = (f32[512,256]{1,0:T(8,128)}, f32[512,256]{1,0:T(8,128)S(1)}, u32[]{:S(2)}, u32[]{:S(2)}) collective-permute-start(f32[512,256]{1,0:T(8,128)} %get-tuple-element.101), channel_id=1, source_target_pairs={{0,4},{2,6},{4,0},{6,2},{8,12},{10,14},{12,8},{14,10},{16,20},{18,... | collective-permute-start | bytes 1572872 | tf_op jit(solution)/shard_map/ppermute | solution.py:14
  399.5 44.1 %collective-permute-start.12 = (f32[512,256]{1,0:T(8,128)S(1)}, f32[512,256]{1,0:T(8,128)S(1)}, u32[]{:S(2)}, u32[]{:S(2)}) collective-permute-start(f32[512,256]{1,0:T(8,128)S(1)} %get-tuple-element.102), channel_id=1, source_target_pairs={{0,2},{2,0},{4,6},{6,4},{8,10},{10,8},{12,14},{14,12},{16,18},{18,... | collective-permute-start | bytes 1572872 | tf_op jit(solution)/shard_map/ppermute | solution.py:14
  415.5 30.0 %copy-start.6 = (f32[512,512]{1,0:T(8,128)S(1)}, f32[512,512]{1,0:T(8,128)}, u32[]{:S(2)}) copy-start(f32[512,512]{1,0:T(8,128)} %fusion.9) | copy-start | bytes 3145732
  443.6 3.6 copy-start.12
  443.6 3.5 copy-start.14
  443.9 26.2 %collective-permute-start.15 = (bf16[4,512,256]{2,1,0:T(8,128)(2,1)S(1)}, bf16[4,512,256]{2,1,0:T(8,128)(2,1)S(1)}, u32[]{:S(2)}, u32[]{:S(2)}) collective-permute-start(bf16[4,512,256]{2,1,0:T(8,128)(2,1)S(1)} %fusion.3), channel_id=1, source_target_pairs={{0,1},{1,0},{2,3},{3,2},{4,5},{5,4},{6,7},{7,6},{8,9},{9,8},{10,11... | collective-permute-start | bytes 3145736 | tf_op jit(solution)/shard_map/ppermute | solution.py:23
  447.1 80.4 %collective-permute-start.24 = (bf16[4,512,512]{2,1,0:T(8,128)(2,1)}, bf16[4,512,512]{2,1,0:T(8,128)(2,1)}, u32[]{:S(2)}, u32[]{:S(2)}) collective-permute-start(bf16[4,512,512]{2,1,0:T(8,128)(2,1)} %fusion.1), channel_id=1, source_target_pairs={{0,1},{1,0},{2,3},{3,2},{4,5},{5,4},{6,7},{7,6},{8,9},{9,8},{10,11... | collective-permute-start | bytes 6291464 | tf_op jit(solution)/shard_map/ppermute | solution.py:23
  450.2 20.1 %collective-permute-start.18 = (f32[512,128]{1,0:T(8,128)S(1)}, f32[512,128]{1,0:T(8,128)S(1)}, u32[]{:S(2)}, u32[]{:S(2)}) collective-permute-start(f32[512,128]{1,0:T(8,128)S(1)} %get-tuple-element.108), channel_id=1, source_target_pairs={{0,6},{2,4},{4,2},{6,0},{8,14},{10,12},{12,10},{14,8},{16,22},{18,... | collective-permute-start | bytes 786440 | tf_op jit(solution)/shard_map/ppermute | solution.py:14
  450.3 20.0 %collective-permute-start.17 = (f32[512,128]{1,0:T(8,128)S(1)}, f32[512,128]{1,0:T(8,128)S(1)}, u32[]{:S(2)}, u32[]{:S(2)}) collective-permute-start(f32[512,128]{1,0:T(8,128)S(1)} %get-tuple-element.109), channel_id=1, source_target_pairs={{0,4},{2,6},{4,0},{6,2},{8,12},{10,14},{12,8},{14,10},{16,20},{18,... | collective-permute-start | bytes 786440 | tf_op jit(solution)/shard_map/ppermute | solution.py:14
  451.1 18.9 %copy-start.13 = (f32[512,256]{1,0:T(8,128)S(1)}, f32[512,256]{1,0:T(8,128)}, u32[]{:S(2)}) copy-start(f32[512,256]{1,0:T(8,128)} %copy-done.12) | copy-start | bytes 1572868
  451.1 18.9 %copy-start.15 = (f32[512,256]{1,0:T(8,128)S(1)}, f32[512,256]{1,0:T(8,128)}, u32[]{:S(2)}) copy-start(f32[512,256]{1,0:T(8,128)} %copy-done.14) | copy-start | bytes 1572868
  451.1 19.2 %collective-permute-start.16 = (f32[512,128]{1,0:T(8,128)S(1)}, f32[512,128]{1,0:T(8,128)S(1)}, u32[]{:S(2)}, u32[]{:S(2)}) collective-permute-start(f32[512,128]{1,0:T(8,128)S(1)} %get-tuple-element.110), channel_id=1, source_target_pairs={{0,2},{2,0},{4,6},{6,4},{8,10},{10,8},{12,14},{14,12},{16,18},{18,... | collective-permute-start | bytes 786440 | tf_op jit(solution)/shard_map/ppermute | solution.py:14
  470.3 0.7 copy-start.17
  470.3 1.5 copy-start.18
  470.4 3.0 copy-start.19
  471.9 52.7 %collective-permute-start.19 = (bf16[4,512,128]{2,1,0:T(8,128)(2,1)}, bf16[4,512,128]{2,1,0:T(8,128)(2,1)}, u32[]{:S(2)}, u32[]{:S(2)}) collective-permute-start(bf16[4,512,128]{2,1,0:T(8,128)(2,1)} %fusion.5), channel_id=1, source_target_pairs={{0,1},{1,0},{2,3},{3,2},{4,5},{5,4},{6,7},{7,6},{8,9},{9,8},{10,11... | collective-permute-start | bytes 1572872 | tf_op jit(solution)/shard_map/ppermute | solution.py:23
  473.4 54.2 %copy-start.5 = (f32[512,512]{1,0:T(8,128)S(1)}, f32[512,512]{1,0:T(8,128)}, u32[]{:S(2)}) copy-start(f32[512,512]{1,0:T(8,128)} %copy-done.4) | copy-start | bytes 3145732
  473.4 54.2 %copy-start.7 = (f32[512,512]{1,0:T(8,128)S(1)}, f32[512,512]{1,0:T(8,128)}, u32[]{:S(2)}) copy-start(f32[512,512]{1,0:T(8,128)} %fusion.9) | copy-start | bytes 3145732
  473.4 54.2 %copy-start.9 = (f32[512,512]{1,0:T(8,128)S(1)}, f32[512,512]{1,0:T(8,128)}, u32[]{:S(2)}) copy-start(f32[512,512]{1,0:T(8,128)} %copy-done.8) | copy-start | bytes 3145732
  473.4 54.3 %copy-start.11 = (f32[512,512]{1,0:T(8,128)S(1)}, f32[512,512]{1,0:T(8,128)}, u32[]{:S(2)}) copy-start(f32[512,512]{1,0:T(8,128)} %copy-done.10) | copy-start | bytes 3145732
  473.5 52.5 %collective-permute-start.22 = (f32[512,128]{1,0:T(8,128)S(1)}, f32[512,128]{1,0:T(8,128)S(1)}, u32[]{:S(2)}, u32[]{:S(2)}) collective-permute-start(f32[512,128]{1,0:T(8,128)S(1)} %get-tuple-element.104), channel_id=1, source_target_pairs={{0,6},{2,4},{4,2},{6,0},{8,14},{10,12},{12,10},{14,8},{16,22},{18,... | collective-permute-start | bytes 786440 | tf_op jit(solution)/shard_map/ppermute | solution.py:14
  473.5 52.4 %collective-permute-start.21 = (f32[512,128]{1,0:T(8,128)S(1)}, f32[512,128]{1,0:T(8,128)S(1)}, u32[]{:S(2)}, u32[]{:S(2)}) collective-permute-start(f32[512,128]{1,0:T(8,128)S(1)} %get-tuple-element.105), channel_id=1, source_target_pairs={{0,4},{2,6},{4,0},{6,2},{8,12},{10,14},{12,8},{14,10},{16,20},{18,... | collective-permute-start | bytes 786440 | tf_op jit(solution)/shard_map/ppermute | solution.py:14
  474.3 51.6 %collective-permute-start.20 = (f32[512,128]{1,0:T(8,128)S(1)}, f32[512,128]{1,0:T(8,128)S(1)}, u32[]{:S(2)}, u32[]{:S(2)}) collective-permute-start(f32[512,128]{1,0:T(8,128)S(1)} %get-tuple-element.106), channel_id=1, source_target_pairs={{0,2},{2,0},{4,6},{6,4},{8,10},{10,8},{12,14},{14,12},{16,18},{18,... | collective-permute-start | bytes 786440 | tf_op jit(solution)/shard_map/ppermute | solution.py:14
  526.0 4.1 copy-start.20
  526.1 12.2 %collective-permute-start.23 = (bf16[4,512,128]{2,1,0:T(8,128)(2,1)S(1)}, bf16[4,512,128]{2,1,0:T(8,128)(2,1)S(1)}, u32[]{:S(2)}, u32[]{:S(2)}) collective-permute-start(bf16[4,512,128]{2,1,0:T(8,128)(2,1)S(1)} %fusion.4), channel_id=1, source_target_pairs={{0,1},{1,0},{2,3},{3,2},{4,5},{5,4},{6,7},{7,6},{8,9},{9,8},{10,11... | collective-permute-start | bytes 1572872 | tf_op jit(solution)/shard_map/ppermute | solution.py:23
  530.1 8.3 %copy-start.1 = (f32[4,512,512]{2,1,0:T(8,128)S(1)}, f32[4,512,512]{2,1,0:T(8,128)}, u32[]{:S(2)}) copy-start(f32[4,512,512]{2,1,0:T(8,128)} %convert_add_fusion.1) | copy-start | bytes 12582916
  539.8 2.2 copy-start.2
Sparse Core Ops, SparseCore 0:
  10.3 50.1 all-gather.1

commit v6 on v5

--- a/solution.py
+++ b/solution.py
@@ -110,12 +110,9 @@
         sums = jnp.stack(sums)
         return sums + trade(sums.astype(jnp.bfloat16)).astype(jnp.float32)
 
+    moving, across_parcel = phase((moving, across_parcel))
     own = gradient_of(parcel)
     beside = swap(own, 1)
-    own_products = [block_product(own, panel) for panel in (own, beside)]
-    moving, across_parcel, beside, own_products = phase(
-        (moving, across_parcel, beside, own_products)
-    )
 
     sums = [None] * (steps + 1)
     made, handed = None, None
@@ -126,24 +123,29 @@
         if step == 1:
             across = gradient_of(across_parcel)
             group = [own, beside, across, swap(across, 1)]
+            own_products = [block_product(own, panel) for panel in (own, beside)]
         else:
             handed = to_owners(made)
-        first, group, handed = phase((first, group, handed))
+        first, group, handed, own_products = phase((first, group, handed, own_products))
         if step > 1:
             sums[steps - step + 1] = over_columns(handed)
         second = from_behind(quarters[1], GROUP)
         made = products(arrived)
-        first, second, made, sums = phase((first, second, made, sums))
+        if step == 1:
+            own_products += [block_product(own, panel) for panel in group[2:]]
+        first, second, made, sums, own_products = phase(
+            (first, second, made, sums, own_products)
+        )
         if step < steps - 1:
             rest = [from_behind(piece, GROUP) for piece in quarters[2:]]
             moving = jnp.concatenate([first, second, *rest])
 
     half = jnp.concatenate([first, second])
     third = from_behind(quarters[2], GROUP)
+    sums[steps] = over_columns(own_products)
     handed = to_owners(made)
     made = products(half)
-    own_products += [block_product(own, panel) for panel in group[2:]]
-    third, handed, made, own_products = phase((third, handed, made, own_products))
+    third, handed, made, sums[steps] = phase((third, handed, made, sums[steps]))
 
     fourth = from_behind(quarters[3], GROUP)
     sums[1] = over_columns(handed)
@@ -151,7 +153,6 @@
     made = products(third)
     fourth, sums[1], handed, made = phase((fourth, sums[1], handed, made))
 
-    sums[steps] = over_columns(own_products)
     last = [over_columns(handed)]
     handed = to_owners(made)
     made = products(fourth)

time: 556 us -> 493 us (0.89)
  waiting for transfers between devices: 343 us -> 275 us
    ppermute x15, waiting for transfers between devices: 155 us -> 113 us  [swap(): return lax.ppermute(array, 'row', [(i, i ^ mask) for i in range(count)])]
    ppermute x5, waiting for transfers between devices: 58.3 us -> 30 us  [from_behind(): lax.ppermute(array, 'row', [(i, (i + by) % count) for i in range(count)])]
    all_gather x1, waiting for transfers between devices: 44.4 us -> 54.9 us  [body(): cotangent_all = lax.all_gather(cotangent, 'row', axis=0, tiled=True)]
    ppermute x5, waiting for transfers between devices: 84 us -> 76.2 us  [trade(): return lax.ppermute(array, 'col', [(0, 1), (1, 0)])]
  transfers between devices with their start and end apart: 26 -> 26, of which waited for: 11 -> 11; matrix products, arithmetic and copies ran while one was open for 13% -> 18% of each run, Pallas kernels for 13% -> 15%
where the time goes in v6:
time: 493 us
  waiting for transfers between devices  275 us (56%)
  Pallas kernels  72.8 us (15%)
  matrix products  50.8 us (10%)
  local copies, waits for them, and re-layouts  28.6 us (6%)
  other arithmetic  25.9 us (5%)
  starting transfers between devices  18.3 us (4%)
  between operations  14.3 us (3%)
  blocking collectives  7.16 us (1%)
    ppermute x15, waiting for transfers between devices, swap(): return lax.ppermute(array, 'row', [(i, i ^ mask) for i in range(count)])  113 us
    ppermute x5, waiting for transfers between devices, trade(): return lax.ppermute(array, 'col', [(0, 1), (1, 0)])  76.2 us
    pallas_call x4, Pallas kernels, panel_products(): pl.pallas_call(products_kernel, grid=(width // depth,), in_specs=[pl.Bloc...  72.8 us
    all_gather x1, waiting for transfers between devices, body(): cotangent_all = lax.all_gather(cotangent, 'row', axis=0, tiled=True)  54.9 us
    dot_general x4, matrix products, block_product(): lax.dot_general(left, right, (((1,), (1,)), ((), ())), preferred_element_...  35 us
    ppermute x5, waiting for transfers between devices, from_behind(): lax.ppermute(array, 'row', [(i, (i + by) % count) for i in range(count)])  30 us
    dot_general x2, matrix products, gradient_tile(): lax.dot_general(columns, cotangent_all, (((1,), (0,)), ((), ())), preferr...  15.8 us
  transfers between devices with their start and end apart: 26, of which 11 were waited for; matrix products, arithmetic and copies ran while one was open for 18% of the time, Pallas kernels for 15%

profile of v6, /device:TPU:0, one launch (start us, length us, event | category | flops | bytes accessed | tf_op | source)
XLA Modules:
  0.0 492.8 jit_solution(12677665955010729189)
XLA Ops:
  7.2 0.7 all-gather.2.cloned.1.call-update
  7.9 1.0 copy.9
  8.9 7.2 %all_gather.6 = bf16[256,512]{0,1:T(8,128)(2,1)S(1)} all-gather(bf16[128,512]{0,1:T(8,128)(2,1)S(1)} %copy.9), channel_id=1, replica_groups=mesh['row'=16,'col'=2] {'col'}, dimensions={0}, use_global_device_ids=true | all-gather | bytes 393216 | tf_op jit(solution)/shard_map/all_gather | solution.py:92
  16.1 6.6 %pad_maximum_fusion.1 = bf16[512,7424]{1,0:T(8,128)(2,1)} fusion(bf16[512,256]{1,0:T(8,128)(2,1)S(1)} %bitcast.92, bf16[512,7168]{1,0:T(8,128)(2,1)} %param.7), kind=kLoop, calls=%fused_computation.3 | loop fusion | flops 15204352 | bytes 15204352 | tf_op jit(solution)/shard_map/concatenate | solution.py:93
  22.7 1.7 collective-permute-start.1
  24.4 1.6 collective-permute-start
  26.0 54.9 %all-gather.2.cloned.1.call-done.refs_6_ = bf16[256,7168]{1,0:T(8,128)(2,1)} async-done(((bf16[16,7168]{1,0:T(8,128)(2,1)}), bf16[256,7168]{1,0:T(8,128)(2,1)}) %all-gather.2.cloned.1.call-update) | async-done | bytes 3670032 | tf_op jit(solution)/shard_map/all_gather | solution.py:96
  80.9 9.4 %add_convert_fusion.1.refs_0_ = bf16[512,7168]{1,0:T(8,128)(2,1)} fusion(bf16[512,7168]{1,0:T(8,128)(2,1)} %param.7, bf16[256,512]{0,1:T(8,128)(2,1)S(1)} %all_gather.6, bf16[256,7168]{1,0:T(8,128)(2,1)} %all-gather.2.cloned.1.call-done.refs_6_), kind=kOutput, calls=%fused_computation.1 | convolution fusion | flops 1890058240 | bytes 18612224 | tf_op jit(solution)/shard_map/dot_general | solution.py:27
  90.6 108.4 %collective-permute-done.1 = bf16[512,7424]{1,0:T(8,128)(2,1)} collective-permute-done((bf16[512,7424]{1,0:T(8,128)(2,1)}, bf16[512,7424]{1,0:T(8,128)(2,1)}, u32[]{:S(2)}, u32[]{:S(2)}) %collective-permute-start.1) | collective-permute-done | bytes 7602208 | tf_op jit(solution)/shard_map/ppermute | solution.py:14
  198.9 11.8 %collective-permute-done = bf16[512,7424]{1,0:T(8,128)(2,1)} collective-permute-done((bf16[512,7424]{1,0:T(8,128)(2,1)}, bf16[512,7424]{1,0:T(8,128)(2,1)}, u32[]{:S(2)}, u32[]{:S(2)}) %collective-permute-start) | collective-permute-done | bytes 7602208 | tf_op jit(solution)/shard_map/ppermute | solution.py:19
  210.8 6.3 %add_convert_fusion.refs_2_ = bf16[512,7168]{1,0:T(8,128)(2,1)} fusion(bf16[256,7168]{1,0:T(8,128)(2,1)S(1)} %copy-done, bf16[512,7424]{1,0:T(8,128)(2,1)} %collective-permute-done.1), kind=kOutput, calls=%fused_computation | convolution fusion | flops 1890058240 | bytes 18612224 | tf_op jit(solution)/shard_map/dot_general | solution.py:27
  217.1 4.7 fusion.7
  221.8 9.5 %fusion.8 = f32[512,512]{1,0:T(8,128)S(1)} fusion(bf16[512,7168]{1,0:T(8,128)(2,1)} %add_convert_fusion.1.refs_0_), kind=kOutput, calls=%fused_computation.47 | convolution fusion | flops 3758096384 | bytes 8388608 | tf_op jit(solution)/shard_map/dot_general | solution.py:34
  231.3 1.0 slice.84.refs_5_
  232.3 6.5 %slice.83.refs_4_ = bf16[512,7168]{1,0:T(8,128)(2,1)} slice(bf16[512,7424]{1,0:T(8,128)(2,1)} %collective-permute-done), slice={[0:512], [0:7168]} | slice | bytes 14680064 | tf_op jit(solution)/shard_map/slice | solution.py:102
  238.7 0.8 collective-permute-start.7
  239.5 1.6 collective-permute-start.3
  241.1 8.5 %fusion.9 = f32[512,512]{1,0:T(8,128)S(1)} fusion(bf16[512,7168]{1,0:T(8,128)(2,1)} %add_convert_fusion.1.refs_0_, bf16[512,7168]{1,0:T(8,128)(2,1)} %collective-permute-done.5.refs_1_), kind=kOutput, calls=%fused_computation.48 | convolution fusion | flops 3758096384 | bytes 15728640 | tf_op jit(solution)/shard_map/dot_general | solution.py:34
  249.6 18.2 %collective-permute-done.4 = bf16[128,7424]{1,0:T(8,128)(2,1)S(1)} collective-permute-done((bf16[128,7424]{1,0:T(8,128)(2,1)S(1)}, bf16[128,7424]{1,0:T(8,128)(2,1)S(1)}, u32[]{:S(2)}, u32[]{:S(2)}) %collective-permute-start.4) | collective-permute-done | bytes 1900576 | tf_op jit(solution)/shard_map/ppermute | solution.py:19
  267.8 8.5 %fusion.10 = f32[512,512]{1,0:T(8,128)S(1)} fusion(bf16[512,7168]{1,0:T(8,128)(2,1)} %add_convert_fusion.1.refs_0_, bf16[512,7168]{1,0:T(8,128)(2,1)} %add_convert_fusion.refs_2_), kind=kOutput, calls=%fused_computation.49 | convolution fusion | flops 3758096384 | bytes 15728640 | tf_op jit(solution)/shard_map/dot_general | solution.py:34
  276.4 8.5 %fusion.11 = f32[512,512]{1,0:T(8,128)S(1)} fusion(bf16[512,7168]{1,0:T(8,128)(2,1)} %add_convert_fusion.1.refs_0_, bf16[512,7168]{1,0:T(8,128)(2,1)} %collective-permute-done.6.refs_3_), kind=kOutput, calls=%fused_computation.50 | convolution fusion | flops 3758096384 | bytes 15728640 | tf_op jit(solution)/shard_map/dot_general | solution.py:34
  284.9 25.8 %shard_map.68 = f32[4,512,512]{2,1,0:T(8,128)} custom-call(bf16[512,7168]{1,0:T(8,128)(2,1)} %add_convert_fusion.1.refs_0_, bf16[512,7168]{1,0:T(8,128)(2,1)} %collective-permute-done.5.refs_1_, bf16[512,7168]{1,0:T(8,128)(2,1)} %add_convert_fusion.refs_2_, bf16[512,7168]{1,0:T(8,128)(2,1)} %collective-permute-done.6.refs_3_, ...), custom_call_target="tpu_custom_call" | custom-call | flops 16911433728 | bytes 44564480 | tf_op jit(solution)/shard_map/pallas_call | solution.py:59
  310.7 1.7 fusion.2
  312.4 1.5 collective-permute-start.11
  314.2 0.5 slice.108.refs_4_
  314.7 1.7 copy-done.4
  316.4 1.7 slice_bitcast_fusion
  318.2 1.4 collective-permute-start.9
  319.9 16.0 %shard_map.69 = f32[4,512,256]{2,1,0:T(8,128)S(1)} custom-call(bf16[512,7168]{1,0:T(8,128)(2,1)} %add_convert_fusion.1.refs_0_, bf16[512,7168]{1,0:T(8,128)(2,1)} %collective-permute-done.5.refs_1_, bf16[512,7168]{1,0:T(8,128)(2,1)} %add_convert_fusion.refs_2_, bf16[512,7168]{1,0:T(8,128)(2,1)} %collective-permute-done.6.refs_3_, ...), custom_call_target="tpu_custom_call" | custom-call | flops 8455716864 | bytes 38797312 | tf_op jit(solution)/shard_map/pallas_call | solution.py:59
  336.0 23.5 %collective-permute-done.11 = bf16[4,512,512]{2,1,0:T(8,128)(2,1)S(1)} collective-permute-done((bf16[4,512,512]{2,1,0:T(8,128)(2,1)}, bf16[4,512,512]{2,1,0:T(8,128)(2,1)S(1)}, u32[]{:S(2)}, u32[]{:S(2)}) %collective-permute-start.11) | collective-permute-done | bytes 2097184 | tf_op jit(solution)/shard_map/ppermute | solution.py:23
  359.5 2.8 convert_add_fusion.1
  362.3 3.9 collective-permute-done.9
  366.2 0.4 fusion.1
  366.6 0.6 collective-permute-start.12
  367.2 0.8 slice.96.refs_5_
  368.1 1.6 slice.95.refs_4_
  369.7 1.2 slice_bitcast_fusion.4
  370.9 1.5 collective-permute-start.14
  372.3 0.4 collective-permute-start.13
  372.7 15.5 %shard_map.70 = f32[4,512,128]{2,1,0:T(8,128)S(1)} custom-call(bf16[512,7168]{1,0:T(8,128)(2,1)} %add_convert_fusion.1.refs_0_, bf16[512,7168]{1,0:T(8,128)(2,1)} %collective-permute-done.5.refs_1_, bf16[512,7168]{1,0:T(8,128)(2,1)} %add_convert_fusion.refs_2_, bf16[512,7168]{1,0:T(8,128)(2,1)} %collective-permute-done.6.refs_3_, ...), custom_call_target="tpu_custom_call" | custom-call | flops 4227858432 | bytes 35913728 | tf_op jit(solution)/shard_map/pallas_call | solution.py:59
  388.2 26.1 %collective-permute-done.12 = bf16[4,512,512]{2,1,0:T(8,128)(2,1)S(1)} collective-permute-done((bf16[4,512,512]{2,1,0:T(8,128)(2,1)S(1)}, bf16[4,512,512]{2,1,0:T(8,128)(2,1)S(1)}, u32[]{:S(2)}, u32[]{:S(2)}) %collective-permute-start.12) | collective-permute-done | bytes 2097184 | tf_op jit(solution)/shard_map/ppermute | solution.py:23
  414.3 2.7 convert_add_fusion
  417.4 0.5 copy-done.5
  417.9 0.5 collective-permute-start.16
  418.8 0.6 collective-permute-start.18
  419.4 1.3 collective-permute-start.17
  420.6 15.5 %shard_map.71 = f32[4,512,128]{2,1,0:T(8,128)S(1)} custom-call(bf16[512,7168]{1,0:T(8,128)(2,1)} %add_convert_fusion.1.refs_0_, bf16[512,7168]{1,0:T(8,128)(2,1)} %collective-permute-done.5.refs_1_, bf16[512,7168]{1,0:T(8,128)(2,1)} %add_convert_fusion.refs_2_, bf16[512,7168]{1,0:T(8,128)(2,1)} %collective-permute-done.6.refs_3_, ...), custom_call_target="tpu_custom_call" | custom-call | flops 4227858432 | bytes 35913728 | tf_op jit(solution)/shard_map/pallas_call | solution.py:59
  436.1 6.1 %collective-permute-done.16 = bf16[4,512,256]{2,1,0:T(8,128)(2,1)S(1)} collective-permute-done((bf16[4,512,256]{2,1,0:T(8,128)(2,1)S(1)}, bf16[4,512,256]{2,1,0:T(8,128)(2,1)S(1)}, u32[]{:S(2)}, u32[]{:S(2)}) %collective-permute-start.16) | collective-permute-done | bytes 1048608 | tf_op jit(solution)/shard_map/ppermute | solution.py:23
  442.6 0.6 collective-permute-start.20
  443.3 1.0 collective-permute-start.22
  444.4 0.8 collective-permute-start.21
  445.2 9.6 %collective-permute-done.20 = bf16[4,512,128]{2,1,0:T(8,128)(2,1)S(1)} collective-permute-done((bf16[4,512,128]{2,1,0:T(8,128)(2,1)S(1)}, bf16[4,512,128]{2,1,0:T(8,128)(2,1)S(1)}, u32[]{:S(2)}, u32[]{:S(2)}) %collective-permute-start.20) | collective-permute-done | bytes 524320 | tf_op jit(solution)/shard_map/ppermute | solution.py:23
  454.8 1.1 convert_add_fusion.4
  455.9 0.8 collective-permute-done.22
  456.7 1.0 fusion.4
  457.7 1.5 collective-permute-start.24
  459.1 2.1 bitcast_add_fusion
  461.2 10.8 %collective-permute-done.24 = bf16[4,512,128]{2,1,0:T(8,128)(2,1)} collective-permute-done((bf16[4,512,128]{2,1,0:T(8,128)(2,1)}, bf16[4,512,128]{2,1,0:T(8,128)(2,1)}, u32[]{:S(2)}, u32[]{:S(2)}) %collective-permute-start.24) | collective-permute-done | bytes 524320 | tf_op jit(solution)/shard_map/ppermute | solution.py:23
  472.0 1.4 convert_add_fusion.3
  473.4 4.0 pad_maximum_fusion
  477.4 0.5 dynamic-slice_bitcast_fusion.3
  477.9 1.7 copy-done.2
  479.6 1.6 fusion
  481.2 4.7 copy.10
  (54 shorter events, 2.2 us)
Async XLA Ops:
  7.2 73.7 %all-gather.2.cloned.1.call-start = ((), (), s32[]{:S(2)}) async-start(), calls=%async_computation | async-start | bytes 3899392 | tf_op jit(solution)/shard_map/all_gather | solution.py:96
  22.7 176.3 %collective-permute-start.1 = (bf16[512,7424]{1,0:T(8,128)(2,1)}, bf16[512,7424]{1,0:T(8,128)(2,1)}, u32[]{:S(2)}, u32[]{:S(2)}) collective-permute-start(bf16[512,7424]{1,0:T(8,128)(2,1)} %pad_maximum_fusion.1), channel_id=1, source_target_pairs={{0,4},{2,6},{4,0},{6,2},{8,12},{10,14},{12,8},{14,10},{16,20},{18,... | collective-permute-start | bytes 22806536 | tf_op jit(solution)/shard_map/ppermute | solution.py:14
  24.4 186.3 %collective-permute-start = (bf16[512,7424]{1,0:T(8,128)(2,1)}, bf16[512,7424]{1,0:T(8,128)(2,1)}, u32[]{:S(2)}, u32[]{:S(2)}) collective-permute-start(bf16[512,7424]{1,0:T(8,128)(2,1)} %pad_maximum_fusion.1), channel_id=1, source_target_pairs={{0,8},{2,10},{4,12},{6,14},{8,16},{10,18},{12,20},{14,22},{16,24},... | collective-permute-start | bytes 22806536 | tf_op jit(solution)/shard_map/ppermute | solution.py:19
  80.9 129.9 %copy-start = (bf16[256,7168]{1,0:T(8,128)(2,1)S(1)}, bf16[256,7168]{1,0:T(8,128)(2,1)}, u32[]{:S(2)}) copy-start(bf16[256,7168]{1,0:T(8,128)(2,1)} %all-gather.2.cloned.1.call-done.refs_6_) | copy-start | bytes 11010052
  90.3 150.8 %collective-permute-start.5 = (bf16[512,7168]{1,0:T(8,128)(2,1)}, bf16[512,7168]{1,0:T(8,128)(2,1)}, u32[]{:S(2)}, u32[]{:S(2)}) collective-permute-start(bf16[512,7168]{1,0:T(8,128)(2,1)} %add_convert_fusion.1.refs_0_), channel_id=1, source_target_pairs={{0,2},{2,0},{4,6},{6,4},{8,10},{10,8},{12,14},{14,12},{16,18},{18,... | collective-permute-start | bytes 22020104 | tf_op jit(solution)/shard_map/ppermute | solution.py:14
  217.1 50.7 %collective-permute-start.6 = (bf16[512,7168]{1,0:T(8,128)(2,1)}, bf16[512,7168]{1,0:T(8,128)(2,1)}, u32[]{:S(2)}, u32[]{:S(2)}) collective-permute-start(bf16[512,7168]{1,0:T(8,128)(2,1)} %add_convert_fusion.refs_2_), channel_id=1, source_target_pairs={{0,2},{2,0},{4,6},{6,4},{8,10},{10,8},{12,14},{14,12},{16,18},{18,... | collective-permute-start | bytes 22020104 | tf_op jit(solution)/shard_map/ppermute | solution.py:14
  221.8 46.0 %collective-permute-start.4 = (bf16[128,7424]{1,0:T(8,128)(2,1)S(1)}, bf16[128,7424]{1,0:T(8,128)(2,1)S(1)}, u32[]{:S(2)}, u32[]{:S(2)}) collective-permute-start(bf16[128,7424]{1,0:T(8,128)(2,1)S(1)} %get-tuple-element.94), channel_id=1, source_target_pairs={{0,8},{2,10},{4,12},{6,14},{8,16},{10,18},{12,20},{14,22},{16,24},... | collective-permute-start | bytes 5701640 | tf_op jit(solution)/shard_map/ppermute | solution.py:19
  238.7 72.0 %collective-permute-start.7 = (bf16[128,7424]{1,0:T(8,128)(2,1)S(1)}, bf16[128,7424]{1,0:T(8,128)(2,1)S(1)}, u32[]{:S(2)}, u32[]{:S(2)}) collective-permute-start(bf16[128,7424]{1,0:T(8,128)(2,1)S(1)} %get-tuple-element.93), channel_id=1, source_target_pairs={{0,8},{2,10},{4,12},{6,14},{8,16},{10,18},{12,20},{14,22},{16,24},... | collective-permute-start | bytes 5701640 | tf_op jit(solution)/shard_map/ppermute | solution.py:19
  239.5 122.8 %collective-permute-start.3 = (bf16[128,7424]{1,0:T(8,128)(2,1)}, bf16[128,7424]{1,0:T(8,128)(2,1)}, u32[]{:S(2)}, u32[]{:S(2)}) collective-permute-start(bf16[128,7424]{1,0:T(8,128)(2,1)} %get-tuple-element.95), channel_id=1, source_target_pairs={{0,8},{2,10},{4,12},{6,14},{8,16},{10,18},{12,20},{14,22},{16,24},... | collective-permute-start | bytes 5701640 | tf_op jit(solution)/shard_map/ppermute | solution.py:19
  312.4 47.1 %collective-permute-start.11 = (bf16[4,512,512]{2,1,0:T(8,128)(2,1)}, bf16[4,512,512]{2,1,0:T(8,128)(2,1)S(1)}, u32[]{:S(2)}, u32[]{:S(2)}) collective-permute-start(bf16[4,512,512]{2,1,0:T(8,128)(2,1)} %fusion.2), channel_id=1, source_target_pairs={{0,1},{1,0},{2,3},{3,2},{4,5},{5,4},{6,7},{7,6},{8,9},{9,8},{10,11... | collective-permute-start | bytes 6291464 | tf_op jit(solution)/shard_map/ppermute | solution.py:23
  314.2 2.2 copy-start.4
  318.1 44.2 %collective-permute-start.10 = (f32[512,512]{1,0:T(8,128)}, f32[512,512]{1,0:T(8,128)S(1)}, u32[]{:S(2)}, u32[]{:S(2)}) collective-permute-start(f32[512,512]{1,0:T(8,128)} %get-tuple-element.96), channel_id=1, source_target_pairs={{0,6},{2,4},{4,2},{6,0},{8,14},{10,12},{12,10},{14,8},{16,22},{18,... | collective-permute-start | bytes 3145736 | tf_op jit(solution)/shard_map/ppermute | solution.py:14
  318.2 48.0 %collective-permute-start.9 = (f32[512,512]{1,0:T(8,128)}, f32[512,512]{1,0:T(8,128)S(1)}, u32[]{:S(2)}, u32[]{:S(2)}) collective-permute-start(f32[512,512]{1,0:T(8,128)} %get-tuple-element.97), channel_id=1, source_target_pairs={{0,4},{2,6},{4,0},{6,2},{8,12},{10,14},{12,8},{14,10},{16,20},{18,... | collective-permute-start | bytes 3145736 | tf_op jit(solution)/shard_map/ppermute | solution.py:14
  319.6 46.6 %collective-permute-start.8 = (f32[512,512]{1,0:T(8,128)}, f32[512,512]{1,0:T(8,128)S(1)}, u32[]{:S(2)}, u32[]{:S(2)}) collective-permute-start(f32[512,512]{1,0:T(8,128)} %get-tuple-element.98), channel_id=1, source_target_pairs={{0,2},{2,0},{4,6},{6,4},{8,10},{10,8},{12,14},{14,12},{16,18},{18,... | collective-permute-start | bytes 3145736 | tf_op jit(solution)/shard_map/ppermute | solution.py:14
  366.6 47.7 %collective-permute-start.12 = (bf16[4,512,512]{2,1,0:T(8,128)(2,1)S(1)}, bf16[4,512,512]{2,1,0:T(8,128)(2,1)S(1)}, u32[]{:S(2)}, u32[]{:S(2)}) collective-permute-start(bf16[4,512,512]{2,1,0:T(8,128)(2,1)S(1)} %fusion.1), channel_id=1, source_target_pairs={{0,1},{1,0},{2,3},{3,2},{4,5},{5,4},{6,7},{7,6},{8,9},{9,8},{10,11... | collective-permute-start | bytes 6291464 | tf_op jit(solution)/shard_map/ppermute | solution.py:23
  367.2 49.8 %collective-permute-start.2 = (bf16[128,7424]{1,0:T(8,128)(2,1)}, bf16[128,7424]{1,0:T(8,128)(2,1)S(1)}, u32[]{:S(2)}, u32[]{:S(2)}) collective-permute-start(bf16[128,7424]{1,0:T(8,128)(2,1)} %get-tuple-element.92), channel_id=1, source_target_pairs={{0,8},{2,10},{4,12},{6,14},{8,16},{10,18},{12,20},{14,22},{16,24},... | collective-permute-start | bytes 5701640 | tf_op jit(solution)/shard_map/ppermute | solution.py:19
  370.9 46.2 %collective-permute-start.15 = (f32[512,256]{1,0:T(8,128)}, f32[512,256]{1,0:T(8,128)S(1)}, u32[]{:S(2)}, u32[]{:S(2)}) collective-permute-start(f32[512,256]{1,0:T(8,128)} %get-tuple-element.100), channel_id=1, source_target_pairs={{0,6},{2,4},{4,2},{6,0},{8,14},{10,12},{12,10},{14,8},{16,22},{18,... | collective-permute-start | bytes 1572872 | tf_op jit(solution)/shard_map/ppermute | solution.py:14
  370.9 46.2 %collective-permute-start.14 = (f32[512,256]{1,0:T(8,128)}, f32[512,256]{1,0:T(8,128)S(1)}, u32[]{:S(2)}, u32[]{:S(2)}) collective-permute-start(f32[512,256]{1,0:T(8,128)} %get-tuple-element.101), channel_id=1, source_target_pairs={{0,4},{2,6},{4,0},{6,2},{8,12},{10,14},{12,8},{14,10},{16,20},{18,... | collective-permute-start | bytes 1572872 | tf_op jit(solution)/shard_map/ppermute | solution.py:14
  372.3 44.7 %collective-permute-start.13 = (f32[512,256]{1,0:T(8,128)S(1)}, f32[512,256]{1,0:T(8,128)S(1)}, u32[]{:S(2)}, u32[]{:S(2)}) collective-permute-start(f32[512,256]{1,0:T(8,128)S(1)} %get-tuple-element.102), channel_id=1, source_target_pairs={{0,2},{2,0},{4,6},{6,4},{8,10},{10,8},{12,14},{14,12},{16,18},{18,... | collective-permute-start | bytes 1572872 | tf_op jit(solution)/shard_map/ppermute | solution.py:14
  417.1 0.8 copy-start.5
  417.9 24.3 %collective-permute-start.16 = (bf16[4,512,256]{2,1,0:T(8,128)(2,1)S(1)}, bf16[4,512,256]{2,1,0:T(8,128)(2,1)S(1)}, u32[]{:S(2)}, u32[]{:S(2)}) collective-permute-start(bf16[4,512,256]{2,1,0:T(8,128)(2,1)S(1)} %fusion.3), channel_id=1, source_target_pairs={{0,1},{1,0},{2,3},{3,2},{4,5},{5,4},{6,7},{7,6},{8,9},{9,8},{10,11... | collective-permute-start | bytes 3145736 | tf_op jit(solution)/shard_map/ppermute | solution.py:23
  418.7 23.8 %collective-permute-start.19 = (f32[512,128]{1,0:T(8,128)S(1)}, f32[512,128]{1,0:T(8,128)S(1)}, u32[]{:S(2)}, u32[]{:S(2)}) collective-permute-start(f32[512,128]{1,0:T(8,128)S(1)} %get-tuple-element.108), channel_id=1, source_target_pairs={{0,6},{2,4},{4,2},{6,0},{8,14},{10,12},{12,10},{14,8},{16,22},{18,... | collective-permute-start | bytes 786440 | tf_op jit(solution)/shard_map/ppermute | solution.py:14
  418.8 23.7 %collective-permute-start.18 = (f32[512,128]{1,0:T(8,128)S(1)}, f32[512,128]{1,0:T(8,128)S(1)}, u32[]{:S(2)}, u32[]{:S(2)}) collective-permute-start(f32[512,128]{1,0:T(8,128)S(1)} %get-tuple-element.109), channel_id=1, source_target_pairs={{0,4},{2,6},{4,0},{6,2},{8,12},{10,14},{12,8},{14,10},{16,20},{18,... | collective-permute-start | bytes 786440 | tf_op jit(solution)/shard_map/ppermute | solution.py:14
  419.3 22.9 %copy-start.6 = (f32[512,256]{1,0:T(8,128)S(1)}, f32[512,256]{1,0:T(8,128)}, u32[]{:S(2)}) copy-start(f32[512,256]{1,0:T(8,128)} %copy-done.5) | copy-start | bytes 1572868
  419.4 23.1 %collective-permute-start.17 = (f32[512,128]{1,0:T(8,128)S(1)}, f32[512,128]{1,0:T(8,128)S(1)}, u32[]{:S(2)}, u32[]{:S(2)}) collective-permute-start(f32[512,128]{1,0:T(8,128)S(1)} %get-tuple-element.110), channel_id=1, source_target_pairs={{0,2},{2,0},{4,6},{6,4},{8,10},{10,8},{12,14},{14,12},{16,18},{18,... | collective-permute-start | bytes 786440 | tf_op jit(solution)/shard_map/ppermute | solution.py:14
  442.6 16.6 %slice-start = ((f32[4,512,512]{2,1,0:T(8,128)}), f32[1,512,512]{2,1,0:T(8,128)S(1)}, s32[]{:S(2)}) async-start(f32[4,512,512]{2,1,0:T(8,128)} %convert_add_fusion.1), calls=%async_computation.1 | async-start | bytes 2097152 | tf_op jit(solution)/shard_map/slice | solution.py:177
  442.6 12.2 %collective-permute-start.20 = (bf16[4,512,128]{2,1,0:T(8,128)(2,1)S(1)}, bf16[4,512,128]{2,1,0:T(8,128)(2,1)S(1)}, u32[]{:S(2)}, u32[]{:S(2)}) collective-permute-start(bf16[4,512,128]{2,1,0:T(8,128)(2,1)S(1)} %fusion.5), channel_id=1, source_target_pairs={{0,1},{1,0},{2,3},{3,2},{4,5},{5,4},{6,7},{7,6},{8,9},{9,8},{10,11... | collective-permute-start | bytes 1572872 | tf_op jit(solution)/shard_map/ppermute | solution.py:23
  443.3 12.7 %collective-permute-start.23 = (f32[512,128]{1,0:T(8,128)S(1)}, f32[512,128]{1,0:T(8,128)S(1)}, u32[]{:S(2)}, u32[]{:S(2)}) collective-permute-start(f32[512,128]{1,0:T(8,128)S(1)} %get-tuple-element.104), channel_id=1, source_target_pairs={{0,6},{2,4},{4,2},{6,0},{8,14},{10,12},{12,10},{14,8},{16,22},{18,... | collective-permute-start | bytes 786440 | tf_op jit(solution)/shard_map/ppermute | solution.py:14
  443.3 13.3 %collective-permute-start.22 = (f32[512,128]{1,0:T(8,128)S(1)}, f32[512,128]{1,0:T(8,128)S(1)}, u32[]{:S(2)}, u32[]{:S(2)}) collective-permute-start(f32[512,128]{1,0:T(8,128)S(1)} %get-tuple-element.105), channel_id=1, source_target_pairs={{0,4},{2,6},{4,0},{6,2},{8,12},{10,14},{12,8},{14,10},{16,20},{18,... | collective-permute-start | bytes 786440 | tf_op jit(solution)/shard_map/ppermute | solution.py:14
  444.4 12.3 %collective-permute-start.21 = (f32[512,128]{1,0:T(8,128)S(1)}, f32[512,128]{1,0:T(8,128)S(1)}, u32[]{:S(2)}, u32[]{:S(2)}) collective-permute-start(f32[512,128]{1,0:T(8,128)S(1)} %get-tuple-element.106), channel_id=1, source_target_pairs={{0,2},{2,0},{4,6},{6,4},{8,10},{10,8},{12,14},{14,12},{16,18},{18,... | collective-permute-start | bytes 786440 | tf_op jit(solution)/shard_map/ppermute | solution.py:14
  455.9 0.8 copy-start.7
  456.7 1.0 copy-start.8
  456.7 2.4 copy-start.9
  457.7 14.4 %collective-permute-start.24 = (bf16[4,512,128]{2,1,0:T(8,128)(2,1)}, bf16[4,512,128]{2,1,0:T(8,128)(2,1)}, u32[]{:S(2)}, u32[]{:S(2)}) collective-permute-start(bf16[4,512,128]{2,1,0:T(8,128)(2,1)} %fusion.4), channel_id=1, source_target_pairs={{0,1},{1,0},{2,3},{3,2},{4,5},{5,4},{6,7},{7,6},{8,9},{9,8},{10,11... | collective-permute-start | bytes 1572872 | tf_op jit(solution)/shard_map/ppermute | solution.py:23
  459.1 14.3 %copy-start.1 = (f32[4,512,512]{2,1,0:T(8,128)S(1)}, f32[4,512,512]{2,1,0:T(8,128)}, u32[]{:S(2)}) copy-start(f32[4,512,512]{2,1,0:T(8,128)} %convert_add_fusion.1) | copy-start | bytes 12582916
  459.1 14.3 %copy-start.3 = (f32[4,512,128]{2,1,0:T(8,128)S(1)}, f32[4,512,128]{2,1,0:T(8,128)}, u32[]{:S(2)}) copy-start(f32[4,512,128]{2,1,0:T(8,128)} %convert_add_fusion.4) | copy-start | bytes 3145732
  477.4 2.2 copy-start.2
Sparse Core Ops, SparseCore 0:
  10.3 70.5 all-gather.1

commit v7 on v6

--- a/solution.py
+++ b/solution.py
@@ -25,7 +25,7 @@
 
 def gradient_tile(columns, cotangent_all, accumulated):
     product = lax.dot_general(
-        columns, cotangent_all, (((1,), (0,)), ((), ())), preferred_element_type=jnp.float32
+        columns, cotangent_all, (((0,), (0,)), ((), ())), preferred_element_type=jnp.float32
     )
     return (product + accumulated.astype(jnp.float32)).astype(jnp.bfloat16)
 
@@ -37,8 +37,10 @@
 
 
 def products_kernel(*refs):
-    *lefts, raw, columns, cotangent, out = refs
-    panel = gradient_tile(columns[...], cotangent[...], raw[...])
+    *panels, columns, cotangent, out = refs
+    lefts, raws = panels[:GROUP], panels[GROUP:]
+    raw = jnp.concatenate([piece[...] for piece in raws])
+    panel = gradient_tile(columns[...], cotangent[...], raw)
     parts = [block_product(left[...], panel) for left in lefts]
 
     @pl.when(pl.program_id(0) == 0)
@@ -52,17 +54,17 @@
             out[u] += part
 
 
-def panel_products(group, raw, columns, cotangent_all):
+def panel_products(group, raws, columns, cotangent_all):
     block, width = group[0].shape
-    rows, tokens = columns.shape
+    tokens, rows = columns.shape
     depth = max(d for d in range(128, 1025, 128) if width % d == 0)
     return pl.pallas_call(
         products_kernel,
         grid=(width // depth,),
         in_specs=[pl.BlockSpec((block, depth), lambda k: (0, k))] * len(group)
+        + [pl.BlockSpec((raw.shape[0], depth), lambda k: (0, k)) for raw in raws]
         + [
-            pl.BlockSpec((rows, depth), lambda k: (0, k)),
-            pl.BlockSpec((rows, tokens), lambda k: (0, 0)),
+            pl.BlockSpec((tokens, rows), lambda k: (0, 0)),
             pl.BlockSpec((tokens, depth), lambda k: (0, k)),
         ],
         out_specs=pl.BlockSpec((len(group), block, rows), lambda k: (0, 0, 0)),
@@ -76,7 +78,7 @@
             + 4 * len(group) * block * rows,
             transcendentals=0,
         ),
-    )(*group, raw, columns, cotangent_all)
+    )(*group, *raws, columns, cotangent_all)
 
 
 def body(activations, cotangent, accumulated, band_old, diagonal_old):
@@ -89,17 +91,26 @@
 
     phase = lax.optimization_barrier
 
-    columns = lax.all_gather(activations, "col", axis=0, tiled=True)
-    parcel = jnp.concatenate([accumulated, columns.T], axis=1)
-    moving = from_behind(parcel, GROUP)
-    across_parcel = swap(parcel, 2)
+    quarter = block // 4
+    quarters = [
+        from_behind(accumulated[q * quarter : (q + 1) * quarter], GROUP) for q in range(4)
+    ]
+    across_raw = swap(accumulated, 2)
+    if n_col == 2:
+        other = trade(activations)
+        columns = jnp.where(
+            y == 0,
+            jnp.concatenate([activations, other]),
+            jnp.concatenate([other, activations]),
+        )
+    else:
+        columns = lax.all_gather(activations, "col", axis=0, tiled=True)
+    across_columns = swap(columns, 2)
+    behind = from_behind(columns, GROUP)
     cotangent_all = lax.all_gather(cotangent, "row", axis=0, tiled=True)
 
-    def gradient_of(parcel):
-        return gradient_tile(parcel[:, width:], cotangent_all, parcel[:, :width])
-
-    def products(parcel):
-        return panel_products(group, parcel[:, :width], parcel[:, width:], cotangent_all)
+    def products(raws, columns):
+        return panel_products(group, raws, columns, cotangent_all)
 
     def to_owners(made):
         return [made[0]] + [swap(made[u], u) for u in range(1, GROUP)]
@@ -110,18 +121,18 @@
         sums = jnp.stack(sums)
         return sums + trade(sums.astype(jnp.bfloat16)).astype(jnp.float32)
 
-    moving, across_parcel = phase((moving, across_parcel))
-    own = gradient_of(parcel)
+    across = gradient_tile(across_columns, cotangent_all, across_raw)
+    quarters, behind, across = phase((quarters, behind, across))
+    own = gradient_tile(columns, cotangent_all, accumulated)
     beside = swap(own, 1)
 
     sums = [None] * (steps + 1)
     made, handed = None, None
     for step in range(1, steps):
-        arrived = moving
-        quarters = jnp.split(arrived, 4)
-        first = from_behind(quarters[0], GROUP)
+        arrived, arrived_columns = quarters, behind
+        behind = from_behind(arrived_columns, GROUP)
+        first = from_behind(arrived[0], GROUP)
         if step == 1:
-            across = gradient_of(across_parcel)
             group = [own, beside, across, swap(across, 1)]
             own_products = [block_product(own, panel) for panel in (own, beside)]
         else:
@@ -129,33 +140,32 @@
         first, group, handed, own_products = phase((first, group, handed, own_products))
         if step > 1:
             sums[steps - step + 1] = over_columns(handed)
-        second = from_behind(quarters[1], GROUP)
-        made = products(arrived)
+        second = from_behind(arrived[1], GROUP)
+        made = products(arrived, arrived_columns)
         if step == 1:
             own_products += [block_product(own, panel) for panel in group[2:]]
-        first, second, made, sums, own_products = phase(
-            (first, second, made, sums, own_products)
+        first, second, behind, made, sums, own_products = phase(
+            (first, second, behind, made, sums, own_products)
         )
         if step < steps - 1:
-            rest = [from_behind(piece, GROUP) for piece in quarters[2:]]
-            moving = jnp.concatenate([first, second, *rest])
-
-    half = jnp.concatenate([first, second])
-    third = from_behind(quarters[2], GROUP)
+            rest = [from_behind(piece, GROUP) for piece in arrived[2:]]
+            quarters = [first, second, *rest]
+
+    third = from_behind(arrived[2], GROUP)
     sums[steps] = over_columns(own_products)
     handed = to_owners(made)
-    made = products(half)
+    made = products([first, second], behind[:, : 2 * quarter])
     third, handed, made, sums[steps] = phase((third, handed, made, sums[steps]))
 
-    fourth = from_behind(quarters[3], GROUP)
+    fourth = from_behind(arrived[3], GROUP)
     sums[1] = over_columns(handed)
     handed = to_owners(made)
-    made = products(third)
+    made = products([third], behind[:, 2 * quarter : 3 * quarter])
     fourth, sums[1], handed, made = phase((fourth, sums[1], handed, made))
 
     last = [over_columns(handed)]
     handed = to_owners(made)
-    made = products(fourth)
+    made = products([fourth], behind[:, 3 * quarter :])
     last, handed, made = phase((last, handed, made))
 
     last.append(over_columns(handed))

time: 493 us -> 499 us (1.012)
  waiting for transfers between devices: 275 us -> 302 us
  local copies, waits for them, and re-layouts: 28.6 us -> 16.5 us
  starting transfers between devices: 18.3 us -> 29.1 us
  matrix products: 50.8 us -> 40.9 us
  blocking collectives: 7.16 us -> 0 us
    all_gather x1, waiting for transfers between devices: 54.9 us -> 0.01 us  [body(): cotangent_all = lax.all_gather(cotangent, 'row', axis=0, tiled=True)]
    ppermute x15 -> x16, waiting for transfers between devices: 113 us -> 162 us  [swap(): return lax.ppermute(array, 'row', [(i, i ^ mask) for i in range(count)])]
    ppermute x5 -> x10, waiting for transfers between devices: 30 us -> 60.8 us  [from_behind(): lax.ppermute(array, 'row', [(i, (i + by) % count) for i in range(count)])]
    dot_general x4, matrix products: 35 us -> 26.6 us  [block_product(): lax.dot_general(left, right, (((1,), (1,)), ((), ())), preferred_element_...]
    all_gather x1 -> x0, blocking collectives: 7.16 us -> none  [body(): columns = lax.all_gather(activations, 'col', axis=0, tiled=True)]
    concatenate x1 -> x0, other arithmetic: 6.6 us -> none  [body(): parcel = jnp.concatenate([accumulated, columns.T], axis=1)]
    ppermute x5 -> x10, starting transfers between devices: 3.99 us -> 9.59 us  [from_behind(): lax.ppermute(array, 'row', [(i, (i + by) % count) for i in range(count)])]
    slice x8 -> x3, local copies, waits for them, and re-layouts: 10.5 us -> 6.54 us  [the longest x1 6.52 us: body(): accumulated[q * quarter:(q + 1) * quarter]]
  transfers between devices with their start and end apart: 26 -> 33, of which waited for: 11 -> 11; matrix products, arithmetic and copies ran while one was open for 18% -> 13% of each run, Pallas kernels for 15% -> 15%
where the time goes in v7:
time: 499 us
  waiting for transfers between devices  302 us (61%)
  Pallas kernels  73.3 us (15%)
  matrix products  40.9 us (8%)
  starting transfers between devices  29.1 us (6%)
  other arithmetic  22.5 us (5%)
  local copies, waits for them, and re-layouts  16.5 us (3%)
  between operations  14.4 us (3%)
    ppermute x16, waiting for transfers between devices, swap(): return lax.ppermute(array, 'row', [(i, i ^ mask) for i in range(count)])  162 us
    ppermute x6, waiting for transfers between devices, trade(): return lax.ppermute(array, 'col', [(0, 1), (1, 0)])  79.1 us
    pallas_call x4, Pallas kernels, panel_products(): pl.pallas_call(products_kernel, grid=(width // depth,), in_specs=[pl.Bloc...  73.3 us
    ppermute x10, waiting for transfers between devices, from_behind(): lax.ppermute(array, 'row', [(i, (i + by) % count) for i in range(count)])  60.8 us
    dot_general x4, matrix products, block_product(): lax.dot_general(left, right, (((1,), (1,)), ((), ())), preferred_element_...  26.6 us
    dot_general x2, matrix products, gradient_tile(): lax.dot_general(columns, cotangent_all, (((0,), (0,)), ((), ())), preferr...  14.3 us
    ppermute x16, starting transfers between devices, swap(): return lax.ppermute(array, 'row', [(i, i ^ mask) for i in range(count)])  11.2 us
    add x5, other arithmetic, over_columns(): return sums + trade(sums.astype(jnp.bfloat16)).astype(jnp.float32)  10.4 us
  transfers between devices with their start and end apart: 33, of which 11 were waited for; matrix products, arithmetic and copies ran while one was open for 13% of the time, Pallas kernels for 15%

profile of v7, /device:TPU:0, one launch (start us, length us, event | category | flops | bytes accessed | tf_op | source)
XLA Modules:
  0.0 499.0 jit_solution(18331712789850469491)
XLA Ops:
  7.2 0.7 all-gather.2.cloned.1.call-update
  7.9 3.0 collective-permute-start.7
  10.9 1.5 collective-permute-start.4
  12.4 3.7 collective-permute-done.4
  16.1 1.0 maximum_select_fusion
  17.1 1.6 collective-permute-start.5
  18.8 0.5 collective-permute-start.6
  19.3 6.5 %fusion.6 = (bf16[128,7168]{1,0:T(8,128)(2,1)}, bf16[128,7168]{1,0:T(8,128)(2,1)}, bf16[128,7168]{1,0:T(8,128)(2,1)}, bf16[128,7168]{1,0:T(8,128)(2,1)}) fusion(bf16[512,7168]{1,0:T(8,128)(2,1)} %param.7), kind=kLoop, calls=%fused_computation.43 | loop fusion | bytes 14680064 | tf_op jit(solution)/shard_map/slice | solution.py:96
  25.8 1.6 collective-permute-start
  27.4 1.6 collective-permute-start.1
  29.0 158.0 %collective-permute-done.6 = bf16[256,512]{1,0:T(8,128)(2,1)S(1)} collective-permute-done((bf16[256,512]{1,0:T(8,128)(2,1)S(1)}, bf16[256,512]{1,0:T(8,128)(2,1)S(1)}, u32[]{:S(2)}, u32[]{:S(2)}) %collective-permute-start.6) | collective-permute-done | bytes 262176 | tf_op jit(solution)/shard_map/ppermute | solution.py:14
  187.0 1.8 collective-permute-start.3
  188.8 6.4 %add_convert_fusion.refs_0_ = bf16[512,7168]{1,0:T(8,128)(2,1)S(1)} fusion(bf16[512,7168]{1,0:T(8,128)(2,1)} %param.7, bf16[256,512]{1,0:T(8,128)(2,1)S(1)} %maximum_select_fusion, bf16[256,7168]{1,0:T(8,128)(2,1)} %all-gather.2.cloned.1.call-done.refs_9_.refs_7_.refs_6_), kind=kOutput, calls=%fused_computation | convolution fusion | flops 1890058240 | bytes 18612224 | tf_op jit(solution)/shard_map/dot_general | solution.py:27
  195.4 7.8 %add_convert_fusion.1.refs_2_ = bf16[512,7168]{1,0:T(8,128)(2,1)S(1)} fusion(bf16[512,7168]{1,0:T(8,128)(2,1)} %collective-permute-done.7, bf16[256,512]{1,0:T(8,128)(2,1)S(1)} %collective-permute-done.6, bf16[256,7168]{1,0:T(8,128)(2,1)S(1)} %copy-done.3), kind=kOutput, calls=%fused_computation.1 | convolution fusion | flops 1890058240 | bytes 18612224 | tf_op jit(solution)/shard_map/dot_general | solution.py:27
  203.3 27.1 %collective-permute-done.3.refs_7_ = bf16[128,7168]{1,0:T(8,128)(2,1)} collective-permute-done((bf16[128,7168]{1,0:T(8,128)(2,1)}, bf16[128,7168]{1,0:T(8,128)(2,1)}, u32[]{:S(2)}, u32[]{:S(2)}) %collective-permute-start.3) | collective-permute-done | bytes 1835040 | tf_op jit(solution)/shard_map/ppermute | solution.py:19
  230.3 4.0 fusion.8
  234.3 1.3 collective-permute-start.13
  235.6 1.6 collective-permute-start.14
  237.2 7.2 %fusion.9 = f32[512,512]{1,0:T(8,128)} fusion(bf16[512,7168]{1,0:T(8,128)(2,1)S(1)} %add_convert_fusion.refs_0_, bf16[512,7168]{1,0:T(8,128)(2,1)} %collective-permute-done.11.refs_1_), kind=kOutput, calls=%fused_computation.46 | convolution fusion | flops 3758096384 | bytes 15728640 | tf_op jit(solution)/shard_map/dot_general | solution.py:34
  244.5 30.7 %collective-permute-done.10.refs_4_ = bf16[128,7168]{1,0:T(8,128)(2,1)S(1)} collective-permute-done((bf16[128,7168]{1,0:T(8,128)(2,1)}, bf16[128,7168]{1,0:T(8,128)(2,1)S(1)}, u32[]{:S(2)}, u32[]{:S(2)}) %collective-permute-start.10) | collective-permute-done | bytes 1835040 | tf_op jit(solution)/shard_map/ppermute | solution.py:19
  275.1 26.0 %shard_map.68 = f32[4,512,512]{2,1,0:T(8,128)} custom-call(bf16[512,7168]{1,0:T(8,128)(2,1)} %copy-done, bf16[512,7168]{1,0:T(8,128)(2,1)} %collective-permute-done.11.refs_1_, bf16[512,7168]{1,0:T(8,128)(2,1)} %copy-done.2, bf16[512,7168]{1,0:T(8,128)(2,1)} %collective-permute-done.12.refs_3_, bf16[128,7168]{1,0:T(8,128)(2,1)} %collective-permute-done.refs_4_, ...), custom_call_target="tpu_custom_call" | custom-call | flops 16911433728 | bytes 44564480 | tf_op jit(solution)/shard_map/pallas_call | solution.py:61
  301.2 8.7 %fusion.10 = f32[512,512]{1,0:T(8,128)S(1)} fusion(bf16[512,7168]{1,0:T(8,128)(2,1)} %copy-done, bf16[512,7168]{1,0:T(8,128)(2,1)} %copy-done.2), kind=kOutput, calls=%fused_computation.47 | convolution fusion | flops 3758096384 | bytes 15728640 | tf_op jit(solution)/shard_map/dot_general | solution.py:34
  309.9 6.8 %fusion.11 = f32[512,512]{1,0:T(8,128)S(1)} fusion(bf16[512,7168]{1,0:T(8,128)(2,1)S(1)} %copy-done.1, bf16[512,7168]{1,0:T(8,128)(2,1)} %collective-permute-done.12.refs_3_), kind=kOutput, calls=%fused_computation.48 | convolution fusion | flops 3758096384 | bytes 15728640 | tf_op jit(solution)/shard_map/dot_general | solution.py:34
  316.7 3.0 collective-permute-done.14
  319.7 1.8 fusion.2
  321.5 1.5 collective-permute-start.18
  323.0 1.7 slice_bitcast_fusion
  324.7 1.5 collective-permute-start.16
  326.2 0.4 collective-permute-start.17
  326.6 16.2 %shard_map.69 = f32[4,512,256]{2,1,0:T(8,128)S(1)} custom-call(bf16[512,7168]{1,0:T(8,128)(2,1)} %copy-done, bf16[512,7168]{1,0:T(8,128)(2,1)} %collective-permute-done.11.refs_1_, bf16[512,7168]{1,0:T(8,128)(2,1)} %copy-done.2, bf16[512,7168]{1,0:T(8,128)(2,1)} %collective-permute-done.12.refs_3_, bf16[128,7168]{1,0:T(8,128)(2,1)S(1)} %collective-permute-done.10.refs_4_, ...), custom_call_target="tpu_custom_call" | custom-call | flops 8455716864 | bytes 38797312 | tf_op jit(solution)/shard_map/pallas_call | solution.py:61
  342.8 26.3 %collective-permute-done.18 = bf16[4,512,512]{2,1,0:T(8,128)(2,1)} collective-permute-done((bf16[4,512,512]{2,1,0:T(8,128)(2,1)}, bf16[4,512,512]{2,1,0:T(8,128)(2,1)}, u32[]{:S(2)}, u32[]{:S(2)}) %collective-permute-start.18) | collective-permute-done | bytes 2097184 | tf_op jit(solution)/shard_map/ppermute | solution.py:23
  369.1 5.0 convert_add_fusion.1
  374.1 0.4 fusion.1
  374.5 1.6 collective-permute-start.19
  376.1 1.2 slice_bitcast_fusion.4
  377.3 1.5 collective-permute-start.21
  378.8 0.4 collective-permute-start.22
  379.1 15.6 %shard_map.70 = f32[4,512,128]{2,1,0:T(8,128)S(1)} custom-call(bf16[512,7168]{1,0:T(8,128)(2,1)} %copy-done, bf16[512,7168]{1,0:T(8,128)(2,1)} %collective-permute-done.11.refs_1_, bf16[512,7168]{1,0:T(8,128)(2,1)} %copy-done.2, bf16[512,7168]{1,0:T(8,128)(2,1)} %collective-permute-done.12.refs_3_, bf16[128,7168]{1,0:T(8,128)(2,1)S(1)} %collective-permute-done.9.refs_4_, ...), custom_call_target="tpu_custom_call" | custom-call | flops 4227858432 | bytes 35913728 | tf_op jit(solution)/shard_map/pallas_call | solution.py:61
  394.7 26.2 %collective-permute-done.19 = bf16[4,512,512]{2,1,0:T(8,128)(2,1)S(1)} collective-permute-done((bf16[4,512,512]{2,1,0:T(8,128)(2,1)S(1)}, bf16[4,512,512]{2,1,0:T(8,128)(2,1)S(1)}, u32[]{:S(2)}, u32[]{:S(2)}) %collective-permute-start.19) | collective-permute-done | bytes 2097184 | tf_op jit(solution)/shard_map/ppermute | solution.py:23
  420.9 2.7 convert_add_fusion
  423.7 0.3 fusion.3
  423.9 1.6 collective-permute-start.23
  425.6 1.6 collective-permute-start.25
  427.2 0.3 collective-permute-start.26
  427.5 15.6 %shard_map.71 = f32[4,512,128]{2,1,0:T(8,128)S(1)} custom-call(bf16[512,7168]{1,0:T(8,128)(2,1)} %copy-done, bf16[512,7168]{1,0:T(8,128)(2,1)} %collective-permute-done.11.refs_1_, bf16[512,7168]{1,0:T(8,128)(2,1)} %copy-done.2, bf16[512,7168]{1,0:T(8,128)(2,1)} %collective-permute-done.12.refs_3_, bf16[128,7168]{1,0:T(8,128)(2,1)S(1)} %collective-permute-done.8.refs_4_, ...), custom_call_target="tpu_custom_call" | custom-call | flops 4227858432 | bytes 35913728 | tf_op jit(solution)/shard_map/pallas_call | solution.py:61
  443.1 3.9 collective-permute-done.23
  447.0 0.2 convert_add_fusion.2
  447.2 0.1 fusion.5
  447.3 1.6 collective-permute-start.27
  449.1 1.6 collective-permute-start.29
  450.6 0.3 collective-permute-start.30
  450.9 7.3 %collective-permute-done.27 = bf16[4,512,128]{2,1,0:T(8,128)(2,1)S(1)} collective-permute-done((bf16[4,512,128]{2,1,0:T(8,128)(2,1)S(1)}, bf16[4,512,128]{2,1,0:T(8,128)(2,1)S(1)}, u32[]{:S(2)}, u32[]{:S(2)}) %collective-permute-start.27) | collective-permute-done | bytes 524320 | tf_op jit(solution)/shard_map/ppermute | solution.py:23
  458.2 1.1 convert_add_fusion.4
  459.4 3.6 collective-permute-done.30
  463.0 0.9 fusion.4
  463.9 0.5 collective-permute-start.31
  464.4 2.1 bitcast_add_fusion
  466.5 11.8 %collective-permute-done.31 = bf16[4,512,128]{2,1,0:T(8,128)(2,1)} collective-permute-done((bf16[4,512,128]{2,1,0:T(8,128)(2,1)}, bf16[4,512,128]{2,1,0:T(8,128)(2,1)}, u32[]{:S(2)}, u32[]{:S(2)}) %collective-permute-start.31) | collective-permute-done | bytes 524320 | tf_op jit(solution)/shard_map/ppermute | solution.py:23
  478.3 1.4 convert_add_fusion.3
  479.7 4.0 pad_maximum_fusion
  483.6 0.5 dynamic-slice_bitcast_fusion.3
  484.1 1.7 copy-done.5
  485.8 1.6 fusion
  487.4 4.7 copy.8
  (68 shorter events, 0.6 us)
Async XLA Ops:
  7.2 181.7 %all-gather.2.cloned.1.call-start = ((), (), s32[]{:S(2)}) async-start(), calls=%async_computation | async-start | bytes 3899392 | tf_op jit(solution)/shard_map/all_gather | solution.py:110
  7.9 187.4 %collective-permute-start.7 = (bf16[512,7168]{1,0:T(8,128)(2,1)}, bf16[512,7168]{1,0:T(8,128)(2,1)}, u32[]{:S(2)}, u32[]{:S(2)}) collective-permute-start(bf16[512,7168]{1,0:T(8,128)(2,1)} %param.7), channel_id=1, source_target_pairs={{0,4},{2,6},{4,0},{6,2},{8,12},{10,14},{12,8},{14,10},{16,20},{18,... | collective-permute-start | bytes 22020104 | tf_op jit(solution)/shard_map/ppermute | solution.py:14
  10.9 5.2 %collective-permute-start.4 = (bf16[128,512]{1,0:T(8,128)(2,1)}, bf16[128,512]{1,0:T(8,128)(2,1)S(1)}, u32[]{:S(2)}, u32[]{:S(2)}) collective-permute-start(bf16[128,512]{1,0:T(8,128)(2,1)} %param.5), channel_id=1, source_target_pairs={{0,1},{1,0},{2,3},{3,2},{4,5},{5,4},{6,7},{7,6},{8,9},{9,8},{10,11... | collective-permute-start | bytes 393224 | tf_op jit(solution)/shard_map/ppermute | solution.py:23
  17.1 11.9 %collective-permute-start.5 = (bf16[256,512]{1,0:T(8,128)(2,1)S(1)}, bf16[256,512]{1,0:T(8,128)(2,1)S(1)}, u32[]{:S(2)}, u32[]{:S(2)}) collective-permute-start(bf16[256,512]{1,0:T(8,128)(2,1)S(1)} %maximum_select_fusion), channel_id=1, source_target_pairs={{0,8},{2,10},{4,12},{6,14},{8,16},{10,18},{12,20},{14,22},{16,24},... | collective-permute-start | bytes 786440 | tf_op jit(solution)/shard_map/ppermute | solution.py:19
  18.8 168.2 %collective-permute-start.6 = (bf16[256,512]{1,0:T(8,128)(2,1)S(1)}, bf16[256,512]{1,0:T(8,128)(2,1)S(1)}, u32[]{:S(2)}, u32[]{:S(2)}) collective-permute-start(bf16[256,512]{1,0:T(8,128)(2,1)S(1)} %maximum_select_fusion), channel_id=1, source_target_pairs={{0,4},{2,6},{4,0},{6,2},{8,12},{10,14},{12,8},{14,10},{16,20},{18,... | collective-permute-start | bytes 786440 | tf_op jit(solution)/shard_map/ppermute | solution.py:14
  25.8 177.4 %collective-permute-start = (bf16[128,7168]{1,0:T(8,128)(2,1)}, bf16[128,7168]{1,0:T(8,128)(2,1)}, u32[]{:S(2)}, u32[]{:S(2)}) collective-permute-start(bf16[128,7168]{1,0:T(8,128)(2,1)} %get-tuple-element.105), channel_id=1, source_target_pairs={{0,8},{2,10},{4,12},{6,14},{8,16},{10,18},{12,20},{14,22},{16,24},... | collective-permute-start | bytes 5505032 | tf_op jit(solution)/shard_map/ppermute | solution.py:19
  27.4 175.8 %collective-permute-start.1 = (bf16[128,7168]{1,0:T(8,128)(2,1)}, bf16[128,7168]{1,0:T(8,128)(2,1)}, u32[]{:S(2)}, u32[]{:S(2)}) collective-permute-start(bf16[128,7168]{1,0:T(8,128)(2,1)} %get-tuple-element.104), channel_id=1, source_target_pairs={{0,8},{2,10},{4,12},{6,14},{8,16},{10,18},{12,20},{14,22},{16,24},... | collective-permute-start | bytes 5505032 | tf_op jit(solution)/shard_map/ppermute | solution.py:19
  29.0 174.3 %collective-permute-start.2 = (bf16[128,7168]{1,0:T(8,128)(2,1)}, bf16[128,7168]{1,0:T(8,128)(2,1)S(1)}, u32[]{:S(2)}, u32[]{:S(2)}) collective-permute-start(bf16[128,7168]{1,0:T(8,128)(2,1)} %get-tuple-element.103), channel_id=1, source_target_pairs={{0,8},{2,10},{4,12},{6,14},{8,16},{10,18},{12,20},{14,22},{16,24},... | collective-permute-start | bytes 5505032 | tf_op jit(solution)/shard_map/ppermute | solution.py:19
  187.0 43.3 %collective-permute-start.3 = (bf16[128,7168]{1,0:T(8,128)(2,1)}, bf16[128,7168]{1,0:T(8,128)(2,1)}, u32[]{:S(2)}, u32[]{:S(2)}) collective-permute-start(bf16[128,7168]{1,0:T(8,128)(2,1)} %get-tuple-element.102), channel_id=1, source_target_pairs={{0,8},{2,10},{4,12},{6,14},{8,16},{10,18},{12,20},{14,22},{16,24},... | collective-permute-start | bytes 5505032 | tf_op jit(solution)/shard_map/ppermute | solution.py:19
  188.8 6.5 %copy-start.3 = (bf16[256,7168]{1,0:T(8,128)(2,1)S(1)}, bf16[256,7168]{1,0:T(8,128)(2,1)}, u32[]{:S(2)}) copy-start(bf16[256,7168]{1,0:T(8,128)(2,1)} %all-gather.2.cloned.1.call-done.refs_9_.refs_7_.refs_6_) | copy-start | bytes 11010052
  195.3 42.0 %copy-start = (bf16[512,7168]{1,0:T(8,128)(2,1)}, bf16[512,7168]{1,0:T(8,128)(2,1)S(1)}, u32[]{:S(2)}) copy-start(bf16[512,7168]{1,0:T(8,128)(2,1)S(1)} %add_convert_fusion.refs_0_) | copy-start | bytes 22020100
  195.3 41.9 %collective-permute-start.11 = (bf16[512,7168]{1,0:T(8,128)(2,1)S(1)}, bf16[512,7168]{1,0:T(8,128)(2,1)}, u32[]{:S(2)}, u32[]{:S(2)}) collective-permute-start(bf16[512,7168]{1,0:T(8,128)(2,1)S(1)} %add_convert_fusion.refs_0_), channel_id=1, source_target_pairs={{0,2},{2,0},{4,6},{6,4},{8,10},{10,8},{12,14},{14,12},{16,18},{18,... | collective-permute-start | bytes 22020104 | tf_op jit(solution)/shard_map/ppermute | solution.py:14
  203.2 31.1 %copy-start.2 = (bf16[512,7168]{1,0:T(8,128)(2,1)}, bf16[512,7168]{1,0:T(8,128)(2,1)S(1)}, u32[]{:S(2)}) copy-start(bf16[512,7168]{1,0:T(8,128)(2,1)S(1)} %add_convert_fusion.1.refs_2_) | copy-start | bytes 22020100
  230.3 44.8 %collective-permute-start.12 = (bf16[512,7168]{1,0:T(8,128)(2,1)S(1)}, bf16[512,7168]{1,0:T(8,128)(2,1)}, u32[]{:S(2)}, u32[]{:S(2)}) collective-permute-start(bf16[512,7168]{1,0:T(8,128)(2,1)S(1)} %add_convert_fusion.1.refs_2_), channel_id=1, source_target_pairs={{0,2},{2,0},{4,6},{6,4},{8,10},{10,8},{12,14},{14,12},{16,18},{18,... | collective-permute-start | bytes 22020104 | tf_op jit(solution)/shard_map/ppermute | solution.py:14
  230.3 44.8 %collective-permute-start.10 = (bf16[128,7168]{1,0:T(8,128)(2,1)}, bf16[128,7168]{1,0:T(8,128)(2,1)S(1)}, u32[]{:S(2)}, u32[]{:S(2)}) collective-permute-start(bf16[128,7168]{1,0:T(8,128)(2,1)} %collective-permute-done.refs_4_), channel_id=1, source_target_pairs={{0,8},{2,10},{4,12},{6,14},{8,16},{10,18},{12,20},{14,22},{16,24},... | collective-permute-start | bytes 5505032 | tf_op jit(solution)/shard_map/ppermute | solution.py:19
  234.3 85.4 %collective-permute-start.13 = (bf16[128,7168]{1,0:T(8,128)(2,1)}, bf16[128,7168]{1,0:T(8,128)(2,1)S(1)}, u32[]{:S(2)}, u32[]{:S(2)}) collective-permute-start(bf16[128,7168]{1,0:T(8,128)(2,1)} %collective-permute-done.1.refs_5_), channel_id=1, source_target_pairs={{0,8},{2,10},{4,12},{6,14},{8,16},{10,18},{12,20},{14,22},{16,24},... | collective-permute-start | bytes 5505032 | tf_op jit(solution)/shard_map/ppermute | solution.py:19
  235.6 84.0 %collective-permute-start.14 = (bf16[256,512]{1,0:T(8,128)(2,1)S(1)}, bf16[256,512]{1,0:T(8,128)(2,1)S(1)}, u32[]{:S(2)}, u32[]{:S(2)}) collective-permute-start(bf16[256,512]{1,0:T(8,128)(2,1)S(1)} %collective-permute-done.5.refs_8_), channel_id=1, source_target_pairs={{0,8},{2,10},{4,12},{6,14},{8,16},{10,18},{12,20},{14,22},{16,24},... | collective-permute-start | bytes 786440 | tf_op jit(solution)/shard_map/ppermute | solution.py:19
  301.2 8.7 %copy-start.1 = (bf16[512,7168]{1,0:T(8,128)(2,1)S(1)}, bf16[512,7168]{1,0:T(8,128)(2,1)}, u32[]{:S(2)}) copy-start(bf16[512,7168]{1,0:T(8,128)(2,1)} %copy-done) | copy-start | bytes 22020100
  309.8 9.9 %copy-start.10 = (f32[512,512]{1,0:T(8,128)}, f32[512,512]{1,0:T(8,128)S(1)}, u32[]{:S(2)}) copy-start(f32[512,512]{1,0:T(8,128)S(1)} %fusion.10) | copy-start | bytes 3145732
  309.9 9.8 %copy-start.8 = (f32[512,512]{1,0:T(8,128)S(1)}, f32[512,512]{1,0:T(8,128)}, u32[]{:S(2)}) copy-start(f32[512,512]{1,0:T(8,128)} %fusion.9) | copy-start | bytes 3145732
  316.6 8.1 %copy-start.11 = (f32[512,512]{1,0:T(8,128)}, f32[512,512]{1,0:T(8,128)S(1)}, u32[]{:S(2)}) copy-start(f32[512,512]{1,0:T(8,128)S(1)} %fusion.11) | copy-start | bytes 3145732
  316.6 6.3 %copy-start.7 = (f32[4,512,512]{2,1,0:T(8,128)S(1)}, f32[4,512,512]{2,1,0:T(8,128)}, u32[]{:S(2)}) copy-start(f32[4,512,512]{2,1,0:T(8,128)} %shard_map.68) | copy-start | bytes 12582916
  321.5 47.6 %collective-permute-start.18 = (bf16[4,512,512]{2,1,0:T(8,128)(2,1)}, bf16[4,512,512]{2,1,0:T(8,128)(2,1)}, u32[]{:S(2)}, u32[]{:S(2)}) collective-permute-start(bf16[4,512,512]{2,1,0:T(8,128)(2,1)} %fusion.2), channel_id=1, source_target_pairs={{0,1},{1,0},{2,3},{3,2},{4,5},{5,4},{6,7},{7,6},{8,9},{9,8},{10,11... | collective-permute-start | bytes 6291464 | tf_op jit(solution)/shard_map/ppermute | solution.py:23
  323.0 51.1 %collective-permute-start.9 = (bf16[128,7168]{1,0:T(8,128)(2,1)S(1)}, bf16[128,7168]{1,0:T(8,128)(2,1)S(1)}, u32[]{:S(2)}, u32[]{:S(2)}) collective-permute-start(bf16[128,7168]{1,0:T(8,128)(2,1)S(1)} %collective-permute-done.2.refs_6_), channel_id=1, source_target_pairs={{0,8},{2,10},{4,12},{6,14},{8,16},{10,18},{12,20},{14,22},{16,24},... | collective-permute-start | bytes 5505032 | tf_op jit(solution)/shard_map/ppermute | solution.py:19
  324.7 49.3 %collective-permute-start.15 = (f32[512,512]{1,0:T(8,128)}, f32[512,512]{1,0:T(8,128)S(1)}, u32[]{:S(2)}, u32[]{:S(2)}) collective-permute-start(f32[512,512]{1,0:T(8,128)} %get-tuple-element.108), channel_id=1, source_target_pairs={{0,2},{2,0},{4,6},{6,4},{8,10},{10,8},{12,14},{14,12},{16,18},{18,... | collective-permute-start | bytes 3145736 | tf_op jit(solution)/shard_map/ppermute | solution.py:14
  324.7 49.3 %collective-permute-start.16 = (f32[512,512]{1,0:T(8,128)}, f32[512,512]{1,0:T(8,128)S(1)}, u32[]{:S(2)}, u32[]{:S(2)}) collective-permute-start(f32[512,512]{1,0:T(8,128)} %get-tuple-element.107), channel_id=1, source_target_pairs={{0,4},{2,6},{4,0},{6,2},{8,12},{10,14},{12,8},{14,10},{16,20},{18,... | collective-permute-start | bytes 3145736 | tf_op jit(solution)/shard_map/ppermute | solution.py:14
  326.2 47.9 %collective-permute-start.17 = (f32[512,512]{1,0:T(8,128)}, f32[512,512]{1,0:T(8,128)S(1)}, u32[]{:S(2)}, u32[]{:S(2)}) collective-permute-start(f32[512,512]{1,0:T(8,128)} %get-tuple-element.106), channel_id=1, source_target_pairs={{0,6},{2,4},{4,2},{6,0},{8,14},{10,12},{12,10},{14,8},{16,22},{18,... | collective-permute-start | bytes 3145736 | tf_op jit(solution)/shard_map/ppermute | solution.py:14
  326.6 42.5 %copy-start.9 = (f32[512,512]{1,0:T(8,128)S(1)}, f32[512,512]{1,0:T(8,128)}, u32[]{:S(2)}) copy-start(f32[512,512]{1,0:T(8,128)} %fusion.9) | copy-start | bytes 3145732
  374.5 46.4 %collective-permute-start.19 = (bf16[4,512,512]{2,1,0:T(8,128)(2,1)S(1)}, bf16[4,512,512]{2,1,0:T(8,128)(2,1)S(1)}, u32[]{:S(2)}, u32[]{:S(2)}) collective-permute-start(bf16[4,512,512]{2,1,0:T(8,128)(2,1)S(1)} %fusion.1), channel_id=1, source_target_pairs={{0,1},{1,0},{2,3},{3,2},{4,5},{5,4},{6,7},{7,6},{8,9},{9,8},{10,11... | collective-permute-start | bytes 6291464 | tf_op jit(solution)/shard_map/ppermute | solution.py:23
  376.1 47.6 %collective-permute-start.8 = (bf16[128,7168]{1,0:T(8,128)(2,1)}, bf16[128,7168]{1,0:T(8,128)(2,1)S(1)}, u32[]{:S(2)}, u32[]{:S(2)}) collective-permute-start(bf16[128,7168]{1,0:T(8,128)(2,1)} %collective-permute-done.3.refs_7_), channel_id=1, source_target_pairs={{0,8},{2,10},{4,12},{6,14},{8,16},{10,18},{12,20},{14,22},{16,24},... | collective-permute-start | bytes 5505032 | tf_op jit(solution)/shard_map/ppermute | solution.py:19
  377.3 46.4 %collective-permute-start.20 = (f32[512,256]{1,0:T(8,128)}, f32[512,256]{1,0:T(8,128)S(1)}, u32[]{:S(2)}, u32[]{:S(2)}) collective-permute-start(f32[512,256]{1,0:T(8,128)} %get-tuple-element.112), channel_id=1, source_target_pairs={{0,2},{2,0},{4,6},{6,4},{8,10},{10,8},{12,14},{14,12},{16,18},{18,... | collective-permute-start | bytes 1572872 | tf_op jit(solution)/shard_map/ppermute | solution.py:14
  377.3 46.4 %collective-permute-start.21 = (f32[512,256]{1,0:T(8,128)}, f32[512,256]{1,0:T(8,128)S(1)}, u32[]{:S(2)}, u32[]{:S(2)}) collective-permute-start(f32[512,256]{1,0:T(8,128)} %get-tuple-element.111), channel_id=1, source_target_pairs={{0,4},{2,6},{4,0},{6,2},{8,12},{10,14},{12,8},{14,10},{16,20},{18,... | collective-permute-start | bytes 1572872 | tf_op jit(solution)/shard_map/ppermute | solution.py:14
  378.8 44.9 %collective-permute-start.22 = (f32[512,256]{1,0:T(8,128)S(1)}, f32[512,256]{1,0:T(8,128)S(1)}, u32[]{:S(2)}, u32[]{:S(2)}) collective-permute-start(f32[512,256]{1,0:T(8,128)S(1)} %get-tuple-element.110), channel_id=1, source_target_pairs={{0,6},{2,4},{4,2},{6,0},{8,14},{10,12},{12,10},{14,8},{16,22},{18,... | collective-permute-start | bytes 1572872 | tf_op jit(solution)/shard_map/ppermute | solution.py:14
  423.9 23.0 %collective-permute-start.23 = (bf16[4,512,256]{2,1,0:T(8,128)(2,1)S(1)}, bf16[4,512,256]{2,1,0:T(8,128)(2,1)S(1)}, u32[]{:S(2)}, u32[]{:S(2)}) collective-permute-start(bf16[4,512,256]{2,1,0:T(8,128)(2,1)S(1)} %fusion.3), channel_id=1, source_target_pairs={{0,1},{1,0},{2,3},{3,2},{4,5},{5,4},{6,7},{7,6},{8,9},{9,8},{10,11... | collective-permute-start | bytes 3145736 | tf_op jit(solution)/shard_map/ppermute | solution.py:23
  425.6 21.7 %collective-permute-start.24 = (f32[512,128]{1,0:T(8,128)S(1)}, f32[512,128]{1,0:T(8,128)S(1)}, u32[]{:S(2)}, u32[]{:S(2)}) collective-permute-start(f32[512,128]{1,0:T(8,128)S(1)} %get-tuple-element.120), channel_id=1, source_target_pairs={{0,2},{2,0},{4,6},{6,4},{8,10},{10,8},{12,14},{14,12},{16,18},{18,... | collective-permute-start | bytes 786440 | tf_op jit(solution)/shard_map/ppermute | solution.py:14
  425.6 21.6 %collective-permute-start.25 = (f32[512,128]{1,0:T(8,128)S(1)}, f32[512,128]{1,0:T(8,128)S(1)}, u32[]{:S(2)}, u32[]{:S(2)}) collective-permute-start(f32[512,128]{1,0:T(8,128)S(1)} %get-tuple-element.119), channel_id=1, source_target_pairs={{0,4},{2,6},{4,0},{6,2},{8,12},{10,14},{12,8},{14,10},{16,20},{18,... | collective-permute-start | bytes 786440 | tf_op jit(solution)/shard_map/ppermute | solution.py:14
  427.2 20.0 %collective-permute-start.26 = (f32[512,128]{1,0:T(8,128)S(1)}, f32[512,128]{1,0:T(8,128)S(1)}, u32[]{:S(2)}, u32[]{:S(2)}) collective-permute-start(f32[512,128]{1,0:T(8,128)S(1)} %get-tuple-element.118), channel_id=1, source_target_pairs={{0,6},{2,4},{4,2},{6,0},{8,14},{10,12},{12,10},{14,8},{16,22},{18,... | collective-permute-start | bytes 786440 | tf_op jit(solution)/shard_map/ppermute | solution.py:14
  447.3 17.0 %slice-start = ((f32[4,512,512]{2,1,0:T(8,128)}), f32[1,512,512]{2,1,0:T(8,128)S(1)}, s32[]{:S(2)}) async-start(f32[4,512,512]{2,1,0:T(8,128)} %convert_add_fusion.1), calls=%async_computation.1 | async-start | bytes 2097152 | tf_op jit(solution)/shard_map/slice | solution.py:187
  447.3 10.9 %collective-permute-start.27 = (bf16[4,512,128]{2,1,0:T(8,128)(2,1)S(1)}, bf16[4,512,128]{2,1,0:T(8,128)(2,1)S(1)}, u32[]{:S(2)}, u32[]{:S(2)}) collective-permute-start(bf16[4,512,128]{2,1,0:T(8,128)(2,1)S(1)} %fusion.5), channel_id=1, source_target_pairs={{0,1},{1,0},{2,3},{3,2},{4,5},{5,4},{6,7},{7,6},{8,9},{9,8},{10,11... | collective-permute-start | bytes 1572872 | tf_op jit(solution)/shard_map/ppermute | solution.py:23
  449.0 10.4 %collective-permute-start.28 = (f32[512,128]{1,0:T(8,128)S(1)}, f32[512,128]{1,0:T(8,128)S(1)}, u32[]{:S(2)}, u32[]{:S(2)}) collective-permute-start(f32[512,128]{1,0:T(8,128)S(1)} %get-tuple-element.116), channel_id=1, source_target_pairs={{0,2},{2,0},{4,6},{6,4},{8,10},{10,8},{12,14},{14,12},{16,18},{18,... | collective-permute-start | bytes 786440 | tf_op jit(solution)/shard_map/ppermute | solution.py:14
  449.1 10.3 %collective-permute-start.29 = (f32[512,128]{1,0:T(8,128)S(1)}, f32[512,128]{1,0:T(8,128)S(1)}, u32[]{:S(2)}, u32[]{:S(2)}) collective-permute-start(f32[512,128]{1,0:T(8,128)S(1)} %get-tuple-element.115), channel_id=1, source_target_pairs={{0,4},{2,6},{4,0},{6,2},{8,12},{10,14},{12,8},{14,10},{16,20},{18,... | collective-permute-start | bytes 786440 | tf_op jit(solution)/shard_map/ppermute | solution.py:14
  450.6 12.3 %collective-permute-start.30 = (f32[512,128]{1,0:T(8,128)S(1)}, f32[512,128]{1,0:T(8,128)S(1)}, u32[]{:S(2)}, u32[]{:S(2)}) collective-permute-start(f32[512,128]{1,0:T(8,128)S(1)} %get-tuple-element.114), channel_id=1, source_target_pairs={{0,6},{2,4},{4,2},{6,0},{8,14},{10,12},{12,10},{14,8},{16,22},{18,... | collective-permute-start | bytes 786440 | tf_op jit(solution)/shard_map/ppermute | solution.py:14
  459.4 3.6 copy-start.12
  459.4 4.5 copy-start.13
  463.0 0.9 copy-start.14
  463.9 14.4 %collective-permute-start.31 = (bf16[4,512,128]{2,1,0:T(8,128)(2,1)}, bf16[4,512,128]{2,1,0:T(8,128)(2,1)}, u32[]{:S(2)}, u32[]{:S(2)}) collective-permute-start(bf16[4,512,128]{2,1,0:T(8,128)(2,1)} %fusion.4), channel_id=1, source_target_pairs={{0,1},{1,0},{2,3},{3,2},{4,5},{5,4},{6,7},{7,6},{8,9},{9,8},{10,11... | collective-permute-start | bytes 1572872 | tf_op jit(solution)/shard_map/ppermute | solution.py:23
  464.4 15.3 %copy-start.4 = (f32[4,512,512]{2,1,0:T(8,128)S(1)}, f32[4,512,512]{2,1,0:T(8,128)}, u32[]{:S(2)}) copy-start(f32[4,512,512]{2,1,0:T(8,128)} %convert_add_fusion.1) | copy-start | bytes 12582916
  464.4 15.3 %copy-start.6 = (f32[4,512,128]{2,1,0:T(8,128)S(1)}, f32[4,512,128]{2,1,0:T(8,128)}, u32[]{:S(2)}) copy-start(f32[4,512,128]{2,1,0:T(8,128)} %convert_add_fusion.4) | copy-start | bytes 3145732
  483.6 2.2 copy-start.5
Sparse Core Ops, SparseCore 0:
  10.3 175.9 all-gather.1

commit v8 on v7

--- a/solution.py
+++ b/solution.py
@@ -92,10 +92,7 @@
     phase = lax.optimization_barrier
 
     quarter = block // 4
-    quarters = [
-        from_behind(accumulated[q * quarter : (q + 1) * quarter], GROUP) for q in range(4)
-    ]
-    across_raw = swap(accumulated, 2)
+    moving = from_behind(accumulated, GROUP)
     if n_col == 2:
         other = trade(activations)
         columns = jnp.where(
@@ -105,8 +102,9 @@
         )
     else:
         columns = lax.all_gather(activations, "col", axis=0, tiled=True)
-    across_columns = swap(columns, 2)
     behind = from_behind(columns, GROUP)
+    across_columns, to_cross = phase((swap(columns, 2), accumulated))
+    across_raw = swap(to_cross, 2)
     cotangent_all = lax.all_gather(cotangent, "row", axis=0, tiled=True)
 
     def products(raws, columns):
@@ -121,43 +119,39 @@
         sums = jnp.stack(sums)
         return sums + trade(sums.astype(jnp.bfloat16)).astype(jnp.float32)
 
-    across = gradient_tile(across_columns, cotangent_all, across_raw)
-    quarters, behind, across = phase((quarters, behind, across))
     own = gradient_tile(columns, cotangent_all, accumulated)
     beside = swap(own, 1)
+    moving, behind, own, beside = phase((moving, behind, own, beside))
 
     sums = [None] * (steps + 1)
-    made, handed = None, None
+    made = None
     for step in range(1, steps):
-        arrived, arrived_columns = quarters, behind
+        arrived, arrived_columns = moving, behind
         behind = from_behind(arrived_columns, GROUP)
-        first = from_behind(arrived[0], GROUP)
+        if step < steps - 1:
+            moving = from_behind(arrived, GROUP)
+        else:
+            quarters = jnp.split(arrived, 4)
+            moving = from_behind(jnp.concatenate(quarters[:2]), GROUP)
         if step == 1:
+            own_products = [block_product(own, panel) for panel in (own, beside)]
+            across = gradient_tile(across_columns, cotangent_all, across_raw)
             group = [own, beside, across, swap(across, 1)]
-            own_products = [block_product(own, panel) for panel in (own, beside)]
+            own_products += [block_product(own, panel) for panel in group[2:]]
         else:
-            handed = to_owners(made)
-        first, group, handed, own_products = phase((first, group, handed, own_products))
-        if step > 1:
-            sums[steps - step + 1] = over_columns(handed)
-        second = from_behind(arrived[1], GROUP)
-        made = products(arrived, arrived_columns)
-        if step == 1:
-            own_products += [block_product(own, panel) for panel in group[2:]]
-        first, second, behind, made, sums, own_products = phase(
-            (first, second, behind, made, sums, own_products)
-        )
-        if step < steps - 1:
-            rest = [from_behind(piece, GROUP) for piece in arrived[2:]]
-            quarters = [first, second, *rest]
-
-    third = from_behind(arrived[2], GROUP)
+            sums[steps - step + 1] = over_columns(to_owners(made))
+        made = products([arrived], arrived_columns)
+        moving, behind, made, sums, own_products = phase(
+            (moving, behind, made, sums, own_products)
+        )
+
+    third = from_behind(quarters[2], GROUP)
     sums[steps] = over_columns(own_products)
     handed = to_owners(made)
-    made = products([first, second], behind[:, : 2 * quarter])
+    made = products([moving], behind[:, : 2 * quarter])
     third, handed, made, sums[steps] = phase((third, handed, made, sums[steps]))
 
-    fourth = from_behind(arrived[3], GROUP)
+    fourth = from_behind(quarters[3], GROUP)
     sums[1] = over_columns(handed)
     handed = to_owners(made)
     made = products([third], behind[:, 2 * quarter : 3 * quarter])

time: 499 us -> 489 us (0.980)
  waiting for transfers between devices: 302 us -> 294 us
    all_gather x1, waiting for transfers between devices: 0.01 us -> 53.8 us  [body(): cotangent_all = lax.all_gather(cotangent, 'row', axis=0, tiled=True)]
    ppermute x16, waiting for transfers between devices: 162 us -> 117 us  [swap(): return lax.ppermute(array, 'row', [(i, i ^ mask) for i in range(count)])]
    ppermute x10 -> x6, waiting for transfers between devices: 60.8 us -> 44.4 us  [from_behind(): lax.ppermute(array, 'row', [(i, (i + by) % count) for i in range(count)])]
    ppermute x10 -> x6, starting transfers between devices: 9.59 us -> 3.88 us  [from_behind(): lax.ppermute(array, 'row', [(i, (i + by) % count) for i in range(count)])]
    slice x2 -> x1, local copies, waits for them, and re-layouts: 6.53 us -> 0.91 us  [body(): made = products([moving], behind[:, :2 * quarter])]
  transfers between devices with their start and end apart: 33 -> 29, of which waited for: 11 -> 13; matrix products, arithmetic and copies ran while one was open for 13% -> 13% of each run, Pallas kernels for 15% -> 15%
where the time goes in v8:
time: 489 us
  waiting for transfers between devices  294 us (60%)
  Pallas kernels  73.6 us (15%)
  matrix products  40.6 us (8%)
  starting transfers between devices  24.5 us (5%)
  other arithmetic  21.9 us (4%)
  local copies, waits for them, and re-layouts  20 us (4%)
  between operations  14.4 us (3%)
    ppermute x16, waiting for transfers between devices, swap(): return lax.ppermute(array, 'row', [(i, i ^ mask) for i in range(count)])  117 us
    ppermute x6, waiting for transfers between devices, trade(): return lax.ppermute(array, 'col', [(0, 1), (1, 0)])  78 us
    pallas_call x4, Pallas kernels, panel_products(): pl.pallas_call(products_kernel, grid=(width // depth,), in_specs=[pl.Bloc...  73.6 us
    all_gather x1, waiting for transfers between devices, body(): cotangent_all = lax.all_gather(cotangent, 'row', axis=0, tiled=True)  53.8 us
    ppermute x6, waiting for transfers between devices, from_behind(): lax.ppermute(array, 'row', [(i, (i + by) % count) for i in range(count)])  44.4 us
    dot_general x4, matrix products, block_product(): lax.dot_general(left, right, (((1,), (1,)), ((), ())), preferred_element_...  25.9 us
    dot_general x2, matrix products, gradient_tile(): lax.dot_general(columns, cotangent_all, (((0,), (0,)), ((), ())), preferr...  14.6 us
    ppermute x16, starting transfers between devices, swap(): return lax.ppermute(array, 'row', [(i, i ^ mask) for i in range(count)])  12.2 us
  transfers between devices with their start and end apart: 29, of which 13 were waited for; matrix products, arithmetic and copies ran while one was open for 13% of the time, Pallas kernels for 15%

profile of v8, /device:TPU:0, one launch (start us, length us, event | category | flops | bytes accessed | tf_op | source)
XLA Modules:
  0.0 488.9 jit_solution(1096727762995040446)
XLA Ops:
  7.2 0.7 all-gather.2.cloned.1.call-update
  7.9 3.0 collective-permute-start.1
  10.9 3.7 collective-permute-done.1
  14.6 1.0 maximum_select_fusion
  15.7 1.8 collective-permute-start.8
  17.5 6.1 %collective-permute-done.8 = bf16[256,512]{1,0:T(8,128)(2,1)S(1)} collective-permute-done((bf16[256,512]{1,0:T(8,128)(2,1)S(1)}, bf16[256,512]{1,0:T(8,128)(2,1)S(1)}, u32[]{:S(2)}, u32[]{:S(2)}) %collective-permute-start.8) | collective-permute-done | bytes 262176 | tf_op jit(solution)/shard_map/ppermute | solution.py:14
  23.6 2.5 collective-permute-start.9
  26.0 1.2 collective-permute-start
  27.3 53.8 %all-gather.2.cloned.1.call-done.refs_6_ = bf16[256,7168]{1,0:T(8,128)(2,1)} async-done(((bf16[16,7168]{1,0:T(8,128)(2,1)}), bf16[256,7168]{1,0:T(8,128)(2,1)}) %all-gather.2.cloned.1.call-update) | async-done | bytes 3670032 | tf_op jit(solution)/shard_map/all_gather | solution.py:108
  81.0 6.4 %add_convert_fusion.1.refs_0_ = bf16[512,7168]{1,0:T(8,128)(2,1)S(1)} fusion(bf16[512,7168]{1,0:T(8,128)(2,1)} %param.7, bf16[256,512]{1,0:T(8,128)(2,1)S(1)} %maximum_select_fusion, bf16[256,7168]{1,0:T(8,128)(2,1)} %all-gather.2.cloned.1.call-done.refs_6_), kind=kOutput, calls=%fused_computation.1 | convolution fusion | flops 1890058240 | bytes 18612224 | tf_op jit(solution)/shard_map/dot_general | solution.py:27
  87.5 0.3 collective-permute-start.3
  87.8 105.5 %collective-permute-done.9 = bf16[512,7168]{1,0:T(8,128)(2,1)} collective-permute-done((bf16[512,7168]{1,0:T(8,128)(2,1)}, bf16[512,7168]{1,0:T(8,128)(2,1)}, u32[]{:S(2)}, u32[]{:S(2)}) %collective-permute-start.9) | collective-permute-done | bytes 7340064 | tf_op jit(solution)/shard_map/ppermute | solution.py:14
  193.3 8.2 %add_convert_fusion.refs_2_ = bf16[512,7168]{1,0:T(8,128)(2,1)} fusion(bf16[512,7168]{1,0:T(8,128)(2,1)} %collective-permute-done.9, bf16[256,512]{1,0:T(8,128)(2,1)S(1)} %collective-permute-done.8, bf16[256,7168]{1,0:T(8,128)(2,1)S(1)} %copy-done), kind=kOutput, calls=%fused_computation | convolution fusion | flops 1890058240 | bytes 18612224 | tf_op jit(solution)/shard_map/dot_general | solution.py:27
  201.5 1.5 collective-permute-start.2
  203.0 9.0 %collective-permute-done.2.refs_5_ = bf16[256,512]{1,0:T(8,128)(2,1)S(1)} collective-permute-done((bf16[256,512]{1,0:T(8,128)(2,1)S(1)}, bf16[256,512]{1,0:T(8,128)(2,1)S(1)}, u32[]{:S(2)}, u32[]{:S(2)}) %collective-permute-start.2) | collective-permute-done | bytes 262176 | tf_op jit(solution)/shard_map/ppermute | solution.py:19
  212.1 4.1 concatenate.17
  216.2 1.2 collective-permute-start.7
  217.3 5.0 %fusion.8 = f32[512,512]{1,0:T(8,128)} fusion(bf16[512,7168]{1,0:T(8,128)(2,1)S(1)} %add_convert_fusion.1.refs_0_), kind=kOutput, calls=%fused_computation.45 | convolution fusion | flops 3758096384 | bytes 8388608 | tf_op jit(solution)/shard_map/dot_general | solution.py:34
  222.3 7.2 %fusion.10 = f32[512,512]{1,0:T(8,128)} fusion(bf16[512,7168]{1,0:T(8,128)(2,1)S(1)} %add_convert_fusion.1.refs_0_, bf16[512,7168]{1,0:T(8,128)(2,1)} %add_convert_fusion.refs_2_), kind=kOutput, calls=%fused_computation.47 | convolution fusion | flops 3758096384 | bytes 15728640 | tf_op jit(solution)/shard_map/dot_general | solution.py:34
  229.6 7.2 %fusion.9 = f32[512,512]{1,0:T(8,128)} fusion(bf16[512,7168]{1,0:T(8,128)(2,1)S(1)} %add_convert_fusion.1.refs_0_, bf16[512,7168]{1,0:T(8,128)(2,1)} %collective-permute-done.3.refs_1_), kind=kOutput, calls=%fused_computation.46 | convolution fusion | flops 3758096384 | bytes 15728640 | tf_op jit(solution)/shard_map/dot_general | solution.py:34
  236.8 26.2 %shard_map.68 = f32[4,512,512]{2,1,0:T(8,128)} custom-call(bf16[512,7168]{1,0:T(8,128)(2,1)} %copy-done.1, bf16[512,7168]{1,0:T(8,128)(2,1)} %collective-permute-done.3.refs_1_, bf16[512,7168]{1,0:T(8,128)(2,1)} %add_convert_fusion.refs_2_, bf16[512,7168]{1,0:T(8,128)(2,1)} %collective-permute-done.10.refs_3_, ...), custom_call_target="tpu_custom_call" | custom-call | flops 16911433728 | bytes 44564480 | tf_op jit(solution)/shard_map/pallas_call | solution.py:61
  263.0 6.5 %fusion.11 = f32[512,512]{1,0:T(8,128)S(1)} fusion(bf16[512,7168]{1,0:T(8,128)(2,1)S(1)} %copy-done.2, bf16[512,7168]{1,0:T(8,128)(2,1)} %collective-permute-done.10.refs_3_), kind=kOutput, calls=%fused_computation.48 | convolution fusion | flops 3758096384 | bytes 15728640 | tf_op jit(solution)/shard_map/dot_general | solution.py:34
  269.5 35.3 %collective-permute-done.7 = bf16[256,512]{1,0:T(8,128)(2,1)} collective-permute-done((bf16[256,512]{1,0:T(8,128)(2,1)S(1)}, bf16[256,512]{1,0:T(8,128)(2,1)}, u32[]{:S(2)}, u32[]{:S(2)}) %collective-permute-start.7) | collective-permute-done | bytes 262176 | tf_op jit(solution)/shard_map/ppermute | solution.py:19
  304.9 1.7 fusion.2
  306.6 1.5 collective-permute-start.14
  308.1 4.1 fusion.6
  312.2 1.7 slice_bitcast_fusion
  314.0 1.2 collective-permute-start.12
  315.1 0.7 collective-permute-start.13
  315.8 0.9 slice.65.refs_5_
  316.8 16.3 %shard_map.69 = f32[4,512,256]{2,1,0:T(8,128)S(1)} custom-call(bf16[512,7168]{1,0:T(8,128)(2,1)} %copy-done.1, bf16[512,7168]{1,0:T(8,128)(2,1)} %collective-permute-done.3.refs_1_, bf16[512,7168]{1,0:T(8,128)(2,1)} %add_convert_fusion.refs_2_, bf16[512,7168]{1,0:T(8,128)(2,1)} %collective-permute-done.10.refs_3_, ...), custom_call_target="tpu_custom_call" | custom-call | flops 8455716864 | bytes 38797312 | tf_op jit(solution)/shard_map/pallas_call | solution.py:61
  333.1 20.2 %collective-permute-done.14 = bf16[4,512,512]{2,1,0:T(8,128)(2,1)} collective-permute-done((bf16[4,512,512]{2,1,0:T(8,128)(2,1)}, bf16[4,512,512]{2,1,0:T(8,128)(2,1)}, u32[]{:S(2)}, u32[]{:S(2)}) %collective-permute-start.14) | collective-permute-done | bytes 2097184 | tf_op jit(solution)/shard_map/ppermute | solution.py:23
  353.3 4.4 convert_add_fusion.1
  357.7 4.1 collective-permute-done.13
  361.8 0.4 fusion.1
  362.3 0.9 collective-permute-start.15
  363.2 0.9 fusion.7
  364.0 1.2 slice_bitcast_fusion.4
  365.2 1.1 collective-permute-start.17
  366.3 0.8 collective-permute-start.18
  367.1 15.6 %shard_map.70 = f32[4,512,128]{2,1,0:T(8,128)S(1)} custom-call(bf16[512,7168]{1,0:T(8,128)(2,1)} %copy-done.1, bf16[512,7168]{1,0:T(8,128)(2,1)} %collective-permute-done.3.refs_1_, bf16[512,7168]{1,0:T(8,128)(2,1)} %add_convert_fusion.refs_2_, bf16[512,7168]{1,0:T(8,128)(2,1)} %collective-permute-done.10.refs_3_, ...), custom_call_target="tpu_custom_call" | custom-call | flops 4227858432 | bytes 35913728 | tf_op jit(solution)/shard_map/pallas_call | solution.py:61
  382.6 27.4 %collective-permute-done.15 = bf16[4,512,512]{2,1,0:T(8,128)(2,1)S(1)} collective-permute-done((bf16[4,512,512]{2,1,0:T(8,128)(2,1)S(1)}, bf16[4,512,512]{2,1,0:T(8,128)(2,1)S(1)}, u32[]{:S(2)}, u32[]{:S(2)}) %collective-permute-start.15) | collective-permute-done | bytes 2097184 | tf_op jit(solution)/shard_map/ppermute | solution.py:23
  410.1 2.7 convert_add_fusion
  413.1 0.9 collective-permute-start.19
  414.1 1.2 collective-permute-start.21
  415.3 0.7 collective-permute-start.22
  416.0 15.6 %shard_map.71 = f32[4,512,128]{2,1,0:T(8,128)S(1)} custom-call(bf16[512,7168]{1,0:T(8,128)(2,1)} %copy-done.1, bf16[512,7168]{1,0:T(8,128)(2,1)} %collective-permute-done.3.refs_1_, bf16[512,7168]{1,0:T(8,128)(2,1)} %add_convert_fusion.refs_2_, bf16[512,7168]{1,0:T(8,128)(2,1)} %collective-permute-done.10.refs_3_, ...), custom_call_target="tpu_custom_call" | custom-call | flops 4227858432 | bytes 35913728 | tf_op jit(solution)/shard_map/pallas_call | solution.py:61
  431.5 6.1 %collective-permute-done.19 = bf16[4,512,256]{2,1,0:T(8,128)(2,1)S(1)} collective-permute-done((bf16[4,512,256]{2,1,0:T(8,128)(2,1)S(1)}, bf16[4,512,256]{2,1,0:T(8,128)(2,1)S(1)}, u32[]{:S(2)}, u32[]{:S(2)}) %collective-permute-start.19) | collective-permute-done | bytes 1048608 | tf_op jit(solution)/shard_map/ppermute | solution.py:23
  438.0 0.9 collective-permute-start.23
  439.0 1.2 collective-permute-start.25
  440.2 0.7 collective-permute-start.26
  440.9 9.5 %collective-permute-done.23 = bf16[4,512,128]{2,1,0:T(8,128)(2,1)S(1)} collective-permute-done((bf16[4,512,128]{2,1,0:T(8,128)(2,1)S(1)}, bf16[4,512,128]{2,1,0:T(8,128)(2,1)S(1)}, u32[]{:S(2)}, u32[]{:S(2)}) %collective-permute-start.23) | collective-permute-done | bytes 524320 | tf_op jit(solution)/shard_map/ppermute | solution.py:23
  450.3 1.1 convert_add_fusion.4
  451.5 1.4 collective-permute-done.26
  452.9 0.9 fusion.4
  453.8 1.2 collective-permute-start.27
  455.0 2.1 bitcast_add_fusion
  457.1 11.1 %collective-permute-done.27 = bf16[4,512,128]{2,1,0:T(8,128)(2,1)} collective-permute-done((bf16[4,512,128]{2,1,0:T(8,128)(2,1)}, bf16[4,512,128]{2,1,0:T(8,128)(2,1)}, u32[]{:S(2)}, u32[]{:S(2)}) %collective-permute-start.27) | collective-permute-done | bytes 524320 | tf_op jit(solution)/shard_map/ppermute | solution.py:23
  468.2 1.4 convert_add_fusion.3
  469.6 4.0 pad_maximum_fusion
  473.6 0.5 dynamic-slice_bitcast_fusion.3
  474.0 1.7 copy-done.4
  475.8 1.6 fusion
  477.4 4.7 copy.8
  (67 shorter events, 1.0 us)
Async XLA Ops:
  7.2 73.9 %all-gather.2.cloned.1.call-start = ((), (), s32[]{:S(2)}) async-start(), calls=%async_computation | async-start | bytes 3899392 | tf_op jit(solution)/shard_map/all_gather | solution.py:108
  7.9 6.7 %collective-permute-start.1 = (bf16[128,512]{1,0:T(8,128)(2,1)}, bf16[128,512]{1,0:T(8,128)(2,1)S(1)}, u32[]{:S(2)}, u32[]{:S(2)}) collective-permute-start(bf16[128,512]{1,0:T(8,128)(2,1)} %param.5), channel_id=1, source_target_pairs={{0,1},{1,0},{2,3},{3,2},{4,5},{5,4},{6,7},{7,6},{8,9},{9,8},{10,11... | collective-permute-start | bytes 393224 | tf_op jit(solution)/shard_map/ppermute | solution.py:23
  15.7 7.9 %collective-permute-start.8 = (bf16[256,512]{1,0:T(8,128)(2,1)S(1)}, bf16[256,512]{1,0:T(8,128)(2,1)S(1)}, u32[]{:S(2)}, u32[]{:S(2)}) collective-permute-start(bf16[256,512]{1,0:T(8,128)(2,1)S(1)} %maximum_select_fusion), channel_id=1, source_target_pairs={{0,4},{2,6},{4,0},{6,2},{8,12},{10,14},{12,8},{14,10},{16,20},{18,... | collective-permute-start | bytes 786440 | tf_op jit(solution)/shard_map/ppermute | solution.py:14
  23.6 169.8 %collective-permute-start.9 = (bf16[512,7168]{1,0:T(8,128)(2,1)}, bf16[512,7168]{1,0:T(8,128)(2,1)}, u32[]{:S(2)}, u32[]{:S(2)}) collective-permute-start(bf16[512,7168]{1,0:T(8,128)(2,1)} %param.7), channel_id=1, source_target_pairs={{0,4},{2,6},{4,0},{6,2},{8,12},{10,14},{12,8},{14,10},{16,20},{18,... | collective-permute-start | bytes 22020104 | tf_op jit(solution)/shard_map/ppermute | solution.py:14
  26.0 186.0 %collective-permute-start = (bf16[512,7168]{1,0:T(8,128)(2,1)}, bf16[512,7168]{1,0:T(8,128)(2,1)}, u32[]{:S(2)}, u32[]{:S(2)}) collective-permute-start(bf16[512,7168]{1,0:T(8,128)(2,1)} %param.7), channel_id=1, source_target_pairs={{0,8},{2,10},{4,12},{6,14},{8,16},{10,18},{12,20},{14,22},{16,24},... | collective-permute-start | bytes 22020104 | tf_op jit(solution)/shard_map/ppermute | solution.py:19
  81.0 112.3 %copy-start = (bf16[256,7168]{1,0:T(8,128)(2,1)S(1)}, bf16[256,7168]{1,0:T(8,128)(2,1)}, u32[]{:S(2)}) copy-start(bf16[256,7168]{1,0:T(8,128)(2,1)} %all-gather.2.cloned.1.call-done.refs_6_) | copy-start | bytes 11010052
  87.5 142.1 %copy-start.1 = (bf16[512,7168]{1,0:T(8,128)(2,1)}, bf16[512,7168]{1,0:T(8,128)(2,1)S(1)}, u32[]{:S(2)}) copy-start(bf16[512,7168]{1,0:T(8,128)(2,1)S(1)} %add_convert_fusion.1.refs_0_) | copy-start | bytes 22020100
  87.5 124.6 %collective-permute-start.3 = (bf16[512,7168]{1,0:T(8,128)(2,1)S(1)}, bf16[512,7168]{1,0:T(8,128)(2,1)}, u32[]{:S(2)}, u32[]{:S(2)}) collective-permute-start(bf16[512,7168]{1,0:T(8,128)(2,1)S(1)} %add_convert_fusion.1.refs_0_), channel_id=1, source_target_pairs={{0,2},{2,0},{4,6},{6,4},{8,10},{10,8},{12,14},{14,12},{16,18},{18,... | collective-permute-start | bytes 22020104 | tf_op jit(solution)/shard_map/ppermute | solution.py:14
  201.5 35.2 %collective-permute-start.10 = (bf16[512,7168]{1,0:T(8,128)(2,1)}, bf16[512,7168]{1,0:T(8,128)(2,1)}, u32[]{:S(2)}, u32[]{:S(2)}) collective-permute-start(bf16[512,7168]{1,0:T(8,128)(2,1)} %add_convert_fusion.refs_2_), channel_id=1, source_target_pairs={{0,2},{2,0},{4,6},{6,4},{8,10},{10,8},{12,14},{14,12},{16,18},{18,... | collective-permute-start | bytes 22020104 | tf_op jit(solution)/shard_map/ppermute | solution.py:14
  201.5 10.5 %collective-permute-start.2 = (bf16[256,512]{1,0:T(8,128)(2,1)S(1)}, bf16[256,512]{1,0:T(8,128)(2,1)S(1)}, u32[]{:S(2)}, u32[]{:S(2)}) collective-permute-start(bf16[256,512]{1,0:T(8,128)(2,1)S(1)} %maximum_select_fusion), channel_id=1, source_target_pairs={{0,8},{2,10},{4,12},{6,14},{8,16},{10,18},{12,20},{14,22},{16,24},... | collective-permute-start | bytes 786440 | tf_op jit(solution)/shard_map/ppermute | solution.py:19
  216.2 88.7 %collective-permute-start.6 = (bf16[256,7168]{1,0:T(8,128)(2,1)}, bf16[256,7168]{1,0:T(8,128)(2,1)S(1)}, u32[]{:S(2)}, u32[]{:S(2)}) collective-permute-start(bf16[256,7168]{1,0:T(8,128)(2,1)} %concatenate.17), channel_id=1, source_target_pairs={{0,8},{2,10},{4,12},{6,14},{8,16},{10,18},{12,20},{14,22},{16,24},... | collective-permute-start | bytes 11010056 | tf_op jit(solution)/shard_map/ppermute | solution.py:19
  216.2 88.7 %collective-permute-start.7 = (bf16[256,512]{1,0:T(8,128)(2,1)S(1)}, bf16[256,512]{1,0:T(8,128)(2,1)}, u32[]{:S(2)}, u32[]{:S(2)}) collective-permute-start(bf16[256,512]{1,0:T(8,128)(2,1)S(1)} %collective-permute-done.2.refs_5_), channel_id=1, source_target_pairs={{0,8},{2,10},{4,12},{6,14},{8,16},{10,18},{12,20},{14,22},{16,24},... | collective-permute-start | bytes 786440 | tf_op jit(solution)/shard_map/ppermute | solution.py:19
  236.8 26.2 %copy-start.2 = (bf16[512,7168]{1,0:T(8,128)(2,1)S(1)}, bf16[512,7168]{1,0:T(8,128)(2,1)}, u32[]{:S(2)}) copy-start(bf16[512,7168]{1,0:T(8,128)(2,1)} %copy-done.1) | copy-start | bytes 22020100
  263.0 41.9 %copy-start.7 = (f32[512,512]{1,0:T(8,128)S(1)}, f32[512,512]{1,0:T(8,128)}, u32[]{:S(2)}) copy-start(f32[512,512]{1,0:T(8,128)} %fusion.8) | copy-start | bytes 3145732
  263.0 41.9 %copy-start.9 = (f32[512,512]{1,0:T(8,128)S(1)}, f32[512,512]{1,0:T(8,128)}, u32[]{:S(2)}) copy-start(f32[512,512]{1,0:T(8,128)} %fusion.10) | copy-start | bytes 3145732
  263.0 41.9 %copy-start.11 = (f32[512,512]{1,0:T(8,128)S(1)}, f32[512,512]{1,0:T(8,128)}, u32[]{:S(2)}) copy-start(f32[512,512]{1,0:T(8,128)} %fusion.9) | copy-start | bytes 3145732
  269.5 42.7 %copy-start.13 = (f32[512,512]{1,0:T(8,128)}, f32[512,512]{1,0:T(8,128)S(1)}, u32[]{:S(2)}) copy-start(f32[512,512]{1,0:T(8,128)S(1)} %fusion.11) | copy-start | bytes 3145732
  306.6 5.6 %copy-start.6 = (f32[4,512,512]{2,1,0:T(8,128)S(1)}, f32[4,512,512]{2,1,0:T(8,128)}, u32[]{:S(2)}) copy-start(f32[4,512,512]{2,1,0:T(8,128)} %shard_map.68) | copy-start | bytes 12582916
  306.6 46.7 %collective-permute-start.14 = (bf16[4,512,512]{2,1,0:T(8,128)(2,1)}, bf16[4,512,512]{2,1,0:T(8,128)(2,1)}, u32[]{:S(2)}, u32[]{:S(2)}) collective-permute-start(bf16[4,512,512]{2,1,0:T(8,128)(2,1)} %fusion.2), channel_id=1, source_target_pairs={{0,1},{1,0},{2,3},{3,2},{4,5},{5,4},{6,7},{7,6},{8,9},{9,8},{10,11... | collective-permute-start | bytes 6291464 | tf_op jit(solution)/shard_map/ppermute | solution.py:23
  312.2 45.5 %collective-permute-start.5 = (bf16[128,7168]{1,0:T(8,128)(2,1)}, bf16[128,7168]{1,0:T(8,128)(2,1)S(1)}, u32[]{:S(2)}, u32[]{:S(2)}) collective-permute-start(bf16[128,7168]{1,0:T(8,128)(2,1)} %get-tuple-element.87), channel_id=1, source_target_pairs={{0,8},{2,10},{4,12},{6,14},{8,16},{10,18},{12,20},{14,22},{16,24},... | collective-permute-start | bytes 5505032 | tf_op jit(solution)/shard_map/ppermute | solution.py:19
  314.0 43.7 %collective-permute-start.11 = (f32[512,512]{1,0:T(8,128)}, f32[512,512]{1,0:T(8,128)S(1)}, u32[]{:S(2)}, u32[]{:S(2)}) collective-permute-start(f32[512,512]{1,0:T(8,128)} %get-tuple-element.90), channel_id=1, source_target_pairs={{0,2},{2,0},{4,6},{6,4},{8,10},{10,8},{12,14},{14,12},{16,18},{18,... | collective-permute-start | bytes 3145736 | tf_op jit(solution)/shard_map/ppermute | solution.py:14
  314.0 43.7 %collective-permute-start.12 = (f32[512,512]{1,0:T(8,128)}, f32[512,512]{1,0:T(8,128)S(1)}, u32[]{:S(2)}, u32[]{:S(2)}) collective-permute-start(f32[512,512]{1,0:T(8,128)} %get-tuple-element.89), channel_id=1, source_target_pairs={{0,4},{2,6},{4,0},{6,2},{8,12},{10,14},{12,8},{14,10},{16,20},{18,... | collective-permute-start | bytes 3145736 | tf_op jit(solution)/shard_map/ppermute | solution.py:14
  315.1 46.7 %collective-permute-start.13 = (f32[512,512]{1,0:T(8,128)}, f32[512,512]{1,0:T(8,128)S(1)}, u32[]{:S(2)}, u32[]{:S(2)}) collective-permute-start(f32[512,512]{1,0:T(8,128)} %get-tuple-element.88), channel_id=1, source_target_pairs={{0,6},{2,4},{4,2},{6,0},{8,14},{10,12},{12,10},{14,8},{16,22},{18,... | collective-permute-start | bytes 3145736 | tf_op jit(solution)/shard_map/ppermute | solution.py:14
  316.7 36.6 %copy-start.8 = (f32[512,512]{1,0:T(8,128)S(1)}, f32[512,512]{1,0:T(8,128)}, u32[]{:S(2)}) copy-start(f32[512,512]{1,0:T(8,128)} %fusion.8) | copy-start | bytes 3145732
  316.8 36.6 %copy-start.10 = (f32[512,512]{1,0:T(8,128)S(1)}, f32[512,512]{1,0:T(8,128)}, u32[]{:S(2)}) copy-start(f32[512,512]{1,0:T(8,128)} %fusion.10) | copy-start | bytes 3145732
  316.8 36.5 %copy-start.12 = (f32[512,512]{1,0:T(8,128)S(1)}, f32[512,512]{1,0:T(8,128)}, u32[]{:S(2)}) copy-start(f32[512,512]{1,0:T(8,128)} %fusion.9) | copy-start | bytes 3145732
  316.8 36.5 %copy-start.14 = (f32[512,512]{1,0:T(8,128)S(1)}, f32[512,512]{1,0:T(8,128)}, u32[]{:S(2)}) copy-start(f32[512,512]{1,0:T(8,128)} %copy-done.13) | copy-start | bytes 3145732
  362.3 47.8 %collective-permute-start.15 = (bf16[4,512,512]{2,1,0:T(8,128)(2,1)S(1)}, bf16[4,512,512]{2,1,0:T(8,128)(2,1)S(1)}, u32[]{:S(2)}, u32[]{:S(2)}) collective-permute-start(bf16[4,512,512]{2,1,0:T(8,128)(2,1)S(1)} %fusion.1), channel_id=1, source_target_pairs={{0,1},{1,0},{2,3},{3,2},{4,5},{5,4},{6,7},{7,6},{8,9},{9,8},{10,11... | collective-permute-start | bytes 6291464 | tf_op jit(solution)/shard_map/ppermute | solution.py:23
  363.2 49.6 %collective-permute-start.4 = (bf16[128,7168]{1,0:T(8,128)(2,1)}, bf16[128,7168]{1,0:T(8,128)(2,1)S(1)}, u32[]{:S(2)}, u32[]{:S(2)}) collective-permute-start(bf16[128,7168]{1,0:T(8,128)(2,1)} %get-tuple-element.86), channel_id=1, source_target_pairs={{0,8},{2,10},{4,12},{6,14},{8,16},{10,18},{12,20},{14,22},{16,24},... | collective-permute-start | bytes 5505032 | tf_op jit(solution)/shard_map/ppermute | solution.py:19
  365.2 47.6 %collective-permute-start.16 = (f32[512,256]{1,0:T(8,128)}, f32[512,256]{1,0:T(8,128)S(1)}, u32[]{:S(2)}, u32[]{:S(2)}) collective-permute-start(f32[512,256]{1,0:T(8,128)} %get-tuple-element.94), channel_id=1, source_target_pairs={{0,2},{2,0},{4,6},{6,4},{8,10},{10,8},{12,14},{14,12},{16,18},{18,... | collective-permute-start | bytes 1572872 | tf_op jit(solution)/shard_map/ppermute | solution.py:14
  365.2 47.6 %collective-permute-start.17 = (f32[512,256]{1,0:T(8,128)}, f32[512,256]{1,0:T(8,128)S(1)}, u32[]{:S(2)}, u32[]{:S(2)}) collective-permute-start(f32[512,256]{1,0:T(8,128)} %get-tuple-element.93), channel_id=1, source_target_pairs={{0,4},{2,6},{4,0},{6,2},{8,12},{10,14},{12,8},{14,10},{16,20},{18,... | collective-permute-start | bytes 1572872 | tf_op jit(solution)/shard_map/ppermute | solution.py:14
  366.3 46.5 %collective-permute-start.18 = (f32[512,256]{1,0:T(8,128)S(1)}, f32[512,256]{1,0:T(8,128)S(1)}, u32[]{:S(2)}, u32[]{:S(2)}) collective-permute-start(f32[512,256]{1,0:T(8,128)S(1)} %get-tuple-element.92), channel_id=1, source_target_pairs={{0,6},{2,4},{4,2},{6,0},{8,14},{10,12},{12,10},{14,8},{16,22},{18,... | collective-permute-start | bytes 1572872 | tf_op jit(solution)/shard_map/ppermute | solution.py:14
  413.1 24.5 %collective-permute-start.19 = (bf16[4,512,256]{2,1,0:T(8,128)(2,1)S(1)}, bf16[4,512,256]{2,1,0:T(8,128)(2,1)S(1)}, u32[]{:S(2)}, u32[]{:S(2)}) collective-permute-start(bf16[4,512,256]{2,1,0:T(8,128)(2,1)S(1)} %fusion.3), channel_id=1, source_target_pairs={{0,1},{1,0},{2,3},{3,2},{4,5},{5,4},{6,7},{7,6},{8,9},{9,8},{10,11... | collective-permute-start | bytes 3145736 | tf_op jit(solution)/shard_map/ppermute | solution.py:23
  414.0 23.8 %collective-permute-start.20 = (f32[512,128]{1,0:T(8,128)S(1)}, f32[512,128]{1,0:T(8,128)S(1)}, u32[]{:S(2)}, u32[]{:S(2)}) collective-permute-start(f32[512,128]{1,0:T(8,128)S(1)} %get-tuple-element.102), channel_id=1, source_target_pairs={{0,2},{2,0},{4,6},{6,4},{8,10},{10,8},{12,14},{14,12},{16,18},{18,... | collective-permute-start | bytes 786440 | tf_op jit(solution)/shard_map/ppermute | solution.py:14
  414.1 23.7 %collective-permute-start.21 = (f32[512,128]{1,0:T(8,128)S(1)}, f32[512,128]{1,0:T(8,128)S(1)}, u32[]{:S(2)}, u32[]{:S(2)}) collective-permute-start(f32[512,128]{1,0:T(8,128)S(1)} %get-tuple-element.101), channel_id=1, source_target_pairs={{0,4},{2,6},{4,0},{6,2},{8,12},{10,14},{12,8},{14,10},{16,20},{18,... | collective-permute-start | bytes 786440 | tf_op jit(solution)/shard_map/ppermute | solution.py:14
  415.3 22.6 %collective-permute-start.22 = (f32[512,128]{1,0:T(8,128)S(1)}, f32[512,128]{1,0:T(8,128)S(1)}, u32[]{:S(2)}, u32[]{:S(2)}) collective-permute-start(f32[512,128]{1,0:T(8,128)S(1)} %get-tuple-element.100), channel_id=1, source_target_pairs={{0,6},{2,4},{4,2},{6,0},{8,14},{10,12},{12,10},{14,8},{16,22},{18,... | collective-permute-start | bytes 786440 | tf_op jit(solution)/shard_map/ppermute | solution.py:14
  438.0 17.0 %slice-start = ((f32[4,512,512]{2,1,0:T(8,128)}), f32[1,512,512]{2,1,0:T(8,128)S(1)}, s32[]{:S(2)}) async-start(f32[4,512,512]{2,1,0:T(8,128)} %convert_add_fusion.1), calls=%async_computation.1 | async-start | bytes 2097152 | tf_op jit(solution)/shard_map/slice | solution.py:181
  438.0 12.4 %collective-permute-start.23 = (bf16[4,512,128]{2,1,0:T(8,128)(2,1)S(1)}, bf16[4,512,128]{2,1,0:T(8,128)(2,1)S(1)}, u32[]{:S(2)}, u32[]{:S(2)}) collective-permute-start(bf16[4,512,128]{2,1,0:T(8,128)(2,1)S(1)} %fusion.5), channel_id=1, source_target_pairs={{0,1},{1,0},{2,3},{3,2},{4,5},{5,4},{6,7},{7,6},{8,9},{9,8},{10,11... | collective-permute-start | bytes 1572872 | tf_op jit(solution)/shard_map/ppermute | solution.py:23
  438.9 12.5 %collective-permute-start.24 = (f32[512,128]{1,0:T(8,128)S(1)}, f32[512,128]{1,0:T(8,128)S(1)}, u32[]{:S(2)}, u32[]{:S(2)}) collective-permute-start(f32[512,128]{1,0:T(8,128)S(1)} %get-tuple-element.98), channel_id=1, source_target_pairs={{0,2},{2,0},{4,6},{6,4},{8,10},{10,8},{12,14},{14,12},{16,18},{18,... | collective-permute-start | bytes 786440 | tf_op jit(solution)/shard_map/ppermute | solution.py:14
  439.0 12.4 %collective-permute-start.25 = (f32[512,128]{1,0:T(8,128)S(1)}, f32[512,128]{1,0:T(8,128)S(1)}, u32[]{:S(2)}, u32[]{:S(2)}) collective-permute-start(f32[512,128]{1,0:T(8,128)S(1)} %get-tuple-element.97), channel_id=1, source_target_pairs={{0,4},{2,6},{4,0},{6,2},{8,12},{10,14},{12,8},{14,10},{16,20},{18,... | collective-permute-start | bytes 786440 | tf_op jit(solution)/shard_map/ppermute | solution.py:14
  440.2 12.7 %collective-permute-start.26 = (f32[512,128]{1,0:T(8,128)S(1)}, f32[512,128]{1,0:T(8,128)S(1)}, u32[]{:S(2)}, u32[]{:S(2)}) collective-permute-start(f32[512,128]{1,0:T(8,128)S(1)} %get-tuple-element.96), channel_id=1, source_target_pairs={{0,6},{2,4},{4,2},{6,0},{8,14},{10,12},{12,10},{14,8},{16,22},{18,... | collective-permute-start | bytes 786440 | tf_op jit(solution)/shard_map/ppermute | solution.py:14
  451.4 1.5 copy-start.15
  451.5 2.3 copy-start.16
  452.9 0.9 copy-start.17
  453.8 14.4 %collective-permute-start.27 = (bf16[4,512,128]{2,1,0:T(8,128)(2,1)}, bf16[4,512,128]{2,1,0:T(8,128)(2,1)}, u32[]{:S(2)}, u32[]{:S(2)}) collective-permute-start(bf16[4,512,128]{2,1,0:T(8,128)(2,1)} %fusion.4), channel_id=1, source_target_pairs={{0,1},{1,0},{2,3},{3,2},{4,5},{5,4},{6,7},{7,6},{8,9},{9,8},{10,11... | collective-permute-start | bytes 1572872 | tf_op jit(solution)/shard_map/ppermute | solution.py:23
  455.0 14.6 %copy-start.3 = (f32[4,512,512]{2,1,0:T(8,128)S(1)}, f32[4,512,512]{2,1,0:T(8,128)}, u32[]{:S(2)}) copy-start(f32[4,512,512]{2,1,0:T(8,128)} %convert_add_fusion.1) | copy-start | bytes 12582916
  455.0 14.6 %copy-start.5 = (f32[4,512,128]{2,1,0:T(8,128)S(1)}, f32[4,512,128]{2,1,0:T(8,128)}, u32[]{:S(2)}) copy-start(f32[4,512,128]{2,1,0:T(8,128)} %convert_add_fusion.4) | copy-start | bytes 3145732
  473.6 2.2 copy-start.4
Sparse Core Ops, SparseCore 0:
  10.3 70.6 all-gather.1

commit v9 on v8

--- a/solution.py
+++ b/solution.py
@@ -81,19 +81,82 @@
     )(*group, *raws, columns, cotangent_all)
 
 
+def update_kernel(at_ref, old, *refs):
+    out, refs = refs[-1], list(refs[:-1])
+    place, y = at_ref[0], at_ref[1]
+    own, one = [refs.pop(0) for _ in range(GROUP - 1)], [refs.pop(0) for _ in range(GROUP)]
+    two = [(refs[i : i + GROUP], refs[i + GROUP]) for i in range(0, len(refs), GROUP + 1)]
+    share = old.shape[1]
+
+    def pick(u, values):
+        chosen = values[-1]
+        for i in range(len(values) - 1):
+            chosen = jnp.where(u == i, values[i], chosen)
+        return chosen
+
+    for s in range(share):
+        t = 2 * GROUP + place - (s + 1 + y * share)
+        u = (t % GROUP) ^ place
+        kept, added = decay_rate * old[:, s, :], 1.0 - decay_rate
+
+        @pl.when(t >= 2 * GROUP)
+        def _():
+            out[:, s, :] = kept + added * pick(u - 1, [ref[...] for ref in own])
+
+        @pl.when((t >= GROUP) & (t < 2 * GROUP))
+        def _():
+            out[:, s, :] = kept + added * pick(u, [ref[...] for ref in one])
+
+        @pl.when(t < GROUP)
+        def _():
+            start = 0
+            for mine, other in two:
+                value = pick(u, [ref[...] for ref in mine]) + other[u].astype(jnp.float32)
+                end = start + value.shape[1]
+                out[:, s, start:end] = kept[:, start:end] + added * value
+                start = end
+
+
+def update(place, y, band_old, two, one, own):
+    block, share, _ = band_old.shape
+    rows = block // 4
+    operands, specs = [], []
+    for piece in [*own, *one]:
+        operands.append(piece)
+        specs.append(pl.BlockSpec((rows, block), lambda i: (i, 0)))
+    for mine, other in two:
+        width = other.shape[2]
+        operands += [*mine, other]
+        specs += [pl.BlockSpec((rows, width), lambda i: (i, 0))] * GROUP
+        specs.append(pl.BlockSpec((GROUP, rows, width), lambda i: (0, i, 0)))
+    whole = pl.BlockSpec((rows, share, block), lambda i: (i, 0, 0))
+    return pl.pallas_call(
+        update_kernel,
+        grid=(block // rows,),
+        in_specs=[pl.BlockSpec(memory_space=pltpu.SMEM), whole, *specs],
+        out_specs=whole,
+        out_shape=jax.ShapeDtypeStruct(band_old.shape, band_old.dtype),
+        compiler_params=pltpu.CompilerParams(
+            dimension_semantics=("arbitrary",), vmem_limit_bytes=48 * 2**20
+        ),
+    )(jnp.stack([place, y]).astype(jnp.int32), band_old, *operands)
+
+
 def body(activations, cotangent, accumulated, band_old, diagonal_old):
     n_row, n_col = lax.axis_size("row"), lax.axis_size("col")
     block, width = accumulated.shape
     band = n_row // 2
     steps = band // GROUP
+    paired = n_col == 2 and steps == 2
     place = lax.axis_index("row") % GROUP
     y = lax.axis_index("col")
 
     phase = lax.optimization_barrier
 
-    quarter = block // 4
-    moving = from_behind(accumulated, GROUP)
-    if n_col == 2:
+    half, quarter = block // 2, block // 4
+    moving = [from_behind(accumulated[:half], GROUP), from_behind(accumulated[half:], GROUP)]
+    across_raw = swap(accumulated, 2)
+    if paired:
         other = trade(activations)
         columns = jnp.where(
             y == 0,
@@ -103,8 +166,7 @@
     else:
         columns = lax.all_gather(activations, "col", axis=0, tiled=True)
     behind = from_behind(columns, GROUP)
-    across_columns, to_cross = phase((swap(columns, 2), accumulated))
-    across_raw = swap(to_cross, 2)
+    across_columns = swap(columns, 2)
     cotangent_all = lax.all_gather(cotangent, "row", axis=0, tiled=True)
 
     def products(raws, columns):
@@ -114,84 +176,92 @@
         return [made[0]] + [swap(made[u], u) for u in range(1, GROUP)]
 
     def over_columns(sums):
-        if n_col != 2:
-            return jnp.stack(sums)
-        sums = jnp.stack(sums)
-        return sums + trade(sums.astype(jnp.bfloat16)).astype(jnp.float32)
+        if not paired:
+            return [None] * len(sums)
+        return trade(jnp.stack(sums).astype(jnp.bfloat16))
+
+    def added(sums, others):
+        if not paired:
+            return sums
+        return [a + b.astype(jnp.float32) for a, b in zip(sums, others)]
 
     own = gradient_tile(columns, cotangent_all, accumulated)
     beside = swap(own, 1)
     moving, behind, own, beside = phase((moving, behind, own, beside))
 
     sums = [None] * (steps + 1)
-    made = None
+    made, diagonal = None, None
     for step in range(1, steps):
         arrived, arrived_columns = moving, behind
         behind = from_behind(arrived_columns, GROUP)
         if step < steps - 1:
-            moving = from_behind(arrived, GROUP)
+            moving = [from_behind(piece, GROUP) for piece in arrived]
         else:
-            quarters = jnp.split(arrived, 4)
-            moving = from_behind(jnp.concatenate(quarters[:2]), GROUP)
+            moving = from_behind(arrived[0], GROUP)
+            quarters = jnp.split(arrived[1], 2)
         if step == 1:
             own_products = [block_product(own, panel) for panel in (own, beside)]
             across = gradient_tile(across_columns, cotangent_all, across_raw)
             group = [own, beside, across, swap(across, 1)]
             own_products += [block_product(own, panel) for panel in group[2:]]
+            if paired:
+                diagonal = lax.dynamic_slice_in_dim(own_products[0], y * half, half, 0) + trade(
+                    lax.dynamic_slice_in_dim(own_products[0], (1 - y) * half, half, 0)
+                )
+                own_products[1:2] = added(own_products[1:2], over_columns(own_products[1:2]))
         else:
-            sums[steps - step + 1] = over_columns(to_owners(made))
-        made = products([arrived], arrived_columns)
-        moving, behind, made, sums, own_products = phase(
-            (moving, behind, made, sums, own_products)
+            handed = to_owners(made)
+            sums[steps - step + 1] = added(handed, over_columns(handed))
+        made = products(arrived, arrived_columns)
+        if step == steps - 1:
+            handed = [made[0], swap(made[1], 1), swap(made[2], 2), made[3]]
+            moving, quarters, handed = phase((moving, quarters, handed))
+        moving, behind, made, sums, own_products, diagonal = phase(
+            (moving, behind, made, sums, own_products, diagonal)
         )
 
-    third = from_behind(quarters[2], GROUP)
-    sums[steps] = over_columns(own_products)
+    third = from_behind(quarters[0], GROUP)
+    one = added(handed[:3], over_columns(handed[:3]))
+    handed = one + [swap(handed[3], 3)]
+    made = products([moving], behind[:, :half])
+    third, handed, made = phase((third, handed, made))
+
+    fourth = from_behind(quarters[1], GROUP)
+    late = [handed[3], *own_products[2:]]
+    late = added(late, over_columns(late))
+    sums[1] = handed[:3] + late[:1]
+    sums[steps] = own_products[:2] + late[1:]
     handed = to_owners(made)
-    made = products([moving], behind[:, : 2 * quarter])
-    third, handed, made, sums[steps] = phase((third, handed, made, sums[steps]))
-
-    fourth = from_behind(quarters[3], GROUP)
-    sums[1] = over_columns(handed)
+    made = products([third], behind[:, half : half + quarter])
+    fourth, sums, handed, made = phase((fourth, sums, handed, made))
+
+    last = [(handed, over_columns(handed))]
     handed = to_owners(made)
-    made = products([third], behind[:, 2 * quarter : 3 * quarter])
-    fourth, sums[1], handed, made = phase((fourth, sums[1], handed, made))
-
-    last = [over_columns(handed)]
-    handed = to_owners(made)
-    made = products([fourth], behind[:, 3 * quarter :])
+    made = products([fourth], behind[:, half + quarter :])
     last, handed, made = phase((last, handed, made))
 
-    last.append(over_columns(handed))
+    last.append((handed, over_columns(handed)))
     handed = to_owners(made)
     last, handed = phase((last, handed))
-    last.append(over_columns(handed))
-    sums[0] = jnp.concatenate(last, axis=2)
-    stacked = jnp.concatenate(sums)
-
-    def at(offset):
-        t = band + place - offset
-        return lax.dynamic_index_in_dim(
-            stacked, t - t % GROUP + ((t % GROUP) ^ place), 0, keepdims=False
-        )
-
-    share = band // n_col
-    if n_col == 2:
-        band_sum = jnp.stack([at(s + y * share) for s in range(1, share + 1)], axis=1)
-        diagonal = lax.dynamic_slice_in_dim(sums[steps][0], y * (block // 2), block // 2, 0)
+    last.append((handed, over_columns(handed)))
+
+    if paired:
+        band_new = update(place, y, band_old, last, sums[1], sums[2][1:])
     else:
-        band_sum = jnp.swapaxes(
-            lax.psum_scatter(
-                jnp.stack([at(s) for s in range(1, band + 1)]),
-                "col",
-                scatter_dimension=0,
-                tiled=True,
-            ),
-            0,
-            1,
-        )
+        pieces = [sums_ for sums_, _ in last]
+        sums[0] = [jnp.concatenate([piece[u] for piece in pieces], axis=1) for u in range(GROUP)]
+        stacked = jnp.stack([piece for row in sums for piece in row])
+
+        def at(offset):
+            t = band + place - offset
+            return lax.dynamic_index_in_dim(
+                stacked, t - t % GROUP + ((t % GROUP) ^ place), 0, keepdims=False
+            )
+
+        shares = jnp.stack([at(s) for s in range(1, band + 1)])
+        summed = lax.psum_scatter(shares, "col", scatter_dimension=0, tiled=True)
         diagonal = lax.psum_scatter(own_products[0], "col", scatter_dimension=0, tiled=True)
-    band_new = decay_rate * band_old + (1.0 - decay_rate) * band_sum
+        band_new = decay_rate * band_old + (1.0 - decay_rate) * jnp.swapaxes(summed, 0, 1)
     diagonal_new = decay_rate * diagonal_old + (1.0 - decay_rate) * diagonal
     return (band_new, diagonal_new)
 

time: 489 us -> 508 us (1.039)
  matrix products: 40.6 us -> 52.2 us
  Pallas kernels: 73.6 us -> 81.7 us
  other arithmetic: 21.9 us -> 14.6 us
    ppermute x6 -> x8, waiting for transfers between devices: 78 us -> 54.5 us  [trade(): return lax.ppermute(array, 'col', [(0, 1), (1, 0)])]
    ppermute x6 -> x7, waiting for transfers between devices: 44.4 us -> 66.7 us  [from_behind(): lax.ppermute(array, 'row', [(i, (i + by) % count) for i in range(count)])]
    dot_general x4, matrix products: 25.9 us -> 34.9 us  [block_product(): lax.dot_general(left, right, (((1,), (1,)), ((), ())), preferred_element_...]
    pallas_call x0 -> x1, Pallas kernels: none -> 8.48 us  [update(): pl.pallas_call(update_kernel, grid=(block // rows,), in_specs=[pl.BlockSp...]
    add x6 -> x4, other arithmetic: 11.4 us -> 7 us  [the longest x3 6.11 us: added(): return [a + b.astype(jnp.float32) for a, b in zip(sums, others)]]
  transfers between devices with their start and end apart: 29 -> 32, of which waited for: 13 -> 13; matrix products, arithmetic and copies ran while one was open for 13% -> 16% of each run, Pallas kernels for 15% -> 14%
where the time goes in v9:
time: 508 us; the launch traced here: 507 us
  waiting for transfers between devices  299 us (59%)
  Pallas kernels  81.7 us (16%)
  matrix products  52.2 us (10%)
  starting transfers between devices  25.4 us (5%)
  local copies, waits for them, and re-layouts  19.7 us (4%)
  other arithmetic  14.6 us (3%)
  between operations  14.4 us (3%)
    ppermute x16, waiting for transfers between devices, swap(): return lax.ppermute(array, 'row', [(i, i ^ mask) for i in range(count)])  121 us
    pallas_call x4, Pallas kernels, panel_products(): pl.pallas_call(products_kernel, grid=(width // depth,), in_specs=[pl.Bloc...  73.2 us
    ppermute x7, waiting for transfers between devices, from_behind(): lax.ppermute(array, 'row', [(i, (i + by) % count) for i in range(count)])  66.7 us
    all_gather x1, waiting for transfers between devices, body(): cotangent_all = lax.all_gather(cotangent, 'row', axis=0, tiled=True)  56.1 us
    ppermute x8, waiting for transfers between devices, trade(): return lax.ppermute(array, 'col', [(0, 1), (1, 0)])  54.5 us
    dot_general x4, matrix products, block_product(): lax.dot_general(left, right, (((1,), (1,)), ((), ())), preferred_element_...  34.9 us
    dot_general x2, matrix products, gradient_tile(): lax.dot_general(columns, cotangent_all, (((0,), (0,)), ((), ())), preferr...  17.4 us
    ppermute x16, starting transfers between devices, swap(): return lax.ppermute(array, 'row', [(i, i ^ mask) for i in range(count)])  10.2 us
  transfers between devices with their start and end apart: 32, of which 13 were waited for; matrix products, arithmetic and copies ran while one was open for 16% of the time, Pallas kernels for 14%

profile of v9, /device:TPU:0, one launch (start us, length us, event | category | flops | bytes accessed | tf_op | source)
XLA Modules:
  0.0 507.0 jit_solution(17580683115777333758)
XLA Ops:
  7.2 0.7 all-gather.2.cloned.1.call-update
  7.9 3.0 collective-permute-start.7
  10.9 1.5 collective-permute-start.2
  12.4 3.7 collective-permute-done.2
  16.1 1.0 maximum_select_fusion
  17.1 56.1 %all-gather.2.cloned.1.call-done.refs_7_.refs_6_ = bf16[256,7168]{1,0:T(8,128)(2,1)} async-done(((bf16[16,7168]{1,0:T(8,128)(2,1)}), bf16[256,7168]{1,0:T(8,128)(2,1)}) %all-gather.2.cloned.1.call-update) | async-done | bytes 3670032 | tf_op jit(solution)/shard_map/all_gather | solution.py:170
  73.2 9.2 %add_convert_fusion.1.refs_0_ = bf16[512,7168]{1,0:T(8,128)(2,1)} fusion(bf16[512,7168]{1,0:T(8,128)(2,1)} %param.7, bf16[256,512]{1,0:T(8,128)(2,1)S(1)} %maximum_select_fusion, bf16[256,7168]{1,0:T(8,128)(2,1)} %all-gather.2.cloned.1.call-done.refs_7_.refs_6_), kind=kOutput, calls=%fused_computation.1 | convolution fusion | flops 1890058240 | bytes 18612224 | tf_op jit(solution)/shard_map/dot_general | solution.py:27
  82.7 6.8 %fusion = (bf16[256,7168]{1,0:T(8,128)(2,1)}, bf16[256,7168]{1,0:T(8,128)(2,1)}) fusion(bf16[512,7168]{1,0:T(8,128)(2,1)} %param.7), kind=kLoop, calls=%fused_computation.60 | loop fusion | bytes 14680064 | tf_op jit(solution)/shard_map/slice | solution.py:157
  89.5 1.7 collective-permute-start
  91.2 0.8 collective-permute-start.1
  92.0 0.6 collective-permute-start.6
  92.6 94.4 %collective-permute-done.6 = bf16[256,512]{1,0:T(8,128)(2,1)S(1)} collective-permute-done((bf16[256,512]{1,0:T(8,128)(2,1)S(1)}, bf16[256,512]{1,0:T(8,128)(2,1)S(1)}, u32[]{:S(2)}, u32[]{:S(2)}) %collective-permute-start.6) | collective-permute-done | bytes 262176 | tf_op jit(solution)/shard_map/ppermute | solution.py:14
  187.0 8.2 %add_convert_fusion.refs_2_ = bf16[512,7168]{1,0:T(8,128)(2,1)} fusion(bf16[512,7168]{1,0:T(8,128)(2,1)} %collective-permute-done.7, bf16[256,512]{1,0:T(8,128)(2,1)S(1)} %collective-permute-done.6, bf16[256,7168]{1,0:T(8,128)(2,1)S(1)} %copy-done.8), kind=kOutput, calls=%fused_computation | convolution fusion | flops 1890058240 | bytes 18612224 | tf_op jit(solution)/shard_map/dot_general | solution.py:27
  195.2 1.8 collective-permute-start.3
  197.0 60.2 %collective-permute-done.3.refs_6_ = bf16[256,512]{1,0:T(8,128)(2,1)S(1)} collective-permute-done((bf16[256,512]{1,0:T(8,128)(2,1)S(1)}, bf16[256,512]{1,0:T(8,128)(2,1)S(1)}, u32[]{:S(2)}, u32[]{:S(2)}) %collective-permute-start.3) | collective-permute-done | bytes 262176 | tf_op jit(solution)/shard_map/ppermute | solution.py:19
  257.3 8.5 %fusion.4 = f32[512,512]{1,0:T(8,128)S(1)} fusion(bf16[512,7168]{1,0:T(8,128)(2,1)} %add_convert_fusion.1.refs_0_, bf16[512,7168]{1,0:T(8,128)(2,1)} %collective-permute-done.4.refs_1_), kind=kOutput, calls=%fused_computation.64 | convolution fusion | flops 3758096384 | bytes 15728640 | tf_op jit(solution)/shard_map/dot_general | solution.py:34
  265.9 1.5 collective-permute-start.16
  267.5 0.7 collective-permute-start.15
  268.2 9.3 %fusion.3 = f32[512,512]{1,0:T(8,128)S(1)} fusion(bf16[512,7168]{1,0:T(8,128)(2,1)} %add_convert_fusion.1.refs_0_), kind=kOutput, calls=%fused_computation.63 | convolution fusion | flops 3758096384 | bytes 8388608 | tf_op jit(solution)/shard_map/dot_general | solution.py:34
  277.6 4.1 fusion.1
  281.7 8.5 %fusion.5 = f32[512,512]{1,0:T(8,128)S(1)} fusion(bf16[512,7168]{1,0:T(8,128)(2,1)} %add_convert_fusion.1.refs_0_, bf16[512,7168]{1,0:T(8,128)(2,1)} %add_convert_fusion.refs_2_), kind=kOutput, calls=%fused_computation.65 | convolution fusion | flops 3758096384 | bytes 15728640 | tf_op jit(solution)/shard_map/dot_general | solution.py:34
  290.2 25.9 %shard_map.68 = f32[4,512,512]{2,1,0:T(8,128)} custom-call(bf16[512,7168]{1,0:T(8,128)(2,1)} %add_convert_fusion.1.refs_0_, bf16[512,7168]{1,0:T(8,128)(2,1)} %collective-permute-done.4.refs_1_, bf16[512,7168]{1,0:T(8,128)(2,1)} %add_convert_fusion.refs_2_, bf16[512,7168]{1,0:T(8,128)(2,1)} %collective-permute-done.8.refs_3_, ...), custom_call_target="tpu_custom_call" | custom-call | flops 16911433728 | bytes 44564480 | tf_op jit(solution)/shard_map/pallas_call | solution.py:61
  316.2 3.6 slice_bitcast_fusion
  319.8 0.6 collective-permute-start.10
  320.4 8.5 %fusion.6 = f32[512,512]{1,0:T(8,128)S(1)} fusion(bf16[512,7168]{1,0:T(8,128)(2,1)} %add_convert_fusion.1.refs_0_, bf16[512,7168]{1,0:T(8,128)(2,1)} %collective-permute-done.8.refs_3_), kind=kOutput, calls=%fused_computation.66 | convolution fusion | flops 3758096384 | bytes 15728640 | tf_op jit(solution)/shard_map/dot_general | solution.py:34
  328.9 14.6 %collective-permute-done.10 = f32[512,512]{1,0:T(8,128)S(1)} collective-permute-done((f32[512,512]{1,0:T(8,128)S(1)}, f32[512,512]{1,0:T(8,128)S(1)}, u32[]{:S(2)}, u32[]{:S(2)}) %collective-permute-start.10) | collective-permute-done | bytes 1048608 | tf_op jit(solution)/shard_map/ppermute | solution.py:14
  343.5 0.5 collective-permute-start.17
  344.2 1.3 pad_maximum_fusion
  345.6 1.5 collective-permute-start.13
  347.0 0.6 collective-permute-start.12
  347.6 1.1 convert_add_fusion.3.refs_0_
  348.7 9.6 %collective-permute-done.17 = f32[256,512]{1,0:T(8,128)S(1)} collective-permute-done((f32[256,512]{1,0:T(8,128)S(1)}, f32[256,512]{1,0:T(8,128)S(1)}, u32[]{:S(2)}, u32[]{:S(2)}) %collective-permute-start.17) | collective-permute-done | bytes 524320 | tf_op jit(solution)/shard_map/ppermute | solution.py:23
  358.3 0.9 dynamic-slice_add_fusion
  359.5 16.1 %shard_map.69 = f32[4,512,256]{2,1,0:T(8,128)S(1)} custom-call(bf16[512,7168]{1,0:T(8,128)(2,1)} %add_convert_fusion.1.refs_0_, bf16[512,7168]{1,0:T(8,128)(2,1)} %collective-permute-done.4.refs_1_, bf16[512,7168]{1,0:T(8,128)(2,1)} %add_convert_fusion.refs_2_, bf16[512,7168]{1,0:T(8,128)(2,1)} %collective-permute-done.8.refs_3_, ...), custom_call_target="tpu_custom_call" | custom-call | flops 8455716864 | bytes 38797312 | tf_op jit(solution)/shard_map/pallas_call | solution.py:61
  375.6 13.2 %collective-permute-done.13 = bf16[3,512,512]{2,1,0:T(8,128)(2,1)} collective-permute-done((bf16[3,512,512]{2,1,0:T(8,128)(2,1)}, bf16[3,512,512]{2,1,0:T(8,128)(2,1)}, u32[]{:S(2)}, u32[]{:S(2)}) %collective-permute-start.13) | collective-permute-done | bytes 1572896 | tf_op jit(solution)/shard_map/ppermute | solution.py:23
  388.8 3.2 convert_add_fusion.4
  392.1 1.3 pad_maximum_fusion.1
  394.0 0.6 collective-permute-start.11
  394.8 0.6 collective-permute-start.20
  395.5 1.2 collective-permute-start.21
  396.7 15.6 %shard_map.70 = f32[4,512,128]{2,1,0:T(8,128)S(1)} custom-call(bf16[512,7168]{1,0:T(8,128)(2,1)} %add_convert_fusion.1.refs_0_, bf16[512,7168]{1,0:T(8,128)(2,1)} %collective-permute-done.4.refs_1_, bf16[512,7168]{1,0:T(8,128)(2,1)} %add_convert_fusion.refs_2_, bf16[512,7168]{1,0:T(8,128)(2,1)} %collective-permute-done.8.refs_3_, ...), custom_call_target="tpu_custom_call" | custom-call | flops 4227858432 | bytes 35913728 | tf_op jit(solution)/shard_map/pallas_call | solution.py:61
  412.3 14.4 %collective-permute-done.18 = bf16[3,512,512]{2,1,0:T(8,128)(2,1)S(1)} collective-permute-done((bf16[3,512,512]{2,1,0:T(8,128)(2,1)}, bf16[3,512,512]{2,1,0:T(8,128)(2,1)S(1)}, u32[]{:S(2)}, u32[]{:S(2)}) %collective-permute-start.18) | collective-permute-done | bytes 1572896 | tf_op jit(solution)/shard_map/ppermute | solution.py:23
  426.6 1.8 convert_add_fusion
  428.5 6.4 %collective-permute-done.11.refs_4_ = bf16[128,7168]{1,0:T(8,128)(2,1)S(1)} collective-permute-done((bf16[128,7168]{1,0:T(8,128)(2,1)S(1)}, bf16[128,7168]{1,0:T(8,128)(2,1)S(1)}, u32[]{:S(2)}, u32[]{:S(2)}) %collective-permute-start.11) | collective-permute-done | bytes 1835040 | tf_op jit(solution)/shard_map/ppermute | solution.py:19
  435.2 1.1 collective-permute-start.22
  436.5 0.6 collective-permute-start.24
  437.1 1.2 collective-permute-start.25
  438.4 15.6 %shard_map.71 = f32[4,512,128]{2,1,0:T(8,128)S(1)} custom-call(bf16[512,7168]{1,0:T(8,128)(2,1)} %add_convert_fusion.1.refs_0_, bf16[512,7168]{1,0:T(8,128)(2,1)} %collective-permute-done.4.refs_1_, bf16[512,7168]{1,0:T(8,128)(2,1)} %add_convert_fusion.refs_2_, bf16[512,7168]{1,0:T(8,128)(2,1)} %collective-permute-done.8.refs_3_, ...), custom_call_target="tpu_custom_call" | custom-call | flops 4227858432 | bytes 35913728 | tf_op jit(solution)/shard_map/pallas_call | solution.py:61
  454.0 2.6 collective-permute-done.22.refs_11_
  456.7 0.9 collective-permute-start.26
  457.7 0.6 collective-permute-start.28
  458.4 1.2 collective-permute-start.29
  459.6 7.3 %collective-permute-done.28.refs_19_ = f32[512,128]{1,0:T(8,128)S(1)} collective-permute-done((f32[512,128]{1,0:T(8,128)S(1)}, f32[512,128]{1,0:T(8,128)S(1)}, u32[]{:S(2)}, u32[]{:S(2)}) %collective-permute-start.28) | collective-permute-done | bytes 262176 | tf_op jit(solution)/shard_map/ppermute | solution.py:14
  466.9 4.7 collective-permute-done.29.refs_20_
  471.7 0.6 copy-done.4
  472.5 0.9 pad_maximum_fusion.4
  473.4 1.2 collective-permute-start.30
  474.7 2.1 multiply_add_fusion
  476.8 11.0 %collective-permute-done.30.refs_21_ = bf16[4,512,128]{2,1,0:T(8,128)(2,1)} collective-permute-done((bf16[4,512,128]{2,1,0:T(8,128)(2,1)}, bf16[4,512,128]{2,1,0:T(8,128)(2,1)}, u32[]{:S(2)}, u32[]{:S(2)}) %collective-permute-start.30) | collective-permute-done | bytes 524320 | tf_op jit(solution)/shard_map/ppermute | solution.py:23
  487.8 0.9 copy-done.1
  488.8 0.9 copy-done.3
  489.7 0.9 copy-done.5
  490.7 1.0 copy-done.7
  491.7 8.5 %shard_map.72 = f32[512,4,512]{2,1,0:T(4,128)} custom-call(s32[2]{0:T(128)S(1)} %pad_add_fusion.at_ref, f32[512,4,512]{2,1,0:T(4,128)} %old.1, f32[512,512]{1,0:T(8,128)} %convert_add_fusion.3.refs_0_, f32[512,512]{1,0:T(8,128)} %get-tuple-element.87.refs_1_, f32[512,512]{1,0:T(8,128)} %get-tuple-element.88.refs_2_, f32[512,512]{1,0:T(8,128)} %get-tuple-element.89.refs_3_, ...), custom_call_target="tpu_custom_call" | custom-call | tf_op jit(solution)/shard_map/pallas_call | solution.py:133
  (72 shorter events, 2.8 us)
Async XLA Ops:
  7.2 66.0 %all-gather.2.cloned.1.call-start = ((), (), s32[]{:S(2)}) async-start(), calls=%async_computation | async-start | bytes 3899392 | tf_op jit(solution)/shard_map/all_gather | solution.py:170
  7.9 179.1 %collective-permute-start.7 = (bf16[512,7168]{1,0:T(8,128)(2,1)}, bf16[512,7168]{1,0:T(8,128)(2,1)}, u32[]{:S(2)}, u32[]{:S(2)}) collective-permute-start(bf16[512,7168]{1,0:T(8,128)(2,1)} %param.7), channel_id=1, source_target_pairs={{0,4},{2,6},{4,0},{6,2},{8,12},{10,14},{12,8},{14,10},{16,20},{18,... | collective-permute-start | bytes 22020104 | tf_op jit(solution)/shard_map/ppermute | solution.py:14
  10.9 5.2 %collective-permute-start.2 = (bf16[128,512]{1,0:T(8,128)(2,1)}, bf16[128,512]{1,0:T(8,128)(2,1)S(1)}, u32[]{:S(2)}, u32[]{:S(2)}) collective-permute-start(bf16[128,512]{1,0:T(8,128)(2,1)} %param.5), channel_id=1, source_target_pairs={{0,1},{1,0},{2,3},{3,2},{4,5},{5,4},{6,7},{7,6},{8,9},{9,8},{10,11... | collective-permute-start | bytes 393224 | tf_op jit(solution)/shard_map/ppermute | solution.py:23
  82.4 104.6 %copy-start.8 = (bf16[256,7168]{1,0:T(8,128)(2,1)S(1)}, bf16[256,7168]{1,0:T(8,128)(2,1)}, u32[]{:S(2)}) copy-start(bf16[256,7168]{1,0:T(8,128)(2,1)} %all-gather.2.cloned.1.call-done.refs_7_.refs_6_) | copy-start | bytes 11010052
  82.4 174.8 %collective-permute-start.4 = (bf16[512,7168]{1,0:T(8,128)(2,1)}, bf16[512,7168]{1,0:T(8,128)(2,1)}, u32[]{:S(2)}, u32[]{:S(2)}) collective-permute-start(bf16[512,7168]{1,0:T(8,128)(2,1)} %add_convert_fusion.1.refs_0_), channel_id=1, source_target_pairs={{0,2},{2,0},{4,6},{6,4},{8,10},{10,8},{12,14},{14,12},{16,18},{18,... | collective-permute-start | bytes 22020104 | tf_op jit(solution)/shard_map/ppermute | solution.py:14
  89.5 167.8 %collective-permute-start = (bf16[256,7168]{1,0:T(8,128)(2,1)}, bf16[256,7168]{1,0:T(8,128)(2,1)}, u32[]{:S(2)}, u32[]{:S(2)}) collective-permute-start(bf16[256,7168]{1,0:T(8,128)(2,1)} %get-tuple-element.125), channel_id=1, source_target_pairs={{0,8},{2,10},{4,12},{6,14},{8,16},{10,18},{12,20},{14,22},{16,24},... | collective-permute-start | bytes 11010056 | tf_op jit(solution)/shard_map/ppermute | solution.py:19
  91.2 166.1 %collective-permute-start.1 = (bf16[256,7168]{1,0:T(8,128)(2,1)}, bf16[256,7168]{1,0:T(8,128)(2,1)}, u32[]{:S(2)}, u32[]{:S(2)}) collective-permute-start(bf16[256,7168]{1,0:T(8,128)(2,1)} %get-tuple-element.124), channel_id=1, source_target_pairs={{0,8},{2,10},{4,12},{6,14},{8,16},{10,18},{12,20},{14,22},{16,24},... | collective-permute-start | bytes 11010056 | tf_op jit(solution)/shard_map/ppermute | solution.py:19
  92.0 95.0 %collective-permute-start.6 = (bf16[256,512]{1,0:T(8,128)(2,1)S(1)}, bf16[256,512]{1,0:T(8,128)(2,1)S(1)}, u32[]{:S(2)}, u32[]{:S(2)}) collective-permute-start(bf16[256,512]{1,0:T(8,128)(2,1)S(1)} %maximum_select_fusion), channel_id=1, source_target_pairs={{0,4},{2,6},{4,0},{6,2},{8,12},{10,14},{12,8},{14,10},{16,20},{18,... | collective-permute-start | bytes 786440 | tf_op jit(solution)/shard_map/ppermute | solution.py:14
  195.2 95.0 %collective-permute-start.8 = (bf16[512,7168]{1,0:T(8,128)(2,1)}, bf16[512,7168]{1,0:T(8,128)(2,1)}, u32[]{:S(2)}, u32[]{:S(2)}) collective-permute-start(bf16[512,7168]{1,0:T(8,128)(2,1)} %add_convert_fusion.refs_2_), channel_id=1, source_target_pairs={{0,2},{2,0},{4,6},{6,4},{8,10},{10,8},{12,14},{14,12},{16,18},{18,... | collective-permute-start | bytes 22020104 | tf_op jit(solution)/shard_map/ppermute | solution.py:14
  195.2 62.1 %collective-permute-start.3 = (bf16[256,512]{1,0:T(8,128)(2,1)S(1)}, bf16[256,512]{1,0:T(8,128)(2,1)S(1)}, u32[]{:S(2)}, u32[]{:S(2)}) collective-permute-start(bf16[256,512]{1,0:T(8,128)(2,1)S(1)} %maximum_select_fusion), channel_id=1, source_target_pairs={{0,8},{2,10},{4,12},{6,14},{8,16},{10,18},{12,20},{14,22},{16,24},... | collective-permute-start | bytes 786440 | tf_op jit(solution)/shard_map/ppermute | solution.py:19
  257.3 86.8 %collective-permute-start.5 = (bf16[256,7168]{1,0:T(8,128)(2,1)}, bf16[256,7168]{1,0:T(8,128)(2,1)S(1)}, u32[]{:S(2)}, u32[]{:S(2)}) collective-permute-start(bf16[256,7168]{1,0:T(8,128)(2,1)} %collective-permute-done.refs_4_), channel_id=1, source_target_pairs={{0,8},{2,10},{4,12},{6,14},{8,16},{10,18},{12,20},{14,22},{16,24},... | collective-permute-start | bytes 11010056 | tf_op jit(solution)/shard_map/ppermute | solution.py:19
  265.9 81.7 %collective-permute-start.16 = (bf16[1,512,512]{2,1,0:T(8,128)(2,1)S(1)}, bf16[1,512,512]{2,1,0:T(8,128)(2,1)S(1)}, u32[]{:S(2)}, u32[]{:S(2)}) collective-permute-start(bf16[1,512,512]{2,1,0:T(8,128)(2,1)S(1)} %convert_bitcast_fusion.3), channel_id=1, source_target_pairs={{0,1},{1,0},{2,3},{3,2},{4,5},{5,4},{6,7},{7,6},{8,9},{9,8},{10,11... | collective-permute-start | bytes 1572872 | tf_op jit(solution)/shard_map/ppermute | solution.py:23
  267.5 91.8 %collective-permute-start.15 = (bf16[256,512]{1,0:T(8,128)(2,1)S(1)}, bf16[256,512]{1,0:T(8,128)(2,1)S(1)}, u32[]{:S(2)}, u32[]{:S(2)}) collective-permute-start(bf16[256,512]{1,0:T(8,128)(2,1)S(1)} %collective-permute-done.3.refs_6_), channel_id=1, source_target_pairs={{0,8},{2,10},{4,12},{6,14},{8,16},{10,18},{12,20},{14,22},{16,24},... | collective-permute-start | bytes 786440 | tf_op jit(solution)/shard_map/ppermute | solution.py:19
  319.8 23.7 %collective-permute-start.10 = (f32[512,512]{1,0:T(8,128)S(1)}, f32[512,512]{1,0:T(8,128)S(1)}, u32[]{:S(2)}, u32[]{:S(2)}) collective-permute-start(f32[512,512]{1,0:T(8,128)S(1)} %get-tuple-element.127), channel_id=1, source_target_pairs={{0,4},{2,6},{4,0},{6,2},{8,12},{10,14},{12,8},{14,10},{16,20},{18,... | collective-permute-start | bytes 3145736 | tf_op jit(solution)/shard_map/ppermute | solution.py:14
  320.4 23.7 %collective-permute-start.9 = (f32[512,512]{1,0:T(8,128)S(1)}, f32[512,512]{1,0:T(8,128)S(1)}, u32[]{:S(2)}, u32[]{:S(2)}) collective-permute-start(f32[512,512]{1,0:T(8,128)S(1)} %get-tuple-element.128), channel_id=1, source_target_pairs={{0,2},{2,0},{4,6},{6,4},{8,10},{10,8},{12,14},{14,12},{16,18},{18,... | collective-permute-start | bytes 3145736 | tf_op jit(solution)/shard_map/ppermute | solution.py:14
  343.5 14.9 %collective-permute-start.17 = (f32[256,512]{1,0:T(8,128)S(1)}, f32[256,512]{1,0:T(8,128)S(1)}, u32[]{:S(2)}, u32[]{:S(2)}) collective-permute-start(f32[256,512]{1,0:T(8,128)S(1)} %constant_dynamic-slice_fusion), channel_id=1, source_target_pairs={{0,1},{1,0},{2,3},{3,2},{4,5},{5,4},{6,7},{7,6},{8,9},{9,8},{10,11... | collective-permute-start | bytes 1572872 | tf_op jit(solution)/shard_map/ppermute | solution.py:23
  345.6 43.2 %collective-permute-start.13 = (bf16[3,512,512]{2,1,0:T(8,128)(2,1)}, bf16[3,512,512]{2,1,0:T(8,128)(2,1)}, u32[]{:S(2)}, u32[]{:S(2)}) collective-permute-start(bf16[3,512,512]{2,1,0:T(8,128)(2,1)} %pad_maximum_fusion), channel_id=1, source_target_pairs={{0,1},{1,0},{2,3},{3,2},{4,5},{5,4},{6,7},{7,6},{8,9},{9,8},{10,11... | collective-permute-start | bytes 4718600 | tf_op jit(solution)/shard_map/ppermute | solution.py:23
  347.0 44.9 %collective-permute-start.12 = (bf16[128,7168]{1,0:T(8,128)(2,1)}, bf16[128,7168]{1,0:T(8,128)(2,1)S(1)}, u32[]{:S(2)}, u32[]{:S(2)}) collective-permute-start(bf16[128,7168]{1,0:T(8,128)(2,1)} %get-tuple-element.69), channel_id=1, source_target_pairs={{0,8},{2,10},{4,12},{6,14},{8,16},{10,18},{12,20},{14,22},{16,24},... | collective-permute-start | bytes 5505032 | tf_op jit(solution)/shard_map/ppermute | solution.py:19
  359.2 32.7 %collective-permute-start.14 = (f32[512,512]{1,0:T(8,128)}, f32[512,512]{1,0:T(8,128)S(1)}, u32[]{:S(2)}, u32[]{:S(2)}) collective-permute-start(f32[512,512]{1,0:T(8,128)} %get-tuple-element.73), channel_id=1, source_target_pairs={{0,6},{2,4},{4,2},{6,0},{8,14},{10,12},{12,10},{14,8},{16,22},{18,... | collective-permute-start | bytes 3145736 | tf_op jit(solution)/shard_map/ppermute | solution.py:14
  392.0 2.1 copy-start.9
  393.4 33.3 %collective-permute-start.18 = (bf16[3,512,512]{2,1,0:T(8,128)(2,1)}, bf16[3,512,512]{2,1,0:T(8,128)(2,1)S(1)}, u32[]{:S(2)}, u32[]{:S(2)}) collective-permute-start(bf16[3,512,512]{2,1,0:T(8,128)(2,1)} %pad_maximum_fusion.1), channel_id=1, source_target_pairs={{0,1},{1,0},{2,3},{3,2},{4,5},{5,4},{6,7},{7,6},{8,9},{9,8},{10,11... | collective-permute-start | bytes 4718600 | tf_op jit(solution)/shard_map/ppermute | solution.py:23
  394.0 40.9 %collective-permute-start.11 = (bf16[128,7168]{1,0:T(8,128)(2,1)S(1)}, bf16[128,7168]{1,0:T(8,128)(2,1)S(1)}, u32[]{:S(2)}, u32[]{:S(2)}) collective-permute-start(bf16[128,7168]{1,0:T(8,128)(2,1)S(1)} %copy-done.9), channel_id=1, source_target_pairs={{0,8},{2,10},{4,12},{6,14},{8,16},{10,18},{12,20},{14,22},{16,24},... | collective-permute-start | bytes 5505032 | tf_op jit(solution)/shard_map/ppermute | solution.py:19
  394.8 40.2 %collective-permute-start.19 = (f32[512,256]{1,0:T(8,128)S(1)}, f32[512,256]{1,0:T(8,128)S(1)}, u32[]{:S(2)}, u32[]{:S(2)}) collective-permute-start(f32[512,256]{1,0:T(8,128)S(1)} %get-tuple-element.134), channel_id=1, source_target_pairs={{0,2},{2,0},{4,6},{6,4},{8,10},{10,8},{12,14},{14,12},{16,18},{18,... | collective-permute-start | bytes 1572872 | tf_op jit(solution)/shard_map/ppermute | solution.py:14
  394.8 40.1 %collective-permute-start.20 = (f32[512,256]{1,0:T(8,128)S(1)}, f32[512,256]{1,0:T(8,128)S(1)}, u32[]{:S(2)}, u32[]{:S(2)}) collective-permute-start(f32[512,256]{1,0:T(8,128)S(1)} %get-tuple-element.133), channel_id=1, source_target_pairs={{0,4},{2,6},{4,0},{6,2},{8,12},{10,14},{12,8},{14,10},{16,20},{18,... | collective-permute-start | bytes 1572872 | tf_op jit(solution)/shard_map/ppermute | solution.py:14
  395.5 39.5 %collective-permute-start.21 = (f32[512,256]{1,0:T(8,128)S(1)}, f32[512,256]{1,0:T(8,128)S(1)}, u32[]{:S(2)}, u32[]{:S(2)}) collective-permute-start(f32[512,256]{1,0:T(8,128)S(1)} %get-tuple-element.132), channel_id=1, source_target_pairs={{0,6},{2,4},{4,2},{6,0},{8,14},{10,12},{12,10},{14,8},{16,22},{18,... | collective-permute-start | bytes 1572872 | tf_op jit(solution)/shard_map/ppermute | solution.py:14
  435.2 21.4 %collective-permute-start.22 = (bf16[4,512,256]{2,1,0:T(8,128)(2,1)S(1)}, bf16[4,512,256]{2,1,0:T(8,128)(2,1)S(1)}, u32[]{:S(2)}, u32[]{:S(2)}) collective-permute-start(bf16[4,512,256]{2,1,0:T(8,128)(2,1)S(1)} %pad_maximum_fusion.2), channel_id=1, source_target_pairs={{0,1},{1,0},{2,3},{3,2},{4,5},{5,4},{6,7},{7,6},{8,9},{9,8},{10,11... | collective-permute-start | bytes 3145736 | tf_op jit(solution)/shard_map/ppermute | solution.py:23
  436.4 17.5 %collective-permute-start.23 = (f32[512,128]{1,0:T(8,128)S(1)}, f32[512,128]{1,0:T(8,128)S(1)}, u32[]{:S(2)}, u32[]{:S(2)}) collective-permute-start(f32[512,128]{1,0:T(8,128)S(1)} %get-tuple-element.148), channel_id=1, source_target_pairs={{0,2},{2,0},{4,6},{6,4},{8,10},{10,8},{12,14},{14,12},{16,18},{18,... | collective-permute-start | bytes 786440 | tf_op jit(solution)/shard_map/ppermute | solution.py:14
  436.5 17.4 %collective-permute-start.24 = (f32[512,128]{1,0:T(8,128)S(1)}, f32[512,128]{1,0:T(8,128)S(1)}, u32[]{:S(2)}, u32[]{:S(2)}) collective-permute-start(f32[512,128]{1,0:T(8,128)S(1)} %get-tuple-element.147), channel_id=1, source_target_pairs={{0,4},{2,6},{4,0},{6,2},{8,12},{10,14},{12,8},{14,10},{16,20},{18,... | collective-permute-start | bytes 786440 | tf_op jit(solution)/shard_map/ppermute | solution.py:14
  437.1 16.8 %collective-permute-start.25 = (f32[512,128]{1,0:T(8,128)S(1)}, f32[512,128]{1,0:T(8,128)S(1)}, u32[]{:S(2)}, u32[]{:S(2)}) collective-permute-start(f32[512,128]{1,0:T(8,128)S(1)} %get-tuple-element.146), channel_id=1, source_target_pairs={{0,6},{2,4},{4,2},{6,0},{8,14},{10,12},{12,10},{14,8},{16,22},{18,... | collective-permute-start | bytes 786440 | tf_op jit(solution)/shard_map/ppermute | solution.py:14
  456.6 16.8 %copy-start.10 = (bf16[4,512,256]{2,1,0:T(8,128)(2,1)}, bf16[4,512,256]{2,1,0:T(8,128)(2,1)S(1)}, u32[]{:S(2)}) copy-start(bf16[4,512,256]{2,1,0:T(8,128)(2,1)S(1)} %collective-permute-done.22.refs_11_) | copy-start | bytes 3145732
  456.7 14.9 %collective-permute-start.26 = (bf16[4,512,128]{2,1,0:T(8,128)(2,1)S(1)}, bf16[4,512,128]{2,1,0:T(8,128)(2,1)S(1)}, u32[]{:S(2)}, u32[]{:S(2)}) collective-permute-start(bf16[4,512,128]{2,1,0:T(8,128)(2,1)S(1)} %pad_maximum_fusion.3), channel_id=1, source_target_pairs={{0,1},{1,0},{2,3},{3,2},{4,5},{5,4},{6,7},{7,6},{8,9},{9,8},{10,11... | collective-permute-start | bytes 1572872 | tf_op jit(solution)/shard_map/ppermute | solution.py:23
  457.7 1.9 collective-permute-start.27
  457.7 9.2 %collective-permute-start.28 = (f32[512,128]{1,0:T(8,128)S(1)}, f32[512,128]{1,0:T(8,128)S(1)}, u32[]{:S(2)}, u32[]{:S(2)}) collective-permute-start(f32[512,128]{1,0:T(8,128)S(1)} %get-tuple-element.143), channel_id=1, source_target_pairs={{0,4},{2,6},{4,0},{6,2},{8,12},{10,14},{12,8},{14,10},{16,20},{18,... | collective-permute-start | bytes 786440 | tf_op jit(solution)/shard_map/ppermute | solution.py:14
  458.4 13.3 %collective-permute-start.29 = (f32[512,128]{1,0:T(8,128)S(1)}, f32[512,128]{1,0:T(8,128)S(1)}, u32[]{:S(2)}, u32[]{:S(2)}) collective-permute-start(f32[512,128]{1,0:T(8,128)S(1)} %get-tuple-element.142), channel_id=1, source_target_pairs={{0,6},{2,4},{4,2},{6,0},{8,14},{10,12},{12,10},{14,8},{16,22},{18,... | collective-permute-start | bytes 786440 | tf_op jit(solution)/shard_map/ppermute | solution.py:14
  459.6 12.1 %copy-start = (f32[512,128]{1,0:T(8,128)}, f32[512,128]{1,0:T(8,128)S(1)}, u32[]{:S(2)}) copy-start(f32[512,128]{1,0:T(8,128)S(1)} %collective-permute-done.27.refs_18_) | copy-start | bytes 786436
  466.9 4.8 copy-start.2
  471.6 0.7 copy-start.4
  471.6 0.9 copy-start.6
  473.4 14.4 %collective-permute-start.30 = (bf16[4,512,128]{2,1,0:T(8,128)(2,1)}, bf16[4,512,128]{2,1,0:T(8,128)(2,1)}, u32[]{:S(2)}, u32[]{:S(2)}) collective-permute-start(bf16[4,512,128]{2,1,0:T(8,128)(2,1)} %pad_maximum_fusion.4), channel_id=1, source_target_pairs={{0,1},{1,0},{2,3},{3,2},{4,5},{5,4},{6,7},{7,6},{8,9},{9,8},{10,11... | collective-permute-start | bytes 1572872 | tf_op jit(solution)/shard_map/ppermute | solution.py:23
  487.8 1.0 copy-start.1
  488.8 0.9 copy-start.3
  489.7 0.9 copy-start.5
  490.7 1.0 copy-start.7
Sparse Core Ops, SparseCore 0:
  10.3 62.8 all-gather.1

commit v10 on v9

--- a/solution.py
+++ b/solution.py
@@ -57,7 +57,7 @@
 def panel_products(group, raws, columns, cotangent_all):
     block, width = group[0].shape
     tokens, rows = columns.shape
-    depth = max(d for d in range(128, 1025, 128) if width % d == 0)
+    depth = max(d for d in range(128, 2049, 128) if width % d == 0)
     return pl.pallas_call(
         products_kernel,
         grid=(width // depth,),
@@ -111,7 +111,7 @@
         def _():
             start = 0
             for mine, other in two:
-                value = pick(u, [ref[...] for ref in mine]) + other[u].astype(jnp.float32)
+                value = pick(u, [ref[...].astype(jnp.float32) for ref in mine]) + other[u].astype(jnp.float32)
                 end = start + value.shape[1]
                 out[:, s, start:end] = kept[:, start:end] + added * value
                 start = end
@@ -154,8 +154,6 @@
     phase = lax.optimization_barrier
 
     half, quarter = block // 2, block // 4
-    moving = [from_behind(accumulated[:half], GROUP), from_behind(accumulated[half:], GROUP)]
-    across_raw = swap(accumulated, 2)
     if paired:
         other = trade(activations)
         columns = jnp.where(
@@ -165,8 +163,11 @@
         )
     else:
         columns = lax.all_gather(activations, "col", axis=0, tiled=True)
-    behind = from_behind(columns, GROUP)
-    across_columns = swap(columns, 2)
+    raw, behind, across_columns = phase(
+        (accumulated, from_behind(columns, GROUP), swap(columns, 2))
+    )
+    moving = from_behind(raw, GROUP)
+    across_raw = swap(raw, 2)
     cotangent_all = lax.all_gather(cotangent, "row", axis=0, tiled=True)
 
     def products(raws, columns):
@@ -178,7 +179,7 @@
     def over_columns(sums):
         if not paired:
             return [None] * len(sums)
-        return trade(jnp.stack(sums).astype(jnp.bfloat16))
+        return trade(jnp.stack([a.astype(jnp.bfloat16) for a in sums]))
 
     def added(sums, others):
         if not paired:
@@ -187,7 +188,7 @@
 
     own = gradient_tile(columns, cotangent_all, accumulated)
     beside = swap(own, 1)
-    moving, behind, own, beside = phase((moving, behind, own, beside))
+    moving, own, beside = phase((moving, own, beside))
 
     sums = [None] * (steps + 1)
     made, diagonal = None, None
@@ -195,10 +196,10 @@
         arrived, arrived_columns = moving, behind
         behind = from_behind(arrived_columns, GROUP)
         if step < steps - 1:
-            moving = [from_behind(piece, GROUP) for piece in arrived]
+            moving = from_behind(arrived, GROUP)
         else:
-            moving = from_behind(arrived[0], GROUP)
-            quarters = jnp.split(arrived[1], 2)
+            moving = from_behind(arrived[:half], GROUP)
+            quarters = jnp.split(arrived[half:], 2)
         if step == 1:
             own_products = [block_product(own, panel) for panel in (own, beside)]
             across = gradient_tile(across_columns, cotangent_all, across_raw)
@@ -212,7 +213,7 @@
         else:
             handed = to_owners(made)
             sums[steps - step + 1] = added(handed, over_columns(handed))
-        made = products(arrived, arrived_columns)
+        made = products([arrived], arrived_columns)
         if step == steps - 1:
             handed = [made[0], swap(made[1], 1), swap(made[2], 2), made[3]]
             moving, quarters, handed = phase((moving, quarters, handed))
@@ -241,6 +242,8 @@
     last, handed, made = phase((last, handed, made))
 
     last.append((handed, over_columns(handed)))
+    if paired:
+        made = [made[0], *(made[u].astype(jnp.bfloat16) for u in range(1, GROUP))]
     handed = to_owners(made)
     last, handed = phase((last, handed))
     last.append((handed, over_columns(handed)))

time: 508 us -> 448 us (0.88)
  waiting for transfers between devices: 299 us -> 242 us
  Pallas kernels: 81.7 us -> 76.3 us
    ppermute x7 -> x6, waiting for transfers between devices: 66.7 us -> 24.6 us  [from_behind(): lax.ppermute(array, 'row', [(i, (i + by) % count) for i in range(count)])]
    ppermute x8, waiting for transfers between devices: 54.5 us -> 40.4 us  [trade(): return lax.ppermute(array, 'col', [(0, 1), (1, 0)])]
    all_gather x1, waiting for transfers between devices: 56.1 us -> 48.9 us  [body(): cotangent_all = lax.all_gather(cotangent, 'row', axis=0, tiled=True)]
    ppermute x16, waiting for transfers between devices: 121 us -> 127 us  [swap(): return lax.ppermute(array, 'row', [(i, i ^ mask) for i in range(count)])]
    pallas_call x4, Pallas kernels: 73.2 us -> 68.1 us  [panel_products(): pl.pallas_call(products_kernel, grid=(width // depth,), in_specs=[pl.Bloc...]
  transfers between devices with their start and end apart: 32 -> 31, of which waited for: 13 -> 18; matrix products, arithmetic and copies ran while one was open for 16% -> 17% of each run, Pallas kernels for 14% -> 15%
where the time goes in v10:
time: 448 us
  waiting for transfers between devices  242 us (54%)
  Pallas kernels  76.3 us (17%)
  matrix products  52.4 us (12%)
  starting transfers between devices  27.2 us (6%)
  local copies, waits for them, and re-layouts  20.2 us (5%)
  other arithmetic  15.2 us (3%)
  between operations  14.4 us (3%)
    ppermute x16, waiting for transfers between devices, swap(): return lax.ppermute(array, 'row', [(i, i ^ mask) for i in range(count)])  127 us
    pallas_call x4, Pallas kernels, panel_products(): pl.pallas_call(products_kernel, grid=(width // depth,), in_specs=[pl.Bloc...  68.1 us
    all_gather x1, waiting for transfers between devices, body(): cotangent_all = lax.all_gather(cotangent, 'row', axis=0, tiled=True)  48.9 us
    ppermute x8, waiting for transfers between devices, trade(): return lax.ppermute(array, 'col', [(0, 1), (1, 0)])  40.4 us
    dot_general x4, matrix products, block_product(): lax.dot_general(left, right, (((1,), (1,)), ((), ())), preferred_element_...  34.8 us
    ppermute x6, waiting for transfers between devices, from_behind(): lax.ppermute(array, 'row', [(i, (i + by) % count) for i in range(count)])  24.6 us
    dot_general x2, matrix products, gradient_tile(): lax.dot_general(columns, cotangent_all, (((0,), (0,)), ((), ())), preferr...  17.6 us
    ppermute x8, starting transfers between devices, trade(): return lax.ppermute(array, 'col', [(0, 1), (1, 0)])  11.7 us
  transfers between devices with their start and end apart: 31, of which 18 were waited for; matrix products, arithmetic and copies ran while one was open for 17% of the time, Pallas kernels for 15%

profile of v10, /device:TPU:0, one launch (start us, length us, event | category | flops | bytes accessed | tf_op | source)
XLA Modules:
  0.0 447.9 jit_solution(2803680728216236214)
XLA Ops:
  7.2 0.7 all-gather.2.cloned.1.call-update
  7.9 3.0 collective-permute-start
  10.9 3.7 collective-permute-done
  14.6 1.0 maximum_select_fusion
  15.7 1.9 collective-permute-start.1
  17.5 1.5 collective-permute-start.2
  19.0 6.1 %collective-permute-done.1.refs_5_ = bf16[256,512]{1,0:T(8,128)(2,1)S(1)} collective-permute-done((bf16[256,512]{1,0:T(8,128)(2,1)S(1)}, bf16[256,512]{1,0:T(8,128)(2,1)S(1)}, u32[]{:S(2)}, u32[]{:S(2)}) %collective-permute-start.1) | collective-permute-done | bytes 262176 | tf_op jit(solution)/shard_map/ppermute | solution.py:19
  25.2 1.5 collective-permute-done.2
  26.7 2.5 collective-permute-start.6
  29.2 1.8 collective-permute-start.3
  30.9 48.9 %all-gather.2.cloned.1.call-done.refs_6_ = bf16[256,7168]{1,0:T(8,128)(2,1)} async-done(((bf16[16,7168]{1,0:T(8,128)(2,1)}), bf16[256,7168]{1,0:T(8,128)(2,1)}) %all-gather.2.cloned.1.call-update) | async-done | bytes 3670032 | tf_op jit(solution)/shard_map/all_gather | solution.py:171
  79.9 9.3 %add_convert_fusion.1.refs_0_ = bf16[512,7168]{1,0:T(8,128)(2,1)} fusion(bf16[512,7168]{1,0:T(8,128)(2,1)} %param.7, bf16[256,512]{1,0:T(8,128)(2,1)S(1)} %maximum_select_fusion, bf16[256,7168]{1,0:T(8,128)(2,1)} %all-gather.2.cloned.1.call-done.refs_6_), kind=kOutput, calls=%fused_computation.1 | convolution fusion | flops 1890058240 | bytes 18612224 | tf_op jit(solution)/shard_map/dot_general | solution.py:27
  89.5 104.6 %collective-permute-done.6 = bf16[512,7168]{1,0:T(8,128)(2,1)} collective-permute-done((bf16[512,7168]{1,0:T(8,128)(2,1)}, bf16[512,7168]{1,0:T(8,128)(2,1)}, u32[]{:S(2)}, u32[]{:S(2)}) %collective-permute-start.6) | collective-permute-done | bytes 7340064 | tf_op jit(solution)/shard_map/ppermute | solution.py:14
  194.1 8.3 %add_convert_fusion.refs_2_ = bf16[512,7168]{1,0:T(8,128)(2,1)} fusion(bf16[512,7168]{1,0:T(8,128)(2,1)} %collective-permute-done.6, bf16[256,512]{1,0:T(8,128)(2,1)S(1)} %collective-permute-done.2, bf16[256,7168]{1,0:T(8,128)(2,1)S(1)} %copy-done), kind=kOutput, calls=%fused_computation | convolution fusion | flops 1890058240 | bytes 18612224 | tf_op jit(solution)/shard_map/dot_general | solution.py:27
  202.4 3.3 collective-permute-done.3.refs_4_
  205.7 4.1 slice.66
  209.8 8.5 %fusion.3 = f32[512,512]{1,0:T(8,128)S(1)} fusion(bf16[512,7168]{1,0:T(8,128)(2,1)} %add_convert_fusion.1.refs_0_, bf16[512,7168]{1,0:T(8,128)(2,1)} %collective-permute-done.4.refs_1_), kind=kOutput, calls=%fused_computation.60 | convolution fusion | flops 3758096384 | bytes 15728640 | tf_op jit(solution)/shard_map/dot_general | solution.py:34
  218.4 1.6 collective-permute-start.15
  220.0 9.3 %fusion.2 = f32[512,512]{1,0:T(8,128)S(1)} fusion(bf16[512,7168]{1,0:T(8,128)(2,1)} %add_convert_fusion.1.refs_0_), kind=kOutput, calls=%fused_computation.59 | convolution fusion | flops 3758096384 | bytes 8388608 | tf_op jit(solution)/shard_map/dot_general | solution.py:34
  229.3 4.3 fusion
  234.2 25.3 %shard_map.68 = f32[4,512,512]{2,1,0:T(8,128)} custom-call(bf16[512,7168]{1,0:T(8,128)(2,1)} %add_convert_fusion.1.refs_0_, bf16[512,7168]{1,0:T(8,128)(2,1)} %collective-permute-done.4.refs_1_, bf16[512,7168]{1,0:T(8,128)(2,1)} %add_convert_fusion.refs_2_, bf16[512,7168]{1,0:T(8,128)(2,1)} %collective-permute-done.7.refs_3_, ...), custom_call_target="tpu_custom_call" | custom-call | flops 16911433728 | bytes 44564480 | tf_op jit(solution)/shard_map/pallas_call | solution.py:61
  259.5 3.6 slice_bitcast_fusion
  263.1 1.1 collective-permute-start.9
  264.2 8.5 %fusion.4 = f32[512,512]{1,0:T(8,128)S(1)} fusion(bf16[512,7168]{1,0:T(8,128)(2,1)} %add_convert_fusion.1.refs_0_, bf16[512,7168]{1,0:T(8,128)(2,1)} %add_convert_fusion.refs_2_), kind=kOutput, calls=%fused_computation.61 | convolution fusion | flops 3758096384 | bytes 15728640 | tf_op jit(solution)/shard_map/dot_general | solution.py:34
  273.3 0.9 dynamic-slice_add_fusion
  274.3 14.3 %collective-permute-done.9 = f32[512,512]{1,0:T(8,128)S(1)} collective-permute-done((f32[512,512]{1,0:T(8,128)S(1)}, f32[512,512]{1,0:T(8,128)S(1)}, u32[]{:S(2)}, u32[]{:S(2)}) %collective-permute-start.9) | collective-permute-done | bytes 1048608 | tf_op jit(solution)/shard_map/ppermute | solution.py:14
  288.6 5.0 %collective-permute-done.5.refs_4_ = bf16[256,7168]{1,0:T(8,128)(2,1)S(1)} collective-permute-done((bf16[256,7168]{1,0:T(8,128)(2,1)}, bf16[256,7168]{1,0:T(8,128)(2,1)S(1)}, u32[]{:S(2)}, u32[]{:S(2)}) %collective-permute-start.5) | collective-permute-done | bytes 3670048 | tf_op jit(solution)/shard_map/ppermute | solution.py:19
  293.8 1.3 pad_maximum_fusion
  295.1 2.0 collective-permute-start.12
  297.2 8.5 %fusion.5 = f32[512,512]{1,0:T(8,128)S(1)} fusion(bf16[512,7168]{1,0:T(8,128)(2,1)} %add_convert_fusion.1.refs_0_, bf16[512,7168]{1,0:T(8,128)(2,1)} %collective-permute-done.7.refs_3_), kind=kOutput, calls=%fused_computation.62 | convolution fusion | flops 3758096384 | bytes 15728640 | tf_op jit(solution)/shard_map/dot_general | solution.py:34
  305.8 0.7 copy-done.17
  306.6 14.6 %shard_map.69 = f32[4,512,256]{2,1,0:T(8,128)S(1)} custom-call(bf16[512,7168]{1,0:T(8,128)(2,1)} %add_convert_fusion.1.refs_0_, bf16[512,7168]{1,0:T(8,128)(2,1)} %collective-permute-done.4.refs_1_, bf16[512,7168]{1,0:T(8,128)(2,1)} %add_convert_fusion.refs_2_, bf16[512,7168]{1,0:T(8,128)(2,1)} %collective-permute-done.7.refs_3_, ...), custom_call_target="tpu_custom_call" | custom-call | flops 8455716864 | bytes 38797312 | tf_op jit(solution)/shard_map/pallas_call | solution.py:61
  321.2 5.8 %collective-permute-done.12 = bf16[3,512,512]{2,1,0:T(8,128)(2,1)} collective-permute-done((bf16[3,512,512]{2,1,0:T(8,128)(2,1)}, bf16[3,512,512]{2,1,0:T(8,128)(2,1)}, u32[]{:S(2)}, u32[]{:S(2)}) %collective-permute-start.12) | collective-permute-done | bytes 1572896 | tf_op jit(solution)/shard_map/ppermute | solution.py:23
  327.0 3.2 convert_add_fusion.4
  330.2 0.6 collective-permute-done.13
  330.8 4.8 %collective-permute-done.11.refs_4_ = bf16[128,7168]{1,0:T(8,128)(2,1)S(1)} collective-permute-done((bf16[128,7168]{1,0:T(8,128)(2,1)}, bf16[128,7168]{1,0:T(8,128)(2,1)S(1)}, u32[]{:S(2)}, u32[]{:S(2)}) %collective-permute-start.11) | collective-permute-done | bytes 1835040 | tf_op jit(solution)/shard_map/ppermute | solution.py:19
  335.7 1.3 pad_maximum_fusion.1
  337.0 1.8 collective-permute-start.17
  339.1 1.1 collective-permute-start.19
  340.1 0.8 collective-permute-start.20
  340.9 14.2 %shard_map.70 = f32[4,512,128]{2,1,0:T(8,128)S(1)} custom-call(bf16[512,7168]{1,0:T(8,128)(2,1)} %add_convert_fusion.1.refs_0_, bf16[512,7168]{1,0:T(8,128)(2,1)} %collective-permute-done.4.refs_1_, bf16[512,7168]{1,0:T(8,128)(2,1)} %add_convert_fusion.refs_2_, bf16[512,7168]{1,0:T(8,128)(2,1)} %collective-permute-done.7.refs_3_, ...), custom_call_target="tpu_custom_call" | custom-call | flops 4227858432 | bytes 35913728 | tf_op jit(solution)/shard_map/pallas_call | solution.py:61
  355.1 15.7 %collective-permute-done.17 = bf16[3,512,512]{2,1,0:T(8,128)(2,1)} collective-permute-done((bf16[3,512,512]{2,1,0:T(8,128)(2,1)}, bf16[3,512,512]{2,1,0:T(8,128)(2,1)}, u32[]{:S(2)}, u32[]{:S(2)}) %collective-permute-start.17) | collective-permute-done | bytes 1572896 | tf_op jit(solution)/shard_map/ppermute | solution.py:23
  370.8 3.2 convert_add_fusion
  373.9 5.4 %collective-permute-done.10.refs_4_ = bf16[128,7168]{1,0:T(8,128)(2,1)S(1)} collective-permute-done((bf16[128,7168]{1,0:T(8,128)(2,1)}, bf16[128,7168]{1,0:T(8,128)(2,1)S(1)}, u32[]{:S(2)}, u32[]{:S(2)}) %collective-permute-start.10) | collective-permute-done | bytes 1835040 | tf_op jit(solution)/shard_map/ppermute | solution.py:19
  380.8 1.7 collective-permute-start.23
  382.6 14.1 %shard_map.71 = f32[4,512,128]{2,1,0:T(8,128)S(1)} custom-call(bf16[512,7168]{1,0:T(8,128)(2,1)} %add_convert_fusion.1.refs_0_, bf16[512,7168]{1,0:T(8,128)(2,1)} %collective-permute-done.4.refs_1_, bf16[512,7168]{1,0:T(8,128)(2,1)} %add_convert_fusion.refs_2_, bf16[512,7168]{1,0:T(8,128)(2,1)} %collective-permute-done.7.refs_3_, ...), custom_call_target="tpu_custom_call" | custom-call | flops 4227858432 | bytes 35913728 | tf_op jit(solution)/shard_map/pallas_call | solution.py:61
  396.8 4.2 collective-permute-done.21.refs_11_
  401.1 0.9 copy-done.16
  402.1 0.7 collective-permute-start.25
  403.0 1.7 collective-permute-start.27
  404.9 4.5 collective-permute-done.27.refs_19_
  409.3 1.9 collective-permute-done.28.refs_20_
  411.2 1.0 collective-permute-done.25.refs_16_
  412.2 1.0 pad_maximum_fusion.4
  413.2 1.6 collective-permute-start.29
  414.8 2.1 multiply_add_fusion
  416.9 10.0 %collective-permute-done.29.refs_21_ = bf16[4,512,128]{2,1,0:T(8,128)(2,1)} collective-permute-done((bf16[4,512,128]{2,1,0:T(8,128)(2,1)}, bf16[4,512,128]{2,1,0:T(8,128)(2,1)}, u32[]{:S(2)}, u32[]{:S(2)}) %collective-permute-start.29) | collective-permute-done | bytes 524320 | tf_op jit(solution)/shard_map/ppermute | solution.py:23
  427.0 1.0 copy-done.3
  428.0 0.9 copy-done.5
  429.0 0.9 copy-done.7
  429.9 0.9 copy-done.9
  430.8 0.9 copy-done.11
  431.7 1.0 copy-done.13
  432.8 8.2 %shard_map.72 = f32[512,4,512]{2,1,0:T(4,128)} custom-call(s32[2]{0:T(128)S(1)} %pad_add_fusion.at_ref, f32[512,4,512]{2,1,0:T(4,128)} %old.1, f32[512,512]{1,0:T(8,128)S(1)} %convert_add_fusion.3.refs_0_, f32[512,512]{1,0:T(8,128)} %get-tuple-element.89.refs_1_, f32[512,512]{1,0:T(8,128)} %get-tuple-element.90.refs_2_, ...), custom_call_target="tpu_custom_call" | custom-call | tf_op jit(solution)/shard_map/pallas_call | solution.py:133
  (85 shorter events, 4.6 us)
Async XLA Ops:
  7.2 72.7 %all-gather.2.cloned.1.call-start = ((), (), s32[]{:S(2)}) async-start(), calls=%async_computation | async-start | bytes 3899392 | tf_op jit(solution)/shard_map/all_gather | solution.py:171
  7.9 6.7 %collective-permute-start = (bf16[128,512]{1,0:T(8,128)(2,1)}, bf16[128,512]{1,0:T(8,128)(2,1)S(1)}, u32[]{:S(2)}, u32[]{:S(2)}) collective-permute-start(bf16[128,512]{1,0:T(8,128)(2,1)} %param.5), channel_id=1, source_target_pairs={{0,1},{1,0},{2,3},{3,2},{4,5},{5,4},{6,7},{7,6},{8,9},{9,8},{10,11... | collective-permute-start | bytes 393224 | tf_op jit(solution)/shard_map/ppermute | solution.py:23
  15.7 9.5 %collective-permute-start.1 = (bf16[256,512]{1,0:T(8,128)(2,1)S(1)}, bf16[256,512]{1,0:T(8,128)(2,1)S(1)}, u32[]{:S(2)}, u32[]{:S(2)}) collective-permute-start(bf16[256,512]{1,0:T(8,128)(2,1)S(1)} %maximum_select_fusion), channel_id=1, source_target_pairs={{0,8},{2,10},{4,12},{6,14},{8,16},{10,18},{12,20},{14,22},{16,24},... | collective-permute-start | bytes 786440 | tf_op jit(solution)/shard_map/ppermute | solution.py:19
  17.5 9.2 %collective-permute-start.2 = (bf16[256,512]{1,0:T(8,128)(2,1)S(1)}, bf16[256,512]{1,0:T(8,128)(2,1)S(1)}, u32[]{:S(2)}, u32[]{:S(2)}) collective-permute-start(bf16[256,512]{1,0:T(8,128)(2,1)S(1)} %maximum_select_fusion), channel_id=1, source_target_pairs={{0,4},{2,6},{4,0},{6,2},{8,12},{10,14},{12,8},{14,10},{16,20},{18,... | collective-permute-start | bytes 786440 | tf_op jit(solution)/shard_map/ppermute | solution.py:14
  26.7 167.4 %collective-permute-start.6 = (bf16[512,7168]{1,0:T(8,128)(2,1)}, bf16[512,7168]{1,0:T(8,128)(2,1)}, u32[]{:S(2)}, u32[]{:S(2)}) collective-permute-start(bf16[512,7168]{1,0:T(8,128)(2,1)} %param.7), channel_id=1, source_target_pairs={{0,4},{2,6},{4,0},{6,2},{8,12},{10,14},{12,8},{14,10},{16,20},{18,... | collective-permute-start | bytes 22020104 | tf_op jit(solution)/shard_map/ppermute | solution.py:14
  29.2 176.5 %collective-permute-start.3 = (bf16[512,7168]{1,0:T(8,128)(2,1)}, bf16[512,7168]{1,0:T(8,128)(2,1)}, u32[]{:S(2)}, u32[]{:S(2)}) collective-permute-start(bf16[512,7168]{1,0:T(8,128)(2,1)} %param.7), channel_id=1, source_target_pairs={{0,8},{2,10},{4,12},{6,14},{8,16},{10,18},{12,20},{14,22},{16,24},... | collective-permute-start | bytes 22020104 | tf_op jit(solution)/shard_map/ppermute | solution.py:19
  79.9 114.2 %copy-start = (bf16[256,7168]{1,0:T(8,128)(2,1)S(1)}, bf16[256,7168]{1,0:T(8,128)(2,1)}, u32[]{:S(2)}) copy-start(bf16[256,7168]{1,0:T(8,128)(2,1)} %all-gather.2.cloned.1.call-done.refs_6_) | copy-start | bytes 11010052
  89.2 116.5 %collective-permute-start.4 = (bf16[512,7168]{1,0:T(8,128)(2,1)}, bf16[512,7168]{1,0:T(8,128)(2,1)}, u32[]{:S(2)}, u32[]{:S(2)}) collective-permute-start(bf16[512,7168]{1,0:T(8,128)(2,1)} %add_convert_fusion.1.refs_0_), channel_id=1, source_target_pairs={{0,2},{2,0},{4,6},{6,4},{8,10},{10,8},{12,14},{14,12},{16,18},{18,... | collective-permute-start | bytes 22020104 | tf_op jit(solution)/shard_map/ppermute | solution.py:14
  202.4 31.8 %collective-permute-start.7 = (bf16[512,7168]{1,0:T(8,128)(2,1)}, bf16[512,7168]{1,0:T(8,128)(2,1)}, u32[]{:S(2)}, u32[]{:S(2)}) collective-permute-start(bf16[512,7168]{1,0:T(8,128)(2,1)} %add_convert_fusion.refs_2_), channel_id=1, source_target_pairs={{0,2},{2,0},{4,6},{6,4},{8,10},{10,8},{12,14},{14,12},{16,18},{18,... | collective-permute-start | bytes 22020104 | tf_op jit(solution)/shard_map/ppermute | solution.py:14
  209.8 83.8 %collective-permute-start.5 = (bf16[256,7168]{1,0:T(8,128)(2,1)}, bf16[256,7168]{1,0:T(8,128)(2,1)S(1)}, u32[]{:S(2)}, u32[]{:S(2)}) collective-permute-start(bf16[256,7168]{1,0:T(8,128)(2,1)} %slice.66), channel_id=1, source_target_pairs={{0,8},{2,10},{4,12},{6,14},{8,16},{10,18},{12,20},{14,22},{16,24},... | collective-permute-start | bytes 11010056 | tf_op jit(solution)/shard_map/ppermute | solution.py:19
  218.4 55.8 %collective-permute-start.15 = (bf16[1,512,512]{2,1,0:T(8,128)(2,1)S(1)}, bf16[1,512,512]{2,1,0:T(8,128)(2,1)S(1)}, u32[]{:S(2)}, u32[]{:S(2)}) collective-permute-start(bf16[1,512,512]{2,1,0:T(8,128)(2,1)S(1)} %convert_bitcast_fusion.3), channel_id=1, source_target_pairs={{0,1},{1,0},{2,3},{3,2},{4,5},{5,4},{6,7},{7,6},{8,9},{9,8},{10,11... | collective-permute-start | bytes 1572872 | tf_op jit(solution)/shard_map/ppermute | solution.py:23
  229.3 4.9 %copy-start.1 = (bf16[256,7168]{1,0:T(8,128)(2,1)S(1)}, bf16[256,7168]{1,0:T(8,128)(2,1)}, u32[]{:S(2)}) copy-start(bf16[256,7168]{1,0:T(8,128)(2,1)} %all-gather.2.cloned.1.call-done.refs_6_) | copy-start | bytes 11010052
  233.7 39.0 %collective-permute-start.16 = (f32[256,512]{1,0:T(8,128)S(1)}, f32[256,512]{1,0:T(8,128)S(1)}, u32[]{:S(2)}, u32[]{:S(2)}) collective-permute-start(f32[256,512]{1,0:T(8,128)S(1)} %constant_dynamic-slice_fusion), channel_id=1, source_target_pairs={{0,1},{1,0},{2,3},{3,2},{4,5},{5,4},{6,7},{7,6},{8,9},{9,8},{10,11... | collective-permute-start | bytes 1572872 | tf_op jit(solution)/shard_map/ppermute | solution.py:23
  263.1 11.2 %collective-permute-start.8 = (f32[512,512]{1,0:T(8,128)S(1)}, f32[512,512]{1,0:T(8,128)S(1)}, u32[]{:S(2)}, u32[]{:S(2)}) collective-permute-start(f32[512,512]{1,0:T(8,128)S(1)} %get-tuple-element.130), channel_id=1, source_target_pairs={{0,2},{2,0},{4,6},{6,4},{8,10},{10,8},{12,14},{14,12},{16,18},{18,... | collective-permute-start | bytes 3145736 | tf_op jit(solution)/shard_map/ppermute | solution.py:14
  263.1 25.6 %collective-permute-start.9 = (f32[512,512]{1,0:T(8,128)S(1)}, f32[512,512]{1,0:T(8,128)S(1)}, u32[]{:S(2)}, u32[]{:S(2)}) collective-permute-start(f32[512,512]{1,0:T(8,128)S(1)} %get-tuple-element.129), channel_id=1, source_target_pairs={{0,4},{2,6},{4,0},{6,2},{8,12},{10,14},{12,8},{14,10},{16,20},{18,... | collective-permute-start | bytes 3145736 | tf_op jit(solution)/shard_map/ppermute | solution.py:14
  272.7 33.0 %collective-permute-start.14 = (bf16[256,512]{1,0:T(8,128)(2,1)S(1)}, bf16[256,512]{1,0:T(8,128)(2,1)S(1)}, u32[]{:S(2)}, u32[]{:S(2)}) collective-permute-start(bf16[256,512]{1,0:T(8,128)(2,1)S(1)} %collective-permute-done.1.refs_5_), channel_id=1, source_target_pairs={{0,8},{2,10},{4,12},{6,14},{8,16},{10,18},{12,20},{14,22},{16,24},... | collective-permute-start | bytes 786440 | tf_op jit(solution)/shard_map/ppermute | solution.py:19
  293.6 42.0 %collective-permute-start.11 = (bf16[128,7168]{1,0:T(8,128)(2,1)}, bf16[128,7168]{1,0:T(8,128)(2,1)S(1)}, u32[]{:S(2)}, u32[]{:S(2)}) collective-permute-start(bf16[128,7168]{1,0:T(8,128)(2,1)} %get-tuple-element.71), channel_id=1, source_target_pairs={{0,8},{2,10},{4,12},{6,14},{8,16},{10,18},{12,20},{14,22},{16,24},... | collective-permute-start | bytes 5505032 | tf_op jit(solution)/shard_map/ppermute | solution.py:19
  295.1 31.8 %collective-permute-start.12 = (bf16[3,512,512]{2,1,0:T(8,128)(2,1)}, bf16[3,512,512]{2,1,0:T(8,128)(2,1)}, u32[]{:S(2)}, u32[]{:S(2)}) collective-permute-start(bf16[3,512,512]{2,1,0:T(8,128)(2,1)} %pad_maximum_fusion), channel_id=1, source_target_pairs={{0,1},{1,0},{2,3},{3,2},{4,5},{5,4},{6,7},{7,6},{8,9},{9,8},{10,11... | collective-permute-start | bytes 4718600 | tf_op jit(solution)/shard_map/ppermute | solution.py:23
  305.7 25.1 %collective-permute-start.13 = (f32[512,512]{1,0:T(8,128)}, f32[512,512]{1,0:T(8,128)S(1)}, u32[]{:S(2)}, u32[]{:S(2)}) collective-permute-start(f32[512,512]{1,0:T(8,128)} %get-tuple-element.75), channel_id=1, source_target_pairs={{0,6},{2,4},{4,2},{6,0},{8,14},{10,12},{12,10},{14,8},{16,22},{18,... | collective-permute-start | bytes 3145736 | tf_op jit(solution)/shard_map/ppermute | solution.py:14
  305.8 0.7 copy-start.17
  321.2 17.6 %copy-start.18 = (bf16[256,512]{1,0:T(8,128)(2,1)S(1)}, bf16[256,512]{1,0:T(8,128)(2,1)}, u32[]{:S(2)}) copy-start(bf16[256,512]{1,0:T(8,128)(2,1)} %copy-done.17) | copy-start | bytes 786436
  330.8 8.0 %copy-start.14 = (f32[512,512]{1,0:T(8,128)}, f32[512,512]{1,0:T(8,128)S(1)}, u32[]{:S(2)}) copy-start(f32[512,512]{1,0:T(8,128)S(1)} %collective-permute-done.13) | copy-start | bytes 3145732
  337.0 33.8 %collective-permute-start.17 = (bf16[3,512,512]{2,1,0:T(8,128)(2,1)}, bf16[3,512,512]{2,1,0:T(8,128)(2,1)}, u32[]{:S(2)}, u32[]{:S(2)}) collective-permute-start(bf16[3,512,512]{2,1,0:T(8,128)(2,1)} %pad_maximum_fusion.1), channel_id=1, source_target_pairs={{0,1},{1,0},{2,3},{3,2},{4,5},{5,4},{6,7},{7,6},{8,9},{9,8},{10,11... | collective-permute-start | bytes 4718600 | tf_op jit(solution)/shard_map/ppermute | solution.py:23
  338.8 40.6 %collective-permute-start.10 = (bf16[128,7168]{1,0:T(8,128)(2,1)}, bf16[128,7168]{1,0:T(8,128)(2,1)S(1)}, u32[]{:S(2)}, u32[]{:S(2)}) collective-permute-start(bf16[128,7168]{1,0:T(8,128)(2,1)} %get-tuple-element.70), channel_id=1, source_target_pairs={{0,8},{2,10},{4,12},{6,14},{8,16},{10,18},{12,20},{14,22},{16,24},... | collective-permute-start | bytes 5505032 | tf_op jit(solution)/shard_map/ppermute | solution.py:19
  339.0 40.4 %collective-permute-start.18 = (f32[512,256]{1,0:T(8,128)S(1)}, f32[512,256]{1,0:T(8,128)S(1)}, u32[]{:S(2)}, u32[]{:S(2)}) collective-permute-start(f32[512,256]{1,0:T(8,128)S(1)} %get-tuple-element.134), channel_id=1, source_target_pairs={{0,2},{2,0},{4,6},{6,4},{8,10},{10,8},{12,14},{14,12},{16,18},{18,... | collective-permute-start | bytes 1572872 | tf_op jit(solution)/shard_map/ppermute | solution.py:14
  339.1 40.3 %collective-permute-start.19 = (f32[512,256]{1,0:T(8,128)S(1)}, f32[512,256]{1,0:T(8,128)S(1)}, u32[]{:S(2)}, u32[]{:S(2)}) collective-permute-start(f32[512,256]{1,0:T(8,128)S(1)} %get-tuple-element.133), channel_id=1, source_target_pairs={{0,4},{2,6},{4,0},{6,2},{8,12},{10,14},{12,8},{14,10},{16,20},{18,... | collective-permute-start | bytes 1572872 | tf_op jit(solution)/shard_map/ppermute | solution.py:14
  340.1 39.2 %collective-permute-start.20 = (f32[512,256]{1,0:T(8,128)S(1)}, f32[512,256]{1,0:T(8,128)S(1)}, u32[]{:S(2)}, u32[]{:S(2)}) collective-permute-start(f32[512,256]{1,0:T(8,128)S(1)} %get-tuple-element.132), channel_id=1, source_target_pairs={{0,6},{2,4},{4,2},{6,0},{8,14},{10,12},{12,10},{14,8},{16,22},{18,... | collective-permute-start | bytes 1572872 | tf_op jit(solution)/shard_map/ppermute | solution.py:14
  340.9 29.8 %copy-start.15 = (f32[512,512]{1,0:T(8,128)S(1)}, f32[512,512]{1,0:T(8,128)}, u32[]{:S(2)}) copy-start(f32[512,512]{1,0:T(8,128)} %copy-done.14) | copy-start | bytes 3145732
  379.4 0.8 copy-start.2
  380.2 20.8 %collective-permute-start.21 = (bf16[4,512,256]{2,1,0:T(8,128)(2,1)S(1)}, bf16[4,512,256]{2,1,0:T(8,128)(2,1)S(1)}, u32[]{:S(2)}, u32[]{:S(2)}) collective-permute-start(bf16[4,512,256]{2,1,0:T(8,128)(2,1)S(1)} %pad_maximum_fusion.2), channel_id=1, source_target_pairs={{0,1},{1,0},{2,3},{3,2},{4,5},{5,4},{6,7},{7,6},{8,9},{9,8},{10,11... | collective-permute-start | bytes 3145736 | tf_op jit(solution)/shard_map/ppermute | solution.py:23
  380.7 16.0 %collective-permute-start.22 = (f32[512,128]{1,0:T(8,128)S(1)}, f32[512,128]{1,0:T(8,128)S(1)}, u32[]{:S(2)}, u32[]{:S(2)}) collective-permute-start(f32[512,128]{1,0:T(8,128)S(1)} %get-tuple-element.144), channel_id=1, source_target_pairs={{0,2},{2,0},{4,6},{6,4},{8,10},{10,8},{12,14},{14,12},{16,18},{18,... | collective-permute-start | bytes 786440 | tf_op jit(solution)/shard_map/ppermute | solution.py:14
  380.8 16.0 %collective-permute-start.23 = (f32[512,128]{1,0:T(8,128)S(1)}, f32[512,128]{1,0:T(8,128)S(1)}, u32[]{:S(2)}, u32[]{:S(2)}) collective-permute-start(f32[512,128]{1,0:T(8,128)S(1)} %get-tuple-element.143), channel_id=1, source_target_pairs={{0,4},{2,6},{4,0},{6,2},{8,12},{10,14},{12,8},{14,10},{16,20},{18,... | collective-permute-start | bytes 786440 | tf_op jit(solution)/shard_map/ppermute | solution.py:14
  382.4 14.3 %collective-permute-start.24 = (f32[512,128]{1,0:T(8,128)S(1)}, f32[512,128]{1,0:T(8,128)S(1)}, u32[]{:S(2)}, u32[]{:S(2)}) collective-permute-start(f32[512,128]{1,0:T(8,128)S(1)} %get-tuple-element.142), channel_id=1, source_target_pairs={{0,6},{2,4},{4,2},{6,0},{8,14},{10,12},{12,10},{14,8},{16,22},{18,... | collective-permute-start | bytes 786440 | tf_op jit(solution)/shard_map/ppermute | solution.py:14
  396.7 7.9 %copy-start.4 = (f32[512,128]{1,0:T(8,128)}, f32[512,128]{1,0:T(8,128)S(1)}, u32[]{:S(2)}) copy-start(f32[512,128]{1,0:T(8,128)S(1)} %collective-permute-done.23.refs_14_) | copy-start | bytes 786436
  396.7 8.1 %copy-start.6 = (f32[512,128]{1,0:T(8,128)}, f32[512,128]{1,0:T(8,128)S(1)}, u32[]{:S(2)}) copy-start(f32[512,128]{1,0:T(8,128)S(1)} %collective-permute-done.24.refs_15_) | copy-start | bytes 786436
  401.0 1.0 copy-start.16
  402.1 10.2 %collective-permute-start.25 = (bf16[4,512,128]{2,1,0:T(8,128)(2,1)S(1)}, bf16[4,512,128]{2,1,0:T(8,128)(2,1)S(1)}, u32[]{:S(2)}, u32[]{:S(2)}) collective-permute-start(bf16[4,512,128]{2,1,0:T(8,128)(2,1)S(1)} %pad_maximum_fusion.3), channel_id=1, source_target_pairs={{0,1},{1,0},{2,3},{3,2},{4,5},{5,4},{6,7},{7,6},{8,9},{9,8},{10,11... | collective-permute-start | bytes 1572872 | tf_op jit(solution)/shard_map/ppermute | solution.py:23
  402.9 2.0 collective-permute-start.26
  403.0 6.4 %collective-permute-start.27 = (bf16[512,128]{1,0:T(8,128)(2,1)S(1)}, bf16[512,128]{1,0:T(8,128)(2,1)S(1)}, u32[]{:S(2)}, u32[]{:S(2)}) collective-permute-start(bf16[512,128]{1,0:T(8,128)(2,1)S(1)} %get-tuple-element.147), channel_id=1, source_target_pairs={{0,4},{2,6},{4,0},{6,2},{8,12},{10,14},{12,8},{14,10},{16,20},{18,... | collective-permute-start | bytes 393224 | tf_op jit(solution)/shard_map/ppermute | solution.py:14
  404.6 6.6 %collective-permute-start.28 = (bf16[512,128]{1,0:T(8,128)(2,1)S(1)}, bf16[512,128]{1,0:T(8,128)(2,1)S(1)}, u32[]{:S(2)}, u32[]{:S(2)}) collective-permute-start(bf16[512,128]{1,0:T(8,128)(2,1)S(1)} %get-tuple-element.146), channel_id=1, source_target_pairs={{0,6},{2,4},{4,2},{6,0},{8,14},{10,12},{12,10},{14,8},{16,22},{18,... | collective-permute-start | bytes 393224 | tf_op jit(solution)/shard_map/ppermute | solution.py:14
  409.3 2.9 copy-start.8
  411.2 2.0 copy-start.10
  412.2 1.0 copy-start.12
  413.2 13.8 %collective-permute-start.29 = (bf16[4,512,128]{2,1,0:T(8,128)(2,1)}, bf16[4,512,128]{2,1,0:T(8,128)(2,1)}, u32[]{:S(2)}, u32[]{:S(2)}) collective-permute-start(bf16[4,512,128]{2,1,0:T(8,128)(2,1)} %pad_maximum_fusion.4), channel_id=1, source_target_pairs={{0,1},{1,0},{2,3},{3,2},{4,5},{5,4},{6,7},{7,6},{8,9},{9,8},{10,11... | collective-permute-start | bytes 1572872 | tf_op jit(solution)/shard_map/ppermute | solution.py:23
  427.0 1.0 copy-start.3
  428.0 0.9 copy-start.5
  429.0 0.9 copy-start.7
  429.9 0.9 copy-start.9
  430.8 0.9 copy-start.11
  431.7 1.0 copy-start.13
Sparse Core Ops, SparseCore 0:
  10.3 69.5 all-gather.1

commit v11 on v10

--- a/solution.py
+++ b/solution.py
@@ -137,7 +137,7 @@
         out_specs=whole,
         out_shape=jax.ShapeDtypeStruct(band_old.shape, band_old.dtype),
         compiler_params=pltpu.CompilerParams(
-            dimension_semantics=("arbitrary",), vmem_limit_bytes=48 * 2**20
+            dimension_semantics=("arbitrary",), vmem_limit_bytes=60 * 2**20
         ),
     )(jnp.stack([place, y]).astype(jnp.int32), band_old, *operands)
 
@@ -154,20 +154,26 @@
     phase = lax.optimization_barrier
 
     half, quarter = block // 2, block // 4
+    raw, *parts = phase(
+        (
+            accumulated,
+            swap(activations, 2),
+            *(from_behind(activations, step * GROUP) for step in range(1, steps + 1)),
+        )
+    )
+    moving = from_behind(raw, GROUP)
+    across_raw = swap(raw, 2)
+    parts = jnp.stack([activations, *parts])
     if paired:
-        other = trade(activations)
-        columns = jnp.where(
+        other = trade(parts)
+        parts = jnp.where(
             y == 0,
-            jnp.concatenate([activations, other]),
-            jnp.concatenate([other, activations]),
+            jnp.concatenate([parts, other], axis=1),
+            jnp.concatenate([other, parts], axis=1),
         )
     else:
-        columns = lax.all_gather(activations, "col", axis=0, tiled=True)
-    raw, behind, across_columns = phase(
-        (accumulated, from_behind(columns, GROUP), swap(columns, 2))
-    )
-    moving = from_behind(raw, GROUP)
-    across_raw = swap(raw, 2)
+        parts = lax.all_gather(parts, "col", axis=1, tiled=True)
+    columns, across_columns, *behind = parts
     cotangent_all = lax.all_gather(cotangent, "row", axis=0, tiled=True)
 
     def products(raws, columns):
@@ -193,8 +199,7 @@
     sums = [None] * (steps + 1)
     made, diagonal = None, None
     for step in range(1, steps):
-        arrived, arrived_columns = moving, behind
-        behind = from_behind(arrived_columns, GROUP)
+        arrived = moving
         if step < steps - 1:
             moving = from_behind(arrived, GROUP)
         else:
@@ -213,18 +218,18 @@
         else:
             handed = to_owners(made)
             sums[steps - step + 1] = added(handed, over_columns(handed))
-        made = products([arrived], arrived_columns)
+        made = products([arrived], behind[step - 1])
         if step == steps - 1:
             handed = [made[0], swap(made[1], 1), swap(made[2], 2), made[3]]
             moving, quarters, handed = phase((moving, quarters, handed))
-        moving, behind, made, sums, own_products, diagonal = phase(
-            (moving, behind, made, sums, own_products, diagonal)
+        moving, made, sums, own_products, diagonal = phase(
+            (moving, made, sums, own_products, diagonal)
         )
 
     third = from_behind(quarters[0], GROUP)
     one = added(handed[:3], over_columns(handed[:3]))
     handed = one + [swap(handed[3], 3)]
-    made = products([moving], behind[:, :half])
+    made = products([moving], behind[-1][:, :half])
     third, handed, made = phase((third, handed, made))
 
     fourth = from_behind(quarters[1], GROUP)
@@ -233,12 +238,12 @@
     sums[1] = handed[:3] + late[:1]
     sums[steps] = own_products[:2] + late[1:]
     handed = to_owners(made)
-    made = products([third], behind[:, half : half + quarter])
+    made = products([third], behind[-1][:, half : half + quarter])
     fourth, sums, handed, made = phase((fourth, sums, handed, made))
 
     last = [(handed, over_columns(handed))]
     handed = to_owners(made)
-    made = products([fourth], behind[:, half + quarter :])
+    made = products([fourth], behind[-1][:, half + quarter :])
     last, handed, made = phase((last, handed, made))
 
     last.append((handed, over_columns(handed)))

time: 448 us -> 443 us (0.989)
  local copies, waits for them, and re-layouts: 20.2 us -> 11.2 us
    ppermute x8, waiting for transfers between devices: 40.4 us -> 57.7 us  [trade(): return lax.ppermute(array, 'col', [(0, 1), (1, 0)])]
    all_gather x1, waiting for transfers between devices: 48.9 us -> 40.1 us  [body(): cotangent_all = lax.all_gather(cotangent, 'row', axis=0, tiled=True)]
    unnamed x38 -> x40, local copies, waits for them, and re-layouts: 7.92 us -> 0.47 us
    ppermute x16, waiting for transfers between devices: 127 us -> 123 us  [swap(): return lax.ppermute(array, 'row', [(i, i ^ mask) for i in range(count)])]
  transfers between devices with their start and end apart: 31 -> 31, of which waited for: 18 -> 17; matrix products, arithmetic and copies ran while one was open for 17% -> 18% of each run, Pallas kernels for 15% -> 15%
where the time goes in v11:
time: 443 us
  waiting for transfers between devices  245 us (55%)
  Pallas kernels  77.6 us (18%)
  matrix products  52.5 us (12%)
  starting transfers between devices  22.8 us (5%)
  other arithmetic  19 us (4%)
  between operations  14.5 us (3%)
  local copies, waits for them, and re-layouts  11.2 us (3%)
    ppermute x16, waiting for transfers between devices, swap(): return lax.ppermute(array, 'row', [(i, i ^ mask) for i in range(count)])  123 us
    pallas_call x4, Pallas kernels, panel_products(): pl.pallas_call(products_kernel, grid=(width // depth,), in_specs=[pl.Bloc...  68.1 us
    ppermute x8, waiting for transfers between devices, trade(): return lax.ppermute(array, 'col', [(0, 1), (1, 0)])  57.7 us
    all_gather x1, waiting for transfers between devices, body(): cotangent_all = lax.all_gather(cotangent, 'row', axis=0, tiled=True)  40.1 us
    dot_general x4, matrix products, block_product(): lax.dot_general(left, right, (((1,), (1,)), ((), ())), preferred_element_...  34.9 us
    ppermute x6, waiting for transfers between devices, from_behind(): lax.ppermute(array, 'row', [(i, (i + by) % count) for i in range(count)])  24 us
    dot_general x2, matrix products, gradient_tile(): lax.dot_general(columns, cotangent_all, (((0,), (0,)), ((), ())), preferr...  17.6 us
    ppermute x16, starting transfers between devices, swap(): return lax.ppermute(array, 'row', [(i, i ^ mask) for i in range(count)])  10.5 us
  transfers between devices with their start and end apart: 31, of which 17 were waited for; matrix products, arithmetic and copies ran while one was open for 18% of the time, Pallas kernels for 15%

profile of v11, /device:TPU:0, one launch (start us, length us, event | category | flops | bytes accessed | tf_op | source)
XLA Modules:
  0.0 443.0 jit_solution(2907757663296106102)
XLA Ops:
  7.2 0.7 all-gather.2.cloned.1.call-update
  7.9 3.0 collective-permute-start
  10.9 1.6 collective-permute-start.1
  12.5 2.6 collective-permute-start.2
  15.1 4.3 collective-permute-done.1
  19.4 4.2 collective-permute-done.2
  23.6 0.5 collective-permute-start.7
  24.1 1.0 pad_maximum_fusion.3
  25.1 1.6 collective-permute-start.4
  26.7 12.0 %collective-permute-done.4 = bf16[4,128,512]{2,1,0:T(8,128)(2,1)S(1)} collective-permute-done((bf16[4,128,512]{2,1,0:T(8,128)(2,1)S(1)}, bf16[4,128,512]{2,1,0:T(8,128)(2,1)S(1)}, u32[]{:S(2)}, u32[]{:S(2)}) %collective-permute-start.4) | collective-permute-done | bytes 524320 | tf_op jit(solution)/shard_map/ppermute | solution.py:23
  38.7 1.4 maximum_select_fusion
  40.1 40.1 %all-gather.2.cloned.1.call-done.refs_6_ = bf16[256,7168]{1,0:T(8,128)(2,1)} async-done(((bf16[16,7168]{1,0:T(8,128)(2,1)}), bf16[256,7168]{1,0:T(8,128)(2,1)}) %all-gather.2.cloned.1.call-update) | async-done | bytes 3670032 | tf_op jit(solution)/shard_map/all_gather | solution.py:177
  80.2 9.4 %add_convert_fusion.1.refs_0_ = bf16[512,7168]{1,0:T(8,128)(2,1)} fusion(bf16[512,7168]{1,0:T(8,128)(2,1)} %param.7, bf16[256,7168]{1,0:T(8,128)(2,1)} %all-gather.2.cloned.1.call-done.refs_6_, bf16[4,256,512]{2,1,0:T(8,128)(2,1)S(1)} %maximum_select_fusion), kind=kOutput, calls=%fused_computation.1 | convolution fusion | flops 1890058240 | bytes 18612224 | tf_op jit(solution)/shard_map/dot_general | solution.py:27
  89.6 0.3 collective-permute-start.5
  89.8 103.8 %collective-permute-done.7 = bf16[512,7168]{1,0:T(8,128)(2,1)} collective-permute-done((bf16[512,7168]{1,0:T(8,128)(2,1)}, bf16[512,7168]{1,0:T(8,128)(2,1)}, u32[]{:S(2)}, u32[]{:S(2)}) %collective-permute-start.7) | collective-permute-done | bytes 7340064 | tf_op jit(solution)/shard_map/ppermute | solution.py:14
  193.6 8.3 %add_convert_fusion.refs_2_ = bf16[512,7168]{1,0:T(8,128)(2,1)} fusion(bf16[512,7168]{1,0:T(8,128)(2,1)} %collective-permute-done.7, bf16[256,7168]{1,0:T(8,128)(2,1)S(1)} %copy-done, bf16[4,256,512]{2,1,0:T(8,128)(2,1)S(1)} %maximum_select_fusion), kind=kOutput, calls=%fused_computation | convolution fusion | flops 1890058240 | bytes 18612224 | tf_op jit(solution)/shard_map/dot_general | solution.py:27
  202.0 4.9 %collective-permute-done.3.refs_4_ = bf16[512,7168]{1,0:T(8,128)(2,1)} collective-permute-done((bf16[512,7168]{1,0:T(8,128)(2,1)}, bf16[512,7168]{1,0:T(8,128)(2,1)}, u32[]{:S(2)}, u32[]{:S(2)}) %collective-permute-start.3) | collective-permute-done | bytes 7340064 | tf_op jit(solution)/shard_map/ppermute | solution.py:19
  206.9 2.3 slice.66
  209.2 0.2 collective-permute-start.6
  209.4 8.5 %fusion.4 = f32[512,512]{1,0:T(8,128)S(1)} fusion(bf16[512,7168]{1,0:T(8,128)(2,1)} %add_convert_fusion.1.refs_0_, bf16[512,7168]{1,0:T(8,128)(2,1)} %collective-permute-done.5.refs_1_), kind=kOutput, calls=%fused_computation.66 | convolution fusion | flops 3758096384 | bytes 15728640 | tf_op jit(solution)/shard_map/dot_general | solution.py:34
  217.9 0.9 convert_bitcast_fusion.3
  218.8 1.1 collective-permute-start.15
  219.9 9.3 %fusion.3 = f32[512,512]{1,0:T(8,128)S(1)} fusion(bf16[512,7168]{1,0:T(8,128)(2,1)} %add_convert_fusion.1.refs_0_), kind=kOutput, calls=%fused_computation.65 | convolution fusion | flops 3758096384 | bytes 8388608 | tf_op jit(solution)/shard_map/dot_general | solution.py:34
  229.3 4.5 %fusion.1 = (bf16[128,7168]{1,0:T(8,128)(2,1)}, bf16[128,7168]{1,0:T(8,128)(2,1)}) fusion(bf16[512,7168]{1,0:T(8,128)(2,1)} %collective-permute-done.3.refs_4_), kind=kLoop, calls=%fused_computation.63 | loop fusion | bytes 7340032 | tf_op jit(solution)/shard_map/split | solution.py:207
  233.8 1.0 collective-permute-start.16
  234.8 25.2 %shard_map.68 = f32[4,512,512]{2,1,0:T(8,128)} custom-call(bf16[512,7168]{1,0:T(8,128)(2,1)} %add_convert_fusion.1.refs_0_, bf16[512,7168]{1,0:T(8,128)(2,1)} %collective-permute-done.5.refs_1_, bf16[512,7168]{1,0:T(8,128)(2,1)} %add_convert_fusion.refs_2_, bf16[512,7168]{1,0:T(8,128)(2,1)} %collective-permute-done.8.refs_3_, ...), custom_call_target="tpu_custom_call" | custom-call | flops 16911433728 | bytes 44564480 | tf_op jit(solution)/shard_map/pallas_call | solution.py:61
  260.1 3.6 slice_bitcast_fusion
  263.7 0.9 collective-permute-start.10
  264.6 8.5 %fusion.5 = f32[512,512]{1,0:T(8,128)S(1)} fusion(bf16[512,7168]{1,0:T(8,128)(2,1)} %add_convert_fusion.1.refs_0_, bf16[512,7168]{1,0:T(8,128)(2,1)} %add_convert_fusion.refs_2_), kind=kOutput, calls=%fused_computation.67 | convolution fusion | flops 3758096384 | bytes 15728640 | tf_op jit(solution)/shard_map/dot_general | solution.py:34
  273.1 1.1 dynamic-slice_add_fusion
  274.3 2.2 convert_add_fusion.3.refs_0_
  276.5 12.8 %collective-permute-done.10 = f32[512,512]{1,0:T(8,128)S(1)} collective-permute-done((f32[512,512]{1,0:T(8,128)S(1)}, f32[512,512]{1,0:T(8,128)S(1)}, u32[]{:S(2)}, u32[]{:S(2)}) %collective-permute-start.10) | collective-permute-done | bytes 1048608 | tf_op jit(solution)/shard_map/ppermute | solution.py:14
  289.3 2.6 collective-permute-done.6.refs_4_
  292.1 1.3 pad_maximum_fusion
  293.4 1.3 collective-permute-start.13
  294.8 8.5 %fusion.6 = f32[512,512]{1,0:T(8,128)S(1)} fusion(bf16[512,7168]{1,0:T(8,128)(2,1)} %add_convert_fusion.1.refs_0_, bf16[512,7168]{1,0:T(8,128)(2,1)} %collective-permute-done.8.refs_3_), kind=kOutput, calls=%fused_computation.68 | convolution fusion | flops 3758096384 | bytes 15728640 | tf_op jit(solution)/shard_map/dot_general | solution.py:34
  303.5 14.6 %shard_map.69 = f32[4,512,256]{2,1,0:T(8,128)S(1)} custom-call(bf16[512,7168]{1,0:T(8,128)(2,1)} %add_convert_fusion.1.refs_0_, bf16[512,7168]{1,0:T(8,128)(2,1)} %collective-permute-done.5.refs_1_, bf16[512,7168]{1,0:T(8,128)(2,1)} %add_convert_fusion.refs_2_, bf16[512,7168]{1,0:T(8,128)(2,1)} %collective-permute-done.8.refs_3_, ...), custom_call_target="tpu_custom_call" | custom-call | flops 8455716864 | bytes 38797312 | tf_op jit(solution)/shard_map/pallas_call | solution.py:61
  318.1 10.5 %collective-permute-done.13 = bf16[3,512,512]{2,1,0:T(8,128)(2,1)} collective-permute-done((bf16[3,512,512]{2,1,0:T(8,128)(2,1)}, bf16[3,512,512]{2,1,0:T(8,128)(2,1)}, u32[]{:S(2)}, u32[]{:S(2)}) %collective-permute-start.13) | collective-permute-done | bytes 1572896 | tf_op jit(solution)/shard_map/ppermute | solution.py:23
  328.6 3.2 convert_add_fusion.4
  331.9 2.5 collective-permute-done.12.refs_4_
  334.5 1.3 pad_maximum_fusion.1
  335.8 1.6 collective-permute-start.17
  337.6 0.4 collective-permute-start.19
  338.0 1.5 collective-permute-start.20
  339.5 14.1 %shard_map.70 = f32[4,512,128]{2,1,0:T(8,128)S(1)} custom-call(bf16[512,7168]{1,0:T(8,128)(2,1)} %add_convert_fusion.1.refs_0_, bf16[512,7168]{1,0:T(8,128)(2,1)} %collective-permute-done.5.refs_1_, bf16[512,7168]{1,0:T(8,128)(2,1)} %add_convert_fusion.refs_2_, bf16[512,7168]{1,0:T(8,128)(2,1)} %collective-permute-done.8.refs_3_, ...), custom_call_target="tpu_custom_call" | custom-call | flops 4227858432 | bytes 35913728 | tf_op jit(solution)/shard_map/pallas_call | solution.py:61
  353.6 16.5 %collective-permute-done.17 = bf16[3,512,512]{2,1,0:T(8,128)(2,1)} collective-permute-done((bf16[3,512,512]{2,1,0:T(8,128)(2,1)}, bf16[3,512,512]{2,1,0:T(8,128)(2,1)}, u32[]{:S(2)}, u32[]{:S(2)}) %collective-permute-start.17) | collective-permute-done | bytes 1572896 | tf_op jit(solution)/shard_map/ppermute | solution.py:23
  370.2 3.2 convert_add_fusion
  373.4 5.4 %collective-permute-done.11.refs_4_ = bf16[128,7168]{1,0:T(8,128)(2,1)S(1)} collective-permute-done((bf16[128,7168]{1,0:T(8,128)(2,1)S(1)}, bf16[128,7168]{1,0:T(8,128)(2,1)S(1)}, u32[]{:S(2)}, u32[]{:S(2)}) %collective-permute-start.11) | collective-permute-done | bytes 1835040 | tf_op jit(solution)/shard_map/ppermute | solution.py:19
  379.1 0.3 collective-permute-start.21
  379.9 0.5 collective-permute-start.23
  380.4 1.4 collective-permute-start.24
  381.7 14.1 %shard_map.71 = f32[4,512,128]{2,1,0:T(8,128)S(1)} custom-call(bf16[512,7168]{1,0:T(8,128)(2,1)} %add_convert_fusion.1.refs_0_, bf16[512,7168]{1,0:T(8,128)(2,1)} %collective-permute-done.5.refs_1_, bf16[512,7168]{1,0:T(8,128)(2,1)} %add_convert_fusion.refs_2_, bf16[512,7168]{1,0:T(8,128)(2,1)} %collective-permute-done.8.refs_3_, ...), custom_call_target="tpu_custom_call" | custom-call | flops 4227858432 | bytes 35913728 | tf_op jit(solution)/shard_map/pallas_call | solution.py:61
  396.0 6.2 %collective-permute-done.21.refs_11_ = bf16[4,512,256]{2,1,0:T(8,128)(2,1)S(1)} collective-permute-done((bf16[4,512,256]{2,1,0:T(8,128)(2,1)S(1)}, bf16[4,512,256]{2,1,0:T(8,128)(2,1)S(1)}, u32[]{:S(2)}, u32[]{:S(2)}) %collective-permute-start.21) | collective-permute-done | bytes 1048608 | tf_op jit(solution)/shard_map/ppermute | solution.py:23
  402.7 0.3 collective-permute-start.27
  403.0 1.6 collective-permute-start.28
  404.6 4.4 %collective-permute-done.27.refs_19_ = bf16[512,128]{1,0:T(8,128)(2,1)S(1)} collective-permute-done((bf16[512,128]{1,0:T(8,128)(2,1)S(1)}, bf16[512,128]{1,0:T(8,128)(2,1)S(1)}, u32[]{:S(2)}, u32[]{:S(2)}) %collective-permute-start.27) | collective-permute-done | bytes 131104 | tf_op jit(solution)/shard_map/ppermute | solution.py:14
  409.0 1.9 collective-permute-done.28.refs_20_
  410.9 1.2 collective-permute-done.25.refs_16_
  412.1 0.9 pad_maximum_fusion.5
  413.1 0.8 collective-permute-start.29
  413.9 0.6 pad_add_fusion.at_ref
  414.6 0.9 multiply_add_fusion
  415.5 11.2 %collective-permute-done.29.refs_21_ = bf16[4,512,128]{2,1,0:T(8,128)(2,1)} collective-permute-done((bf16[4,512,128]{2,1,0:T(8,128)(2,1)}, bf16[4,512,128]{2,1,0:T(8,128)(2,1)}, u32[]{:S(2)}, u32[]{:S(2)}) %collective-permute-start.29) | collective-permute-done | bytes 524320 | tf_op jit(solution)/shard_map/ppermute | solution.py:23
  426.7 9.5 %shard_map.72 = f32[512,4,512]{2,1,0:T(4,128)} custom-call(s32[2]{0:T(128)} %pad_add_fusion.at_ref, f32[512,4,512]{2,1,0:T(4,128)} %old.1, f32[512,512]{1,0:T(8,128)} %convert_add_fusion.3.refs_0_, f32[512,512]{1,0:T(8,128)} %get-tuple-element.89.refs_1_, f32[512,512]{1,0:T(8,128)} %get-tuple-element.90.refs_2_, f32[512,512]{1,0:T(8,128)} %get-tuple-element.91.refs_3_, ...), custom_call_target="tpu_custom_call" | custom-call | tf_op jit(solution)/shard_map/pallas_call | solution.py:133
  (89 shorter events, 2.1 us)
Async XLA Ops:
  7.2 73.1 %all-gather.2.cloned.1.call-start = ((), (), s32[]{:S(2)}) async-start(), calls=%async_computation | async-start | bytes 3899392 | tf_op jit(solution)/shard_map/all_gather | solution.py:177
  7.9 7.2 %collective-permute-start = (bf16[128,512]{1,0:T(8,128)(2,1)}, bf16[128,512]{1,0:T(8,128)(2,1)S(1)}, u32[]{:S(2)}, u32[]{:S(2)}) collective-permute-start(bf16[128,512]{1,0:T(8,128)(2,1)} %param.5), channel_id=1, source_target_pairs={{0,4},{2,6},{4,0},{6,2},{8,12},{10,14},{12,8},{14,10},{16,20},{18,... | collective-permute-start | bytes 393224 | tf_op jit(solution)/shard_map/ppermute | solution.py:14
  10.9 8.5 %collective-permute-start.1 = (bf16[128,512]{1,0:T(8,128)(2,1)}, bf16[128,512]{1,0:T(8,128)(2,1)S(1)}, u32[]{:S(2)}, u32[]{:S(2)}) collective-permute-start(bf16[128,512]{1,0:T(8,128)(2,1)} %param.5), channel_id=1, source_target_pairs={{0,8},{2,10},{4,12},{6,14},{8,16},{10,18},{12,20},{14,22},{16,24},... | collective-permute-start | bytes 393224 | tf_op jit(solution)/shard_map/ppermute | solution.py:19
  12.5 11.1 %collective-permute-start.2 = (bf16[128,512]{1,0:T(8,128)(2,1)}, bf16[128,512]{1,0:T(8,128)(2,1)S(1)}, u32[]{:S(2)}, u32[]{:S(2)}) collective-permute-start(bf16[128,512]{1,0:T(8,128)(2,1)} %param.5), channel_id=1, source_target_pairs={{0,16},{2,18},{4,20},{6,22},{8,24},{10,26},{12,28},{14,30},{16,0},... | collective-permute-start | bytes 393224 | tf_op jit(solution)/shard_map/ppermute | solution.py:19
  23.6 170.1 %collective-permute-start.7 = (bf16[512,7168]{1,0:T(8,128)(2,1)}, bf16[512,7168]{1,0:T(8,128)(2,1)}, u32[]{:S(2)}, u32[]{:S(2)}) collective-permute-start(bf16[512,7168]{1,0:T(8,128)(2,1)} %param.7), channel_id=1, source_target_pairs={{0,4},{2,6},{4,0},{6,2},{8,12},{10,14},{12,8},{14,10},{16,20},{18,... | collective-permute-start | bytes 22020104 | tf_op jit(solution)/shard_map/ppermute | solution.py:14
  25.1 13.6 %collective-permute-start.4 = (bf16[4,128,512]{2,1,0:T(8,128)(2,1)S(1)}, bf16[4,128,512]{2,1,0:T(8,128)(2,1)S(1)}, u32[]{:S(2)}, u32[]{:S(2)}) collective-permute-start(bf16[4,128,512]{2,1,0:T(8,128)(2,1)S(1)} %pad_maximum_fusion.3), channel_id=1, source_target_pairs={{0,1},{1,0},{2,3},{3,2},{4,5},{5,4},{6,7},{7,6},{8,9},{9,8},{10,11... | collective-permute-start | bytes 1572872 | tf_op jit(solution)/shard_map/ppermute | solution.py:23
  26.7 180.2 %collective-permute-start.3 = (bf16[512,7168]{1,0:T(8,128)(2,1)}, bf16[512,7168]{1,0:T(8,128)(2,1)}, u32[]{:S(2)}, u32[]{:S(2)}) collective-permute-start(bf16[512,7168]{1,0:T(8,128)(2,1)} %param.7), channel_id=1, source_target_pairs={{0,8},{2,10},{4,12},{6,14},{8,16},{10,18},{12,20},{14,22},{16,24},... | collective-permute-start | bytes 22020104 | tf_op jit(solution)/shard_map/ppermute | solution.py:19
  80.2 113.4 %copy-start = (bf16[256,7168]{1,0:T(8,128)(2,1)S(1)}, bf16[256,7168]{1,0:T(8,128)(2,1)}, u32[]{:S(2)}) copy-start(bf16[256,7168]{1,0:T(8,128)(2,1)} %all-gather.2.cloned.1.call-done.refs_6_) | copy-start | bytes 11010052
  89.6 117.3 %collective-permute-start.5 = (bf16[512,7168]{1,0:T(8,128)(2,1)}, bf16[512,7168]{1,0:T(8,128)(2,1)}, u32[]{:S(2)}, u32[]{:S(2)}) collective-permute-start(bf16[512,7168]{1,0:T(8,128)(2,1)} %add_convert_fusion.1.refs_0_), channel_id=1, source_target_pairs={{0,2},{2,0},{4,6},{6,4},{8,10},{10,8},{12,14},{14,12},{16,18},{18,... | collective-permute-start | bytes 22020104 | tf_op jit(solution)/shard_map/ppermute | solution.py:14
  201.9 32.9 %collective-permute-start.8 = (bf16[512,7168]{1,0:T(8,128)(2,1)}, bf16[512,7168]{1,0:T(8,128)(2,1)}, u32[]{:S(2)}, u32[]{:S(2)}) collective-permute-start(bf16[512,7168]{1,0:T(8,128)(2,1)} %add_convert_fusion.refs_2_), channel_id=1, source_target_pairs={{0,2},{2,0},{4,6},{6,4},{8,10},{10,8},{12,14},{14,12},{16,18},{18,... | collective-permute-start | bytes 22020104 | tf_op jit(solution)/shard_map/ppermute | solution.py:14
  209.2 82.8 %collective-permute-start.6 = (bf16[256,7168]{1,0:T(8,128)(2,1)S(1)}, bf16[256,7168]{1,0:T(8,128)(2,1)S(1)}, u32[]{:S(2)}, u32[]{:S(2)}) collective-permute-start(bf16[256,7168]{1,0:T(8,128)(2,1)S(1)} %slice.66), channel_id=1, source_target_pairs={{0,8},{2,10},{4,12},{6,14},{8,16},{10,18},{12,20},{14,22},{16,24},... | collective-permute-start | bytes 11010056 | tf_op jit(solution)/shard_map/ppermute | solution.py:19
  218.8 55.4 %collective-permute-start.15 = (bf16[1,512,512]{2,1,0:T(8,128)(2,1)}, bf16[1,512,512]{2,1,0:T(8,128)(2,1)}, u32[]{:S(2)}, u32[]{:S(2)}) collective-permute-start(bf16[1,512,512]{2,1,0:T(8,128)(2,1)} %convert_bitcast_fusion.3), channel_id=1, source_target_pairs={{0,1},{1,0},{2,3},{3,2},{4,5},{5,4},{6,7},{7,6},{8,9},{9,8},{10,11... | collective-permute-start | bytes 1572872 | tf_op jit(solution)/shard_map/ppermute | solution.py:23
  229.3 4.6 %copy-start.13 = (f32[512,512]{1,0:T(8,128)}, f32[512,512]{1,0:T(8,128)S(1)}, u32[]{:S(2)}) copy-start(f32[512,512]{1,0:T(8,128)S(1)} %fusion.3) | copy-start | bytes 3145732
  229.3 5.6 %copy-start.1 = (bf16[256,7168]{1,0:T(8,128)(2,1)S(1)}, bf16[256,7168]{1,0:T(8,128)(2,1)}, u32[]{:S(2)}) copy-start(bf16[256,7168]{1,0:T(8,128)(2,1)} %all-gather.2.cloned.1.call-done.refs_6_) | copy-start | bytes 11010052
  233.8 39.3 %collective-permute-start.16 = (f32[256,512]{1,0:T(8,128)S(1)}, f32[256,512]{1,0:T(8,128)}, u32[]{:S(2)}, u32[]{:S(2)}) collective-permute-start(f32[256,512]{1,0:T(8,128)S(1)} %constant_dynamic-slice_fusion), channel_id=1, source_target_pairs={{0,1},{1,0},{2,3},{3,2},{4,5},{5,4},{6,7},{7,6},{8,9},{9,8},{10,11... | collective-permute-start | bytes 1572872 | tf_op jit(solution)/shard_map/ppermute | solution.py:23
  263.7 12.8 %collective-permute-start.9 = (f32[512,512]{1,0:T(8,128)S(1)}, f32[512,512]{1,0:T(8,128)S(1)}, u32[]{:S(2)}, u32[]{:S(2)}) collective-permute-start(f32[512,512]{1,0:T(8,128)S(1)} %get-tuple-element.130), channel_id=1, source_target_pairs={{0,2},{2,0},{4,6},{6,4},{8,10},{10,8},{12,14},{14,12},{16,18},{18,... | collective-permute-start | bytes 3145736 | tf_op jit(solution)/shard_map/ppermute | solution.py:14
  263.7 9.4 %copy-start.14 = (f32[512,512]{1,0:T(8,128)S(1)}, f32[512,512]{1,0:T(8,128)}, u32[]{:S(2)}) copy-start(f32[512,512]{1,0:T(8,128)} %copy-done.13) | copy-start | bytes 3145732
  263.7 25.6 %collective-permute-start.10 = (f32[512,512]{1,0:T(8,128)S(1)}, f32[512,512]{1,0:T(8,128)S(1)}, u32[]{:S(2)}, u32[]{:S(2)}) collective-permute-start(f32[512,512]{1,0:T(8,128)S(1)} %get-tuple-element.129), channel_id=1, source_target_pairs={{0,4},{2,6},{4,0},{6,2},{8,12},{10,14},{12,8},{14,10},{16,20},{18,... | collective-permute-start | bytes 3145736 | tf_op jit(solution)/shard_map/ppermute | solution.py:14
  291.9 42.5 %collective-permute-start.12 = (bf16[128,7168]{1,0:T(8,128)(2,1)}, bf16[128,7168]{1,0:T(8,128)(2,1)S(1)}, u32[]{:S(2)}, u32[]{:S(2)}) collective-permute-start(bf16[128,7168]{1,0:T(8,128)(2,1)} %get-tuple-element.72), channel_id=1, source_target_pairs={{0,8},{2,10},{4,12},{6,14},{8,16},{10,18},{12,20},{14,22},{16,24},... | collective-permute-start | bytes 5505032 | tf_op jit(solution)/shard_map/ppermute | solution.py:19
  293.4 35.2 %collective-permute-start.13 = (bf16[3,512,512]{2,1,0:T(8,128)(2,1)}, bf16[3,512,512]{2,1,0:T(8,128)(2,1)}, u32[]{:S(2)}, u32[]{:S(2)}) collective-permute-start(bf16[3,512,512]{2,1,0:T(8,128)(2,1)} %pad_maximum_fusion), channel_id=1, source_target_pairs={{0,1},{1,0},{2,3},{3,2},{4,5},{5,4},{6,7},{7,6},{8,9},{9,8},{10,11... | collective-permute-start | bytes 4718600 | tf_op jit(solution)/shard_map/ppermute | solution.py:23
  303.3 28.5 %collective-permute-start.14 = (f32[512,512]{1,0:T(8,128)}, f32[512,512]{1,0:T(8,128)S(1)}, u32[]{:S(2)}, u32[]{:S(2)}) collective-permute-start(f32[512,512]{1,0:T(8,128)} %get-tuple-element.76), channel_id=1, source_target_pairs={{0,6},{2,4},{4,2},{6,0},{8,14},{10,12},{12,10},{14,8},{16,22},{18,... | collective-permute-start | bytes 3145736 | tf_op jit(solution)/shard_map/ppermute | solution.py:14
  331.8 5.5 %copy-start.8 = (bf16[128,7168]{1,0:T(8,128)(2,1)S(1)}, bf16[128,7168]{1,0:T(8,128)(2,1)}, u32[]{:S(2)}) copy-start(bf16[128,7168]{1,0:T(8,128)(2,1)} %get-tuple-element.71) | copy-start | bytes 5505028
  335.8 34.4 %collective-permute-start.17 = (bf16[3,512,512]{2,1,0:T(8,128)(2,1)}, bf16[3,512,512]{2,1,0:T(8,128)(2,1)}, u32[]{:S(2)}, u32[]{:S(2)}) collective-permute-start(bf16[3,512,512]{2,1,0:T(8,128)(2,1)} %pad_maximum_fusion.1), channel_id=1, source_target_pairs={{0,1},{1,0},{2,3},{3,2},{4,5},{5,4},{6,7},{7,6},{8,9},{9,8},{10,11... | collective-permute-start | bytes 4718600 | tf_op jit(solution)/shard_map/ppermute | solution.py:23
  337.4 41.3 %collective-permute-start.11 = (bf16[128,7168]{1,0:T(8,128)(2,1)S(1)}, bf16[128,7168]{1,0:T(8,128)(2,1)S(1)}, u32[]{:S(2)}, u32[]{:S(2)}) collective-permute-start(bf16[128,7168]{1,0:T(8,128)(2,1)S(1)} %copy-done.8), channel_id=1, source_target_pairs={{0,8},{2,10},{4,12},{6,14},{8,16},{10,18},{12,20},{14,22},{16,24},... | collective-permute-start | bytes 5505032 | tf_op jit(solution)/shard_map/ppermute | solution.py:19
  337.6 41.3 %copy-start.2 = (f32[512,256]{1,0:T(8,128)}, f32[512,256]{1,0:T(8,128)S(1)}, u32[]{:S(2)}) copy-start(f32[512,256]{1,0:T(8,128)S(1)} %get-tuple-element.111.refs_7_) | copy-start | bytes 1572868
  337.6 41.2 %collective-permute-start.18 = (f32[512,256]{1,0:T(8,128)S(1)}, f32[512,256]{1,0:T(8,128)S(1)}, u32[]{:S(2)}, u32[]{:S(2)}) collective-permute-start(f32[512,256]{1,0:T(8,128)S(1)} %get-tuple-element.134), channel_id=1, source_target_pairs={{0,2},{2,0},{4,6},{6,4},{8,10},{10,8},{12,14},{14,12},{16,18},{18,... | collective-permute-start | bytes 1572872 | tf_op jit(solution)/shard_map/ppermute | solution.py:14
  337.6 41.1 %collective-permute-start.19 = (f32[512,256]{1,0:T(8,128)S(1)}, f32[512,256]{1,0:T(8,128)S(1)}, u32[]{:S(2)}, u32[]{:S(2)}) collective-permute-start(f32[512,256]{1,0:T(8,128)S(1)} %get-tuple-element.133), channel_id=1, source_target_pairs={{0,4},{2,6},{4,0},{6,2},{8,12},{10,14},{12,8},{14,10},{16,20},{18,... | collective-permute-start | bytes 1572872 | tf_op jit(solution)/shard_map/ppermute | solution.py:14
  338.0 40.7 %collective-permute-start.20 = (f32[512,256]{1,0:T(8,128)S(1)}, f32[512,256]{1,0:T(8,128)S(1)}, u32[]{:S(2)}, u32[]{:S(2)}) collective-permute-start(f32[512,256]{1,0:T(8,128)S(1)} %get-tuple-element.132), channel_id=1, source_target_pairs={{0,6},{2,4},{4,2},{6,0},{8,14},{10,12},{12,10},{14,8},{16,22},{18,... | collective-permute-start | bytes 1572872 | tf_op jit(solution)/shard_map/ppermute | solution.py:14
  378.7 0.8 copy-start.5
  378.7 1.0 copy-start.6
  378.8 1.1 copy-start.7
  379.1 23.1 %collective-permute-start.21 = (bf16[4,512,256]{2,1,0:T(8,128)(2,1)S(1)}, bf16[4,512,256]{2,1,0:T(8,128)(2,1)S(1)}, u32[]{:S(2)}, u32[]{:S(2)}) collective-permute-start(bf16[4,512,256]{2,1,0:T(8,128)(2,1)S(1)} %pad_maximum_fusion.2), channel_id=1, source_target_pairs={{0,1},{1,0},{2,3},{3,2},{4,5},{5,4},{6,7},{7,6},{8,9},{9,8},{10,11... | collective-permute-start | bytes 3145736 | tf_op jit(solution)/shard_map/ppermute | solution.py:23
  379.9 22.4 %copy-start.4 = (f32[512,128]{1,0:T(8,128)}, f32[512,128]{1,0:T(8,128)S(1)}, u32[]{:S(2)}) copy-start(f32[512,128]{1,0:T(8,128)S(1)} %get-tuple-element.116.refs_12_) | copy-start | bytes 786436
  379.9 16.0 %collective-permute-start.22 = (f32[512,128]{1,0:T(8,128)S(1)}, f32[512,128]{1,0:T(8,128)S(1)}, u32[]{:S(2)}, u32[]{:S(2)}) collective-permute-start(f32[512,128]{1,0:T(8,128)S(1)} %get-tuple-element.144), channel_id=1, source_target_pairs={{0,2},{2,0},{4,6},{6,4},{8,10},{10,8},{12,14},{14,12},{16,18},{18,... | collective-permute-start | bytes 786440 | tf_op jit(solution)/shard_map/ppermute | solution.py:14
  379.9 16.0 %collective-permute-start.23 = (f32[512,128]{1,0:T(8,128)S(1)}, f32[512,128]{1,0:T(8,128)S(1)}, u32[]{:S(2)}, u32[]{:S(2)}) collective-permute-start(f32[512,128]{1,0:T(8,128)S(1)} %get-tuple-element.143), channel_id=1, source_target_pairs={{0,4},{2,6},{4,0},{6,2},{8,12},{10,14},{12,8},{14,10},{16,20},{18,... | collective-permute-start | bytes 786440 | tf_op jit(solution)/shard_map/ppermute | solution.py:14
  380.4 15.5 %collective-permute-start.24 = (f32[512,128]{1,0:T(8,128)S(1)}, f32[512,128]{1,0:T(8,128)S(1)}, u32[]{:S(2)}, u32[]{:S(2)}) collective-permute-start(f32[512,128]{1,0:T(8,128)S(1)} %get-tuple-element.142), channel_id=1, source_target_pairs={{0,6},{2,4},{4,2},{6,0},{8,14},{10,12},{12,10},{14,8},{16,22},{18,... | collective-permute-start | bytes 786440 | tf_op jit(solution)/shard_map/ppermute | solution.py:14
  395.9 18.7 %copy-start.18 = (f32[256,512]{1,0:T(8,128)S(1)}, f32[256,512]{1,0:T(8,128)}, u32[]{:S(2)}) copy-start(f32[256,512]{1,0:T(8,128)} %param.9) | copy-start | bytes 1572868
  395.9 19.6 %copy-start.9 = (f32[512,128]{1,0:T(8,128)}, f32[512,128]{1,0:T(8,128)S(1)}, u32[]{:S(2)}) copy-start(f32[512,128]{1,0:T(8,128)S(1)} %collective-permute-done.22.refs_13_) | copy-start | bytes 786436
  395.9 19.5 %copy-start.10 = (f32[512,128]{1,0:T(8,128)}, f32[512,128]{1,0:T(8,128)S(1)}, u32[]{:S(2)}) copy-start(f32[512,128]{1,0:T(8,128)S(1)} %collective-permute-done.23.refs_14_) | copy-start | bytes 786436
  396.0 19.5 %copy-start.11 = (f32[512,128]{1,0:T(8,128)}, f32[512,128]{1,0:T(8,128)S(1)}, u32[]{:S(2)}) copy-start(f32[512,128]{1,0:T(8,128)S(1)} %collective-permute-done.24.refs_15_) | copy-start | bytes 786436
  402.2 2.3 copy-start.12
  402.4 9.7 %collective-permute-start.25 = (bf16[4,512,128]{2,1,0:T(8,128)(2,1)S(1)}, bf16[4,512,128]{2,1,0:T(8,128)(2,1)S(1)}, u32[]{:S(2)}, u32[]{:S(2)}) collective-permute-start(bf16[4,512,128]{2,1,0:T(8,128)(2,1)S(1)} %pad_maximum_fusion.4), channel_id=1, source_target_pairs={{0,1},{1,0},{2,3},{3,2},{4,5},{5,4},{6,7},{7,6},{8,9},{9,8},{10,11... | collective-permute-start | bytes 1572872 | tf_op jit(solution)/shard_map/ppermute | solution.py:23
  402.6 2.0 collective-permute-start.26
  402.7 6.4 %collective-permute-start.27 = (bf16[512,128]{1,0:T(8,128)(2,1)S(1)}, bf16[512,128]{1,0:T(8,128)(2,1)S(1)}, u32[]{:S(2)}, u32[]{:S(2)}) collective-permute-start(bf16[512,128]{1,0:T(8,128)(2,1)S(1)} %get-tuple-element.149), channel_id=1, source_target_pairs={{0,4},{2,6},{4,0},{6,2},{8,12},{10,14},{12,8},{14,10},{16,20},{18,... | collective-permute-start | bytes 393224 | tf_op jit(solution)/shard_map/ppermute | solution.py:14
  403.0 8.0 %collective-permute-start.28 = (bf16[512,128]{1,0:T(8,128)(2,1)S(1)}, bf16[512,128]{1,0:T(8,128)(2,1)S(1)}, u32[]{:S(2)}, u32[]{:S(2)}) collective-permute-start(bf16[512,128]{1,0:T(8,128)(2,1)S(1)} %get-tuple-element.148), channel_id=1, source_target_pairs={{0,6},{2,4},{4,2},{6,0},{8,14},{10,12},{12,10},{14,8},{16,22},{18,... | collective-permute-start | bytes 393224 | tf_op jit(solution)/shard_map/ppermute | solution.py:14
  404.6 22.1 %copy-start.3 = (f32[512,128]{1,0:T(8,128)}, f32[512,128]{1,0:T(8,128)S(1)}, u32[]{:S(2)}) copy-start(f32[512,128]{1,0:T(8,128)S(1)} %slice_bitcast_fusion.22.refs_17_) | copy-start | bytes 786436
  404.6 22.1 %copy-start.15 = (bf16[512,128]{1,0:T(8,128)(2,1)}, bf16[512,128]{1,0:T(8,128)(2,1)S(1)}, u32[]{:S(2)}) copy-start(bf16[512,128]{1,0:T(8,128)(2,1)S(1)} %collective-permute-done.26.refs_18_) | copy-start | bytes 393220
  409.0 17.6 %copy-start.16 = (bf16[512,128]{1,0:T(8,128)(2,1)}, bf16[512,128]{1,0:T(8,128)(2,1)S(1)}, u32[]{:S(2)}) copy-start(bf16[512,128]{1,0:T(8,128)(2,1)S(1)} %collective-permute-done.27.refs_19_) | copy-start | bytes 393220
  410.9 15.7 %copy-start.17 = (bf16[512,128]{1,0:T(8,128)(2,1)}, bf16[512,128]{1,0:T(8,128)(2,1)S(1)}, u32[]{:S(2)}) copy-start(bf16[512,128]{1,0:T(8,128)(2,1)S(1)} %collective-permute-done.28.refs_20_) | copy-start | bytes 393220
  412.1 14.5 %copy-start.19 = (bf16[4,512,128]{2,1,0:T(8,128)(2,1)}, bf16[4,512,128]{2,1,0:T(8,128)(2,1)S(1)}, u32[]{:S(2)}) copy-start(bf16[4,512,128]{2,1,0:T(8,128)(2,1)S(1)} %collective-permute-done.25.refs_16_) | copy-start | bytes 1572868
  413.1 13.5 %collective-permute-start.29 = (bf16[4,512,128]{2,1,0:T(8,128)(2,1)}, bf16[4,512,128]{2,1,0:T(8,128)(2,1)}, u32[]{:S(2)}, u32[]{:S(2)}) collective-permute-start(bf16[4,512,128]{2,1,0:T(8,128)(2,1)} %pad_maximum_fusion.5), channel_id=1, source_target_pairs={{0,1},{1,0},{2,3},{3,2},{4,5},{5,4},{6,7},{7,6},{8,9},{9,8},{10,11... | collective-permute-start | bytes 1572872 | tf_op jit(solution)/shard_map/ppermute | solution.py:23
Sparse Core Ops, SparseCore 0:
  10.3 69.9 all-gather.1

commit v12 on v11

--- a/solution.py
+++ b/solution.py
@@ -81,19 +81,19 @@
     )(*group, *raws, columns, cotangent_all)
 
 
+def pick(u, values):
+    chosen = values[-1]
+    for i in range(len(values) - 1):
+        chosen = jnp.where(u == i, values[i], chosen)
+    return chosen
+
+
 def update_kernel(at_ref, old, *refs):
     out, refs = refs[-1], list(refs[:-1])
     place, y = at_ref[0], at_ref[1]
     own, one = [refs.pop(0) for _ in range(GROUP - 1)], [refs.pop(0) for _ in range(GROUP)]
     two = [(refs[i : i + GROUP], refs[i + GROUP]) for i in range(0, len(refs), GROUP + 1)]
     share = old.shape[1]
-
-    def pick(u, values):
-        chosen = values[-1]
-        for i in range(len(values) - 1):
-            chosen = jnp.where(u == i, values[i], chosen)
-        return chosen
-
     for s in range(share):
         t = 2 * GROUP + place - (s + 1 + y * share)
         u = (t % GROUP) ^ place
@@ -111,35 +111,69 @@
         def _():
             start = 0
             for mine, other in two:
-                value = pick(u, [ref[...].astype(jnp.float32) for ref in mine]) + other[u].astype(jnp.float32)
+                value = pick(u, [ref[...].astype(jnp.float32) for ref in mine])
+                value += other[u].astype(jnp.float32)
                 end = start + value.shape[1]
                 out[:, s, start:end] = kept[:, start:end] + added * value
                 start = end
+            out[:, s, start:] = kept[:, start:]
+
+
+def last_chunk_kernel(at_ref, band, *refs):
+    *mine, other, out = refs
+    place, y = at_ref[0], at_ref[1]
+    share = band.shape[1]
+    for s in range(share):
+        t = 2 * GROUP + place - (s + 1 + y * share)
+        u = (t % GROUP) ^ place
+        value = pick(u, [ref[...].astype(jnp.float32) for ref in mine])
+        value += other[u].astype(jnp.float32)
+        added = jnp.where(t < GROUP, (1.0 - decay_rate) * value, 0.0)
+        out[:, s, :] = band[:, s, :] + added
 
 
 def update(place, y, band_old, two, one, own):
     block, share, _ = band_old.shape
     rows = block // 4
-    operands, specs = [], []
-    for piece in [*own, *one]:
-        operands.append(piece)
-        specs.append(pl.BlockSpec((rows, block), lambda i: (i, 0)))
-    for mine, other in two:
+    at = jnp.stack([place, y]).astype(jnp.int32)
+    scalars = pl.BlockSpec(memory_space=pltpu.SMEM)
+
+    def chunk_specs(mine, other):
         width = other.shape[2]
+        specs = [pl.BlockSpec((rows, width), lambda i: (i, 0))] * GROUP
+        return specs + [pl.BlockSpec((GROUP, rows, width), lambda i: (0, i, 0))]
+
+    params = pltpu.CompilerParams(
+        dimension_semantics=("arbitrary",), vmem_limit_bytes=60 * 2**20
+    )
+    operands, specs = [*own, *one], [pl.BlockSpec((rows, block), lambda i: (i, 0))] * (
+        len(own) + len(one)
+    )
+    for mine, other in two[:-1]:
         operands += [*mine, other]
-        specs += [pl.BlockSpec((rows, width), lambda i: (i, 0))] * GROUP
-        specs.append(pl.BlockSpec((GROUP, rows, width), lambda i: (0, i, 0)))
+        specs += chunk_specs(mine, other)
     whole = pl.BlockSpec((rows, share, block), lambda i: (i, 0, 0))
-    return pl.pallas_call(
+    band = pl.pallas_call(
         update_kernel,
         grid=(block // rows,),
-        in_specs=[pl.BlockSpec(memory_space=pltpu.SMEM), whole, *specs],
+        in_specs=[scalars, whole, *specs],
         out_specs=whole,
         out_shape=jax.ShapeDtypeStruct(band_old.shape, band_old.dtype),
-        compiler_params=pltpu.CompilerParams(
-            dimension_semantics=("arbitrary",), vmem_limit_bytes=60 * 2**20
-        ),
-    )(jnp.stack([place, y]).astype(jnp.int32), band_old, *operands)
+        compiler_params=params,
+    )(at, band_old, *operands)
+    mine, other = two[-1]
+    width = other.shape[2]
+    place_of = block // width - 1
+    columns = pl.BlockSpec((rows, share, width), lambda i: (i, 0, place_of))
+    return pl.pallas_call(
+        last_chunk_kernel,
+        grid=(block // rows,),
+        in_specs=[scalars, columns, *chunk_specs(mine, other)],
+        out_specs=columns,
+        out_shape=jax.ShapeDtypeStruct(band_old.shape, band_old.dtype),
+        input_output_aliases={1: 0},
+        compiler_params=params,
+    )(at, band, *mine, other)
 
 
 def body(activations, cotangent, accumulated, band_old, diagonal_old):

time: 443 us -> 438 us (0.989)
  waiting for transfers between devices: 245 us -> 236 us
    ppermute x8, waiting for transfers between devices: 57.7 us -> 48.4 us  [trade(): return lax.ppermute(array, 'col', [(0, 1), (1, 0)])]
    pallas_call x1 -> x2, Pallas kernels: 9.5 us -> 13.5 us  [the longest x1 9.22 us: update(): pl.pallas_call(update_kernel, grid=(block // rows,), in_specs=[scalars, w...]
  transfers between devices with their start and end apart: 31 -> 31, of which waited for: 17 -> 17; matrix products, arithmetic and copies ran while one was open for 18% -> 18% of each run, Pallas kernels for 15% -> 18%
where the time goes in v12:
time: 438 us
  waiting for transfers between devices  236 us (54%)
  Pallas kernels  81.6 us (19%)
  matrix products  52.5 us (12%)
  starting transfers between devices  22.8 us (5%)
  other arithmetic  19 us (4%)
  between operations  14.5 us (3%)
  local copies, waits for them, and re-layouts  11.2 us (3%)
    ppermute x16, waiting for transfers between devices, swap(): return lax.ppermute(array, 'row', [(i, i ^ mask) for i in range(count)])  123 us
    pallas_call x4, Pallas kernels, panel_products(): pl.pallas_call(products_kernel, grid=(width // depth,), in_specs=[pl.Bloc...  68.1 us
    ppermute x8, waiting for transfers between devices, trade(): return lax.ppermute(array, 'col', [(0, 1), (1, 0)])  48.4 us
    all_gather x1, waiting for transfers between devices, body(): cotangent_all = lax.all_gather(cotangent, 'row', axis=0, tiled=True)  40.1 us
    dot_general x4, matrix products, block_product(): lax.dot_general(left, right, (((1,), (1,)), ((), ())), preferred_element_...  34.9 us
    ppermute x6, waiting for transfers between devices, from_behind(): lax.ppermute(array, 'row', [(i, (i + by) % count) for i in range(count)])  24 us
    dot_general x2, matrix products, gradient_tile(): lax.dot_general(columns, cotangent_all, (((0,), (0,)), ((), ())), preferr...  17.6 us
    ppermute x16, starting transfers between devices, swap(): return lax.ppermute(array, 'row', [(i, i ^ mask) for i in range(count)])  10.5 us
  transfers between devices with their start and end apart: 31, of which 17 were waited for; matrix products, arithmetic and copies ran while one was open for 18% of the time, Pallas kernels for 18%

profile of v12, /device:TPU:0, one launch (start us, length us, event | category | flops | bytes accessed | tf_op | source)
XLA Modules:
  0.0 437.8 jit_solution(6401984227567122319)
XLA Ops:
  7.2 0.7 all-gather.2.cloned.1.call-update
  7.9 3.0 collective-permute-start
  10.9 1.6 collective-permute-start.1
  12.5 2.6 collective-permute-start.2
  15.1 4.3 collective-permute-done.1
  19.4 4.2 collective-permute-done.2
  23.6 0.5 collective-permute-start.7
  24.1 1.0 pad_maximum_fusion.3
  25.1 1.6 collective-permute-start.4
  26.7 12.0 %collective-permute-done.4 = bf16[4,128,512]{2,1,0:T(8,128)(2,1)S(1)} collective-permute-done((bf16[4,128,512]{2,1,0:T(8,128)(2,1)S(1)}, bf16[4,128,512]{2,1,0:T(8,128)(2,1)S(1)}, u32[]{:S(2)}, u32[]{:S(2)}) %collective-permute-start.4) | collective-permute-done | bytes 524320 | tf_op jit(solution)/shard_map/ppermute | solution.py:23
  38.7 1.4 maximum_select_fusion
  40.1 40.1 %all-gather.2.cloned.1.call-done.refs_6_ = bf16[256,7168]{1,0:T(8,128)(2,1)} async-done(((bf16[16,7168]{1,0:T(8,128)(2,1)}), bf16[256,7168]{1,0:T(8,128)(2,1)}) %all-gather.2.cloned.1.call-update) | async-done | bytes 3670032 | tf_op jit(solution)/shard_map/all_gather | solution.py:211
  80.2 9.4 %add_convert_fusion.1.refs_0_ = bf16[512,7168]{1,0:T(8,128)(2,1)} fusion(bf16[512,7168]{1,0:T(8,128)(2,1)} %param.7, bf16[256,7168]{1,0:T(8,128)(2,1)} %all-gather.2.cloned.1.call-done.refs_6_, bf16[4,256,512]{2,1,0:T(8,128)(2,1)S(1)} %maximum_select_fusion), kind=kOutput, calls=%fused_computation.1 | convolution fusion | flops 1890058240 | bytes 18612224 | tf_op jit(solution)/shard_map/dot_general | solution.py:27
  89.6 0.3 collective-permute-start.5
  89.8 103.8 %collective-permute-done.7 = bf16[512,7168]{1,0:T(8,128)(2,1)} collective-permute-done((bf16[512,7168]{1,0:T(8,128)(2,1)}, bf16[512,7168]{1,0:T(8,128)(2,1)}, u32[]{:S(2)}, u32[]{:S(2)}) %collective-permute-start.7) | collective-permute-done | bytes 7340064 | tf_op jit(solution)/shard_map/ppermute | solution.py:14
  193.6 8.3 %add_convert_fusion.refs_2_ = bf16[512,7168]{1,0:T(8,128)(2,1)} fusion(bf16[512,7168]{1,0:T(8,128)(2,1)} %collective-permute-done.7, bf16[256,7168]{1,0:T(8,128)(2,1)S(1)} %copy-done, bf16[4,256,512]{2,1,0:T(8,128)(2,1)S(1)} %maximum_select_fusion), kind=kOutput, calls=%fused_computation | convolution fusion | flops 1890058240 | bytes 18612224 | tf_op jit(solution)/shard_map/dot_general | solution.py:27
  202.0 4.9 %collective-permute-done.3.refs_4_ = bf16[512,7168]{1,0:T(8,128)(2,1)} collective-permute-done((bf16[512,7168]{1,0:T(8,128)(2,1)}, bf16[512,7168]{1,0:T(8,128)(2,1)}, u32[]{:S(2)}, u32[]{:S(2)}) %collective-permute-start.3) | collective-permute-done | bytes 7340064 | tf_op jit(solution)/shard_map/ppermute | solution.py:19
  206.9 2.3 slice.66
  209.4 8.5 %fusion.4 = f32[512,512]{1,0:T(8,128)S(1)} fusion(bf16[512,7168]{1,0:T(8,128)(2,1)} %add_convert_fusion.1.refs_0_, bf16[512,7168]{1,0:T(8,128)(2,1)} %collective-permute-done.5.refs_1_), kind=kOutput, calls=%fused_computation.66 | convolution fusion | flops 3758096384 | bytes 15728640 | tf_op jit(solution)/shard_map/dot_general | solution.py:34
  217.9 0.9 convert_bitcast_fusion.3
  218.8 1.1 collective-permute-start.15
  219.9 9.3 %fusion.3 = f32[512,512]{1,0:T(8,128)S(1)} fusion(bf16[512,7168]{1,0:T(8,128)(2,1)} %add_convert_fusion.1.refs_0_), kind=kOutput, calls=%fused_computation.65 | convolution fusion | flops 3758096384 | bytes 8388608 | tf_op jit(solution)/shard_map/dot_general | solution.py:34
  229.3 4.5 %fusion.1 = (bf16[128,7168]{1,0:T(8,128)(2,1)}, bf16[128,7168]{1,0:T(8,128)(2,1)}) fusion(bf16[512,7168]{1,0:T(8,128)(2,1)} %collective-permute-done.3.refs_4_), kind=kLoop, calls=%fused_computation.63 | loop fusion | bytes 7340032 | tf_op jit(solution)/shard_map/split | solution.py:241
  233.8 1.0 collective-permute-start.16
  234.8 25.2 %shard_map.68 = f32[4,512,512]{2,1,0:T(8,128)} custom-call(bf16[512,7168]{1,0:T(8,128)(2,1)} %add_convert_fusion.1.refs_0_, bf16[512,7168]{1,0:T(8,128)(2,1)} %collective-permute-done.5.refs_1_, bf16[512,7168]{1,0:T(8,128)(2,1)} %add_convert_fusion.refs_2_, bf16[512,7168]{1,0:T(8,128)(2,1)} %collective-permute-done.8.refs_3_, ...), custom_call_target="tpu_custom_call" | custom-call | flops 16911433728 | bytes 44564480 | tf_op jit(solution)/shard_map/pallas_call | solution.py:61
  260.1 3.6 slice_bitcast_fusion
  263.7 0.9 collective-permute-start.10
  264.6 8.5 %fusion.5 = f32[512,512]{1,0:T(8,128)S(1)} fusion(bf16[512,7168]{1,0:T(8,128)(2,1)} %add_convert_fusion.1.refs_0_, bf16[512,7168]{1,0:T(8,128)(2,1)} %add_convert_fusion.refs_2_), kind=kOutput, calls=%fused_computation.67 | convolution fusion | flops 3758096384 | bytes 15728640 | tf_op jit(solution)/shard_map/dot_general | solution.py:34
  273.1 1.1 dynamic-slice_add_fusion
  274.3 2.2 convert_add_fusion.3.refs_0_
  276.5 12.8 %collective-permute-done.10 = f32[512,512]{1,0:T(8,128)S(1)} collective-permute-done((f32[512,512]{1,0:T(8,128)S(1)}, f32[512,512]{1,0:T(8,128)S(1)}, u32[]{:S(2)}, u32[]{:S(2)}) %collective-permute-start.10) | collective-permute-done | bytes 1048608 | tf_op jit(solution)/shard_map/ppermute | solution.py:14
  289.3 2.6 collective-permute-done.6.refs_4_
  292.1 1.3 pad_maximum_fusion
  293.4 1.3 collective-permute-start.13
  294.8 8.5 %fusion.6 = f32[512,512]{1,0:T(8,128)S(1)} fusion(bf16[512,7168]{1,0:T(8,128)(2,1)} %add_convert_fusion.1.refs_0_, bf16[512,7168]{1,0:T(8,128)(2,1)} %collective-permute-done.8.refs_3_), kind=kOutput, calls=%fused_computation.68 | convolution fusion | flops 3758096384 | bytes 15728640 | tf_op jit(solution)/shard_map/dot_general | solution.py:34
  303.5 14.6 %shard_map.69 = f32[4,512,256]{2,1,0:T(8,128)S(1)} custom-call(bf16[512,7168]{1,0:T(8,128)(2,1)} %add_convert_fusion.1.refs_0_, bf16[512,7168]{1,0:T(8,128)(2,1)} %collective-permute-done.5.refs_1_, bf16[512,7168]{1,0:T(8,128)(2,1)} %add_convert_fusion.refs_2_, bf16[512,7168]{1,0:T(8,128)(2,1)} %collective-permute-done.8.refs_3_, ...), custom_call_target="tpu_custom_call" | custom-call | flops 8455716864 | bytes 38797312 | tf_op jit(solution)/shard_map/pallas_call | solution.py:61
  318.1 10.5 %collective-permute-done.13 = bf16[3,512,512]{2,1,0:T(8,128)(2,1)} collective-permute-done((bf16[3,512,512]{2,1,0:T(8,128)(2,1)}, bf16[3,512,512]{2,1,0:T(8,128)(2,1)}, u32[]{:S(2)}, u32[]{:S(2)}) %collective-permute-start.13) | collective-permute-done | bytes 1572896 | tf_op jit(solution)/shard_map/ppermute | solution.py:23
  328.6 3.2 convert_add_fusion.4
  331.9 2.5 collective-permute-done.12.refs_4_
  334.5 1.3 pad_maximum_fusion.1
  335.8 1.6 collective-permute-start.17
  337.6 0.4 collective-permute-start.19
  338.0 1.5 collective-permute-start.20
  339.5 14.1 %shard_map.70 = f32[4,512,128]{2,1,0:T(8,128)S(1)} custom-call(bf16[512,7168]{1,0:T(8,128)(2,1)} %add_convert_fusion.1.refs_0_, bf16[512,7168]{1,0:T(8,128)(2,1)} %collective-permute-done.5.refs_1_, bf16[512,7168]{1,0:T(8,128)(2,1)} %add_convert_fusion.refs_2_, bf16[512,7168]{1,0:T(8,128)(2,1)} %collective-permute-done.8.refs_3_, ...), custom_call_target="tpu_custom_call" | custom-call | flops 4227858432 | bytes 35913728 | tf_op jit(solution)/shard_map/pallas_call | solution.py:61
  353.6 16.5 %collective-permute-done.17 = bf16[3,512,512]{2,1,0:T(8,128)(2,1)} collective-permute-done((bf16[3,512,512]{2,1,0:T(8,128)(2,1)}, bf16[3,512,512]{2,1,0:T(8,128)(2,1)}, u32[]{:S(2)}, u32[]{:S(2)}) %collective-permute-start.17) | collective-permute-done | bytes 1572896 | tf_op jit(solution)/shard_map/ppermute | solution.py:23
  370.2 3.2 convert_add_fusion
  373.4 5.4 %collective-permute-done.11.refs_4_ = bf16[128,7168]{1,0:T(8,128)(2,1)S(1)} collective-permute-done((bf16[128,7168]{1,0:T(8,128)(2,1)S(1)}, bf16[128,7168]{1,0:T(8,128)(2,1)S(1)}, u32[]{:S(2)}, u32[]{:S(2)}) %collective-permute-start.11) | collective-permute-done | bytes 1835040 | tf_op jit(solution)/shard_map/ppermute | solution.py:19
  379.1 0.3 collective-permute-start.21
  379.9 0.5 collective-permute-start.23
  380.4 1.4 collective-permute-start.24
  381.7 14.1 %shard_map.71 = f32[4,512,128]{2,1,0:T(8,128)S(1)} custom-call(bf16[512,7168]{1,0:T(8,128)(2,1)} %add_convert_fusion.1.refs_0_, bf16[512,7168]{1,0:T(8,128)(2,1)} %collective-permute-done.5.refs_1_, bf16[512,7168]{1,0:T(8,128)(2,1)} %add_convert_fusion.refs_2_, bf16[512,7168]{1,0:T(8,128)(2,1)} %collective-permute-done.8.refs_3_, ...), custom_call_target="tpu_custom_call" | custom-call | flops 4227858432 | bytes 35913728 | tf_op jit(solution)/shard_map/pallas_call | solution.py:61
  396.0 6.2 %collective-permute-done.21.refs_11_ = bf16[4,512,256]{2,1,0:T(8,128)(2,1)S(1)} collective-permute-done((bf16[4,512,256]{2,1,0:T(8,128)(2,1)S(1)}, bf16[4,512,256]{2,1,0:T(8,128)(2,1)S(1)}, u32[]{:S(2)}, u32[]{:S(2)}) %collective-permute-start.21) | collective-permute-done | bytes 1048608 | tf_op jit(solution)/shard_map/ppermute | solution.py:23
  402.7 0.3 collective-permute-start.27
  403.0 1.6 collective-permute-start.28
  404.6 4.4 %collective-permute-done.27.refs_2_ = bf16[512,128]{1,0:T(8,128)(2,1)S(1)} collective-permute-done((bf16[512,128]{1,0:T(8,128)(2,1)S(1)}, bf16[512,128]{1,0:T(8,128)(2,1)S(1)}, u32[]{:S(2)}, u32[]{:S(2)}) %collective-permute-start.27) | collective-permute-done | bytes 131104 | tf_op jit(solution)/shard_map/ppermute | solution.py:14
  409.0 1.9 collective-permute-done.28.refs_3_
  410.9 1.2 collective-permute-done.25.refs_16_
  412.1 0.9 pad_maximum_fusion.5
  413.1 0.8 collective-permute-start.29
  413.9 0.7 pad_add_fusion.at_ref
  414.6 0.9 multiply_add_fusion
  415.5 9.2 %shard_map.72.band = f32[512,4,512]{2,1,0:T(4,128)} custom-call(s32[2]{0:T(128)} %pad_add_fusion.at_ref, f32[512,4,512]{2,1,0:T(4,128)} %old.1, f32[512,512]{1,0:T(8,128)} %convert_add_fusion.3.refs_0_, f32[512,512]{1,0:T(8,128)} %get-tuple-element.89.refs_1_, f32[512,512]{1,0:T(8,128)} %get-tuple-element.90.refs_2_, f32[512,512]{1,0:T(8,128)} %get-tuple-element.91.refs_3_, ...), custom_call_target="tpu_custom_call" | custom-call | tf_op jit(solution)/shard_map/pallas_call | solution.py:156
  424.8 1.9 collective-permute-done.29.refs_4_
  426.6 4.3 shard_map.73
  (90 shorter events, 2.3 us)
Async XLA Ops:
  7.2 73.1 %all-gather.2.cloned.1.call-start = ((), (), s32[]{:S(2)}) async-start(), calls=%async_computation | async-start | bytes 3899392 | tf_op jit(solution)/shard_map/all_gather | solution.py:211
  7.9 7.2 %collective-permute-start = (bf16[128,512]{1,0:T(8,128)(2,1)}, bf16[128,512]{1,0:T(8,128)(2,1)S(1)}, u32[]{:S(2)}, u32[]{:S(2)}) collective-permute-start(bf16[128,512]{1,0:T(8,128)(2,1)} %param.5), channel_id=1, source_target_pairs={{0,4},{2,6},{4,0},{6,2},{8,12},{10,14},{12,8},{14,10},{16,20},{18,... | collective-permute-start | bytes 393224 | tf_op jit(solution)/shard_map/ppermute | solution.py:14
  10.9 8.5 %collective-permute-start.1 = (bf16[128,512]{1,0:T(8,128)(2,1)}, bf16[128,512]{1,0:T(8,128)(2,1)S(1)}, u32[]{:S(2)}, u32[]{:S(2)}) collective-permute-start(bf16[128,512]{1,0:T(8,128)(2,1)} %param.5), channel_id=1, source_target_pairs={{0,8},{2,10},{4,12},{6,14},{8,16},{10,18},{12,20},{14,22},{16,24},... | collective-permute-start | bytes 393224 | tf_op jit(solution)/shard_map/ppermute | solution.py:19
  12.5 11.1 %collective-permute-start.2 = (bf16[128,512]{1,0:T(8,128)(2,1)}, bf16[128,512]{1,0:T(8,128)(2,1)S(1)}, u32[]{:S(2)}, u32[]{:S(2)}) collective-permute-start(bf16[128,512]{1,0:T(8,128)(2,1)} %param.5), channel_id=1, source_target_pairs={{0,16},{2,18},{4,20},{6,22},{8,24},{10,26},{12,28},{14,30},{16,0},... | collective-permute-start | bytes 393224 | tf_op jit(solution)/shard_map/ppermute | solution.py:19
  23.6 170.1 %collective-permute-start.7 = (bf16[512,7168]{1,0:T(8,128)(2,1)}, bf16[512,7168]{1,0:T(8,128)(2,1)}, u32[]{:S(2)}, u32[]{:S(2)}) collective-permute-start(bf16[512,7168]{1,0:T(8,128)(2,1)} %param.7), channel_id=1, source_target_pairs={{0,4},{2,6},{4,0},{6,2},{8,12},{10,14},{12,8},{14,10},{16,20},{18,... | collective-permute-start | bytes 22020104 | tf_op jit(solution)/shard_map/ppermute | solution.py:14
  25.1 13.6 %collective-permute-start.4 = (bf16[4,128,512]{2,1,0:T(8,128)(2,1)S(1)}, bf16[4,128,512]{2,1,0:T(8,128)(2,1)S(1)}, u32[]{:S(2)}, u32[]{:S(2)}) collective-permute-start(bf16[4,128,512]{2,1,0:T(8,128)(2,1)S(1)} %pad_maximum_fusion.3), channel_id=1, source_target_pairs={{0,1},{1,0},{2,3},{3,2},{4,5},{5,4},{6,7},{7,6},{8,9},{9,8},{10,11... | collective-permute-start | bytes 1572872 | tf_op jit(solution)/shard_map/ppermute | solution.py:23
  26.7 180.2 %collective-permute-start.3 = (bf16[512,7168]{1,0:T(8,128)(2,1)}, bf16[512,7168]{1,0:T(8,128)(2,1)}, u32[]{:S(2)}, u32[]{:S(2)}) collective-permute-start(bf16[512,7168]{1,0:T(8,128)(2,1)} %param.7), channel_id=1, source_target_pairs={{0,8},{2,10},{4,12},{6,14},{8,16},{10,18},{12,20},{14,22},{16,24},... | collective-permute-start | bytes 22020104 | tf_op jit(solution)/shard_map/ppermute | solution.py:19
  80.2 113.4 %copy-start = (bf16[256,7168]{1,0:T(8,128)(2,1)S(1)}, bf16[256,7168]{1,0:T(8,128)(2,1)}, u32[]{:S(2)}) copy-start(bf16[256,7168]{1,0:T(8,128)(2,1)} %all-gather.2.cloned.1.call-done.refs_6_) | copy-start | bytes 11010052
  89.6 117.3 %collective-permute-start.5 = (bf16[512,7168]{1,0:T(8,128)(2,1)}, bf16[512,7168]{1,0:T(8,128)(2,1)}, u32[]{:S(2)}, u32[]{:S(2)}) collective-permute-start(bf16[512,7168]{1,0:T(8,128)(2,1)} %add_convert_fusion.1.refs_0_), channel_id=1, source_target_pairs={{0,2},{2,0},{4,6},{6,4},{8,10},{10,8},{12,14},{14,12},{16,18},{18,... | collective-permute-start | bytes 22020104 | tf_op jit(solution)/shard_map/ppermute | solution.py:14
  201.9 32.9 %collective-permute-start.8 = (bf16[512,7168]{1,0:T(8,128)(2,1)}, bf16[512,7168]{1,0:T(8,128)(2,1)}, u32[]{:S(2)}, u32[]{:S(2)}) collective-permute-start(bf16[512,7168]{1,0:T(8,128)(2,1)} %add_convert_fusion.refs_2_), channel_id=1, source_target_pairs={{0,2},{2,0},{4,6},{6,4},{8,10},{10,8},{12,14},{14,12},{16,18},{18,... | collective-permute-start | bytes 22020104 | tf_op jit(solution)/shard_map/ppermute | solution.py:14
  209.2 82.8 %collective-permute-start.6 = (bf16[256,7168]{1,0:T(8,128)(2,1)S(1)}, bf16[256,7168]{1,0:T(8,128)(2,1)S(1)}, u32[]{:S(2)}, u32[]{:S(2)}) collective-permute-start(bf16[256,7168]{1,0:T(8,128)(2,1)S(1)} %slice.66), channel_id=1, source_target_pairs={{0,8},{2,10},{4,12},{6,14},{8,16},{10,18},{12,20},{14,22},{16,24},... | collective-permute-start | bytes 11010056 | tf_op jit(solution)/shard_map/ppermute | solution.py:19
  218.8 55.4 %collective-permute-start.15 = (bf16[1,512,512]{2,1,0:T(8,128)(2,1)}, bf16[1,512,512]{2,1,0:T(8,128)(2,1)}, u32[]{:S(2)}, u32[]{:S(2)}) collective-permute-start(bf16[1,512,512]{2,1,0:T(8,128)(2,1)} %convert_bitcast_fusion.3), channel_id=1, source_target_pairs={{0,1},{1,0},{2,3},{3,2},{4,5},{5,4},{6,7},{7,6},{8,9},{9,8},{10,11... | collective-permute-start | bytes 1572872 | tf_op jit(solution)/shard_map/ppermute | solution.py:23
  229.3 4.6 %copy-start.13 = (f32[512,512]{1,0:T(8,128)}, f32[512,512]{1,0:T(8,128)S(1)}, u32[]{:S(2)}) copy-start(f32[512,512]{1,0:T(8,128)S(1)} %fusion.3) | copy-start | bytes 3145732
  229.3 5.6 %copy-start.1 = (bf16[256,7168]{1,0:T(8,128)(2,1)S(1)}, bf16[256,7168]{1,0:T(8,128)(2,1)}, u32[]{:S(2)}) copy-start(bf16[256,7168]{1,0:T(8,128)(2,1)} %all-gather.2.cloned.1.call-done.refs_6_) | copy-start | bytes 11010052
  233.8 39.3 %collective-permute-start.16 = (f32[256,512]{1,0:T(8,128)S(1)}, f32[256,512]{1,0:T(8,128)}, u32[]{:S(2)}, u32[]{:S(2)}) collective-permute-start(f32[256,512]{1,0:T(8,128)S(1)} %constant_dynamic-slice_fusion), channel_id=1, source_target_pairs={{0,1},{1,0},{2,3},{3,2},{4,5},{5,4},{6,7},{7,6},{8,9},{9,8},{10,11... | collective-permute-start | bytes 1572872 | tf_op jit(solution)/shard_map/ppermute | solution.py:23
  263.7 12.8 %collective-permute-start.9 = (f32[512,512]{1,0:T(8,128)S(1)}, f32[512,512]{1,0:T(8,128)S(1)}, u32[]{:S(2)}, u32[]{:S(2)}) collective-permute-start(f32[512,512]{1,0:T(8,128)S(1)} %get-tuple-element.130), channel_id=1, source_target_pairs={{0,2},{2,0},{4,6},{6,4},{8,10},{10,8},{12,14},{14,12},{16,18},{18,... | collective-permute-start | bytes 3145736 | tf_op jit(solution)/shard_map/ppermute | solution.py:14
  263.7 9.4 %copy-start.14 = (f32[512,512]{1,0:T(8,128)S(1)}, f32[512,512]{1,0:T(8,128)}, u32[]{:S(2)}) copy-start(f32[512,512]{1,0:T(8,128)} %copy-done.13) | copy-start | bytes 3145732
  263.7 25.6 %collective-permute-start.10 = (f32[512,512]{1,0:T(8,128)S(1)}, f32[512,512]{1,0:T(8,128)S(1)}, u32[]{:S(2)}, u32[]{:S(2)}) collective-permute-start(f32[512,512]{1,0:T(8,128)S(1)} %get-tuple-element.129), channel_id=1, source_target_pairs={{0,4},{2,6},{4,0},{6,2},{8,12},{10,14},{12,8},{14,10},{16,20},{18,... | collective-permute-start | bytes 3145736 | tf_op jit(solution)/shard_map/ppermute | solution.py:14
  291.9 42.5 %collective-permute-start.12 = (bf16[128,7168]{1,0:T(8,128)(2,1)}, bf16[128,7168]{1,0:T(8,128)(2,1)S(1)}, u32[]{:S(2)}, u32[]{:S(2)}) collective-permute-start(bf16[128,7168]{1,0:T(8,128)(2,1)} %get-tuple-element.72), channel_id=1, source_target_pairs={{0,8},{2,10},{4,12},{6,14},{8,16},{10,18},{12,20},{14,22},{16,24},... | collective-permute-start | bytes 5505032 | tf_op jit(solution)/shard_map/ppermute | solution.py:19
  293.4 35.2 %collective-permute-start.13 = (bf16[3,512,512]{2,1,0:T(8,128)(2,1)}, bf16[3,512,512]{2,1,0:T(8,128)(2,1)}, u32[]{:S(2)}, u32[]{:S(2)}) collective-permute-start(bf16[3,512,512]{2,1,0:T(8,128)(2,1)} %pad_maximum_fusion), channel_id=1, source_target_pairs={{0,1},{1,0},{2,3},{3,2},{4,5},{5,4},{6,7},{7,6},{8,9},{9,8},{10,11... | collective-permute-start | bytes 4718600 | tf_op jit(solution)/shard_map/ppermute | solution.py:23
  303.3 28.5 %collective-permute-start.14 = (f32[512,512]{1,0:T(8,128)}, f32[512,512]{1,0:T(8,128)S(1)}, u32[]{:S(2)}, u32[]{:S(2)}) collective-permute-start(f32[512,512]{1,0:T(8,128)} %get-tuple-element.76), channel_id=1, source_target_pairs={{0,6},{2,4},{4,2},{6,0},{8,14},{10,12},{12,10},{14,8},{16,22},{18,... | collective-permute-start | bytes 3145736 | tf_op jit(solution)/shard_map/ppermute | solution.py:14
  331.8 5.5 %copy-start.8 = (bf16[128,7168]{1,0:T(8,128)(2,1)S(1)}, bf16[128,7168]{1,0:T(8,128)(2,1)}, u32[]{:S(2)}) copy-start(bf16[128,7168]{1,0:T(8,128)(2,1)} %get-tuple-element.71) | copy-start | bytes 5505028
  335.8 34.4 %collective-permute-start.17 = (bf16[3,512,512]{2,1,0:T(8,128)(2,1)}, bf16[3,512,512]{2,1,0:T(8,128)(2,1)}, u32[]{:S(2)}, u32[]{:S(2)}) collective-permute-start(bf16[3,512,512]{2,1,0:T(8,128)(2,1)} %pad_maximum_fusion.1), channel_id=1, source_target_pairs={{0,1},{1,0},{2,3},{3,2},{4,5},{5,4},{6,7},{7,6},{8,9},{9,8},{10,11... | collective-permute-start | bytes 4718600 | tf_op jit(solution)/shard_map/ppermute | solution.py:23
  337.4 41.3 %collective-permute-start.11 = (bf16[128,7168]{1,0:T(8,128)(2,1)S(1)}, bf16[128,7168]{1,0:T(8,128)(2,1)S(1)}, u32[]{:S(2)}, u32[]{:S(2)}) collective-permute-start(bf16[128,7168]{1,0:T(8,128)(2,1)S(1)} %copy-done.8), channel_id=1, source_target_pairs={{0,8},{2,10},{4,12},{6,14},{8,16},{10,18},{12,20},{14,22},{16,24},... | collective-permute-start | bytes 5505032 | tf_op jit(solution)/shard_map/ppermute | solution.py:19
  337.6 41.3 %copy-start.2 = (f32[512,256]{1,0:T(8,128)}, f32[512,256]{1,0:T(8,128)S(1)}, u32[]{:S(2)}) copy-start(f32[512,256]{1,0:T(8,128)S(1)} %get-tuple-element.111.refs_7_) | copy-start | bytes 1572868
  337.6 41.2 %collective-permute-start.18 = (f32[512,256]{1,0:T(8,128)S(1)}, f32[512,256]{1,0:T(8,128)S(1)}, u32[]{:S(2)}, u32[]{:S(2)}) collective-permute-start(f32[512,256]{1,0:T(8,128)S(1)} %get-tuple-element.134), channel_id=1, source_target_pairs={{0,2},{2,0},{4,6},{6,4},{8,10},{10,8},{12,14},{14,12},{16,18},{18,... | collective-permute-start | bytes 1572872 | tf_op jit(solution)/shard_map/ppermute | solution.py:14
  337.6 41.1 %collective-permute-start.19 = (f32[512,256]{1,0:T(8,128)S(1)}, f32[512,256]{1,0:T(8,128)S(1)}, u32[]{:S(2)}, u32[]{:S(2)}) collective-permute-start(f32[512,256]{1,0:T(8,128)S(1)} %get-tuple-element.133), channel_id=1, source_target_pairs={{0,4},{2,6},{4,0},{6,2},{8,12},{10,14},{12,8},{14,10},{16,20},{18,... | collective-permute-start | bytes 1572872 | tf_op jit(solution)/shard_map/ppermute | solution.py:14
  338.0 40.7 %collective-permute-start.20 = (f32[512,256]{1,0:T(8,128)S(1)}, f32[512,256]{1,0:T(8,128)S(1)}, u32[]{:S(2)}, u32[]{:S(2)}) collective-permute-start(f32[512,256]{1,0:T(8,128)S(1)} %get-tuple-element.132), channel_id=1, source_target_pairs={{0,6},{2,4},{4,2},{6,0},{8,14},{10,12},{12,10},{14,8},{16,22},{18,... | collective-permute-start | bytes 1572872 | tf_op jit(solution)/shard_map/ppermute | solution.py:14
  378.7 0.8 copy-start.5
  378.7 1.0 copy-start.6
  378.8 1.1 copy-start.7
  379.1 23.1 %collective-permute-start.21 = (bf16[4,512,256]{2,1,0:T(8,128)(2,1)S(1)}, bf16[4,512,256]{2,1,0:T(8,128)(2,1)S(1)}, u32[]{:S(2)}, u32[]{:S(2)}) collective-permute-start(bf16[4,512,256]{2,1,0:T(8,128)(2,1)S(1)} %pad_maximum_fusion.2), channel_id=1, source_target_pairs={{0,1},{1,0},{2,3},{3,2},{4,5},{5,4},{6,7},{7,6},{8,9},{9,8},{10,11... | collective-permute-start | bytes 3145736 | tf_op jit(solution)/shard_map/ppermute | solution.py:23
  379.9 22.4 %copy-start.3 = (f32[512,128]{1,0:T(8,128)}, f32[512,128]{1,0:T(8,128)S(1)}, u32[]{:S(2)}) copy-start(f32[512,128]{1,0:T(8,128)S(1)} %get-tuple-element.116.refs_12_) | copy-start | bytes 786436
  379.9 16.0 %collective-permute-start.22 = (f32[512,128]{1,0:T(8,128)S(1)}, f32[512,128]{1,0:T(8,128)S(1)}, u32[]{:S(2)}, u32[]{:S(2)}) collective-permute-start(f32[512,128]{1,0:T(8,128)S(1)} %get-tuple-element.144), channel_id=1, source_target_pairs={{0,2},{2,0},{4,6},{6,4},{8,10},{10,8},{12,14},{14,12},{16,18},{18,... | collective-permute-start | bytes 786440 | tf_op jit(solution)/shard_map/ppermute | solution.py:14
  379.9 16.0 %collective-permute-start.23 = (f32[512,128]{1,0:T(8,128)S(1)}, f32[512,128]{1,0:T(8,128)S(1)}, u32[]{:S(2)}, u32[]{:S(2)}) collective-permute-start(f32[512,128]{1,0:T(8,128)S(1)} %get-tuple-element.143), channel_id=1, source_target_pairs={{0,4},{2,6},{4,0},{6,2},{8,12},{10,14},{12,8},{14,10},{16,20},{18,... | collective-permute-start | bytes 786440 | tf_op jit(solution)/shard_map/ppermute | solution.py:14
  380.4 15.5 %collective-permute-start.24 = (f32[512,128]{1,0:T(8,128)S(1)}, f32[512,128]{1,0:T(8,128)S(1)}, u32[]{:S(2)}, u32[]{:S(2)}) collective-permute-start(f32[512,128]{1,0:T(8,128)S(1)} %get-tuple-element.142), channel_id=1, source_target_pairs={{0,6},{2,4},{4,2},{6,0},{8,14},{10,12},{12,10},{14,8},{16,22},{18,... | collective-permute-start | bytes 786440 | tf_op jit(solution)/shard_map/ppermute | solution.py:14
  395.9 18.7 %copy-start.18 = (f32[256,512]{1,0:T(8,128)S(1)}, f32[256,512]{1,0:T(8,128)}, u32[]{:S(2)}) copy-start(f32[256,512]{1,0:T(8,128)} %param.9) | copy-start | bytes 1572868
  395.9 19.6 %copy-start.9 = (f32[512,128]{1,0:T(8,128)}, f32[512,128]{1,0:T(8,128)S(1)}, u32[]{:S(2)}) copy-start(f32[512,128]{1,0:T(8,128)S(1)} %collective-permute-done.22.refs_13_) | copy-start | bytes 786436
  395.9 19.6 %copy-start.10 = (f32[512,128]{1,0:T(8,128)}, f32[512,128]{1,0:T(8,128)S(1)}, u32[]{:S(2)}) copy-start(f32[512,128]{1,0:T(8,128)S(1)} %collective-permute-done.23.refs_14_) | copy-start | bytes 786436
  396.0 19.5 %copy-start.11 = (f32[512,128]{1,0:T(8,128)}, f32[512,128]{1,0:T(8,128)S(1)}, u32[]{:S(2)}) copy-start(f32[512,128]{1,0:T(8,128)S(1)} %collective-permute-done.24.refs_15_) | copy-start | bytes 786436
  402.2 2.3 copy-start.12
  402.4 9.7 %collective-permute-start.25 = (bf16[4,512,128]{2,1,0:T(8,128)(2,1)S(1)}, bf16[4,512,128]{2,1,0:T(8,128)(2,1)S(1)}, u32[]{:S(2)}, u32[]{:S(2)}) collective-permute-start(bf16[4,512,128]{2,1,0:T(8,128)(2,1)S(1)} %pad_maximum_fusion.4), channel_id=1, source_target_pairs={{0,1},{1,0},{2,3},{3,2},{4,5},{5,4},{6,7},{7,6},{8,9},{9,8},{10,11... | collective-permute-start | bytes 1572872 | tf_op jit(solution)/shard_map/ppermute | solution.py:23
  402.6 2.0 collective-permute-start.26
  402.7 6.4 %collective-permute-start.27 = (bf16[512,128]{1,0:T(8,128)(2,1)S(1)}, bf16[512,128]{1,0:T(8,128)(2,1)S(1)}, u32[]{:S(2)}, u32[]{:S(2)}) collective-permute-start(bf16[512,128]{1,0:T(8,128)(2,1)S(1)} %get-tuple-element.149), channel_id=1, source_target_pairs={{0,4},{2,6},{4,0},{6,2},{8,12},{10,14},{12,8},{14,10},{16,20},{18,... | collective-permute-start | bytes 393224 | tf_op jit(solution)/shard_map/ppermute | solution.py:14
  403.0 8.0 %collective-permute-start.28 = (bf16[512,128]{1,0:T(8,128)(2,1)S(1)}, bf16[512,128]{1,0:T(8,128)(2,1)S(1)}, u32[]{:S(2)}, u32[]{:S(2)}) collective-permute-start(bf16[512,128]{1,0:T(8,128)(2,1)S(1)} %get-tuple-element.148), channel_id=1, source_target_pairs={{0,6},{2,4},{4,2},{6,0},{8,14},{10,12},{12,10},{14,8},{16,22},{18,... | collective-permute-start | bytes 393224 | tf_op jit(solution)/shard_map/ppermute | solution.py:14
  404.6 20.2 %copy-start.4 = (f32[512,128]{1,0:T(8,128)}, f32[512,128]{1,0:T(8,128)S(1)}, u32[]{:S(2)}) copy-start(f32[512,128]{1,0:T(8,128)S(1)} %slice_bitcast_fusion.22.refs_0_) | copy-start | bytes 786436
  404.6 20.2 %copy-start.15 = (bf16[512,128]{1,0:T(8,128)(2,1)}, bf16[512,128]{1,0:T(8,128)(2,1)S(1)}, u32[]{:S(2)}) copy-start(bf16[512,128]{1,0:T(8,128)(2,1)S(1)} %collective-permute-done.26.refs_1_) | copy-start | bytes 393220
  409.0 15.7 %copy-start.16 = (bf16[512,128]{1,0:T(8,128)(2,1)}, bf16[512,128]{1,0:T(8,128)(2,1)S(1)}, u32[]{:S(2)}) copy-start(bf16[512,128]{1,0:T(8,128)(2,1)S(1)} %collective-permute-done.27.refs_2_) | copy-start | bytes 393220
  410.9 13.8 %copy-start.17 = (bf16[512,128]{1,0:T(8,128)(2,1)}, bf16[512,128]{1,0:T(8,128)(2,1)S(1)}, u32[]{:S(2)}) copy-start(bf16[512,128]{1,0:T(8,128)(2,1)S(1)} %collective-permute-done.28.refs_3_) | copy-start | bytes 393220
  412.1 3.4 copy-start.19
  413.1 13.5 %collective-permute-start.29 = (bf16[4,512,128]{2,1,0:T(8,128)(2,1)}, bf16[4,512,128]{2,1,0:T(8,128)(2,1)}, u32[]{:S(2)}, u32[]{:S(2)}) collective-permute-start(bf16[4,512,128]{2,1,0:T(8,128)(2,1)} %pad_maximum_fusion.5), channel_id=1, source_target_pairs={{0,1},{1,0},{2,3},{3,2},{4,5},{5,4},{6,7},{7,6},{8,9},{9,8},{10,11... | collective-permute-start | bytes 1572872 | tf_op jit(solution)/shard_map/ppermute | solution.py:23
Sparse Core Ops, SparseCore 0:
  10.3 69.9 all-gather.1

commit v13 on v12

--- a/solution.py
+++ b/solution.py
@@ -278,13 +278,13 @@
     last = [(handed, over_columns(handed))]
     handed = to_owners(made)
     made = products([fourth], behind[-1][:, half + quarter :])
-    last, handed, made = phase((last, handed, made))
+    handed, made = phase((handed, made))
 
     last.append((handed, over_columns(handed)))
     if paired:
         made = [made[0], *(made[u].astype(jnp.bfloat16) for u in range(1, GROUP))]
     handed = to_owners(made)
-    last, handed = phase((last, handed))
+    handed = phase(handed)
     last.append((handed, over_columns(handed)))
 
     if paired:

time: 438 us -> 436 us (level)
  waiting for transfers between devices: 236 us -> 231 us
    ppermute x8, waiting for transfers between devices: 48.4 us -> 43.3 us  [trade(): return lax.ppermute(array, 'col', [(0, 1), (1, 0)])]
  transfers between devices with their start and end apart: 31 -> 31, of which waited for: 17 -> 16; matrix products, arithmetic and copies ran while one was open for 18% -> 19% of each run, Pallas kernels for 18% -> 18%
where the time goes in v13:
time: 436 us
  waiting for transfers between devices  231 us (53%)
  Pallas kernels  81.5 us (19%)
  matrix products  52.5 us (12%)
  starting transfers between devices  23.9 us (5%)
  other arithmetic  20.8 us (5%)
  between operations  14.5 us (3%)
  local copies, waits for them, and re-layouts  11.6 us (3%)
    ppermute x16, waiting for transfers between devices, swap(): return lax.ppermute(array, 'row', [(i, i ^ mask) for i in range(count)])  123 us
    pallas_call x4, Pallas kernels, panel_products(): pl.pallas_call(products_kernel, grid=(width // depth,), in_specs=[pl.Bloc...  68 us
    ppermute x8, waiting for transfers between devices, trade(): return lax.ppermute(array, 'col', [(0, 1), (1, 0)])  43.3 us
    all_gather x1, waiting for transfers between devices, body(): cotangent_all = lax.all_gather(cotangent, 'row', axis=0, tiled=True)  40.1 us
    dot_general x4, matrix products, block_product(): lax.dot_general(left, right, (((1,), (1,)), ((), ())), preferred_element_...  34.9 us
    ppermute x6, waiting for transfers between devices, from_behind(): lax.ppermute(array, 'row', [(i, (i + by) % count) for i in range(count)])  24 us
    dot_general x2, matrix products, gradient_tile(): lax.dot_general(columns, cotangent_all, (((0,), (0,)), ((), ())), preferr...  17.6 us
    ppermute x16, starting transfers between devices, swap(): return lax.ppermute(array, 'row', [(i, i ^ mask) for i in range(count)])  10.5 us
  transfers between devices with their start and end apart: 31, of which 16 were waited for; matrix products, arithmetic and copies ran while one was open for 19% of the time, Pallas kernels for 18%

profile of v13, /device:TPU:0, one launch (start us, length us, event | category | flops | bytes accessed | tf_op | source)
XLA Modules:
  0.0 435.9 jit_solution(8464109211245000100)
XLA Ops:
  7.2 0.7 all-gather.2.cloned.1.call-update
  7.9 3.0 collective-permute-start
  10.9 1.6 collective-permute-start.1
  12.5 2.6 collective-permute-start.2
  15.1 4.3 collective-permute-done.1
  19.4 4.2 collective-permute-done.2
  23.6 0.5 collective-permute-start.7
  24.1 1.0 pad_maximum_fusion.3
  25.1 1.6 collective-permute-start.4
  26.7 12.0 %collective-permute-done.4 = bf16[4,128,512]{2,1,0:T(8,128)(2,1)S(1)} collective-permute-done((bf16[4,128,512]{2,1,0:T(8,128)(2,1)S(1)}, bf16[4,128,512]{2,1,0:T(8,128)(2,1)S(1)}, u32[]{:S(2)}, u32[]{:S(2)}) %collective-permute-start.4) | collective-permute-done | bytes 524320 | tf_op jit(solution)/shard_map/ppermute | solution.py:23
  38.7 1.4 maximum_select_fusion
  40.1 40.1 %all-gather.2.cloned.1.call-done.refs_6_ = bf16[256,7168]{1,0:T(8,128)(2,1)} async-done(((bf16[16,7168]{1,0:T(8,128)(2,1)}), bf16[256,7168]{1,0:T(8,128)(2,1)}) %all-gather.2.cloned.1.call-update) | async-done | bytes 3670032 | tf_op jit(solution)/shard_map/all_gather | solution.py:211
  80.2 9.4 %add_convert_fusion.1.refs_0_ = bf16[512,7168]{1,0:T(8,128)(2,1)} fusion(bf16[512,7168]{1,0:T(8,128)(2,1)} %param.7, bf16[256,7168]{1,0:T(8,128)(2,1)} %all-gather.2.cloned.1.call-done.refs_6_, bf16[4,256,512]{2,1,0:T(8,128)(2,1)S(1)} %maximum_select_fusion), kind=kOutput, calls=%fused_computation.1 | convolution fusion | flops 1890058240 | bytes 18612224 | tf_op jit(solution)/shard_map/dot_general | solution.py:27
  89.8 103.8 %collective-permute-done.7 = bf16[512,7168]{1,0:T(8,128)(2,1)} collective-permute-done((bf16[512,7168]{1,0:T(8,128)(2,1)}, bf16[512,7168]{1,0:T(8,128)(2,1)}, u32[]{:S(2)}, u32[]{:S(2)}) %collective-permute-start.7) | collective-permute-done | bytes 7340064 | tf_op jit(solution)/shard_map/ppermute | solution.py:14
  193.6 8.2 %add_convert_fusion.refs_2_ = bf16[512,7168]{1,0:T(8,128)(2,1)} fusion(bf16[512,7168]{1,0:T(8,128)(2,1)} %collective-permute-done.7, bf16[256,7168]{1,0:T(8,128)(2,1)S(1)} %copy-done, bf16[4,256,512]{2,1,0:T(8,128)(2,1)S(1)} %maximum_select_fusion), kind=kOutput, calls=%fused_computation | convolution fusion | flops 1890058240 | bytes 18612224 | tf_op jit(solution)/shard_map/dot_general | solution.py:27
  201.9 4.9 %collective-permute-done.3.refs_4_ = bf16[512,7168]{1,0:T(8,128)(2,1)} collective-permute-done((bf16[512,7168]{1,0:T(8,128)(2,1)}, bf16[512,7168]{1,0:T(8,128)(2,1)}, u32[]{:S(2)}, u32[]{:S(2)}) %collective-permute-start.3) | collective-permute-done | bytes 7340064 | tf_op jit(solution)/shard_map/ppermute | solution.py:19
  206.9 2.3 slice.66
  209.4 8.5 %fusion.4 = f32[512,512]{1,0:T(8,128)S(1)} fusion(bf16[512,7168]{1,0:T(8,128)(2,1)} %add_convert_fusion.1.refs_0_, bf16[512,7168]{1,0:T(8,128)(2,1)} %collective-permute-done.5.refs_1_), kind=kOutput, calls=%fused_computation.66 | convolution fusion | flops 3758096384 | bytes 15728640 | tf_op jit(solution)/shard_map/dot_general | solution.py:34
  217.9 0.9 convert_bitcast_fusion.3
  218.8 1.1 collective-permute-start.15
  219.9 9.3 %fusion.3 = f32[512,512]{1,0:T(8,128)S(1)} fusion(bf16[512,7168]{1,0:T(8,128)(2,1)} %add_convert_fusion.1.refs_0_), kind=kOutput, calls=%fused_computation.65 | convolution fusion | flops 3758096384 | bytes 8388608 | tf_op jit(solution)/shard_map/dot_general | solution.py:34
  229.3 4.5 %fusion.1 = (bf16[128,7168]{1,0:T(8,128)(2,1)}, bf16[128,7168]{1,0:T(8,128)(2,1)}) fusion(bf16[512,7168]{1,0:T(8,128)(2,1)} %collective-permute-done.3.refs_4_), kind=kLoop, calls=%fused_computation.63 | loop fusion | bytes 7340032 | tf_op jit(solution)/shard_map/split | solution.py:241
  233.8 1.0 collective-permute-start.16
  234.8 25.2 %shard_map.68 = f32[4,512,512]{2,1,0:T(8,128)} custom-call(bf16[512,7168]{1,0:T(8,128)(2,1)} %add_convert_fusion.1.refs_0_, bf16[512,7168]{1,0:T(8,128)(2,1)} %collective-permute-done.5.refs_1_, bf16[512,7168]{1,0:T(8,128)(2,1)} %add_convert_fusion.refs_2_, bf16[512,7168]{1,0:T(8,128)(2,1)} %collective-permute-done.8.refs_3_, ...), custom_call_target="tpu_custom_call" | custom-call | flops 16911433728 | bytes 44564480 | tf_op jit(solution)/shard_map/pallas_call | solution.py:61
  260.1 3.6 slice_bitcast_fusion
  263.7 0.9 collective-permute-start.10
  264.6 8.5 %fusion.5 = f32[512,512]{1,0:T(8,128)S(1)} fusion(bf16[512,7168]{1,0:T(8,128)(2,1)} %add_convert_fusion.1.refs_0_, bf16[512,7168]{1,0:T(8,128)(2,1)} %add_convert_fusion.refs_2_), kind=kOutput, calls=%fused_computation.67 | convolution fusion | flops 3758096384 | bytes 15728640 | tf_op jit(solution)/shard_map/dot_general | solution.py:34
  273.1 1.1 dynamic-slice_add_fusion
  274.3 2.2 convert_add_fusion.3.refs_0_
  276.5 12.8 %collective-permute-done.10 = f32[512,512]{1,0:T(8,128)S(1)} collective-permute-done((f32[512,512]{1,0:T(8,128)S(1)}, f32[512,512]{1,0:T(8,128)S(1)}, u32[]{:S(2)}, u32[]{:S(2)}) %collective-permute-start.10) | collective-permute-done | bytes 1048608 | tf_op jit(solution)/shard_map/ppermute | solution.py:14
  289.3 2.6 collective-permute-done.6.refs_4_
  292.1 1.3 pad_maximum_fusion
  293.4 1.3 collective-permute-start.13
  294.8 8.5 %fusion.6 = f32[512,512]{1,0:T(8,128)S(1)} fusion(bf16[512,7168]{1,0:T(8,128)(2,1)} %add_convert_fusion.1.refs_0_, bf16[512,7168]{1,0:T(8,128)(2,1)} %collective-permute-done.8.refs_3_), kind=kOutput, calls=%fused_computation.68 | convolution fusion | flops 3758096384 | bytes 15728640 | tf_op jit(solution)/shard_map/dot_general | solution.py:34
  303.5 14.6 %shard_map.69 = f32[4,512,256]{2,1,0:T(8,128)S(1)} custom-call(bf16[512,7168]{1,0:T(8,128)(2,1)} %add_convert_fusion.1.refs_0_, bf16[512,7168]{1,0:T(8,128)(2,1)} %collective-permute-done.5.refs_1_, bf16[512,7168]{1,0:T(8,128)(2,1)} %add_convert_fusion.refs_2_, bf16[512,7168]{1,0:T(8,128)(2,1)} %collective-permute-done.8.refs_3_, ...), custom_call_target="tpu_custom_call" | custom-call | flops 8455716864 | bytes 38797312 | tf_op jit(solution)/shard_map/pallas_call | solution.py:61
  318.1 10.5 %collective-permute-done.13 = bf16[3,512,512]{2,1,0:T(8,128)(2,1)} collective-permute-done((bf16[3,512,512]{2,1,0:T(8,128)(2,1)}, bf16[3,512,512]{2,1,0:T(8,128)(2,1)}, u32[]{:S(2)}, u32[]{:S(2)}) %collective-permute-start.13) | collective-permute-done | bytes 1572896 | tf_op jit(solution)/shard_map/ppermute | solution.py:23
  328.6 3.2 convert_add_fusion.4
  331.8 2.6 collective-permute-done.12.refs_4_
  334.5 1.3 pad_maximum_fusion.1
  335.8 1.6 collective-permute-start.17
  337.6 0.4 collective-permute-start.19
  338.0 1.5 collective-permute-start.20
  339.5 14.1 %shard_map.70 = f32[4,512,128]{2,1,0:T(8,128)S(1)} custom-call(bf16[512,7168]{1,0:T(8,128)(2,1)} %add_convert_fusion.1.refs_0_, bf16[512,7168]{1,0:T(8,128)(2,1)} %collective-permute-done.5.refs_1_, bf16[512,7168]{1,0:T(8,128)(2,1)} %add_convert_fusion.refs_2_, bf16[512,7168]{1,0:T(8,128)(2,1)} %collective-permute-done.8.refs_3_, ...), custom_call_target="tpu_custom_call" | custom-call | flops 4227858432 | bytes 35913728 | tf_op jit(solution)/shard_map/pallas_call | solution.py:61
  353.6 16.6 %collective-permute-done.17 = bf16[3,512,512]{2,1,0:T(8,128)(2,1)} collective-permute-done((bf16[3,512,512]{2,1,0:T(8,128)(2,1)}, bf16[3,512,512]{2,1,0:T(8,128)(2,1)}, u32[]{:S(2)}, u32[]{:S(2)}) %collective-permute-start.17) | collective-permute-done | bytes 1572896 | tf_op jit(solution)/shard_map/ppermute | solution.py:23
  370.2 3.2 convert_add_fusion
  373.4 5.3 %collective-permute-done.11.refs_4_ = bf16[128,7168]{1,0:T(8,128)(2,1)S(1)} collective-permute-done((bf16[128,7168]{1,0:T(8,128)(2,1)S(1)}, bf16[128,7168]{1,0:T(8,128)(2,1)S(1)}, u32[]{:S(2)}, u32[]{:S(2)}) %collective-permute-start.11) | collective-permute-done | bytes 1835040 | tf_op jit(solution)/shard_map/ppermute | solution.py:19
  378.9 1.3 pad_maximum_fusion.2
  380.2 0.3 collective-permute-start.21
  380.7 0.8 collective-permute-start.23
  381.5 1.1 collective-permute-start.24
  382.6 14.1 %shard_map.71 = f32[4,512,128]{2,1,0:T(8,128)S(1)} custom-call(bf16[512,7168]{1,0:T(8,128)(2,1)} %add_convert_fusion.1.refs_0_, bf16[512,7168]{1,0:T(8,128)(2,1)} %collective-permute-done.5.refs_1_, bf16[512,7168]{1,0:T(8,128)(2,1)} %add_convert_fusion.refs_2_, bf16[512,7168]{1,0:T(8,128)(2,1)} %collective-permute-done.8.refs_3_, ...), custom_call_target="tpu_custom_call" | custom-call | flops 4227858432 | bytes 35913728 | tf_op jit(solution)/shard_map/pallas_call | solution.py:61
  396.8 0.9 pad_maximum_fusion.4
  397.7 1.7 collective-permute-start.25
  399.7 0.3 collective-permute-start.27
  400.0 1.5 collective-permute-start.28
  401.5 4.4 %collective-permute-done.27.refs_2_ = bf16[512,128]{1,0:T(8,128)(2,1)S(1)} collective-permute-done((bf16[512,128]{1,0:T(8,128)(2,1)S(1)}, bf16[512,128]{1,0:T(8,128)(2,1)S(1)}, u32[]{:S(2)}, u32[]{:S(2)}) %collective-permute-start.27) | collective-permute-done | bytes 131104 | tf_op jit(solution)/shard_map/ppermute | solution.py:14
  406.0 1.9 collective-permute-done.28.refs_3_
  407.9 0.9 pad_maximum_fusion.5
  409.0 0.6 pad_add_fusion.at_ref
  409.7 0.9 multiply_add_fusion
  410.6 4.0 collective-permute-done.25.refs_16_
  414.6 0.8 copy-done.18
  415.4 9.2 %shard_map.72.band = f32[512,4,512]{2,1,0:T(4,128)} custom-call(s32[2]{0:T(128)} %pad_add_fusion.at_ref, f32[512,4,512]{2,1,0:T(4,128)} %old.1, f32[512,512]{1,0:T(8,128)} %convert_add_fusion.3.refs_0_, f32[512,512]{1,0:T(8,128)} %get-tuple-element.74.refs_1_, f32[512,512]{1,0:T(8,128)} %get-tuple-element.75.refs_2_, f32[512,512]{1,0:T(8,128)} %get-tuple-element.76.refs_3_, ...), custom_call_target="tpu_custom_call" | custom-call | tf_op jit(solution)/shard_map/pallas_call | solution.py:156
  424.8 4.3 shard_map.73
  (88 shorter events, 2.4 us)
Async XLA Ops:
  7.2 73.1 %all-gather.2.cloned.1.call-start = ((), (), s32[]{:S(2)}) async-start(), calls=%async_computation | async-start | bytes 3899392 | tf_op jit(solution)/shard_map/all_gather | solution.py:211
  7.9 7.2 %collective-permute-start = (bf16[128,512]{1,0:T(8,128)(2,1)}, bf16[128,512]{1,0:T(8,128)(2,1)S(1)}, u32[]{:S(2)}, u32[]{:S(2)}) collective-permute-start(bf16[128,512]{1,0:T(8,128)(2,1)} %param.5), channel_id=1, source_target_pairs={{0,4},{2,6},{4,0},{6,2},{8,12},{10,14},{12,8},{14,10},{16,20},{18,... | collective-permute-start | bytes 393224 | tf_op jit(solution)/shard_map/ppermute | solution.py:14
  10.9 8.5 %collective-permute-start.1 = (bf16[128,512]{1,0:T(8,128)(2,1)}, bf16[128,512]{1,0:T(8,128)(2,1)S(1)}, u32[]{:S(2)}, u32[]{:S(2)}) collective-permute-start(bf16[128,512]{1,0:T(8,128)(2,1)} %param.5), channel_id=1, source_target_pairs={{0,8},{2,10},{4,12},{6,14},{8,16},{10,18},{12,20},{14,22},{16,24},... | collective-permute-start | bytes 393224 | tf_op jit(solution)/shard_map/ppermute | solution.py:19
  12.5 11.1 %collective-permute-start.2 = (bf16[128,512]{1,0:T(8,128)(2,1)}, bf16[128,512]{1,0:T(8,128)(2,1)S(1)}, u32[]{:S(2)}, u32[]{:S(2)}) collective-permute-start(bf16[128,512]{1,0:T(8,128)(2,1)} %param.5), channel_id=1, source_target_pairs={{0,16},{2,18},{4,20},{6,22},{8,24},{10,26},{12,28},{14,30},{16,0},... | collective-permute-start | bytes 393224 | tf_op jit(solution)/shard_map/ppermute | solution.py:19
  23.6 170.1 %collective-permute-start.7 = (bf16[512,7168]{1,0:T(8,128)(2,1)}, bf16[512,7168]{1,0:T(8,128)(2,1)}, u32[]{:S(2)}, u32[]{:S(2)}) collective-permute-start(bf16[512,7168]{1,0:T(8,128)(2,1)} %param.7), channel_id=1, source_target_pairs={{0,4},{2,6},{4,0},{6,2},{8,12},{10,14},{12,8},{14,10},{16,20},{18,... | collective-permute-start | bytes 22020104 | tf_op jit(solution)/shard_map/ppermute | solution.py:14
  25.1 13.6 %collective-permute-start.4 = (bf16[4,128,512]{2,1,0:T(8,128)(2,1)S(1)}, bf16[4,128,512]{2,1,0:T(8,128)(2,1)S(1)}, u32[]{:S(2)}, u32[]{:S(2)}) collective-permute-start(bf16[4,128,512]{2,1,0:T(8,128)(2,1)S(1)} %pad_maximum_fusion.3), channel_id=1, source_target_pairs={{0,1},{1,0},{2,3},{3,2},{4,5},{5,4},{6,7},{7,6},{8,9},{9,8},{10,11... | collective-permute-start | bytes 1572872 | tf_op jit(solution)/shard_map/ppermute | solution.py:23
  26.7 180.2 %collective-permute-start.3 = (bf16[512,7168]{1,0:T(8,128)(2,1)}, bf16[512,7168]{1,0:T(8,128)(2,1)}, u32[]{:S(2)}, u32[]{:S(2)}) collective-permute-start(bf16[512,7168]{1,0:T(8,128)(2,1)} %param.7), channel_id=1, source_target_pairs={{0,8},{2,10},{4,12},{6,14},{8,16},{10,18},{12,20},{14,22},{16,24},... | collective-permute-start | bytes 22020104 | tf_op jit(solution)/shard_map/ppermute | solution.py:19
  80.2 113.4 %copy-start = (bf16[256,7168]{1,0:T(8,128)(2,1)S(1)}, bf16[256,7168]{1,0:T(8,128)(2,1)}, u32[]{:S(2)}) copy-start(bf16[256,7168]{1,0:T(8,128)(2,1)} %all-gather.2.cloned.1.call-done.refs_6_) | copy-start | bytes 11010052
  89.6 117.3 %collective-permute-start.5 = (bf16[512,7168]{1,0:T(8,128)(2,1)}, bf16[512,7168]{1,0:T(8,128)(2,1)}, u32[]{:S(2)}, u32[]{:S(2)}) collective-permute-start(bf16[512,7168]{1,0:T(8,128)(2,1)} %add_convert_fusion.1.refs_0_), channel_id=1, source_target_pairs={{0,2},{2,0},{4,6},{6,4},{8,10},{10,8},{12,14},{14,12},{16,18},{18,... | collective-permute-start | bytes 22020104 | tf_op jit(solution)/shard_map/ppermute | solution.py:14
  201.9 32.9 %collective-permute-start.8 = (bf16[512,7168]{1,0:T(8,128)(2,1)}, bf16[512,7168]{1,0:T(8,128)(2,1)}, u32[]{:S(2)}, u32[]{:S(2)}) collective-permute-start(bf16[512,7168]{1,0:T(8,128)(2,1)} %add_convert_fusion.refs_2_), channel_id=1, source_target_pairs={{0,2},{2,0},{4,6},{6,4},{8,10},{10,8},{12,14},{14,12},{16,18},{18,... | collective-permute-start | bytes 22020104 | tf_op jit(solution)/shard_map/ppermute | solution.py:14
  209.2 82.8 %collective-permute-start.6 = (bf16[256,7168]{1,0:T(8,128)(2,1)S(1)}, bf16[256,7168]{1,0:T(8,128)(2,1)S(1)}, u32[]{:S(2)}, u32[]{:S(2)}) collective-permute-start(bf16[256,7168]{1,0:T(8,128)(2,1)S(1)} %slice.66), channel_id=1, source_target_pairs={{0,8},{2,10},{4,12},{6,14},{8,16},{10,18},{12,20},{14,22},{16,24},... | collective-permute-start | bytes 11010056 | tf_op jit(solution)/shard_map/ppermute | solution.py:19
  218.8 55.5 %collective-permute-start.15 = (bf16[1,512,512]{2,1,0:T(8,128)(2,1)}, bf16[1,512,512]{2,1,0:T(8,128)(2,1)}, u32[]{:S(2)}, u32[]{:S(2)}) collective-permute-start(bf16[1,512,512]{2,1,0:T(8,128)(2,1)} %convert_bitcast_fusion.3), channel_id=1, source_target_pairs={{0,1},{1,0},{2,3},{3,2},{4,5},{5,4},{6,7},{7,6},{8,9},{9,8},{10,11... | collective-permute-start | bytes 1572872 | tf_op jit(solution)/shard_map/ppermute | solution.py:23
  229.3 4.6 %copy-start.12 = (f32[512,512]{1,0:T(8,128)}, f32[512,512]{1,0:T(8,128)S(1)}, u32[]{:S(2)}) copy-start(f32[512,512]{1,0:T(8,128)S(1)} %fusion.3) | copy-start | bytes 3145732
  229.3 5.6 %copy-start.1 = (bf16[256,7168]{1,0:T(8,128)(2,1)S(1)}, bf16[256,7168]{1,0:T(8,128)(2,1)}, u32[]{:S(2)}) copy-start(bf16[256,7168]{1,0:T(8,128)(2,1)} %all-gather.2.cloned.1.call-done.refs_6_) | copy-start | bytes 11010052
  233.8 39.3 %collective-permute-start.16 = (f32[256,512]{1,0:T(8,128)S(1)}, f32[256,512]{1,0:T(8,128)}, u32[]{:S(2)}, u32[]{:S(2)}) collective-permute-start(f32[256,512]{1,0:T(8,128)S(1)} %constant_dynamic-slice_fusion), channel_id=1, source_target_pairs={{0,1},{1,0},{2,3},{3,2},{4,5},{5,4},{6,7},{7,6},{8,9},{9,8},{10,11... | collective-permute-start | bytes 1572872 | tf_op jit(solution)/shard_map/ppermute | solution.py:23
  263.7 12.8 %collective-permute-start.9 = (f32[512,512]{1,0:T(8,128)S(1)}, f32[512,512]{1,0:T(8,128)S(1)}, u32[]{:S(2)}, u32[]{:S(2)}) collective-permute-start(f32[512,512]{1,0:T(8,128)S(1)} %get-tuple-element.100), channel_id=1, source_target_pairs={{0,2},{2,0},{4,6},{6,4},{8,10},{10,8},{12,14},{14,12},{16,18},{18,... | collective-permute-start | bytes 3145736 | tf_op jit(solution)/shard_map/ppermute | solution.py:14
  263.7 9.4 %copy-start.13 = (f32[512,512]{1,0:T(8,128)S(1)}, f32[512,512]{1,0:T(8,128)}, u32[]{:S(2)}) copy-start(f32[512,512]{1,0:T(8,128)} %copy-done.12) | copy-start | bytes 3145732
  263.7 25.6 %collective-permute-start.10 = (f32[512,512]{1,0:T(8,128)S(1)}, f32[512,512]{1,0:T(8,128)S(1)}, u32[]{:S(2)}, u32[]{:S(2)}) collective-permute-start(f32[512,512]{1,0:T(8,128)S(1)} %get-tuple-element.99), channel_id=1, source_target_pairs={{0,4},{2,6},{4,0},{6,2},{8,12},{10,14},{12,8},{14,10},{16,20},{18,... | collective-permute-start | bytes 3145736 | tf_op jit(solution)/shard_map/ppermute | solution.py:14
  291.9 42.5 %collective-permute-start.12 = (bf16[128,7168]{1,0:T(8,128)(2,1)}, bf16[128,7168]{1,0:T(8,128)(2,1)S(1)}, u32[]{:S(2)}, u32[]{:S(2)}) collective-permute-start(bf16[128,7168]{1,0:T(8,128)(2,1)} %get-tuple-element.57), channel_id=1, source_target_pairs={{0,8},{2,10},{4,12},{6,14},{8,16},{10,18},{12,20},{14,22},{16,24},... | collective-permute-start | bytes 5505032 | tf_op jit(solution)/shard_map/ppermute | solution.py:19
  293.4 35.2 %collective-permute-start.13 = (bf16[3,512,512]{2,1,0:T(8,128)(2,1)}, bf16[3,512,512]{2,1,0:T(8,128)(2,1)}, u32[]{:S(2)}, u32[]{:S(2)}) collective-permute-start(bf16[3,512,512]{2,1,0:T(8,128)(2,1)} %pad_maximum_fusion), channel_id=1, source_target_pairs={{0,1},{1,0},{2,3},{3,2},{4,5},{5,4},{6,7},{7,6},{8,9},{9,8},{10,11... | collective-permute-start | bytes 4718600 | tf_op jit(solution)/shard_map/ppermute | solution.py:23
  303.3 28.5 %collective-permute-start.14 = (f32[512,512]{1,0:T(8,128)}, f32[512,512]{1,0:T(8,128)S(1)}, u32[]{:S(2)}, u32[]{:S(2)}) collective-permute-start(f32[512,512]{1,0:T(8,128)} %get-tuple-element.61), channel_id=1, source_target_pairs={{0,6},{2,4},{4,2},{6,0},{8,14},{10,12},{12,10},{14,8},{16,22},{18,... | collective-permute-start | bytes 3145736 | tf_op jit(solution)/shard_map/ppermute | solution.py:14
  331.8 5.6 %copy-start.8 = (bf16[128,7168]{1,0:T(8,128)(2,1)S(1)}, bf16[128,7168]{1,0:T(8,128)(2,1)}, u32[]{:S(2)}) copy-start(bf16[128,7168]{1,0:T(8,128)(2,1)} %get-tuple-element.56) | copy-start | bytes 5505028
  335.8 34.4 %collective-permute-start.17 = (bf16[3,512,512]{2,1,0:T(8,128)(2,1)}, bf16[3,512,512]{2,1,0:T(8,128)(2,1)}, u32[]{:S(2)}, u32[]{:S(2)}) collective-permute-start(bf16[3,512,512]{2,1,0:T(8,128)(2,1)} %pad_maximum_fusion.1), channel_id=1, source_target_pairs={{0,1},{1,0},{2,3},{3,2},{4,5},{5,4},{6,7},{7,6},{8,9},{9,8},{10,11... | collective-permute-start | bytes 4718600 | tf_op jit(solution)/shard_map/ppermute | solution.py:23
  337.4 41.3 %collective-permute-start.11 = (bf16[128,7168]{1,0:T(8,128)(2,1)S(1)}, bf16[128,7168]{1,0:T(8,128)(2,1)S(1)}, u32[]{:S(2)}, u32[]{:S(2)}) collective-permute-start(bf16[128,7168]{1,0:T(8,128)(2,1)S(1)} %copy-done.8), channel_id=1, source_target_pairs={{0,8},{2,10},{4,12},{6,14},{8,16},{10,18},{12,20},{14,22},{16,24},... | collective-permute-start | bytes 5505032 | tf_op jit(solution)/shard_map/ppermute | solution.py:19
  337.6 41.3 %copy-start.2 = (f32[512,256]{1,0:T(8,128)}, f32[512,256]{1,0:T(8,128)S(1)}, u32[]{:S(2)}) copy-start(f32[512,256]{1,0:T(8,128)S(1)} %get-tuple-element.80.refs_7_) | copy-start | bytes 1572868
  337.6 41.2 %collective-permute-start.18 = (f32[512,256]{1,0:T(8,128)S(1)}, f32[512,256]{1,0:T(8,128)S(1)}, u32[]{:S(2)}, u32[]{:S(2)}) collective-permute-start(f32[512,256]{1,0:T(8,128)S(1)} %get-tuple-element.104), channel_id=1, source_target_pairs={{0,2},{2,0},{4,6},{6,4},{8,10},{10,8},{12,14},{14,12},{16,18},{18,... | collective-permute-start | bytes 1572872 | tf_op jit(solution)/shard_map/ppermute | solution.py:14
  337.6 41.1 %collective-permute-start.19 = (f32[512,256]{1,0:T(8,128)S(1)}, f32[512,256]{1,0:T(8,128)S(1)}, u32[]{:S(2)}, u32[]{:S(2)}) collective-permute-start(f32[512,256]{1,0:T(8,128)S(1)} %get-tuple-element.103), channel_id=1, source_target_pairs={{0,4},{2,6},{4,0},{6,2},{8,12},{10,14},{12,8},{14,10},{16,20},{18,... | collective-permute-start | bytes 1572872 | tf_op jit(solution)/shard_map/ppermute | solution.py:14
  338.0 40.7 %collective-permute-start.20 = (f32[512,256]{1,0:T(8,128)S(1)}, f32[512,256]{1,0:T(8,128)S(1)}, u32[]{:S(2)}, u32[]{:S(2)}) collective-permute-start(f32[512,256]{1,0:T(8,128)S(1)} %get-tuple-element.102), channel_id=1, source_target_pairs={{0,6},{2,4},{4,2},{6,0},{8,14},{10,12},{12,10},{14,8},{16,22},{18,... | collective-permute-start | bytes 1572872 | tf_op jit(solution)/shard_map/ppermute | solution.py:14
  378.7 1.8 copy-start.5
  378.7 1.8 copy-start.6
  378.8 1.8 copy-start.7
  380.2 34.4 %collective-permute-start.21 = (bf16[4,512,256]{2,1,0:T(8,128)(2,1)}, bf16[4,512,256]{2,1,0:T(8,128)(2,1)}, u32[]{:S(2)}, u32[]{:S(2)}) collective-permute-start(bf16[4,512,256]{2,1,0:T(8,128)(2,1)} %pad_maximum_fusion.2), channel_id=1, source_target_pairs={{0,1},{1,0},{2,3},{3,2},{4,5},{5,4},{6,7},{7,6},{8,9},{9,8},{10,11... | collective-permute-start | bytes 3145736 | tf_op jit(solution)/shard_map/ppermute | solution.py:23
  380.6 16.2 %copy-start.3 = (f32[512,128]{1,0:T(8,128)}, f32[512,128]{1,0:T(8,128)S(1)}, u32[]{:S(2)}) copy-start(f32[512,128]{1,0:T(8,128)S(1)} %get-tuple-element.86.refs_12_) | copy-start | bytes 786436
  380.6 16.0 %collective-permute-start.22 = (f32[512,128]{1,0:T(8,128)S(1)}, f32[512,128]{1,0:T(8,128)S(1)}, u32[]{:S(2)}, u32[]{:S(2)}) collective-permute-start(f32[512,128]{1,0:T(8,128)S(1)} %get-tuple-element.114), channel_id=1, source_target_pairs={{0,2},{2,0},{4,6},{6,4},{8,10},{10,8},{12,14},{14,12},{16,18},{18,... | collective-permute-start | bytes 786440 | tf_op jit(solution)/shard_map/ppermute | solution.py:14
  380.7 16.0 %collective-permute-start.23 = (f32[512,128]{1,0:T(8,128)S(1)}, f32[512,128]{1,0:T(8,128)S(1)}, u32[]{:S(2)}, u32[]{:S(2)}) collective-permute-start(f32[512,128]{1,0:T(8,128)S(1)} %get-tuple-element.113), channel_id=1, source_target_pairs={{0,4},{2,6},{4,0},{6,2},{8,12},{10,14},{12,8},{14,10},{16,20},{18,... | collective-permute-start | bytes 786440 | tf_op jit(solution)/shard_map/ppermute | solution.py:14
  381.5 15.2 %collective-permute-start.24 = (f32[512,128]{1,0:T(8,128)S(1)}, f32[512,128]{1,0:T(8,128)S(1)}, u32[]{:S(2)}, u32[]{:S(2)}) collective-permute-start(f32[512,128]{1,0:T(8,128)S(1)} %get-tuple-element.112), channel_id=1, source_target_pairs={{0,6},{2,4},{4,2},{6,0},{8,14},{10,12},{12,10},{14,8},{16,22},{18,... | collective-permute-start | bytes 786440 | tf_op jit(solution)/shard_map/ppermute | solution.py:14
  396.6 13.1 %copy-start.17 = (f32[256,512]{1,0:T(8,128)S(1)}, f32[256,512]{1,0:T(8,128)}, u32[]{:S(2)}) copy-start(f32[256,512]{1,0:T(8,128)} %param.9) | copy-start | bytes 1572868
  396.7 13.9 %copy-start.9 = (f32[512,128]{1,0:T(8,128)}, f32[512,128]{1,0:T(8,128)S(1)}, u32[]{:S(2)}) copy-start(f32[512,128]{1,0:T(8,128)S(1)} %collective-permute-done.22.refs_13_) | copy-start | bytes 786436
  396.7 13.9 %copy-start.10 = (f32[512,128]{1,0:T(8,128)}, f32[512,128]{1,0:T(8,128)S(1)}, u32[]{:S(2)}) copy-start(f32[512,128]{1,0:T(8,128)S(1)} %collective-permute-done.23.refs_14_) | copy-start | bytes 786436
  396.7 13.9 %copy-start.11 = (f32[512,128]{1,0:T(8,128)}, f32[512,128]{1,0:T(8,128)S(1)}, u32[]{:S(2)}) copy-start(f32[512,128]{1,0:T(8,128)S(1)} %collective-permute-done.24.refs_15_) | copy-start | bytes 786436
  397.7 17.0 %collective-permute-start.25 = (bf16[4,512,128]{2,1,0:T(8,128)(2,1)}, bf16[4,512,128]{2,1,0:T(8,128)(2,1)S(1)}, u32[]{:S(2)}, u32[]{:S(2)}) collective-permute-start(bf16[4,512,128]{2,1,0:T(8,128)(2,1)} %pad_maximum_fusion.4), channel_id=1, source_target_pairs={{0,1},{1,0},{2,3},{3,2},{4,5},{5,4},{6,7},{7,6},{8,9},{9,8},{10,11... | collective-permute-start | bytes 1572872 | tf_op jit(solution)/shard_map/ppermute | solution.py:23
  399.5 2.0 collective-permute-start.26
  399.7 6.3 %collective-permute-start.27 = (bf16[512,128]{1,0:T(8,128)(2,1)S(1)}, bf16[512,128]{1,0:T(8,128)(2,1)S(1)}, u32[]{:S(2)}, u32[]{:S(2)}) collective-permute-start(bf16[512,128]{1,0:T(8,128)(2,1)S(1)} %get-tuple-element.119), channel_id=1, source_target_pairs={{0,4},{2,6},{4,0},{6,2},{8,12},{10,14},{12,8},{14,10},{16,20},{18,... | collective-permute-start | bytes 393224 | tf_op jit(solution)/shard_map/ppermute | solution.py:14
  400.0 7.9 %collective-permute-start.28 = (bf16[512,128]{1,0:T(8,128)(2,1)S(1)}, bf16[512,128]{1,0:T(8,128)(2,1)S(1)}, u32[]{:S(2)}, u32[]{:S(2)}) collective-permute-start(bf16[512,128]{1,0:T(8,128)(2,1)S(1)} %get-tuple-element.118), channel_id=1, source_target_pairs={{0,6},{2,4},{4,2},{6,0},{8,14},{10,12},{12,10},{14,8},{16,22},{18,... | collective-permute-start | bytes 393224 | tf_op jit(solution)/shard_map/ppermute | solution.py:14
  401.5 23.1 %copy-start.4 = (f32[512,128]{1,0:T(8,128)}, f32[512,128]{1,0:T(8,128)S(1)}, u32[]{:S(2)}) copy-start(f32[512,128]{1,0:T(8,128)S(1)} %slice_bitcast_fusion.22.refs_0_) | copy-start | bytes 786436
  401.5 23.1 %copy-start.14 = (bf16[512,128]{1,0:T(8,128)(2,1)}, bf16[512,128]{1,0:T(8,128)(2,1)S(1)}, u32[]{:S(2)}) copy-start(bf16[512,128]{1,0:T(8,128)(2,1)S(1)} %collective-permute-done.26.refs_1_) | copy-start | bytes 393220
  406.0 18.7 %copy-start.15 = (bf16[512,128]{1,0:T(8,128)(2,1)}, bf16[512,128]{1,0:T(8,128)(2,1)S(1)}, u32[]{:S(2)}) copy-start(bf16[512,128]{1,0:T(8,128)(2,1)S(1)} %collective-permute-done.27.refs_2_) | copy-start | bytes 393220
  407.9 16.8 %copy-start.16 = (bf16[512,128]{1,0:T(8,128)(2,1)}, bf16[512,128]{1,0:T(8,128)(2,1)S(1)}, u32[]{:S(2)}) copy-start(bf16[512,128]{1,0:T(8,128)(2,1)S(1)} %collective-permute-done.28.refs_3_) | copy-start | bytes 393220
  408.8 16.0 %collective-permute-start.29 = (bf16[4,512,128]{2,1,0:T(8,128)(2,1)}, bf16[4,512,128]{2,1,0:T(8,128)(2,1)}, u32[]{:S(2)}, u32[]{:S(2)}) collective-permute-start(bf16[4,512,128]{2,1,0:T(8,128)(2,1)} %pad_maximum_fusion.5), channel_id=1, source_target_pairs={{0,1},{1,0},{2,3},{3,2},{4,5},{5,4},{6,7},{7,6},{8,9},{9,8},{10,11... | collective-permute-start | bytes 1572872 | tf_op jit(solution)/shard_map/ppermute | solution.py:23
  414.6 0.8 copy-start.18
Sparse Core Ops, SparseCore 0:
  10.3 69.9 all-gather.1
